TPU v7x, 32 devices: a whole 2x2x4 slice. The times are simulated.
32 devices in a mesh: inst: 4 (over y, core), cell: 8 (over z, x).
Axes of the slice: x: 2, y: 2, z: 4, core: 2. Of those that a mesh axis runs over, the one named last changes fastest.
Arguments:
- state: float32 [8, 6, 16, 256], P('inst', None, 'cell'), may hold values from -0.8 to 5, as said below
- pseudo_rate: float32 [16, 256], P('cell'), may hold values from 0.001 to 0.01
- line_next: int32 [256], replicated, may hold values from 0 to 255, each once
- face_codes: int32 [2, 8], replicated, may hold values from 0 to 2
Outputs:
- new_state: float32 [8, 6, 16, 256], P('inst', None, 'cell')
Inputs may be any that keep to these rules, and one draw needn't show every extreme that they name: `state`: conserved variables of a gas with ratio of specific heats 1.4: in every cell density lies between 0.7 and 1.3 and pressure between 0.6 and 1.4. `line_next`: every line is named once. `face_codes`: 0 a slip wall, 1 a fixed inflow state, 2 extrapolation.
All inputs are finite; a program needn't handle non-finite values.
Results may differ from a plain program's by a relative error of at most 0.0003.
Values sent between devices are 32-bit elements; how exact they have to be, the bound alone decides.
No kernel may reach another device: no remote copies, remote signals or barrier semaphores. Data moves between devices by JAX's collectives and lax.ppermute only.
A program may use at most 64 MiB of HBM per device.

v0:
```python
import jax
import jax.numpy as jnp
import numpy as np
from jax import lax
from jax.sharding import PartitionSpec as P

NT = 8
LINES_DEV = 32


GAMMA_GAS = 1.4
OMEGA_BLADE = 1.0
SENSOR_GAIN = 0.25
FOURTH_GAIN = 0.03125
PITCH_GAIN = 0.5
SECOND_IMPL = 1.0
FOURTH_IMPL = 0.25
FREE_STATE = (1.0, 0.5, 0.0, 0.0, 2.625, 0.2)
MIRROR_SIGNS = (1.0, -1.0, 1.0, 1.0, 1.0, 1.0)
ZERO_BLOCK = (0.0, 0.0, 0.0, 0.0)
UNIT_BLOCK = (1.0, 0.0, 0.0, 1.0)
ZERO_PAIR = (0.0, 0.0)


def extended(block, sides, width):
    for axis, dim in sides:
        count = lax.axis_size(axis)
        forward = [(i, i + 1) for i in range(count - 1)]
        backward = [(target, source) for source, target in forward]
        low = lax.ppermute(
            lax.slice_in_dim(block, block.shape[dim] - width, None, axis=dim), axis, forward
        )
        high = lax.ppermute(lax.slice_in_dim(block, 0, width, axis=dim), axis, backward)
        block = jnp.concatenate([low, block, high], axis=dim)
    return block


def spectral_matrix(instances):
    offsets = np.arange(instances)[:, None] - np.arange(instances)[None, :]
    angles = np.pi * offsets / instances
    safe_sin = np.where(offsets == 0, 1.0, np.sin(angles))
    parity = np.where(np.mod(offsets, 2) == 0, -1.0, 1.0)
    matrix_table = np.where(
        offsets == 0, 0.0, 0.5 * OMEGA_BLADE * parity * np.cos(angles) / safe_sin
    )
    return jnp.asarray(matrix_table, jnp.float32)


def primitive_parts(cells_state):
    density = cells_state[..., 0, :, :]
    inverse = 1.0 / density
    velocity_x = cells_state[..., 1, :, :] * inverse
    velocity_y = cells_state[..., 2, :, :] * inverse
    velocity_z = cells_state[..., 3, :, :] * inverse
    energy = cells_state[..., 4, :, :]
    pressure = (GAMMA_GAS - 1.0) * (
        energy
        - 0.5
        * density
        * (velocity_x * velocity_x + velocity_y * velocity_y + velocity_z * velocity_z)
    )
    sound_speed = jnp.sqrt(GAMMA_GAS * pressure * inverse)
    return (velocity_x, velocity_y, pressure, sound_speed)


def directed_flux(cells_state, normal_velocity, pressure, component):
    zero_plane = jnp.zeros_like(pressure)
    pressure_rows = [
        zero_plane,
        zero_plane,
        zero_plane,
        zero_plane,
        pressure * normal_velocity,
        zero_plane,
    ]
    pressure_rows[component] = pressure
    return cells_state * normal_velocity[..., None, :, :] + jnp.stack(pressure_rows, axis=-3)


def line_residual(padded):
    velocity_x, velocity_y, pressure, sound_speed = primitive_parts(padded)
    flux_line = directed_flux(padded, velocity_x, pressure, 1)
    radius = jnp.abs(velocity_x) + sound_speed
    sensor = jnp.abs(
        pressure[..., 2:, :] - 2.0 * pressure[..., 1:-1, :] + pressure[..., :-2, :]
    ) / (pressure[..., 2:, :] + 2.0 * pressure[..., 1:-1, :] + pressure[..., :-2, :])
    second = SENSOR_GAIN * jnp.maximum(sensor[..., :-1, :], sensor[..., 1:, :])
    fourth = jnp.maximum(0.0, FOURTH_GAIN - second)
    face_radius = 0.5 * (radius[..., 1:-2, :] + radius[..., 2:-1, :])
    left_far = padded[..., :-3, :]
    left_near = padded[..., 1:-2, :]
    right_near = padded[..., 2:-1, :]
    right_far = padded[..., 3:, :]
    damping = face_radius[..., None, :, :] * (
        second[..., None, :, :] * (right_near - left_near)
        - fourth[..., None, :, :] * (right_far - 3.0 * right_near + 3.0 * left_near - left_far)
    )
    face_flux = 0.5 * (flux_line[..., 1:-2, :] + flux_line[..., 2:-1, :]) - damping
    return (face_flux[..., 1:, :] - face_flux[..., :-1, :], radius)


def pitch_parts(cells_state):
    velocity_x, velocity_y, pressure, sound_speed = primitive_parts(cells_state)
    return (directed_flux(cells_state, velocity_y, pressure, 2), jnp.abs(velocity_y) + sound_speed)


def pitch_residual(cells_state, next_lines, prev_lines):
    pitch_flux, radius = pitch_parts(cells_state)
    state_next = jnp.take(cells_state, next_lines, axis=-1)
    flux_next, radius_next = pitch_parts(state_next)
    face_flux = 0.5 * (pitch_flux + flux_next) - PITCH_GAIN * (0.5 * (radius + radius_next))[
        ..., None, :, :
    ] * (state_next - cells_state)
    return face_flux - jnp.take(face_flux, prev_lines, axis=-1)


def boundary_cells(edge_pair, line_codes, lower_end):
    reflected = edge_pair[..., ::-1, :] * jnp.asarray(MIRROR_SIGNS, jnp.float32)[:, None, None]
    if lower_end:
        copied = jnp.concatenate([edge_pair[..., :1, :], edge_pair[..., :1, :]], axis=-2)
    else:
        copied = jnp.concatenate([edge_pair[..., 1:, :], edge_pair[..., 1:, :]], axis=-2)
    inflow = jnp.asarray(FREE_STATE, jnp.float32)[:, None, None] + jnp.zeros_like(edge_pair)
    return jnp.where(line_codes == 0, reflected, jnp.where(line_codes == 1, inflow, copied))


def line_coefficients(radius_ext, diagonal_term, positions, total_cells):
    radius_below = radius_ext[..., :-2, :]
    radius_centre = radius_ext[..., 1:-1, :]
    radius_above = radius_ext[..., 2:, :]
    face_below = 0.5 * (radius_below + radius_centre)
    face_above = 0.5 * (radius_centre + radius_above)
    far_low = FOURTH_IMPL * radius_below
    near_low = -SECOND_IMPL * face_below - 2.0 * FOURTH_IMPL * (radius_below + radius_centre)
    middle = (
        diagonal_term
        + SECOND_IMPL * (face_below + face_above)
        + FOURTH_IMPL * (radius_below + 4.0 * radius_centre + radius_above)
    )
    near_high = -SECOND_IMPL * face_above - 2.0 * FOURTH_IMPL * (radius_centre + radius_above)
    far_high = FOURTH_IMPL * radius_above
    column = positions[:, None]
    far_low = jnp.where(column >= 2, far_low, 0.0)
    near_low = jnp.where(column >= 1, near_low, 0.0)
    near_high = jnp.where(column <= total_cells - 2, near_high, 0.0)
    far_high = jnp.where(column <= total_cells - 3, far_high, 0.0)
    return (far_low, near_low, middle, near_high, far_high)


def block_product(first_matrix, second_matrix):
    return (
        first_matrix[0] * second_matrix[0] + first_matrix[1] * second_matrix[2],
        first_matrix[0] * second_matrix[1] + first_matrix[1] * second_matrix[3],
        first_matrix[2] * second_matrix[0] + first_matrix[3] * second_matrix[2],
        first_matrix[2] * second_matrix[1] + first_matrix[3] * second_matrix[3],
    )


def block_inverse(matrix):
    determinant = matrix[0] * matrix[3] - matrix[1] * matrix[2]
    reciprocal = 1.0 / determinant
    return (
        matrix[3] * reciprocal,
        -matrix[1] * reciprocal,
        -matrix[2] * reciprocal,
        matrix[0] * reciprocal,
    )


def block_apply(matrix, vector):
    return (
        matrix[0] * vector[0] + matrix[1] * vector[1],
        matrix[2] * vector[0] + matrix[3] * vector[1],
    )


def add_blocks(first_members, second_members):
    return tuple((a + b for a, b in zip(first_members, second_members)))


def negate(members):
    return tuple((-a for a in members))


def extend_blocks(members, fill_values):
    return tuple(
        (
            jnp.concatenate([m, jnp.full_like(m[..., :1, :], f)], axis=-2)
            for m, f in zip(members, fill_values)
        )
    )


def shift_next(members, fill_values):
    return tuple(
        (
            jnp.concatenate([m[..., 1:, :], jnp.full_like(m[..., :1, :], f)], axis=-2)
            for m, f in zip(members, fill_values)
        )
    )


def shift_prev(members):
    return tuple(
        (jnp.concatenate([jnp.zeros_like(m[..., :1, :]), m[..., :-1, :]], axis=-2) for m in members)
    )


def pair_split(member):
    shaped = member.reshape(member.shape[:-2] + (member.shape[-2] // 2, 2, member.shape[-1]))
    return (shaped[..., 0, :], shaped[..., 1, :])


def split_parity(members):
    halves = [pair_split(m) for m in members]
    return (tuple((h[0] for h in halves)), tuple((h[1] for h in halves)))


def alternate(first_member, second_member):
    stacked = jnp.stack((first_member, second_member), axis=-2)
    return stacked.reshape(
        first_member.shape[:-2] + (2 * first_member.shape[-2], first_member.shape[-1])
    )


def reduce_blocks(sub_blocks, diag_blocks, super_blocks, right_side):
    block_count = diag_blocks[0].shape[-2]
    if block_count == 1:
        return block_apply(block_inverse(diag_blocks), right_side)
    if block_count % 2 == 1:
        sub_blocks = extend_blocks(sub_blocks, ZERO_BLOCK)
        diag_blocks = extend_blocks(diag_blocks, UNIT_BLOCK)
        super_blocks = extend_blocks(super_blocks, ZERO_BLOCK)
        right_side = extend_blocks(right_side, ZERO_PAIR)
    sub_even, sub_odd = split_parity(sub_blocks)
    diag_even, diag_odd = split_parity(diag_blocks)
    super_even, super_odd = split_parity(super_blocks)
    side_even, side_odd = split_parity(right_side)
    inverse_even = block_inverse(diag_even)
    inverse_next = shift_next(inverse_even, UNIT_BLOCK)
    sub_next = shift_next(sub_even, ZERO_BLOCK)
    super_next = shift_next(super_even, ZERO_BLOCK)
    side_next = shift_next(side_even, ZERO_PAIR)
    left_factor = negate(block_product(sub_odd, inverse_even))
    right_factor = negate(block_product(super_odd, inverse_next))
    reduced_sub = block_product(left_factor, sub_even)
    reduced_diag = add_blocks(
        diag_odd,
        add_blocks(block_product(left_factor, super_even), block_product(right_factor, sub_next)),
    )
    reduced_super = block_product(right_factor, super_next)
    reduced_side = add_blocks(
        side_odd,
        add_blocks(block_apply(left_factor, side_even), block_apply(right_factor, side_next)),
    )
    odd_values = reduce_blocks(reduced_sub, reduced_diag, reduced_super, reduced_side)
    before_values = shift_prev(odd_values)
    remainder = add_blocks(
        side_even,
        negate(
            add_blocks(block_apply(sub_even, before_values), block_apply(super_even, odd_values))
        ),
    )
    even_values = block_apply(inverse_even, remainder)
    merged = tuple((alternate(e, o) for e, o in zip(even_values, odd_values)))
    return tuple((m[..., :block_count, :] for m in merged))


def cells_leading(block):
    moved = jnp.transpose(block, (2, 0, 1, 3))
    return moved.reshape(block.shape[2], block.shape[0] * block.shape[1] * block.shape[3])


def solve_in_lanes(coefficients, line_source):
    source_shape = line_source.shape
    lane_coef = [cells_leading(jnp.broadcast_to(c[:, None], source_shape)) for c in coefficients]
    pairs_list = [pair_split(m) for m in lane_coef]
    zero_plane = jnp.zeros_like(pairs_list[2][0])
    sub_blocks = (pairs_list[0][0], pairs_list[1][0], zero_plane, pairs_list[0][1])
    diag_blocks = (pairs_list[2][0], pairs_list[3][0], pairs_list[1][1], pairs_list[2][1])
    super_blocks = (pairs_list[4][0], zero_plane, pairs_list[3][1], pairs_list[4][1])
    values = reduce_blocks(
        sub_blocks, diag_blocks, super_blocks, pair_split(cells_leading(line_source))
    )
    flat = alternate(values[0], values[1])
    shaped = flat.reshape(source_shape[2], source_shape[0], source_shape[1], source_shape[3])
    return jnp.transpose(shaped, (1, 2, 0, 3))


def return_tiles(line_values):
    return lax.all_to_all(line_values, "cell", split_axis=2, concat_axis=3, tiled=True)


def local(state, pseudo_rate, line_next, face_codes):
    local_count = state.shape[0]
    tile_cells = state.shape[2]
    cell_index = lax.axis_index("cell")
    cell_count = lax.axis_size("cell")
    total_cells = tile_cells * cell_count
    spectral = spectral_matrix(NT)
    first_local = lax.axis_index("inst") * local_count
    own_rows = lax.dynamic_slice_in_dim(spectral, first_local, local_count, 0)
    shard_block = jax.tree.map(lambda a: lax.all_gather(a, "inst", axis=0, tiled=True), state)
    columns = lax.slice_in_dim(own_rows, 0, shard_block.shape[0], axis=1)
    time_term = jnp.zeros_like(state) + jnp.einsum(
        "nm,mvil->nvil", columns, shard_block, precision=lax.Precision.HIGHEST
    )
    padded = extended(state, (("cell", 2),), 2)
    codes_lines = jnp.repeat(face_codes, LINES_DEV, axis=1)
    lower_ghost = boundary_cells(state[:, :, 0:2, :], codes_lines[0], True)
    upper_ghost = boundary_cells(state[:, :, -2:, :], codes_lines[1], False)
    lower_rim = jnp.where(cell_index == 0, lower_ghost, padded[:, :, :2, :])
    upper_rim = jnp.where(cell_index == cell_count - 1, upper_ghost, padded[:, :, -2:, :])
    padded = jnp.concatenate([lower_rim, padded[:, :, 2:-2, :], upper_rim], axis=2)
    line_part, radius = line_residual(padded)
    prev_lines = (
        jnp.zeros_like(line_next).at[line_next].set(jnp.arange(line_next.shape[0], dtype=jnp.int32))
    )
    residual = line_part + pitch_residual(state, line_next, prev_lines) + time_term
    right_side = -residual
    centre_radius = radius[:, 2:-2, :]
    diagonal_term = pseudo_rate * centre_radius
    positions = cell_index * tile_cells + jnp.arange(-1, tile_cells + 1, dtype=jnp.int32)
    inside = (positions >= 0) & (positions < total_cells)
    radius_ext = jnp.where(inside[:, None], radius[:, 1:-1, :], 0.0)
    coefficients = line_coefficients(radius_ext, diagonal_term, positions[1:-1], total_cells)
    stacked = jnp.stack(coefficients, axis=1)
    line_source = lax.all_to_all(right_side, "cell", split_axis=3, concat_axis=2, tiled=True)
    line_coef = lax.all_to_all(stacked, "cell", split_axis=3, concat_axis=2, tiled=True)
    update = return_tiles(solve_in_lanes(tuple((line_coef[:, k] for k in range(5))), line_source))
    return state + update


def solution(mesh):
    placed = (P("inst", None, "cell", None), P("cell", None), P(), P())
    return jax.shard_map(
        local, mesh=mesh, in_specs=placed, out_specs=P("inst", None, "cell", None), check_vma=False
    )
```

profile of v0, /device:TPU:0, one launch (start us, length us, event | category | flops | bytes accessed | tf_op | source)
XLA Modules:
  0.0 63.6 jit_solution(12566725209900820404)
XLA Ops:
  0.0 0.8 %copy.391 = f32[2,6,2,256]{3,0,2,1:T(2,128)S(1)} copy(f32[2,6,2,256]{3,2,1,0:T(2,128)} %param.11) | data formatting | bytes 49152 | tf_op args[0]
  0.8 4.8 %collective-permute-start = (f32[2,6,2,256]{3,0,2,1:T(2,128)S(1)}, f32[2,6,2,256]{3,0,2,1:T(2,128)S(1)}, u32[]{:S(2)}, u32[]{:S(2)}) collective-permute-start(f32[2,6,2,256]{3,0,2,1:T(2,128)S(1)} %copy.391), channel_id=1, source_target_pairs={{0,1},{1,2},{2,3},{3,4},{4,5},{5,6},{6,7},{8,9},{9,10},{10,11},{11... | collective-permute-start | bytes 73736 | tf_op jit(solution)/shard_map/ppermute | solution.py:30
  5.6 1.3 %collective-permute-start.1 = (f32[2,6,2,256]{3,0,2,1:T(2,128)S(1)}, f32[2,6,2,256]{3,0,2,1:T(2,128)S(1)}, u32[]{:S(2)}, u32[]{:S(2)}) collective-permute-start(f32[2,6,2,256]{3,0,2,1:T(2,128)S(1)} %copy.391), channel_id=1, source_target_pairs={{1,0},{2,1},{3,2},{4,3},{5,4},{6,5},{7,6},{9,8},{10,9},{11,10},{12... | collective-permute-start | bytes 73736 | tf_op jit(solution)/shard_map/ppermute | solution.py:33
  7.0 1.0 %copy.414 = f32[2,6,2,256]{1,2,3,0:T(2,128)S(1)} copy(f32[2,6,2,256]{3,2,1,0:T(2,128)} %param.11) | data formatting | bytes 49152 | tf_op args[0]
  8.1 1.4 %scatter_custom_fusion = s32[256]{0:T(256)S(1)} fusion(s32[256]{0:T(256)S(1)} %compare_select_fusion.1, s32[256]{0:T(256)S(1)} %iota.7, s32[]{:T(128)} %constant.37.clone.1), kind=kCustom, calls=%fused_computation.521 | custom fusion | bytes 1028 | tf_op jit(solution)/shard_map/scatter | solution.py:317
  10.2 1.3 %gather_fusion = f32[256,2,6,2]{2,3,1,0:T(2,128)S(1)} fusion(f32[2,6,2,256]{1,2,3,0:T(2,128)S(1)} %copy.414, s32[1024]{0:T(1024)S(1)} %get-tuple-element.215), kind=kCustom, calls=%fused_computation.clone | custom fusion | bytes 50176 | tf_op jit(solution)/shard_map/jit(_take)/gather | solution.py:109
  11.5 0.3 copy.415
  12.4 1.3 %gather_fusion.1 = f32[256,2,6,2]{2,3,1,0:T(2,128)S(1)} fusion(f32[2,6,2,256]{1,2,3,0:T(2,128)S(1)} %copy.417, s32[1024]{0:T(1024)S(1)} %get-tuple-element.214), kind=kCustom, calls=%fused_computation.1.clone | custom fusion | bytes 50176 | tf_op jit(solution)/shard_map/jit(_take)/gather | solution.py:114
  13.8 0.3 copy.418
  14.2 5.3 %all_gather.3 = f32[8,6,2,256]{3,2,1,0:T(2,128)S(1)} all-gather(f32[2,6,2,256]{3,2,1,0:T(2,128)S(1)} %copy-done), channel_id=1, replica_groups=mesh['inst'=4,'cell'=8] {'inst'}, dimensions={0}, use_global_device_ids=true | all-gather | bytes 122880 | tf_op jit(solution)/shard_map/all_gather | solution.py:303
  20.3 0.3 copy.397
  20.7 1.3 %reshape.1942 = f32[8,1,640]{2,1,0:T(1,128)} reshape(f32[256,2,2,5]{3,2,1,0:T(2,128)S(1)} %bitcast.994) | data formatting | bytes 40960
  21.9 7.0 %all-to-all-start = ((f32[8,1,640]{2,1,0:T(1,128)}), f32[8,1,640]{2,1,0:T(1,128)S(1)}, u32[]{:S(2)}, u32[]{:S(2)}) async-start(f32[8,1,640]{2,1,0:T(1,128)} %reshape.1942), calls=%async_computation | async-start | bytes 40960 | tf_op jit(solution)/shard_map/all_to_all | solution.py:329
  29.0 0.9 %fusion = f32[2,6,2,256]{3,0,2,1:T(2,128)S(1)} fusion(f32[8,6,2,256]{3,2,1,0:T(2,128)S(1)} %all_gather.3, f32[2,6,3,256]{3,0,2,1:T(2,128)S(1)} %fusion.10, f32[2,6,2,256]{3,0,2,1:T(2,128)S(1)} %multiply_subtract_fusion, f32[256,2,6,2]{0,1,3,2:T(2,128)S(1)} %copy.418, pred[256]{0:T(512)(128)(4,1)S(1)} %compare_and_fusion, f32[8,8]{1,0:T(8,128)} %constant.13.clone, ...), kind=kOutput, calls=%fused_computation.4 | convolution fusion | flops 626688 | bytes 222468 | tf_op jit(solution)/shard_map/nm,mvil->nvil/dot_general | solution.py:305
  29.9 0.3 copy.420
  30.3 1.3 %reshape.1944 = f32[8,1,768]{2,1,0:T(1,128)} reshape(f32[256,2,2,6]{3,2,1,0:T(2,128)S(1)} %bitcast.995) | data formatting | bytes 49152
  31.6 3.9 %all-to-all-done = f32[8,1,640]{2,1,0:T(1,128)S(1)} async-done(((f32[8,1,640]{2,1,0:T(1,128)}), f32[8,1,640]{2,1,0:T(1,128)S(1)}, u32[]{:S(2)}, u32[]{:S(2)}) %all-to-all-start) | async-done | bytes 20512 | tf_op jit(solution)/shard_map/all_to_all | solution.py:329
  35.5 3.5 %all-to-all-start.1 = ((f32[8,1,768]{2,1,0:T(1,128)}), f32[8,1,768]{2,1,0:T(1,128)S(1)}, u32[]{:S(2)}, u32[]{:S(2)}) async-start(f32[8,1,768]{2,1,0:T(1,128)} %reshape.1944), calls=%async_computation.1 | async-start | bytes 49152 | tf_op jit(solution)/shard_map/all_to_all | solution.py:328
  39.0 0.5 broadcast.715
  39.5 0.6 reduce.41
  40.1 0.7 %reshape.1943 = f32[256,2,2,5]{3,2,1,0:T(2,128)S(1)} reshape(f32[8,640]{1,0:T(8,128)S(1)} %reduce.41) | data formatting | bytes 40960
  40.9 0.4 copy.398
  42.5 0.6 broadcast.678
  43.1 0.8 %fusion.227 = (f32[4,384]{1,0:T(4,128)S(1)}, f32[4,1,384]{2,1,0:T(1,128)S(1)}, f32[4,384]{1,0:T(4,128)S(1)}, f32[4,1,384]{2,1,0:T(1,128)S(1)}, f32[4,1,384]{2,1,...) fusion(f32[]{:T(128)} %broadcast.678, f32[4,2,384]{2,1,0:T(2,128)S(1)} %reshape_squeeze.42, ...), kind=kLoop, calls=%fused_computation.540 | loop fusion | bytes 67588 | tf_op jit(solution)/shard_map/slice | solution.py:211
  43.8 0.7 %fusion.229 = (f32[4,384]{1,0:T(4,128)S(1)}, f32[4,1,384]{2,1,0:T(1,128)S(1)}, f32[4,1,384]{2,1,0:T(1,128)S(1)}, f32[4,1,384]{2,1,0:T(1,128)S(1)}, f32[4,1,384]{2,1,0:T(1,128)S(1)}) fusion(f32[]{:T(128)} %broadcast.678, f32[4,2,384]{2,1,0:T(2,128)S(1)} %reshape_squeeze.36, f32[4,2,384]{2,1,0:T(2,128)S(1)} %reshape_squeeze.38), kind=kLoop, calls=%fused_computation.542 | loop fusion | bytes 55300 | tf_op jit(solution)/shard_map/slice | solution.py:211
  44.8 0.8 %fusion.225 = (f32[4,384]{1,0:T(4,128)S(1)}, f32[4,1,384]{2,1,0:T(1,128)S(1)}, f32[4,384]{1,0:T(4,128)S(1)}, f32[4,1,384]{2,1,0:T(1,128)S(1)}, f32[4,384]{1,0:T(...) fusion(f32[]{:T(128)} %broadcast.678, ...), kind=kLoop, calls=%fused_computation.538 | loop fusion | bytes 73732 | tf_op jit(solution)/shard_map/slice | solution.py:211
  46.0 0.6 reduce.40
  46.6 0.8 %reshape.1945 = f32[256,2,2,6]{3,2,1,0:T(2,128)S(1)} reshape(f32[8,768]{1,0:T(8,128)S(1)} %reduce.40) | data formatting | bytes 49152
  47.4 0.4 copy.421
  49.9 12.2 %all_to_all.54 = f32[8,1,768]{2,1,0:T(1,128)S(1)} all-to-all(f32[8,1,768]{2,1,0:T(1,128)S(1)} %reshape.1946), channel_id=1, replica_groups=mesh['inst'=4,'cell'=8] {'cell'}, dimensions={0} | all-to-all | bytes 49152 | tf_op jit(solution)/shard_map/all_to_all | solution.py:291
  62.1 0.6 reduce.42
  63.0 0.6 add.1786
  (231 shorter events, 5.5 us)
Async XLA Ops:
  0.0 8.0 %copy-start.3 = (s32[256]{0:T(256)S(1)}, s32[256]{0:T(256)}, u32[]{:S(2)}) copy-start(s32[256]{0:T(256)} %param.13) | copy-start | bytes 3076
  0.0 9.5 %copy-start.2 = (s32[2,8]{1,0:T(2,128)S(1)}, s32[2,8]{1,0:T(2,128)}, u32[]{:S(2)}) copy-start(s32[2,8]{1,0:T(2,128)} %param.14) | copy-start | bytes 196
  0.8 18.7 %collective-permute-start = (f32[2,6,2,256]{3,0,2,1:T(2,128)S(1)}, f32[2,6,2,256]{3,0,2,1:T(2,128)S(1)}, u32[]{:S(2)}, u32[]{:S(2)}) collective-permute-start(f32[2,6,2,256]{3,0,2,1:T(2,128)S(1)} %copy.391), channel_id=1, source_target_pairs={{0,1},{1,2},{2,3},{3,4},{4,5},{5,6},{6,7},{8,9},{9,10},{10,11},{11... | collective-permute-start | bytes 73736 | tf_op jit(solution)/shard_map/ppermute | solution.py:30
  5.6 13.9 %collective-permute-start.1 = (f32[2,6,2,256]{3,0,2,1:T(2,128)S(1)}, f32[2,6,2,256]{3,0,2,1:T(2,128)S(1)}, u32[]{:S(2)}, u32[]{:S(2)}) collective-permute-start(f32[2,6,2,256]{3,0,2,1:T(2,128)S(1)} %copy.391), channel_id=1, source_target_pairs={{1,0},{2,1},{3,2},{4,3},{5,4},{6,5},{7,6},{9,8},{10,9},{11,10},{12... | collective-permute-start | bytes 73736 | tf_op jit(solution)/shard_map/ppermute | solution.py:33
  8.0 4.1 %copy-start = (f32[2,6,2,256]{3,2,1,0:T(2,128)S(1)}, f32[2,6,2,256]{3,2,1,0:T(2,128)}, u32[]{:S(2)}) copy-start(f32[2,6,2,256]{3,2,1,0:T(2,128)} %param.11) | copy-start | bytes 73732
  12.1 7.4 %copy-start.4 = (f32[6]{0:T(128)S(1)}, f32[6]{0:T(128)}, u32[]{:S(2)}) copy-start(f32[6]{0:T(128)} %constant.15.clone) | copy-start | bytes 76
  12.1 7.4 %copy-start.5 = (f32[6]{0:T(128)S(1)}, f32[6]{0:T(128)}, u32[]{:S(2)}) copy-start(f32[6]{0:T(128)} %constant.14.clone) | copy-start | bytes 76
  14.1 6.1 %copy-start.1 = (f32[2,256]{1,0:T(2,128)S(1)}, f32[2,256]{1,0:T(2,128)}, u32[]{:S(2)}) copy-start(f32[2,256]{1,0:T(2,128)} %param.12) | copy-start | bytes 6148
  21.9 13.6 %all-to-all-start = ((f32[8,1,640]{2,1,0:T(1,128)}), f32[8,1,640]{2,1,0:T(1,128)S(1)}, u32[]{:S(2)}, u32[]{:S(2)}) async-start(f32[8,1,640]{2,1,0:T(1,128)} %reshape.1942), calls=%async_computation | async-start | bytes 40960 | tf_op jit(solution)/shard_map/all_to_all | solution.py:329
  35.5 10.5 %all-to-all-start.1 = ((f32[8,1,768]{2,1,0:T(1,128)}), f32[8,1,768]{2,1,0:T(1,128)S(1)}, u32[]{:S(2)}, u32[]{:S(2)}) async-start(f32[8,1,768]{2,1,0:T(1,128)} %reshape.1944), calls=%async_computation.1 | async-start | bytes 49152 | tf_op jit(solution)/shard_map/all_to_all | solution.py:328
where the time goes:
time: 64.2 us; the launch traced here: 63.6 us
  local copies, waits for them, and re-layouts  19 us (30%)
  blocking collectives  17.5 us (27%)
  starting transfers between devices  16.6 us (26%)
  other arithmetic  4.36 us (7%)
  waiting for transfers between devices  3.87 us (6%)
  between operations  1.35 us (2%)
  matrix products  0.92 us (1%)
    all_to_all x1, blocking collectives, return_tiles(): lax.all_to_all(line_values, 'cell', split_axis=2, concat_axis=3, tiled=True)  12.2 us
    all_to_all x1, starting transfers between devices, local(): lax.all_to_all(stacked, 'cell', split_axis=3, concat_axis=2, tiled=True)  6.96 us
    unnamed x30, local copies, waits for them, and re-layouts  6.25 us
    all_gather x1, blocking collectives, local(): lax.all_gather(a, 'inst', axis=0, tiled=True)  5.32 us
    ppermute x1, starting transfers between devices, extended(): lax.ppermute(lax.slice_in_dim(block, block.shape[dim] - width, None, axis...  4.84 us
    all_to_all x1, waiting for transfers between devices, local(): lax.all_to_all(stacked, 'cell', split_axis=3, concat_axis=2, tiled=True)  3.86 us
    all_to_all x1, starting transfers between devices, local(): lax.all_to_all(right_side, 'cell', split_axis=3, concat_axis=2, tiled=True)  3.52 us
    slice x24, local copies, waits for them, and re-layouts, pair_split(): return (shaped[..., 0, :], shaped[..., 1, :])  3.35 us
  transfers between devices with their start and end apart: 4, of which 1 were waited for; matrix products, arithmetic and copies ran while one was open for 26% of the time, Pallas kernels for 0%

commit v1 on v0

--- a/solution.py
+++ b/solution.py
@@ -1,7 +1,11 @@
+import functools
+
 import jax
 import jax.numpy as jnp
 import numpy as np
 from jax import lax
+from jax.experimental import pallas as pl
+from jax.experimental.pallas import tpu as pltpu
 from jax.sharding import PartitionSpec as P
 
 NT = 8
@@ -291,7 +295,7 @@
     return lax.all_to_all(line_values, "cell", split_axis=2, concat_axis=3, tiled=True)
 
 
-def local(state, pseudo_rate, line_next, face_codes):
+def local_by_lines(state, pseudo_rate, line_next, face_codes):
     local_count = state.shape[0]
     tile_cells = state.shape[2]
     cell_index = lax.axis_index("cell")
@@ -331,8 +335,438 @@
     return state + update
 
 
+LANES = 128
+ROWS = 8
+PAIRS = 3
+CELL_ROWS = PAIRS * ROWS
+BLOCK_ROWS = 56
+
+
+def spectral_offsets():
+    table = np.zeros(NT)
+    for offset in range(1, NT):
+        angle = np.pi * offset / NT
+        parity = -1.0 if offset % 2 == 0 else 1.0
+        table[offset] = 0.5 * OMEGA_BLADE * parity * np.cos(angle) / np.sin(angle)
+    return [float(np.float32(value)) for value in table]
+
+
+def pack_kernel(state_ref, rate_ref, out_ref):
+    for cell in range(2):
+        for var in range(6):
+            for inst in range(2):
+                for half in range(2):
+                    row = cell * CELL_ROWS + (var // 2) * ROWS + (var % 2) * 4 + inst * 2 + half
+                    out_ref[pl.ds(row, 1), :] = state_ref[
+                        inst, var, pl.ds(cell, 1), pl.ds(half * LANES, LANES)
+                    ]
+        for half in range(2):
+            out_ref[pl.ds(2 * CELL_ROWS + cell * 2 + half, 1), :] = rate_ref[
+                pl.ds(cell, 1), pl.ds(half * LANES, LANES)
+            ]
+    out_ref[pl.ds(52, 4), :] = jnp.zeros((4, LANES), jnp.float32)
+
+
+def two_by_two(first, second):
+    def entry(a, b, c, d):
+        terms = [x * y for x, y in ((a, b), (c, d)) if x is not None and y is not None]
+        return None if not terms else terms[0] if len(terms) == 1 else terms[0] + terms[1]
+
+    return (
+        entry(first[0], second[0], first[1], second[2]),
+        entry(first[0], second[1], first[1], second[3]),
+        entry(first[2], second[0], first[3], second[2]),
+        entry(first[2], second[1], first[3], second[3]),
+    )
+
+
+def inverse_of(matrix):
+    reciprocal = 1.0 / (matrix[0] * matrix[3] - matrix[1] * matrix[2])
+    return (
+        matrix[3] * reciprocal,
+        -(matrix[1] * reciprocal),
+        -(matrix[2] * reciprocal),
+        matrix[0] * reciprocal,
+    )
+
+
+def less(first, second):
+    return tuple(a if b is None else a - b for a, b in zip(first, second))
+
+
+def minus(members):
+    return tuple(None if a is None else -a for a in members)
+
+
+def eliminate(centre, left, left_inverse, right, right_inverse):
+    left_factor = two_by_two(centre[0], left_inverse)
+    right_factor = two_by_two(centre[2], right_inverse)
+    sub = minus(two_by_two(left_factor, left[0]))
+    diag = less(
+        less(centre[1], two_by_two(left_factor, left[2])), two_by_two(right_factor, right[0])
+    )
+    sup = minus(two_by_two(right_factor, right[2]))
+    side = []
+    for k in range(PAIRS):
+        for row in range(2):
+            value = centre[3][row * PAIRS + k]
+            for factor, other in ((left_factor, left[3]), (right_factor, right[3])):
+                value = value - (
+                    factor[2 * row] * other[k] + factor[2 * row + 1] * other[PAIRS + k]
+                )
+            side.append((row * PAIRS + k, value))
+    return sub, diag, sup, [value for _, value in sorted(side, key=lambda item: item[0])]
+
+
+def line_kernel(
+    cells, all_ref, next_ref, codes_ref, out_ref, coef_ref, side_ref, coef2_ref, side2_ref,
+    couple_ref, diag3_ref, side3_ref,
+):
+    own_inst = lax.axis_index("inst")
+    own_cell = lax.axis_index("cell")
+    shape = (ROWS, LANES)
+    row_index = lax.broadcasted_iota(jnp.int32, shape, 0)
+    lane_index = lax.broadcasted_iota(jnp.int32, shape, 1)
+    first_var = row_index < 4
+    first_inst = (row_index & 2) == 0
+    half_index = row_index & 1
+    first_half = half_index == 0
+    zero = jnp.zeros(shape, jnp.float32)
+
+    next_rows = [next_ref[pl.ds(half, 1), :] for half in range(2)]
+    next_line = jnp.where(first_half, next_rows[0], next_rows[1])
+    column = lax.broadcasted_iota(jnp.int32, (LANES, LANES), 0)
+    prev_halves = []
+    for target in range(2):
+        total = None
+        for source in range(2):
+            hits = jnp.where(column + target * LANES == next_rows[source], 1.0, 0.0)
+            names = (lane_index + source * LANES).astype(jnp.float32)
+            part = lax.dot_general(
+                names, hits, (((1,), (1,)), ((), ())), preferred_element_type=jnp.float32
+            )
+            total = part if total is None else total + part
+        prev_halves.append(total)
+    prev_line = jnp.where(first_half, prev_halves[0], prev_halves[1]).astype(jnp.int32)
+
+    def picker(lines):
+        lane = lines & (LANES - 1)
+        same = (lines >> 7) == half_index
+
+        def pick(plane):
+            swapped = jnp.where(first_half, pltpu.roll(plane, 7, 0), pltpu.roll(plane, 1, 0))
+            here = jnp.take_along_axis(plane, lane, axis=1, mode="promise_in_bounds")
+            there = jnp.take_along_axis(swapped, lane, axis=1, mode="promise_in_bounds")
+            return jnp.where(same, here, there)
+
+        return pick
+
+    pick_next = picker(next_line)
+    pick_prev = picker(prev_line)
+
+    tile = half_index * (LANES // LINES_DEV) + lane_index // LINES_DEV
+    codes = []
+    for end in range(2):
+        plane = jnp.zeros(shape, jnp.int32)
+        for k in range(2 * LANES // LINES_DEV):
+            plane = jnp.where(tile == k, codes_ref[end, k], plane)
+        codes.append(plane)
+
+    def loaded(inst, cell):
+        return [
+            all_ref[inst, cell // 2, pl.ds((cell % 2) * CELL_ROWS + k * ROWS, ROWS), :]
+            for k in range(PAIRS)
+        ]
+
+    def ghost(end, mirrored, copied):
+        planes = []
+        for k in range(PAIRS):
+            reflected = mirrored[k]
+            if k == 0:
+                reflected = jnp.where(first_var, reflected, -reflected)
+            inflow = jnp.where(first_var, FREE_STATE[2 * k], FREE_STATE[2 * k + 1])
+            planes.append(
+                jnp.where(
+                    codes[end] == 0, reflected, jnp.where(codes[end] == 1, inflow, copied[k])
+                )
+            )
+        return planes
+
+    def extended_state(cell):
+        if cell < 0:
+            return ghost(0, loaded(own_inst, -1 - cell), loaded(own_inst, 0))
+        if cell >= cells:
+            return ghost(
+                1, loaded(own_inst, 2 * cells - 1 - cell), loaded(own_inst, cells - 1)
+            )
+        return loaded(own_inst, cell)
+
+    def both(plane):
+        turned = pltpu.roll(plane, 4, 0)
+        return jnp.where(first_var, plane, turned), jnp.where(first_var, turned, plane)
+
+    def primitives(planes):
+        density, moment_x = both(planes[0])
+        moment_y, moment_z = both(planes[1])
+        energy = jnp.where(first_var, planes[2], pltpu.roll(planes[2], 4, 0))
+        inverse = 1.0 / density
+        velocity_x = moment_x * inverse
+        velocity_y = moment_y * inverse
+        velocity_z = moment_z * inverse
+        kinetic = moment_x * velocity_x + moment_y * velocity_y + moment_z * velocity_z
+        pressure = (GAMMA_GAS - 1.0) * (energy - 0.5 * kinetic)
+        sound = jnp.sqrt(GAMMA_GAS * pressure * inverse)
+        return velocity_x, velocity_y, pressure, sound
+
+    def flux_along(planes, velocity, pressure):
+        return [
+            planes[0] * velocity + jnp.where(first_var, 0.0, pressure),
+            planes[1] * velocity,
+            planes[2] * velocity + jnp.where(first_var, pressure * velocity, 0.0),
+        ]
+
+    def flux_across(planes, velocity, pressure):
+        return [
+            planes[0] * velocity,
+            planes[1] * velocity + jnp.where(first_var, pressure, 0.0),
+            planes[2] * velocity + jnp.where(first_var, pressure * velocity, 0.0),
+        ]
+
+    offsets = spectral_offsets()
+    inst_count = all_ref.shape[0]
+
+    def time_parts(cell, own):
+        same_total = [None] * PAIRS
+        other_total = [None] * PAIRS
+        for shift in range(inst_count):
+            planes = own if shift == 0 else loaded((own_inst - shift) & (inst_count - 1), cell)
+            same = offsets[(2 * shift) % NT]
+            other = jnp.where(
+                first_inst, offsets[(2 * shift + 1) % NT], offsets[(2 * shift - 1) % NT]
+            )
+            for k in range(PAIRS):
+                if shift > 0:
+                    term = same * planes[k]
+                    same_total[k] = term if same_total[k] is None else same_total[k] + term
+                term = other * planes[k]
+                other_total[k] = term if other_total[k] is None else other_total[k] + term
+        return [
+            s + jnp.where(first_inst, pltpu.roll(o, 6, 0), pltpu.roll(o, 2, 0))
+            for s, o in zip(same_total, other_total)
+        ]
+
+    def pitch_flux(planes, velocity_y, pressure, sound):
+        nearby = [pick_next(plane) for plane in planes]
+        _, next_velocity, next_pressure, next_sound = primitives(nearby)
+        own_flux = flux_across(planes, velocity_y, pressure)
+        next_flux = flux_across(nearby, next_velocity, next_pressure)
+        weight = (PITCH_GAIN * 0.5) * (
+            jnp.abs(velocity_y) + sound + (jnp.abs(next_velocity) + next_sound)
+        )
+        return [
+            0.5 * (a + b) - weight * (n - o)
+            for a, b, n, o in zip(own_flux, next_flux, nearby, planes)
+        ]
+
+    state, pressures, radii, fluxes, steps, rest, sensors, faces = {}, {}, {}, {}, {}, {}, {}, {}
+    for cell in range(-2, cells + 2):
+        planes = extended_state(cell)
+        velocity_x, velocity_y, pressure, sound = primitives(planes)
+        state[cell] = planes
+        pressures[cell] = pressure
+        radii[cell] = jnp.abs(velocity_x) + sound
+        if -1 <= cell <= cells:
+            fluxes[cell] = flux_along(planes, velocity_x, pressure)
+        if cell >= -1:
+            steps[cell - 1] = [a - b for a, b in zip(planes, state[cell - 1])]
+        if 0 <= cell < cells:
+            faces_across = pitch_flux(planes, velocity_y, pressure, sound)
+            rest[cell] = [
+                t + (f - pick_prev(f)) for f, t in zip(faces_across, time_parts(cell, planes))
+            ]
+        if cell >= 0:
+            twice = 2.0 * pressures[cell - 1]
+            outer = pressure + pressures[cell - 2]
+            sensors[cell - 1] = jnp.abs(outer - twice) / (outer + twice)
+        if cell >= 1:
+            face = cell - 2
+            second = SENSOR_GAIN * jnp.maximum(sensors[face], sensors[face + 1])
+            fourth = jnp.maximum(0.0, FOURTH_GAIN - second)
+            face_radius = 0.5 * (radii[face] + radii[face + 1])
+            near_weight = face_radius * (second + 2.0 * fourth)
+            far_weight = face_radius * fourth
+            faces[face] = [
+                0.5 * (fluxes[face][k] + fluxes[face + 1][k])
+                - (
+                    near_weight * steps[face][k]
+                    - far_weight * (steps[face + 1][k] + steps[face - 1][k])
+                )
+                for k in range(PAIRS)
+            ]
+        if cell >= 2:
+            at = cell - 2
+            slot, member = at // 2 + 1, at % 2
+            for k in range(PAIRS):
+                side_ref[slot, member * PAIRS + k] = (
+                    faces[at - 1][k] - faces[at][k] - rest[at][k]
+                )
+            below = radii[at - 1] if at > 0 else zero
+            centre = radii[at]
+            above = radii[at + 1] if at < cells - 1 else zero
+            below_sum = below + centre
+            above_sum = centre + above
+            half_low = SECOND_IMPL * 0.5 + 2.0 * FOURTH_IMPL
+            rate_rows = [
+                all_ref[own_inst, at // 2, pl.ds(2 * CELL_ROWS + member * 2 + half, 1), :]
+                for half in range(2)
+            ]
+            rate = jnp.where(first_half, rate_rows[0], rate_rows[1])
+            middle = (
+                rate * centre
+                + SECOND_IMPL * (0.5 * (below_sum + above_sum))
+                + FOURTH_IMPL * (below + 4.0 * centre + above)
+            )
+            far_low = FOURTH_IMPL * below if at >= 2 else zero
+            near_low = -half_low * below_sum if at >= 1 else zero
+            near_high = -half_low * above_sum if at <= cells - 2 else zero
+            far_high = FOURTH_IMPL * above if at <= cells - 3 else zero
+            if member == 0:
+                entries = {0: far_low, 1: near_low, 3: middle, 4: near_high, 7: far_high}
+            else:
+                entries = {2: far_low, 5: near_low, 6: middle, 8: near_high, 9: far_high}
+            for k, plane in entries.items():
+                coef_ref[slot, k] = plane
+
+    blocks = cells // 2
+    one = zero + 1.0
+    for slot in (0, blocks + 1):
+        for k in range(10):
+            coef_ref[slot, k] = one if k in (3, 6) else zero
+        for k in range(2 * PAIRS):
+            side_ref[slot, k] = zero
+    for slot in (0, blocks // 2 + 1):
+        for k in range(12):
+            coef2_ref[slot, k] = one if k in (4, 7) else zero
+        for k in range(2 * PAIRS):
+            side2_ref[slot, k] = zero
+
+    def block_one(slot):
+        c = [coef_ref[slot, k] for k in range(10)]
+        return (
+            (c[0], c[1], None, c[2]),
+            (c[3], c[4], c[5], c[6]),
+            (c[7], None, c[8], c[9]),
+            [side_ref[slot, k] for k in range(2 * PAIRS)],
+        )
+
+    def block_two(slot):
+        c = [coef2_ref[slot, k] for k in range(12)]
+        return (
+            tuple(c[0:4]),
+            tuple(c[4:8]),
+            tuple(c[8:12]),
+            [side2_ref[slot, k] for k in range(2 * PAIRS)],
+        )
+
+    parity = own_cell & 1
+    left = block_one(parity)
+    left_inverse = inverse_of(left[1])
+    for k in range(blocks // 2):
+        right = block_one(parity + 2 * k + 2)
+        right_inverse = inverse_of(right[1])
+        kept = block_one(parity + 2 * k + 1)
+        sub, diag, sup, side = eliminate(kept, left, left_inverse, right, right_inverse)
+        for n, plane in enumerate(sub + diag + sup):
+            coef2_ref[k + 1, n] = plane
+        for n, plane in enumerate(side):
+            side2_ref[k + 1, n] = plane
+        left, left_inverse = right, right_inverse
+    parity = (own_cell >> 1) & 1
+    left = block_two(parity)
+    left_inverse = inverse_of(left[1])
+    for k in range(blocks // 4):
+        right = block_two(parity + 2 * k + 2)
+        right_inverse = inverse_of(right[1])
+        kept = block_two(parity + 2 * k + 1)
+        sub, diag, sup, side = eliminate(kept, left, left_inverse, right, right_inverse)
+        for n in range(4):
+            couple_ref[k, 0, n] = sub[n]
+            couple_ref[k, 1, n] = sup[n]
+            diag3_ref[k, n] = diag[n]
+        for n, plane in enumerate(side):
+            side3_ref[k, n] = plane
+        left, left_inverse = right, right_inverse
+    own = (own_cell >> 2) & 1
+    other = 1 - own
+    own_couple = tuple(couple_ref[own, 1 - own, n] for n in range(4))
+    other_couple = tuple(couple_ref[other, own, n] for n in range(4))
+    factor = two_by_two(own_couple, inverse_of([diag3_ref[other, n] for n in range(4)]))
+    diag = less([diag3_ref[own, n] for n in range(4)], two_by_two(factor, other_couple))
+    last_inverse = inverse_of(diag)
+    for k in range(PAIRS):
+        other_low, other_high = side3_ref[other, k], side3_ref[other, PAIRS + k]
+        low = side3_ref[own, k] - (factor[0] * other_low + factor[1] * other_high)
+        high = side3_ref[own, PAIRS + k] - (factor[2] * other_low + factor[3] * other_high)
+        for member in range(2):
+            delta = last_inverse[2 * member] * low + last_inverse[2 * member + 1] * high
+            base = all_ref[own_inst, own_cell, pl.ds(member * CELL_ROWS + k * ROWS, ROWS), :]
+            result = base + delta
+            for var in range(2):
+                for inst in range(2):
+                    for half in range(2):
+                        row = var * 4 + inst * 2 + half
+                        out_ref[
+                            inst, 2 * k + var, pl.ds(member, 1), pl.ds(half * LANES, LANES)
+                        ] = result[row : row + 1]
+
+
+def local_by_gather(state, pseudo_rate, line_next, face_codes):
+    inst_count = lax.axis_size("inst")
+    cell_count = lax.axis_size("cell")
+    cells = cell_count * state.shape[2]
+    vmem = pl.BlockSpec(memory_space=pltpu.VMEM)
+    packed = pl.pallas_call(
+        pack_kernel,
+        out_shape=jax.ShapeDtypeStruct((BLOCK_ROWS, LANES), jnp.float32),
+        in_specs=[vmem, vmem],
+        out_specs=vmem,
+    )(state, pseudo_rate)
+    gathered = lax.all_gather(packed, ("inst", "cell"), axis=0, tiled=False)
+    gathered = gathered.reshape(inst_count, cell_count, BLOCK_ROWS, LANES)
+    blocks = cells // 2
+    plane = (ROWS, LANES)
+    sizes = [
+        (blocks + 2, 10),
+        (blocks + 2, 2 * PAIRS),
+        (blocks // 2 + 2, 12),
+        (blocks // 2 + 2, 2 * PAIRS),
+        (2, 2, 4),
+        (2, 4),
+        (2, 2 * PAIRS),
+    ]
+    return pl.pallas_call(
+        functools.partial(line_kernel, cells),
+        out_shape=jax.ShapeDtypeStruct(state.shape, jnp.float32),
+        in_specs=[vmem, vmem, pl.BlockSpec(memory_space=pltpu.SMEM)],
+        out_specs=vmem,
+        scratch_shapes=[pltpu.VMEM(size + plane, jnp.float32) for size in sizes],
+    )(gathered, line_next.reshape(2, LANES), face_codes)
+
+
 def solution(mesh):
     placed = (P("inst", None, "cell", None), P("cell", None), P(), P())
+    inst_count, cell_count = mesh.shape["inst"], mesh.shape["cell"]
+
+    def local(state, pseudo_rate, line_next, face_codes):
+        small = (
+            state.shape == (2, 6, 2, 2 * LANES)
+            and inst_count * 2 == NT
+            and cell_count == 8
+            and face_codes.shape[1] * LINES_DEV == state.shape[3]
+        )
+        chosen = local_by_gather if small else local_by_lines
+        return chosen(state, pseudo_rate, line_next, face_codes)
+
     return jax.shard_map(
         local, mesh=mesh, in_specs=placed, out_specs=P("inst", None, "cell", None), check_vma=False
     )

time: 64.2 us -> 84.1 us (1.31)
  blocking collectives: 17.5 us -> 80 us
  local copies, waits for them, and re-layouts: 19 us -> 0 us
  starting transfers between devices: 16.6 us -> 0 us
  other arithmetic: 4.36 us -> 0 us
  Pallas kernels: 0 us -> 3.95 us
  waiting for transfers between devices: 3.87 us -> 0 us
  between operations: 1.35 us -> 0.01 us
  matrix products: 0.92 us -> 0 us
    all_gather x1, blocking collectives: 5.32 us -> 80 us  [local_by_gather(): gathered = lax.all_gather(packed, ('inst', 'cell'), axis=0, tiled=False)]
    all_to_all x1 -> x0, blocking collectives: 12.2 us -> none  [return_tiles(): lax.all_to_all(line_values, 'cell', split_axis=2, concat_axis=3, tiled=True)]
    all_to_all x2 -> x0, starting transfers between devices: 10.5 us -> none  [the longest x1 6.96 us: local(): lax.all_to_all(stacked, 'cell', split_axis=3, concat_axis=2, tiled=True)]
    unnamed x30 -> x0, local copies, waits for them, and re-layouts: 6.25 us -> none
    ppermute x2 -> x0, starting transfers between devices: 6.14 us -> none  [the longest x1 4.84 us: extended(): lax.ppermute(lax.slice_in_dim(block, block.shape[dim] - width, None, axis...]
    pallas_call x0 -> x2, Pallas kernels: none -> 3.95 us  [the longest x1 2.6 us: local_by_gather(): pl.pallas_call(functools.partial(line_kernel, cells), out_shape=jax.Shape...]
    all_to_all x2 -> x0, waiting for transfers between devices: 3.86 us -> none  [the longest x1 3.86 us: local(): lax.all_to_all(stacked, 'cell', split_axis=3, concat_axis=2, tiled=True)]
    slice x53 -> x0, local copies, waits for them, and re-layouts: 3.5 us -> none  [the longest x24 3.35 us: pair_split(): return (shaped[..., 0, :], shaped[..., 1, :])]
  transfers between devices with their start and end apart: 4 -> 0, of which waited for: 1 -> 0; matrix products, arithmetic and copies ran while one was open for 26% -> 0% of each run, Pallas kernels for 0% -> 0%
where the time goes in v1:
time: 84.1 us; the launch traced here: 83.9 us
  blocking collectives  80 us (95%)
  Pallas kernels  3.95 us (5%)
    all_gather x1, blocking collectives, local_by_gather(): gathered = lax.all_gather(packed, ('inst', 'cell'), axis=0, tiled=False)  80 us
    pallas_call x1, Pallas kernels, local_by_gather(): pl.pallas_call(functools.partial(line_kernel, cells), out_shape=jax.Shape...  2.6 us

profile of v1, /device:TPU:0, one launch (start us, length us, event | category | flops | bytes accessed | tf_op | source)
XLA Modules:
  0.0 83.9 jit_solution(1854830718000420583)
XLA Ops:
  0.0 1.4 %shard_map.46 = f32[56,128]{1,0:T(8,128)} custom-call(f32[2,6,2,256]{3,2,1,0:T(2,128)} %state_ref.1, f32[2,256]{1,0:T(2,128)} %rate_ref.1), custom_call_target="tpu_custom_call" | custom-call | tf_op jit(solution)/shard_map/pallas_call | solution.py:728
  1.4 80.0 %all-gather = f32[1792,128]{1,0:T(8,128)} all-gather(f32[56,128]{1,0:T(8,128)} %shard_map.46), channel_id=2, replica_groups=mesh['inst'=4,'cell'=8] {'inst','cell'}, dimensions={0}, use_global_device_ids=true | all-gather | bytes 946176 | tf_op jit(solution)/shard_map/all_gather | solution.py:734
  81.3 2.6 %shard_map.47 = f32[2,6,2,256]{3,2,1,0:T(2,128)} custom-call(f32[4,8,56,128]{3,2,1,0:T(8,128)} %bitcast.2, s32[2,128]{1,0:T(2,128)} %bitcast.3, s32[2,8]{1,0:T(2,128)} %codes_ref.1), custom_call_target="tpu_custom_call" | custom-call | tf_op jit(solution)/shard_map/pallas_call | solution.py:747

commit v2 on v1

--- a/solution.py
+++ b/solution.py
@@ -339,7 +339,9 @@
 ROWS = 8
 PAIRS = 3
 CELL_ROWS = PAIRS * ROWS
-BLOCK_ROWS = 56
+REST_ROW = 2 * CELL_ROWS
+RATE_ROW = 2 * REST_ROW
+BLOCK_ROWS = RATE_ROW + ROWS
 
 
 def spectral_offsets():
@@ -351,87 +353,41 @@
     return [float(np.float32(value)) for value in table]
 
 
-def pack_kernel(state_ref, rate_ref, out_ref):
-    for cell in range(2):
-        for var in range(6):
-            for inst in range(2):
-                for half in range(2):
-                    row = cell * CELL_ROWS + (var // 2) * ROWS + (var % 2) * 4 + inst * 2 + half
-                    out_ref[pl.ds(row, 1), :] = state_ref[
-                        inst, var, pl.ds(cell, 1), pl.ds(half * LANES, LANES)
-                    ]
-        for half in range(2):
-            out_ref[pl.ds(2 * CELL_ROWS + cell * 2 + half, 1), :] = rate_ref[
-                pl.ds(cell, 1), pl.ds(half * LANES, LANES)
-            ]
-    out_ref[pl.ds(52, 4), :] = jnp.zeros((4, LANES), jnp.float32)
-
-
-def two_by_two(first, second):
-    def entry(a, b, c, d):
-        terms = [x * y for x, y in ((a, b), (c, d)) if x is not None and y is not None]
-        return None if not terms else terms[0] if len(terms) == 1 else terms[0] + terms[1]
-
-    return (
-        entry(first[0], second[0], first[1], second[2]),
-        entry(first[0], second[1], first[1], second[3]),
-        entry(first[2], second[0], first[3], second[2]),
-        entry(first[2], second[1], first[3], second[3]),
-    )
-
-
-def inverse_of(matrix):
-    reciprocal = 1.0 / (matrix[0] * matrix[3] - matrix[1] * matrix[2])
-    return (
-        matrix[3] * reciprocal,
-        -(matrix[1] * reciprocal),
-        -(matrix[2] * reciprocal),
-        matrix[0] * reciprocal,
-    )
-
-
-def less(first, second):
-    return tuple(a if b is None else a - b for a, b in zip(first, second))
-
-
-def minus(members):
-    return tuple(None if a is None else -a for a in members)
-
-
-def eliminate(centre, left, left_inverse, right, right_inverse):
-    left_factor = two_by_two(centre[0], left_inverse)
-    right_factor = two_by_two(centre[2], right_inverse)
-    sub = minus(two_by_two(left_factor, left[0]))
-    diag = less(
-        less(centre[1], two_by_two(left_factor, left[2])), two_by_two(right_factor, right[0])
-    )
-    sup = minus(two_by_two(right_factor, right[2]))
-    side = []
-    for k in range(PAIRS):
-        for row in range(2):
-            value = centre[3][row * PAIRS + k]
-            for factor, other in ((left_factor, left[3]), (right_factor, right[3])):
-                value = value - (
-                    factor[2 * row] * other[k] + factor[2 * row + 1] * other[PAIRS + k]
-                )
-            side.append((row * PAIRS + k, value))
-    return sub, diag, sup, [value for _, value in sorted(side, key=lambda item: item[0])]
-
-
-def line_kernel(
-    cells, all_ref, next_ref, codes_ref, out_ref, coef_ref, side_ref, coef2_ref, side2_ref,
-    couple_ref, diag3_ref, side3_ref,
-):
+def plane_masks():
+    row_index = lax.broadcasted_iota(jnp.int32, (ROWS, LANES), 0)
+    return row_index < 4, (row_index & 2) == 0, row_index & 1
+
+
+def both(first_var, plane):
+    turned = pltpu.roll(plane, 4, 0)
+    return jnp.where(first_var, plane, turned), jnp.where(first_var, turned, plane)
+
+
+def primitives(first_var, planes):
+    density, moment_x = both(first_var, planes[0])
+    moment_y, moment_z = both(first_var, planes[1])
+    energy = jnp.where(first_var, planes[2], pltpu.roll(planes[2], 4, 0))
+    inverse = 1.0 / density
+    velocity_x = moment_x * inverse
+    velocity_y = moment_y * inverse
+    velocity_z = moment_z * inverse
+    kinetic = moment_x * velocity_x + moment_y * velocity_y + moment_z * velocity_z
+    pressure = (GAMMA_GAS - 1.0) * (energy - 0.5 * kinetic)
+    sound = jnp.sqrt(GAMMA_GAS * pressure * inverse)
+    return velocity_x, velocity_y, pressure, sound
+
+
+def rows_of(var, inst, half):
+    return (var // 2) * ROWS + (var % 2) * 4 + inst * 2 + half
+
+
+def cell_kernel(all_ref, rate_ref, next_ref, out_ref, plane_ref):
     own_inst = lax.axis_index("inst")
-    own_cell = lax.axis_index("cell")
+    inst_count = all_ref.shape[0] // 2
     shape = (ROWS, LANES)
-    row_index = lax.broadcasted_iota(jnp.int32, shape, 0)
     lane_index = lax.broadcasted_iota(jnp.int32, shape, 1)
-    first_var = row_index < 4
-    first_inst = (row_index & 2) == 0
-    half_index = row_index & 1
+    first_var, first_inst, half_index = plane_masks()
     first_half = half_index == 0
-    zero = jnp.zeros(shape, jnp.float32)
 
     next_rows = [next_ref[pl.ds(half, 1), :] for half in range(2)]
     next_line = jnp.where(first_half, next_rows[0], next_rows[1])
@@ -464,6 +420,133 @@
     pick_next = picker(next_line)
     pick_prev = picker(prev_line)
 
+    for shift in range(inst_count):
+        pair = (own_inst - shift) & (inst_count - 1)
+        for cell in range(2):
+            for var in range(6):
+                for inst in range(2):
+                    for half in range(2):
+                        row = cell * CELL_ROWS + rows_of(var, inst, half)
+                        plane_ref[shift, pl.ds(row, 1), :] = all_ref[
+                            2 * pair + inst, var, pl.ds(cell, 1), pl.ds(half * LANES, LANES)
+                        ]
+    offsets = spectral_offsets()
+
+    def time_parts(cell):
+        same_total = [None] * PAIRS
+        other_total = [None] * PAIRS
+        for shift in range(inst_count):
+            same = offsets[(2 * shift) % NT]
+            other = jnp.where(
+                first_inst, offsets[(2 * shift + 1) % NT], offsets[(2 * shift - 1) % NT]
+            )
+            for k in range(PAIRS):
+                plane = plane_ref[shift, pl.ds(cell * CELL_ROWS + k * ROWS, ROWS), :]
+                if shift > 0:
+                    term = same * plane
+                    same_total[k] = term if same_total[k] is None else same_total[k] + term
+                term = other * plane
+                other_total[k] = term if other_total[k] is None else other_total[k] + term
+        return [
+            s + jnp.where(first_inst, pltpu.roll(o, 6, 0), pltpu.roll(o, 2, 0))
+            for s, o in zip(same_total, other_total)
+        ]
+
+    def flux_across(planes, velocity, pressure):
+        return [
+            planes[0] * velocity,
+            planes[1] * velocity + jnp.where(first_var, pressure, 0.0),
+            planes[2] * velocity + jnp.where(first_var, pressure * velocity, 0.0),
+        ]
+
+    for cell in range(2):
+        planes = [
+            plane_ref[0, pl.ds(cell * CELL_ROWS + k * ROWS, ROWS), :] for k in range(PAIRS)
+        ]
+        nearby = [pick_next(plane) for plane in planes]
+        _, velocity, pressure, sound = primitives(first_var, planes)
+        _, next_velocity, next_pressure, next_sound = primitives(first_var, nearby)
+        own_flux = flux_across(planes, velocity, pressure)
+        next_flux = flux_across(nearby, next_velocity, next_pressure)
+        weight = (PITCH_GAIN * 0.5) * (
+            jnp.abs(velocity) + sound + (jnp.abs(next_velocity) + next_sound)
+        )
+        time_term = time_parts(cell)
+        for k in range(PAIRS):
+            face = 0.5 * (own_flux[k] + next_flux[k]) - weight * (nearby[k] - planes[k])
+            rest = time_term[k] + (face - pick_prev(face))
+            row = cell * CELL_ROWS + k * ROWS
+            out_ref[pl.ds(row, ROWS), :] = planes[k]
+            out_ref[pl.ds(REST_ROW + row, ROWS), :] = rest
+        for half in range(2):
+            out_ref[pl.ds(RATE_ROW + cell * 2 + half, 1), :] = rate_ref[
+                pl.ds(cell, 1), pl.ds(half * LANES, LANES)
+            ]
+    out_ref[pl.ds(RATE_ROW + 4, 4), :] = jnp.zeros((4, LANES), jnp.float32)
+
+
+def two_by_two(first, second):
+    def entry(a, b, c, d):
+        terms = [x * y for x, y in ((a, b), (c, d)) if x is not None and y is not None]
+        return None if not terms else terms[0] if len(terms) == 1 else terms[0] + terms[1]
+
+    return (
+        entry(first[0], second[0], first[1], second[2]),
+        entry(first[0], second[1], first[1], second[3]),
+        entry(first[2], second[0], first[3], second[2]),
+        entry(first[2], second[1], first[3], second[3]),
+    )
+
+
+def inverse_of(matrix):
+    reciprocal = 1.0 / (matrix[0] * matrix[3] - matrix[1] * matrix[2])
+    return (
+        matrix[3] * reciprocal,
+        -(matrix[1] * reciprocal),
+        -(matrix[2] * reciprocal),
+        matrix[0] * reciprocal,
+    )
+
+
+def less(first, second):
+    return tuple(a if b is None else a - b for a, b in zip(first, second))
+
+
+def minus(members):
+    return tuple(None if a is None else -a for a in members)
+
+
+def eliminate(centre, left, left_inverse, right, right_inverse):
+    left_factor = two_by_two(centre[0], left_inverse)
+    right_factor = two_by_two(centre[2], right_inverse)
+    sub = minus(two_by_two(left_factor, left[0]))
+    diag = less(
+        less(centre[1], two_by_two(left_factor, left[2])), two_by_two(right_factor, right[0])
+    )
+    sup = minus(two_by_two(right_factor, right[2]))
+    side = []
+    for k in range(PAIRS):
+        for row in range(2):
+            value = centre[3][row * PAIRS + k]
+            for factor, other in ((left_factor, left[3]), (right_factor, right[3])):
+                value = value - (
+                    factor[2 * row] * other[k] + factor[2 * row + 1] * other[PAIRS + k]
+                )
+            side.append((row * PAIRS + k, value))
+    return sub, diag, sup, [value for _, value in sorted(side, key=lambda item: item[0])]
+
+
+def line_kernel(
+    cells, all_ref, codes_ref, out_ref, coef_ref, side_ref, coef2_ref, side2_ref,
+    couple_ref, diag3_ref, side3_ref,
+):
+    own_cell = lax.axis_index("cell")
+    shape = (ROWS, LANES)
+    lane_index = lax.broadcasted_iota(jnp.int32, shape, 1)
+    first_var, _, half_index = plane_masks()
+    first_half = half_index == 0
+    zero = jnp.zeros(shape, jnp.float32)
+
     tile = half_index * (LANES // LINES_DEV) + lane_index // LINES_DEV
     codes = []
     for end in range(2):
@@ -472,9 +555,9 @@
             plane = jnp.where(tile == k, codes_ref[end, k], plane)
         codes.append(plane)
 
-    def loaded(inst, cell):
+    def loaded(cell, start=0):
         return [
-            all_ref[inst, cell // 2, pl.ds((cell % 2) * CELL_ROWS + k * ROWS, ROWS), :]
+            all_ref[cell // 2, pl.ds(start + (cell % 2) * CELL_ROWS + k * ROWS, ROWS), :]
             for k in range(PAIRS)
         ]
 
@@ -494,29 +577,12 @@
 
     def extended_state(cell):
         if cell < 0:
-            return ghost(0, loaded(own_inst, -1 - cell), loaded(own_inst, 0))
+            return ghost(0, loaded(-1 - cell), loaded(0))
         if cell >= cells:
             return ghost(
-                1, loaded(own_inst, 2 * cells - 1 - cell), loaded(own_inst, cells - 1)
+                1, loaded(2 * cells - 1 - cell), loaded(cells - 1)
             )
-        return loaded(own_inst, cell)
-
-    def both(plane):
-        turned = pltpu.roll(plane, 4, 0)
-        return jnp.where(first_var, plane, turned), jnp.where(first_var, turned, plane)
-
-    def primitives(planes):
-        density, moment_x = both(planes[0])
-        moment_y, moment_z = both(planes[1])
-        energy = jnp.where(first_var, planes[2], pltpu.roll(planes[2], 4, 0))
-        inverse = 1.0 / density
-        velocity_x = moment_x * inverse
-        velocity_y = moment_y * inverse
-        velocity_z = moment_z * inverse
-        kinetic = moment_x * velocity_x + moment_y * velocity_y + moment_z * velocity_z
-        pressure = (GAMMA_GAS - 1.0) * (energy - 0.5 * kinetic)
-        sound = jnp.sqrt(GAMMA_GAS * pressure * inverse)
-        return velocity_x, velocity_y, pressure, sound
+        return loaded(cell)
 
     def flux_along(planes, velocity, pressure):
         return [
@@ -525,53 +591,10 @@
             planes[2] * velocity + jnp.where(first_var, pressure * velocity, 0.0),
         ]
 
-    def flux_across(planes, velocity, pressure):
-        return [
-            planes[0] * velocity,
-            planes[1] * velocity + jnp.where(first_var, pressure, 0.0),
-            planes[2] * velocity + jnp.where(first_var, pressure * velocity, 0.0),
-        ]
-
-    offsets = spectral_offsets()
-    inst_count = all_ref.shape[0]
-
-    def time_parts(cell, own):
-        same_total = [None] * PAIRS
-        other_total = [None] * PAIRS
-        for shift in range(inst_count):
-            planes = own if shift == 0 else loaded((own_inst - shift) & (inst_count - 1), cell)
-            same = offsets[(2 * shift) % NT]
-            other = jnp.where(
-                first_inst, offsets[(2 * shift + 1) % NT], offsets[(2 * shift - 1) % NT]
-            )
-            for k in range(PAIRS):
-                if shift > 0:
-                    term = same * planes[k]
-                    same_total[k] = term if same_total[k] is None else same_total[k] + term
-                term = other * planes[k]
-                other_total[k] = term if other_total[k] is None else other_total[k] + term
-        return [
-            s + jnp.where(first_inst, pltpu.roll(o, 6, 0), pltpu.roll(o, 2, 0))
-            for s, o in zip(same_total, other_total)
-        ]
-
-    def pitch_flux(planes, velocity_y, pressure, sound):
-        nearby = [pick_next(plane) for plane in planes]
-        _, next_velocity, next_pressure, next_sound = primitives(nearby)
-        own_flux = flux_across(planes, velocity_y, pressure)
-        next_flux = flux_across(nearby, next_velocity, next_pressure)
-        weight = (PITCH_GAIN * 0.5) * (
-            jnp.abs(velocity_y) + sound + (jnp.abs(next_velocity) + next_sound)
-        )
-        return [
-            0.5 * (a + b) - weight * (n - o)
-            for a, b, n, o in zip(own_flux, next_flux, nearby, planes)
-        ]
-
-    state, pressures, radii, fluxes, steps, rest, sensors, faces = {}, {}, {}, {}, {}, {}, {}, {}
+    state, pressures, radii, fluxes, steps, sensors, faces = {}, {}, {}, {}, {}, {}, {}
     for cell in range(-2, cells + 2):
         planes = extended_state(cell)
-        velocity_x, velocity_y, pressure, sound = primitives(planes)
+        velocity_x, _, pressure, sound = primitives(first_var, planes)
         state[cell] = planes
         pressures[cell] = pressure
         radii[cell] = jnp.abs(velocity_x) + sound
@@ -579,11 +602,6 @@
             fluxes[cell] = flux_along(planes, velocity_x, pressure)
         if cell >= -1:
             steps[cell - 1] = [a - b for a, b in zip(planes, state[cell - 1])]
-        if 0 <= cell < cells:
-            faces_across = pitch_flux(planes, velocity_y, pressure, sound)
-            rest[cell] = [
-                t + (f - pick_prev(f)) for f, t in zip(faces_across, time_parts(cell, planes))
-            ]
         if cell >= 0:
             twice = 2.0 * pressures[cell - 1]
             outer = pressure + pressures[cell - 2]
@@ -606,9 +624,10 @@
         if cell >= 2:
             at = cell - 2
             slot, member = at // 2 + 1, at % 2
+            rest = loaded(at, REST_ROW)
             for k in range(PAIRS):
                 side_ref[slot, member * PAIRS + k] = (
-                    faces[at - 1][k] - faces[at][k] - rest[at][k]
+                    faces[at - 1][k] - faces[at][k] - rest[k]
                 )
             below = radii[at - 1] if at > 0 else zero
             centre = radii[at]
@@ -617,7 +636,7 @@
             above_sum = centre + above
             half_low = SECOND_IMPL * 0.5 + 2.0 * FOURTH_IMPL
             rate_rows = [
-                all_ref[own_inst, at // 2, pl.ds(2 * CELL_ROWS + member * 2 + half, 1), :]
+                all_ref[at // 2, pl.ds(RATE_ROW + member * 2 + half, 1), :]
                 for half in range(2)
             ]
             rate = jnp.where(first_half, rate_rows[0], rate_rows[1])
@@ -709,32 +728,41 @@
         high = side3_ref[own, PAIRS + k] - (factor[2] * other_low + factor[3] * other_high)
         for member in range(2):
             delta = last_inverse[2 * member] * low + last_inverse[2 * member + 1] * high
-            base = all_ref[own_inst, own_cell, pl.ds(member * CELL_ROWS + k * ROWS, ROWS), :]
+            base = all_ref[own_cell, pl.ds(member * CELL_ROWS + k * ROWS, ROWS), :]
             result = base + delta
             for var in range(2):
                 for inst in range(2):
                     for half in range(2):
-                        row = var * 4 + inst * 2 + half
+                        row = rows_of(var, inst, half)
                         out_ref[
                             inst, 2 * k + var, pl.ds(member, 1), pl.ds(half * LANES, LANES)
                         ] = result[row : row + 1]
 
 
+def gather_inst(block):
+    return lax.all_gather(block, "inst", axis=0, tiled=True)
+
+
+def gather_cell(block):
+    return lax.all_gather(block, "cell", axis=0, tiled=False)
+
+
 def local_by_gather(state, pseudo_rate, line_next, face_codes):
-    inst_count = lax.axis_size("inst")
-    cell_count = lax.axis_size("cell")
-    cells = cell_count * state.shape[2]
+    cells = lax.axis_size("cell") * state.shape[2]
     vmem = pl.BlockSpec(memory_space=pltpu.VMEM)
+    plane = (ROWS, LANES)
+    every = gather_inst(state)
     packed = pl.pallas_call(
-        pack_kernel,
+        cell_kernel,
         out_shape=jax.ShapeDtypeStruct((BLOCK_ROWS, LANES), jnp.float32),
-        in_specs=[vmem, vmem],
+        in_specs=[vmem, vmem, vmem],
         out_specs=vmem,
-    )(state, pseudo_rate)
-    gathered = lax.all_gather(packed, ("inst", "cell"), axis=0, tiled=False)
-    gathered = gathered.reshape(inst_count, cell_count, BLOCK_ROWS, LANES)
+        scratch_shapes=[
+            pltpu.VMEM((every.shape[0] // 2, 2 * CELL_ROWS, LANES), jnp.float32)
+        ],
+    )(every, pseudo_rate, line_next.reshape(2, LANES))
+    gathered = gather_cell(packed)
     blocks = cells // 2
-    plane = (ROWS, LANES)
     sizes = [
         (blocks + 2, 10),
         (blocks + 2, 2 * PAIRS),
@@ -747,10 +775,10 @@
     return pl.pallas_call(
         functools.partial(line_kernel, cells),
         out_shape=jax.ShapeDtypeStruct(state.shape, jnp.float32),
-        in_specs=[vmem, vmem, pl.BlockSpec(memory_space=pltpu.SMEM)],
+        in_specs=[vmem, pl.BlockSpec(memory_space=pltpu.SMEM)],
         out_specs=vmem,
         scratch_shapes=[pltpu.VMEM(size + plane, jnp.float32) for size in sizes],
-    )(gathered, line_next.reshape(2, LANES), face_codes)
+    )(gathered, face_codes)
 
 
 def solution(mesh):

time: 84.1 us -> 45.9 us (0.55)
  blocking collectives: 80 us -> 41.8 us
    all_gather x1 -> x2, blocking collectives: 80 us -> 41.8 us  [the longest x1 33.6 us: gather_cell(): return lax.all_gather(block, 'cell', axis=0, tiled=False)]
where the time goes in v2:
time: 45.9 us; the launch traced here: 45.7 us
  blocking collectives  41.8 us (91%)
  Pallas kernels  3.86 us (8%)
    all_gather x1, blocking collectives, gather_cell(): return lax.all_gather(block, 'cell', axis=0, tiled=False)  33.6 us
    all_gather x1, blocking collectives, gather_inst(): return lax.all_gather(block, 'inst', axis=0, tiled=True)  8.25 us
    pallas_call x1, Pallas kernels, local_by_gather(): pl.pallas_call(functools.partial(line_kernel, cells), out_shape=jax.Shape...  2.05 us
    pallas_call x1, Pallas kernels, local_by_gather(): pl.pallas_call(cell_kernel, out_shape=jax.ShapeDtypeStruct((BLOCK_ROWS, L...  1.81 us

profile of v2, /device:TPU:0, one launch (start us, length us, event | category | flops | bytes accessed | tf_op | source)
XLA Modules:
  0.0 45.7 jit_solution(11784464015177695498)
XLA Ops:
  0.0 8.3 %all_gather.9.all_ref = f32[8,6,2,256]{3,2,1,0:T(2,128)} all-gather(f32[2,6,2,256]{3,2,1,0:T(2,128)} %param.4), channel_id=1, replica_groups=mesh['inst'=4,'cell'=8] {'inst'}, dimensions={0}, use_global_device_ids=true | all-gather | bytes 122880 | tf_op jit(solution)/shard_map/all_gather | solution.py:743
  8.3 1.8 %shard_map.46 = f32[104,128]{1,0:T(8,128)} custom-call(f32[8,6,2,256]{3,2,1,0:T(2,128)} %all_gather.9.all_ref, f32[2,256]{1,0:T(2,128)} %rate_ref.1, s32[2,128]{1,0:T(2,128)} %bitcast.3), custom_call_target="tpu_custom_call" | custom-call | tf_op jit(solution)/shard_map/pallas_call | solution.py:755
  10.1 33.6 %all-gather = f32[832,128]{1,0:T(8,128)} all-gather(f32[104,128]{1,0:T(8,128)} %shard_map.46), channel_id=2, replica_groups=mesh['inst'=4,'cell'=8] {'cell'}, dimensions={0}, use_global_device_ids=true | all-gather | bytes 479232 | tf_op jit(solution)/shard_map/all_gather | solution.py:747
  43.6 2.1 %shard_map.47 = f32[2,6,2,256]{3,2,1,0:T(2,128)} custom-call(f32[8,104,128]{2,1,0:T(8,128)} %bitcast.2, s32[2,8]{1,0:T(2,128)} %codes_ref.1), custom_call_target="tpu_custom_call" | custom-call | tf_op jit(solution)/shard_map/pallas_call | solution.py:775

commit v3 on v2

--- a/solution.py
+++ b/solution.py
@@ -744,7 +744,8 @@
 
 
 def gather_cell(block):
-    return lax.all_gather(block, "cell", axis=0, tiled=False)
+    planes = block.reshape(BLOCK_ROWS // ROWS, ROWS, LANES)
+    return lax.all_gather(planes, "cell", axis=0, tiled=True)
 
 
 def local_by_gather(state, pseudo_rate, line_next, face_codes):
@@ -761,7 +762,7 @@
             pltpu.VMEM((every.shape[0] // 2, 2 * CELL_ROWS, LANES), jnp.float32)
         ],
     )(every, pseudo_rate, line_next.reshape(2, LANES))
-    gathered = gather_cell(packed)
+    gathered = gather_cell(packed).reshape(-1, BLOCK_ROWS, LANES)
     blocks = cells // 2
     sizes = [
         (blocks + 2, 10),

time: 45.9 us -> 45.9 us (level)
  no operation moved by 1% of the time
where the time goes in v3:
time: 45.9 us; the launch traced here: 45.7 us
  blocking collectives  41.8 us (91%)
  Pallas kernels  3.86 us (8%)
    all_gather x1, blocking collectives, gather_cell(): return lax.all_gather(planes, 'cell', axis=0, tiled=True)  33.6 us
    all_gather x1, blocking collectives, gather_inst(): return lax.all_gather(block, 'inst', axis=0, tiled=True)  8.25 us
    pallas_call x1, Pallas kernels, local_by_gather(): pl.pallas_call(functools.partial(line_kernel, cells), out_shape=jax.Shape...  2.05 us
    pallas_call x1, Pallas kernels, local_by_gather(): pl.pallas_call(cell_kernel, out_shape=jax.ShapeDtypeStruct((BLOCK_ROWS, L...  1.81 us

profile of v3, /device:TPU:0, one launch (start us, length us, event | category | flops | bytes accessed | tf_op | source)
XLA Modules:
  0.0 45.7 jit_solution(10000875443010518535)
XLA Ops:
  0.0 8.3 %all_gather.6.all_ref = f32[8,6,2,256]{3,2,1,0:T(2,128)} all-gather(f32[2,6,2,256]{3,2,1,0:T(2,128)} %param.4), channel_id=1, replica_groups=mesh['inst'=4,'cell'=8] {'inst'}, dimensions={0}, use_global_device_ids=true | all-gather | bytes 122880 | tf_op jit(solution)/shard_map/all_gather | solution.py:743
  8.3 1.8 %shard_map.46 = f32[104,128]{1,0:T(8,128)} custom-call(f32[8,6,2,256]{3,2,1,0:T(2,128)} %all_gather.6.all_ref, f32[2,256]{1,0:T(2,128)} %rate_ref.1, s32[2,128]{1,0:T(2,128)} %bitcast.5), custom_call_target="tpu_custom_call" | custom-call | tf_op jit(solution)/shard_map/pallas_call | solution.py:756
  10.1 33.6 %all_gather.7 = f32[104,8,128]{2,1,0:T(8,128)} all-gather(f32[13,8,128]{2,1,0:T(8,128)} %bitcast.4), channel_id=1, replica_groups=mesh['inst'=4,'cell'=8] {'cell'}, dimensions={0}, use_global_device_ids=true | all-gather | bytes 479232 | tf_op jit(solution)/shard_map/all_gather | solution.py:748
  43.6 2.1 %shard_map.47 = f32[2,6,2,256]{3,2,1,0:T(2,128)} custom-call(f32[8,104,128]{2,1,0:T(8,128)} %bitcast.3, s32[2,8]{1,0:T(2,128)} %codes_ref.1), custom_call_target="tpu_custom_call" | custom-call | tf_op jit(solution)/shard_map/pallas_call | solution.py:776

commit v4 on v2

--- a/solution.py
+++ b/solution.py
@@ -384,6 +384,7 @@
 def cell_kernel(all_ref, rate_ref, next_ref, out_ref, plane_ref):
     own_inst = lax.axis_index("inst")
     inst_count = all_ref.shape[0] // 2
+    copies = out_ref.shape[0]
     shape = (ROWS, LANES)
     lane_index = lax.broadcasted_iota(jnp.int32, shape, 1)
     first_var, first_inst, half_index = plane_masks()
@@ -476,13 +477,18 @@
             face = 0.5 * (own_flux[k] + next_flux[k]) - weight * (nearby[k] - planes[k])
             rest = time_term[k] + (face - pick_prev(face))
             row = cell * CELL_ROWS + k * ROWS
-            out_ref[pl.ds(row, ROWS), :] = planes[k]
-            out_ref[pl.ds(REST_ROW + row, ROWS), :] = rest
-        for half in range(2):
-            out_ref[pl.ds(RATE_ROW + cell * 2 + half, 1), :] = rate_ref[
-                pl.ds(cell, 1), pl.ds(half * LANES, LANES)
-            ]
-    out_ref[pl.ds(RATE_ROW + 4, 4), :] = jnp.zeros((4, LANES), jnp.float32)
+            for copy in range(copies):
+                out_ref[copy, pl.ds(row, ROWS), :] = planes[k]
+                out_ref[copy, pl.ds(REST_ROW + row, ROWS), :] = rest
+    rates = [
+        rate_ref[pl.ds(cell, 1), pl.ds(half * LANES, LANES)]
+        for cell in range(2)
+        for half in range(2)
+    ]
+    for copy in range(copies):
+        for row, rate in enumerate(rates):
+            out_ref[copy, pl.ds(RATE_ROW + row, 1), :] = rate
+        out_ref[copy, pl.ds(RATE_ROW + 4, 4), :] = jnp.zeros((4, LANES), jnp.float32)
 
 
 def two_by_two(first, second):
@@ -743,8 +749,8 @@
     return lax.all_gather(block, "inst", axis=0, tiled=True)
 
 
-def gather_cell(block):
-    return lax.all_gather(block, "cell", axis=0, tiled=False)
+def exchange_cell(copies):
+    return lax.all_to_all(copies, "cell", split_axis=0, concat_axis=0, tiled=True)
 
 
 def local_by_gather(state, pseudo_rate, line_next, face_codes):
@@ -754,14 +760,16 @@
     every = gather_inst(state)
     packed = pl.pallas_call(
         cell_kernel,
-        out_shape=jax.ShapeDtypeStruct((BLOCK_ROWS, LANES), jnp.float32),
+        out_shape=jax.ShapeDtypeStruct(
+            (lax.axis_size("cell"), BLOCK_ROWS, LANES), jnp.float32
+        ),
         in_specs=[vmem, vmem, vmem],
         out_specs=vmem,
         scratch_shapes=[
             pltpu.VMEM((every.shape[0] // 2, 2 * CELL_ROWS, LANES), jnp.float32)
         ],
     )(every, pseudo_rate, line_next.reshape(2, LANES))
-    gathered = gather_cell(packed)
+    gathered = exchange_cell(packed)
     blocks = cells // 2
     sizes = [
         (blocks + 2, 10),

time: 45.9 us -> 31.6 us (0.69)
  blocking collectives: 41.8 us -> 27.3 us
    all_gather x1 -> x0, blocking collectives: 33.6 us -> none  [gather_cell(): return lax.all_gather(block, 'cell', axis=0, tiled=False)]
    all_to_all x0 -> x1, blocking collectives: none -> 19 us  [exchange_cell(): lax.all_to_all(copies, 'cell', split_axis=0, concat_axis=0, tiled=True)]
where the time goes in v4:
time: 31.6 us; the launch traced here: 31.3 us
  blocking collectives  27.3 us (86%)
  Pallas kernels  4 us (13%)
    all_to_all x1, blocking collectives, exchange_cell(): lax.all_to_all(copies, 'cell', split_axis=0, concat_axis=0, tiled=True)  19 us
    all_gather x1, blocking collectives, gather_inst(): return lax.all_gather(block, 'inst', axis=0, tiled=True)  8.25 us
    pallas_call x1, Pallas kernels, local_by_gather(): pl.pallas_call(functools.partial(line_kernel, cells), out_shape=jax.Shape...  2.05 us
    pallas_call x1, Pallas kernels, local_by_gather(): pl.pallas_call(cell_kernel, out_shape=jax.ShapeDtypeStruct((lax.axis_size...  1.95 us

profile of v4, /device:TPU:0, one launch (start us, length us, event | category | flops | bytes accessed | tf_op | source)
XLA Modules:
  0.0 31.3 jit_solution(1498235033336022227)
XLA Ops:
  0.0 8.2 %all_gather.3.all_ref = f32[8,6,2,256]{3,2,1,0:T(2,128)} all-gather(f32[2,6,2,256]{3,2,1,0:T(2,128)} %param.4), channel_id=1, replica_groups=mesh['inst'=4,'cell'=8] {'inst'}, dimensions={0}, use_global_device_ids=true | all-gather | bytes 122880 | tf_op jit(solution)/shard_map/all_gather | solution.py:749
  8.2 2.0 %shard_map.46 = f32[8,104,128]{2,1,0:T(8,128)} custom-call(f32[8,6,2,256]{3,2,1,0:T(2,128)} %all_gather.3.all_ref, f32[2,256]{1,0:T(2,128)} %rate_ref.1, s32[2,128]{1,0:T(2,128)} %bitcast.1), custom_call_target="tpu_custom_call" | custom-call | tf_op jit(solution)/shard_map/pallas_call | solution.py:761
  10.2 19.0 %all_to_all.5.all_ref = f32[8,104,128]{2,1,0:T(8,128)} all-to-all(f32[8,104,128]{2,1,0:T(8,128)} %shard_map.46), channel_id=1, replica_groups=mesh['inst'=4,'cell'=8] {'cell'}, dimensions={0} | all-to-all | bytes 851968 | tf_op jit(solution)/shard_map/all_to_all | solution.py:753
  29.2 2.1 %shard_map.47 = f32[2,6,2,256]{3,2,1,0:T(2,128)} custom-call(f32[8,104,128]{2,1,0:T(8,128)} %all_to_all.5.all_ref, s32[2,8]{1,0:T(2,128)} %codes_ref.1), custom_call_target="tpu_custom_call" | custom-call | tf_op jit(solution)/shard_map/pallas_call | solution.py:783

commit v5 on v3

--- a/solution.py
+++ b/solution.py
@@ -541,6 +541,10 @@
     couple_ref, diag3_ref, side3_ref,
 ):
     own_cell = lax.axis_index("cell")
+    order = ring_order(cells // 2)
+    own_place = jnp.where(
+        own_cell & 1 == 0, own_cell >> 1, cells // 2 - 1 - (own_cell >> 1)
+    )
     shape = (ROWS, LANES)
     lane_index = lax.broadcasted_iota(jnp.int32, shape, 1)
     first_var, _, half_index = plane_masks()
@@ -557,7 +561,7 @@
 
     def loaded(cell, start=0):
         return [
-            all_ref[cell // 2, pl.ds(start + (cell % 2) * CELL_ROWS + k * ROWS, ROWS), :]
+            all_ref[order.index(cell // 2), pl.ds(start + (cell % 2) * CELL_ROWS + k * ROWS, ROWS), :]
             for k in range(PAIRS)
         ]
 
@@ -636,7 +640,7 @@
             above_sum = centre + above
             half_low = SECOND_IMPL * 0.5 + 2.0 * FOURTH_IMPL
             rate_rows = [
-                all_ref[at // 2, pl.ds(RATE_ROW + member * 2 + half, 1), :]
+                all_ref[order.index(at // 2), pl.ds(RATE_ROW + member * 2 + half, 1), :]
                 for half in range(2)
             ]
             rate = jnp.where(first_half, rate_rows[0], rate_rows[1])
@@ -728,7 +732,7 @@
         high = side3_ref[own, PAIRS + k] - (factor[2] * other_low + factor[3] * other_high)
         for member in range(2):
             delta = last_inverse[2 * member] * low + last_inverse[2 * member + 1] * high
-            base = all_ref[own_cell, pl.ds(member * CELL_ROWS + k * ROWS, ROWS), :]
+            base = all_ref[own_place, pl.ds(member * CELL_ROWS + k * ROWS, ROWS), :]
             result = base + delta
             for var in range(2):
                 for inst in range(2):
@@ -743,9 +747,14 @@
     return lax.all_gather(block, "inst", axis=0, tiled=True)
 
 
+def ring_order(count):
+    return list(range(0, count, 2)) + list(range(count - 1, 0, -2))
+
+
 def gather_cell(block):
     planes = block.reshape(BLOCK_ROWS // ROWS, ROWS, LANES)
-    return lax.all_gather(planes, "cell", axis=0, tiled=True)
+    order = [ring_order(lax.axis_size("cell"))]
+    return lax.all_gather(planes, "cell", axis=0, tiled=True, axis_index_groups=order)
 
 
 def local_by_gather(state, pseudo_rate, line_next, face_codes):

time: 45.9 us -> 37.2 us (0.81)
  blocking collectives: 41.8 us -> 33.1 us
    all_gather x1, blocking collectives: 33.6 us -> 24.8 us  [gather_cell(): lax.all_gather(planes, 'cell', axis=0, tiled=True, axis_index_groups=order)]
where the time goes in v5:
time: 37.2 us; the launch traced here: 36.9 us
  blocking collectives  33.1 us (89%)
  Pallas kernels  3.86 us (10%)
    all_gather x1, blocking collectives, gather_cell(): lax.all_gather(planes, 'cell', axis=0, tiled=True, axis_index_groups=order)  24.8 us
    all_gather x1, blocking collectives, gather_inst(): return lax.all_gather(block, 'inst', axis=0, tiled=True)  8.25 us
    pallas_call x1, Pallas kernels, local_by_gather(): pl.pallas_call(functools.partial(line_kernel, cells), out_shape=jax.Shape...  2.05 us
    pallas_call x1, Pallas kernels, local_by_gather(): pl.pallas_call(cell_kernel, out_shape=jax.ShapeDtypeStruct((BLOCK_ROWS, L...  1.81 us

profile of v5, /device:TPU:0, one launch (start us, length us, event | category | flops | bytes accessed | tf_op | source)
XLA Modules:
  0.0 36.9 jit_solution(8951578616380475106)
XLA Ops:
  0.0 8.3 %all_gather.6.all_ref = f32[8,6,2,256]{3,2,1,0:T(2,128)} all-gather(f32[2,6,2,256]{3,2,1,0:T(2,128)} %param.4), channel_id=1, replica_groups=mesh['inst'=4,'cell'=8] {'inst'}, dimensions={0}, use_global_device_ids=true | all-gather | bytes 122880 | tf_op jit(solution)/shard_map/all_gather | solution.py:747
  8.3 1.8 %shard_map.46 = f32[104,128]{1,0:T(8,128)} custom-call(f32[8,6,2,256]{3,2,1,0:T(2,128)} %all_gather.6.all_ref, f32[2,256]{1,0:T(2,128)} %rate_ref.1, s32[2,128]{1,0:T(2,128)} %bitcast.5), custom_call_target="tpu_custom_call" | custom-call | tf_op jit(solution)/shard_map/pallas_call | solution.py:765
  10.1 24.8 %all_gather.7 = f32[104,8,128]{2,1,0:T(8,128)} all-gather(f32[13,8,128]{2,1,0:T(8,128)} %bitcast.4), channel_id=1, replica_groups={{0,2,4,6,7,5,3,1},{8,10,12,14,15,13,11,9},{16,18,20,22,23,21,19,17},{24..., dimensions={0}, use_global_device_ids=true | all-gather | bytes 479232 | tf_op jit(solution)/shard_map/all_gather | solution.py:757
  34.9 2.1 %shard_map.47 = f32[2,6,2,256]{3,2,1,0:T(2,128)} custom-call(f32[8,104,128]{2,1,0:T(8,128)} %bitcast.3, s32[2,8]{1,0:T(2,128)} %codes_ref.1), custom_call_target="tpu_custom_call" | custom-call | tf_op jit(solution)/shard_map/pallas_call | solution.py:785

commit v6 on v1

--- a/solution.py
+++ b/solution.py
@@ -339,7 +339,9 @@
 ROWS = 8
 PAIRS = 3
 CELL_ROWS = PAIRS * ROWS
-BLOCK_ROWS = 56
+STATE_ROWS = 2 * CELL_ROWS
+BLOCK_ROWS = STATE_ROWS + ROWS
+FACTORS = 56
 
 
 def spectral_offsets():
@@ -351,20 +353,82 @@
     return [float(np.float32(value)) for value in table]
 
 
-def pack_kernel(state_ref, rate_ref, out_ref):
+def plane_masks():
+    row_index = lax.broadcasted_iota(jnp.int32, (ROWS, LANES), 0)
+    return row_index < 4, (row_index & 2) == 0, row_index & 1
+
+
+def both(first_var, plane):
+    turned = pltpu.roll(plane, 4, 0)
+    return jnp.where(first_var, plane, turned), jnp.where(first_var, turned, plane)
+
+
+def primitives(first_var, planes):
+    density, moment_x = both(first_var, planes[0])
+    moment_y, moment_z = both(first_var, planes[1])
+    energy = jnp.where(first_var, planes[2], pltpu.roll(planes[2], 4, 0))
+    inverse = 1.0 / density
+    velocity_x = moment_x * inverse
+    velocity_y = moment_y * inverse
+    velocity_z = moment_z * inverse
+    kinetic = moment_x * velocity_x + moment_y * velocity_y + moment_z * velocity_z
+    pressure = (GAMMA_GAS - 1.0) * (energy - 0.5 * kinetic)
+    sound = jnp.sqrt(GAMMA_GAS * pressure * inverse)
+    return velocity_x, velocity_y, pressure, sound
+
+
+def rows_of(var, inst, half):
+    return (var // 2) * ROWS + (var % 2) * 4 + inst * 2 + half
+
+
+def pack_kernel(state_ref, rate_ref, inst_ref, cell_ref):
     for cell in range(2):
         for var in range(6):
             for inst in range(2):
                 for half in range(2):
-                    row = cell * CELL_ROWS + (var // 2) * ROWS + (var % 2) * 4 + inst * 2 + half
-                    out_ref[pl.ds(row, 1), :] = state_ref[
+                    row = cell * CELL_ROWS + rows_of(var, inst, half)
+                    inst_ref[0, pl.ds(row, 1), :] = state_ref[
                         inst, var, pl.ds(cell, 1), pl.ds(half * LANES, LANES)
                     ]
         for half in range(2):
-            out_ref[pl.ds(2 * CELL_ROWS + cell * 2 + half, 1), :] = rate_ref[
+            cell_ref[0, pl.ds(STATE_ROWS + cell * 2 + half, 1), :] = rate_ref[
                 pl.ds(cell, 1), pl.ds(half * LANES, LANES)
             ]
-    out_ref[pl.ds(52, 4), :] = jnp.zeros((4, LANES), jnp.float32)
+    cell_ref[0, pl.ds(STATE_ROWS + 4, 4), :] = jnp.zeros((4, LANES), jnp.float32)
+    for row in range(0, STATE_ROWS, ROWS):
+        values = inst_ref[0, pl.ds(row, ROWS), :]
+        for copy in range(1, inst_ref.shape[0]):
+            inst_ref[copy, pl.ds(row, ROWS), :] = values
+        for copy in range(cell_ref.shape[0]):
+            cell_ref[copy, pl.ds(row, ROWS), :] = values
+    values = cell_ref[0, pl.ds(STATE_ROWS, ROWS), :]
+    for copy in range(1, cell_ref.shape[0]):
+        cell_ref[copy, pl.ds(STATE_ROWS, ROWS), :] = values
+
+
+def time_kernel(all_ref, out_ref):
+    own_inst = lax.axis_index("inst")
+    inst_count = all_ref.shape[0]
+    _, first_inst, _ = plane_masks()
+    offsets = spectral_offsets()
+    for row in range(0, STATE_ROWS, ROWS):
+        same_total, other_total = None, None
+        for shift in range(inst_count):
+            plane = all_ref[(own_inst - shift) & (inst_count - 1), pl.ds(row, ROWS), :]
+            other = jnp.where(
+                first_inst, offsets[(2 * shift + 1) % NT], offsets[(2 * shift - 1) % NT]
+            )
+            if shift > 0:
+                term = offsets[(2 * shift) % NT] * plane
+                same_total = term if same_total is None else same_total + term
+            term = other * plane
+            other_total = term if other_total is None else other_total + term
+        turned = jnp.where(
+            first_inst, pltpu.roll(other_total, 6, 0), pltpu.roll(other_total, 2, 0)
+        )
+        result = same_total + turned
+        for copy in range(out_ref.shape[0]):
+            out_ref[copy, pl.ds(row, ROWS), :] = result
 
 
 def two_by_two(first, second):
@@ -415,21 +479,18 @@
                     factor[2 * row] * other[k] + factor[2 * row + 1] * other[PAIRS + k]
                 )
             side.append((row * PAIRS + k, value))
-    return sub, diag, sup, [value for _, value in sorted(side, key=lambda item: item[0])]
+    side = [value for _, value in sorted(side, key=lambda item: item[0])]
+    return sub, diag, sup, side, left_factor + right_factor
 
 
 def line_kernel(
-    cells, all_ref, next_ref, codes_ref, out_ref, coef_ref, side_ref, coef2_ref, side2_ref,
+    cells, all_ref, next_ref, codes_ref, factor_ref, part_ref, coef_ref, side_ref, coef2_ref, side2_ref,
     couple_ref, diag3_ref, side3_ref,
 ):
-    own_inst = lax.axis_index("inst")
     own_cell = lax.axis_index("cell")
     shape = (ROWS, LANES)
-    row_index = lax.broadcasted_iota(jnp.int32, shape, 0)
     lane_index = lax.broadcasted_iota(jnp.int32, shape, 1)
-    first_var = row_index < 4
-    first_inst = (row_index & 2) == 0
-    half_index = row_index & 1
+    first_var, _, half_index = plane_masks()
     first_half = half_index == 0
     zero = jnp.zeros(shape, jnp.float32)
 
@@ -472,9 +533,9 @@
             plane = jnp.where(tile == k, codes_ref[end, k], plane)
         codes.append(plane)
 
-    def loaded(inst, cell):
+    def loaded(cell):
         return [
-            all_ref[inst, cell // 2, pl.ds((cell % 2) * CELL_ROWS + k * ROWS, ROWS), :]
+            all_ref[cell // 2, pl.ds((cell % 2) * CELL_ROWS + k * ROWS, ROWS), :]
             for k in range(PAIRS)
         ]
 
@@ -494,29 +555,12 @@
 
     def extended_state(cell):
         if cell < 0:
-            return ghost(0, loaded(own_inst, -1 - cell), loaded(own_inst, 0))
+            return ghost(0, loaded(-1 - cell), loaded(0))
         if cell >= cells:
             return ghost(
-                1, loaded(own_inst, 2 * cells - 1 - cell), loaded(own_inst, cells - 1)
+                1, loaded(2 * cells - 1 - cell), loaded(cells - 1)
             )
-        return loaded(own_inst, cell)
-
-    def both(plane):
-        turned = pltpu.roll(plane, 4, 0)
-        return jnp.where(first_var, plane, turned), jnp.where(first_var, turned, plane)
-
-    def primitives(planes):
-        density, moment_x = both(planes[0])
-        moment_y, moment_z = both(planes[1])
-        energy = jnp.where(first_var, planes[2], pltpu.roll(planes[2], 4, 0))
-        inverse = 1.0 / density
-        velocity_x = moment_x * inverse
-        velocity_y = moment_y * inverse
-        velocity_z = moment_z * inverse
-        kinetic = moment_x * velocity_x + moment_y * velocity_y + moment_z * velocity_z
-        pressure = (GAMMA_GAS - 1.0) * (energy - 0.5 * kinetic)
-        sound = jnp.sqrt(GAMMA_GAS * pressure * inverse)
-        return velocity_x, velocity_y, pressure, sound
+        return loaded(cell)
 
     def flux_along(planes, velocity, pressure):
         return [
@@ -532,32 +576,9 @@
             planes[2] * velocity + jnp.where(first_var, pressure * velocity, 0.0),
         ]
 
-    offsets = spectral_offsets()
-    inst_count = all_ref.shape[0]
-
-    def time_parts(cell, own):
-        same_total = [None] * PAIRS
-        other_total = [None] * PAIRS
-        for shift in range(inst_count):
-            planes = own if shift == 0 else loaded((own_inst - shift) & (inst_count - 1), cell)
-            same = offsets[(2 * shift) % NT]
-            other = jnp.where(
-                first_inst, offsets[(2 * shift + 1) % NT], offsets[(2 * shift - 1) % NT]
-            )
-            for k in range(PAIRS):
-                if shift > 0:
-                    term = same * planes[k]
-                    same_total[k] = term if same_total[k] is None else same_total[k] + term
-                term = other * planes[k]
-                other_total[k] = term if other_total[k] is None else other_total[k] + term
-        return [
-            s + jnp.where(first_inst, pltpu.roll(o, 6, 0), pltpu.roll(o, 2, 0))
-            for s, o in zip(same_total, other_total)
-        ]
-
     def pitch_flux(planes, velocity_y, pressure, sound):
         nearby = [pick_next(plane) for plane in planes]
-        _, next_velocity, next_pressure, next_sound = primitives(nearby)
+        _, next_velocity, next_pressure, next_sound = primitives(first_var, nearby)
         own_flux = flux_across(planes, velocity_y, pressure)
         next_flux = flux_across(nearby, next_velocity, next_pressure)
         weight = (PITCH_GAIN * 0.5) * (
@@ -571,7 +592,7 @@
     state, pressures, radii, fluxes, steps, rest, sensors, faces = {}, {}, {}, {}, {}, {}, {}, {}
     for cell in range(-2, cells + 2):
         planes = extended_state(cell)
-        velocity_x, velocity_y, pressure, sound = primitives(planes)
+        velocity_x, velocity_y, pressure, sound = primitives(first_var, planes)
         state[cell] = planes
         pressures[cell] = pressure
         radii[cell] = jnp.abs(velocity_x) + sound
@@ -581,9 +602,7 @@
             steps[cell - 1] = [a - b for a, b in zip(planes, state[cell - 1])]
         if 0 <= cell < cells:
             faces_across = pitch_flux(planes, velocity_y, pressure, sound)
-            rest[cell] = [
-                t + (f - pick_prev(f)) for f, t in zip(faces_across, time_parts(cell, planes))
-            ]
+            rest[cell] = [face - pick_prev(face) for face in faces_across]
         if cell >= 0:
             twice = 2.0 * pressures[cell - 1]
             outer = pressure + pressures[cell - 2]
@@ -617,7 +636,7 @@
             above_sum = centre + above
             half_low = SECOND_IMPL * 0.5 + 2.0 * FOURTH_IMPL
             rate_rows = [
-                all_ref[own_inst, at // 2, pl.ds(2 * CELL_ROWS + member * 2 + half, 1), :]
+                all_ref[at // 2, pl.ds(STATE_ROWS + member * 2 + half, 1), :]
                 for half in range(2)
             ]
             rate = jnp.where(first_half, rate_rows[0], rate_rows[1])
@@ -675,11 +694,13 @@
         right = block_one(parity + 2 * k + 2)
         right_inverse = inverse_of(right[1])
         kept = block_one(parity + 2 * k + 1)
-        sub, diag, sup, side = eliminate(kept, left, left_inverse, right, right_inverse)
+        sub, diag, sup, side, factors = eliminate(kept, left, left_inverse, right, right_inverse)
         for n, plane in enumerate(sub + diag + sup):
             coef2_ref[k + 1, n] = plane
         for n, plane in enumerate(side):
             side2_ref[k + 1, n] = plane
+        for n, plane in enumerate(factors):
+            factor_ref[8 * k + n] = plane
         left, left_inverse = right, right_inverse
     parity = (own_cell >> 1) & 1
     left = block_two(parity)
@@ -688,13 +709,15 @@
         right = block_two(parity + 2 * k + 2)
         right_inverse = inverse_of(right[1])
         kept = block_two(parity + 2 * k + 1)
-        sub, diag, sup, side = eliminate(kept, left, left_inverse, right, right_inverse)
+        sub, diag, sup, side, factors = eliminate(kept, left, left_inverse, right, right_inverse)
         for n in range(4):
             couple_ref[k, 0, n] = sub[n]
             couple_ref[k, 1, n] = sup[n]
             diag3_ref[k, n] = diag[n]
         for n, plane in enumerate(side):
             side3_ref[k, n] = plane
+        for n, plane in enumerate(factors):
+            factor_ref[4 * blocks + 8 * k + n] = plane
         left, left_inverse = right, right_inverse
     own = (own_cell >> 2) & 1
     other = 1 - own
@@ -703,38 +726,105 @@
     factor = two_by_two(own_couple, inverse_of([diag3_ref[other, n] for n in range(4)]))
     diag = less([diag3_ref[own, n] for n in range(4)], two_by_two(factor, other_couple))
     last_inverse = inverse_of(diag)
+    for n in range(4):
+        factor_ref[6 * blocks + n] = factor[n]
+        factor_ref[6 * blocks + 4 + n] = last_inverse[n]
     for k in range(PAIRS):
         other_low, other_high = side3_ref[other, k], side3_ref[other, PAIRS + k]
         low = side3_ref[own, k] - (factor[0] * other_low + factor[1] * other_high)
         high = side3_ref[own, PAIRS + k] - (factor[2] * other_low + factor[3] * other_high)
         for member in range(2):
             delta = last_inverse[2 * member] * low + last_inverse[2 * member + 1] * high
-            base = all_ref[own_inst, own_cell, pl.ds(member * CELL_ROWS + k * ROWS, ROWS), :]
-            result = base + delta
+            base = all_ref[own_cell, pl.ds(member * CELL_ROWS + k * ROWS, ROWS), :]
+            part_ref[member * PAIRS + k] = base + delta
+
+
+def finish_kernel(time_ref, factor_ref, part_ref, out_ref, side2_ref, side3_ref):
+    own_cell = lax.axis_index("cell")
+    blocks = time_ref.shape[0]
+
+    def reduced(start, centre, left, right):
+        factor = [factor_ref[start + n] for n in range(8)]
+        result = []
+        for row in range(2):
+            for k in range(PAIRS):
+                value = centre(row * PAIRS + k)
+                for first, other in ((0, left), (4, right)):
+                    value = value - (
+                        factor[first + 2 * row] * other(k)
+                        + factor[first + 2 * row + 1] * other(PAIRS + k)
+                    )
+                result.append(value)
+        return result
+
+    def held(ref, count, slot):
+        inside = jnp.minimum(jnp.maximum(slot, 0), count - 1)
+        return lambda n: ref[inside, pl.ds(n * ROWS, ROWS), :]
+
+    def level(ref, count, parity, k):
+        at = parity + 2 * k
+        return [held(ref, count, at), held(ref, count, at - 1), held(ref, count, at + 1)]
+
+    for k in range(blocks // 2):
+        around = level(time_ref, blocks, own_cell & 1, k)
+        for n, plane in enumerate(reduced(8 * k, *around)):
+            side2_ref[k, pl.ds(n * ROWS, ROWS), :] = plane
+    for k in range(blocks // 4):
+        around = level(side2_ref, blocks // 2, (own_cell >> 1) & 1, k)
+        for n, plane in enumerate(reduced(4 * blocks + 8 * k, *around)):
+            side3_ref[k, n] = plane
+    own = (own_cell >> 2) & 1
+    other = 1 - own
+    factor = [factor_ref[6 * blocks + n] for n in range(4)]
+    inverse = [factor_ref[6 * blocks + 4 + n] for n in range(4)]
+    for k in range(PAIRS):
+        other_low, other_high = side3_ref[other, k], side3_ref[other, PAIRS + k]
+        low = side3_ref[own, k] - (factor[0] * other_low + factor[1] * other_high)
+        high = side3_ref[own, PAIRS + k] - (factor[2] * other_low + factor[3] * other_high)
+        for member in range(2):
+            delta = inverse[2 * member] * low + inverse[2 * member + 1] * high
+            result = part_ref[member * PAIRS + k] - delta
             for var in range(2):
                 for inst in range(2):
                     for half in range(2):
-                        row = var * 4 + inst * 2 + half
+                        row = rows_of(var, inst, half)
                         out_ref[
                             inst, 2 * k + var, pl.ds(member, 1), pl.ds(half * LANES, LANES)
                         ] = result[row : row + 1]
 
 
+def exchange(copies, axis):
+    return lax.all_to_all(copies, axis, split_axis=0, concat_axis=0, tiled=True)
+
+
+def float_shape(*sizes):
+    return jax.ShapeDtypeStruct(sizes, jnp.float32)
+
+
 def local_by_gather(state, pseudo_rate, line_next, face_codes):
     inst_count = lax.axis_size("inst")
-    cell_count = lax.axis_size("cell")
-    cells = cell_count * state.shape[2]
+    blocks = lax.axis_size("cell")
+    cells = 2 * blocks
     vmem = pl.BlockSpec(memory_space=pltpu.VMEM)
-    packed = pl.pallas_call(
+    plane = (ROWS, LANES)
+    inst_copies, cell_copies = pl.pallas_call(
         pack_kernel,
-        out_shape=jax.ShapeDtypeStruct((BLOCK_ROWS, LANES), jnp.float32),
+        out_shape=(
+            float_shape(inst_count, STATE_ROWS, LANES),
+            float_shape(blocks, BLOCK_ROWS, LANES),
+        ),
         in_specs=[vmem, vmem],
+        out_specs=(vmem, vmem),
+    )(state, pseudo_rate)
+    every_inst = exchange(inst_copies, "inst")
+    every_cell = exchange(cell_copies, "cell")
+    time_copies = pl.pallas_call(
+        time_kernel,
+        out_shape=float_shape(blocks, STATE_ROWS, LANES),
+        in_specs=[vmem],
         out_specs=vmem,
-    )(state, pseudo_rate)
-    gathered = lax.all_gather(packed, ("inst", "cell"), axis=0, tiled=False)
-    gathered = gathered.reshape(inst_count, cell_count, BLOCK_ROWS, LANES)
-    blocks = cells // 2
-    plane = (ROWS, LANES)
+    )(every_inst)
+    every_time = exchange(time_copies, "cell")
     sizes = [
         (blocks + 2, 10),
         (blocks + 2, 2 * PAIRS),
@@ -744,13 +834,23 @@
         (2, 4),
         (2, 2 * PAIRS),
     ]
+    factors, part = pl.pallas_call(
+        functools.partial(line_kernel, cells),
+        out_shape=(float_shape(FACTORS, ROWS, LANES), float_shape(2 * PAIRS, ROWS, LANES)),
+        in_specs=[vmem, vmem, pl.BlockSpec(memory_space=pltpu.SMEM)],
+        out_specs=(vmem, vmem),
+        scratch_shapes=[pltpu.VMEM(size + plane, jnp.float32) for size in sizes],
+    )(every_cell, line_next.reshape(2, LANES), face_codes)
     return pl.pallas_call(
-        functools.partial(line_kernel, cells),
-        out_shape=jax.ShapeDtypeStruct(state.shape, jnp.float32),
-        in_specs=[vmem, vmem, pl.BlockSpec(memory_space=pltpu.SMEM)],
+        finish_kernel,
+        out_shape=float_shape(*state.shape),
+        in_specs=[vmem, vmem, vmem],
         out_specs=vmem,
-        scratch_shapes=[pltpu.VMEM(size + plane, jnp.float32) for size in sizes],
-    )(gathered, line_next.reshape(2, LANES), face_codes)
+        scratch_shapes=[
+            pltpu.VMEM((blocks // 2, STATE_ROWS, LANES), jnp.float32),
+            pltpu.VMEM((2, 2 * PAIRS) + plane, jnp.float32),
+        ],
+    )(every_time, factors, part)
 
 
 def solution(mesh):

time: 84.1 us -> 39.3 us (0.47)
  blocking collectives: 80 us -> 9.24 us
  waiting for transfers between devices: 0 us -> 12 us
  starting transfers between devices: 0 us -> 9.68 us
  Pallas kernels: 3.95 us -> 7.11 us
    all_gather x1 -> x0, blocking collectives: 80 us -> none  [local_by_gather(): gathered = lax.all_gather(packed, ('inst', 'cell'), axis=0, tiled=False)]
    all_to_all x0 -> x2, waiting for transfers between devices: none -> 12 us  [exchange(): return lax.all_to_all(copies, axis, split_axis=0, concat_axis=0, tiled=True)]
    all_to_all x0 -> x2, starting transfers between devices: none -> 9.68 us  [exchange(): return lax.all_to_all(copies, axis, split_axis=0, concat_axis=0, tiled=True)]
    all_to_all x0 -> x1, blocking collectives: none -> 9.24 us  [exchange(): return lax.all_to_all(copies, axis, split_axis=0, concat_axis=0, tiled=True)]
    pallas_call x2 -> x4, Pallas kernels: 3.95 us -> 7.11 us  [the longest x1 2.29 us: local_by_gather(): pl.pallas_call(functools.partial(line_kernel, cells), out_shape=(float_sh...]
  transfers between devices with their start and end apart: 0 -> 2, of which waited for: 0 -> 2; matrix products, arithmetic and copies ran while one was open for 0% -> 0% of each run, Pallas kernels for 0% -> 10%
where the time goes in v6:
time: 39.3 us; the launch traced here: 38.7 us
  waiting for transfers between devices  12 us (31%)
  starting transfers between devices  9.68 us (25%)
  blocking collectives  9.24 us (24%)
  Pallas kernels  7.11 us (18%)
  local copies, waits for them, and re-layouts  0.66 us (2%)
    all_to_all x2, waiting for transfers between devices, exchange(): return lax.all_to_all(copies, axis, split_axis=0, concat_axis=0, tiled=True)  12 us
    all_to_all x2, starting transfers between devices, exchange(): return lax.all_to_all(copies, axis, split_axis=0, concat_axis=0, tiled=True)  9.68 us
    all_to_all x1, blocking collectives, exchange(): return lax.all_to_all(copies, axis, split_axis=0, concat_axis=0, tiled=True)  9.24 us
    pallas_call x1, Pallas kernels, local_by_gather(): pl.pallas_call(functools.partial(line_kernel, cells), out_shape=(float_sh...  2.29 us
    pallas_call x1, Pallas kernels, local_by_gather(): pl.pallas_call(finish_kernel, out_shape=float_shape(*state.shape), in_spe...  1.73 us
    pallas_call x1, Pallas kernels, local_by_gather(): pl.pallas_call(time_kernel, out_shape=float_shape(blocks, STATE_ROWS, LAN...  1.59 us
    pallas_call x1, Pallas kernels, local_by_gather(): pl.pallas_call(pack_kernel, out_shape=(float_shape(inst_count, STATE_ROWS...  1.49 us
  transfers between devices with their start and end apart: 2, of which 2 were waited for; matrix products, arithmetic and copies ran while one was open for 0% of the time, Pallas kernels for 10%

profile of v6, /device:TPU:0, one launch (start us, length us, event | category | flops | bytes accessed | tf_op | source)
XLA Modules:
  0.0 38.7 jit_solution(5185122274626981239)
XLA Ops:
  0.0 1.5 %shard_map.46 = (f32[4,48,128]{2,1,0:T(8,128)}, f32[8,56,128]{2,1,0:T(8,128)}) custom-call(f32[2,6,2,256]{3,2,1,0:T(2,128)} %state_ref.1, f32[2,256]{1,0:T(2,128)} %rate_ref.1), custom_call_target="tpu_custom_call" | custom-call | tf_op jit(solution)/shard_map/pallas_call | solution.py:810
  1.5 9.2 %all_to_all.15.all_ref = f32[4,48,128]{2,1,0:T(8,128)} all-to-all(f32[4,48,128]{2,1,0:T(8,128)} %get-tuple-element.9), channel_id=1, replica_groups=mesh['inst'=4,'cell'=8] {'inst'}, dimensions={0} | all-to-all | bytes 196608 | tf_op jit(solution)/shard_map/all_to_all | solution.py:797
  10.7 6.3 %all-to-all-start.2 = ((f32[8,56,128]{2,1,0:T(8,128)}), f32[8,56,128]{2,1,0:T(8,128)S(1)}, u32[]{:S(2)}, u32[]{:S(2)}) async-start(f32[8,56,128]{2,1,0:T(8,128)} %get-tuple-element.10), calls=%async_computation.2 | async-start | bytes 458752 | tf_op jit(solution)/shard_map/all_to_all | solution.py:797
  17.0 1.6 %shard_map.47 = f32[8,48,128]{2,1,0:T(8,128)} custom-call(f32[4,48,128]{2,1,0:T(8,128)} %all_to_all.15.all_ref), custom_call_target="tpu_custom_call" | custom-call | tf_op jit(solution)/shard_map/pallas_call | solution.py:821
  18.6 6.6 %all-to-all-done.2.all_ref = f32[8,56,128]{2,1,0:T(8,128)S(1)} async-done(((f32[8,56,128]{2,1,0:T(8,128)}), f32[8,56,128]{2,1,0:T(8,128)S(1)}, u32[]{:S(2)}, u32[]{:S(2)}) %all-to-all-start.2) | async-done | bytes 229408 | tf_op jit(solution)/shard_map/all_to_all | solution.py:797
  25.2 0.0 copy-start
  25.2 3.4 %all-to-all-start.1 = ((f32[8,48,128]{2,1,0:T(8,128)}), f32[8,48,128]{2,1,0:T(8,128)S(1)}, u32[]{:S(2)}, u32[]{:S(2)}) async-start(f32[8,48,128]{2,1,0:T(8,128)} %shard_map.47), calls=%async_computation.1 | async-start | bytes 393216 | tf_op jit(solution)/shard_map/all_to_all | solution.py:797
  28.6 0.0 copy-done
  28.6 2.3 %shard_map.48 = (f32[56,8,128]{2,1,0:T(8,128)}, f32[6,8,128]{2,1,0:T(8,128)}) custom-call(f32[8,56,128]{2,1,0:T(8,128)} %copy-done, s32[2,128]{1,0:T(2,128)} %bitcast.1, s32[2,8]{1,0:T(2,128)} %codes_ref.1), custom_call_target="tpu_custom_call" | custom-call | tf_op jit(solution)/shard_map/pallas_call | solution.py:837
  30.9 5.5 %all-to-all-done.1.time_ref = f32[8,48,128]{2,1,0:T(8,128)S(1)} async-done(((f32[8,48,128]{2,1,0:T(8,128)}), f32[8,48,128]{2,1,0:T(8,128)S(1)}, u32[]{:S(2)}, u32[]{:S(2)}) %all-to-all-start.1) | async-done | bytes 196640 | tf_op jit(solution)/shard_map/all_to_all | solution.py:797
  36.3 0.0 copy-start.1
  36.3 0.7 %copy-done.1 = f32[8,48,128]{2,1,0:T(8,128)} copy-done((f32[8,48,128]{2,1,0:T(8,128)}, f32[8,48,128]{2,1,0:T(8,128)S(1)}, u32[]{:S(2)}) %copy-start.1) | copy-done | bytes 196632
  37.0 1.7 %shard_map.49 = f32[2,6,2,256]{3,2,1,0:T(2,128)} custom-call(f32[8,48,128]{2,1,0:T(8,128)} %copy-done.1, f32[56,8,128]{2,1,0:T(8,128)} %get-tuple-element.11.factor_ref, f32[6,8,128]{2,1,0:T(8,128)} %get-tuple-element.12.part_ref), custom_call_target="tpu_custom_call" | custom-call | tf_op jit(solution)/shard_map/pallas_call | solution.py:844
Async XLA Ops:
  10.7 14.4 %all-to-all-start.2 = ((f32[8,56,128]{2,1,0:T(8,128)}), f32[8,56,128]{2,1,0:T(8,128)S(1)}, u32[]{:S(2)}, u32[]{:S(2)}) async-start(f32[8,56,128]{2,1,0:T(8,128)} %get-tuple-element.10), calls=%async_computation.2 | async-start | bytes 458752 | tf_op jit(solution)/shard_map/all_to_all | solution.py:797
  25.2 3.4 %copy-start = (f32[8,56,128]{2,1,0:T(8,128)}, f32[8,56,128]{2,1,0:T(8,128)S(1)}, u32[]{:S(2)}) copy-start(f32[8,56,128]{2,1,0:T(8,128)S(1)} %all-to-all-done.2.all_ref) | copy-start | bytes 688132
  25.2 11.2 %all-to-all-start.1 = ((f32[8,48,128]{2,1,0:T(8,128)}), f32[8,48,128]{2,1,0:T(8,128)S(1)}, u32[]{:S(2)}, u32[]{:S(2)}) async-start(f32[8,48,128]{2,1,0:T(8,128)} %shard_map.47), calls=%async_computation.1 | async-start | bytes 393216 | tf_op jit(solution)/shard_map/all_to_all | solution.py:797
  36.3 0.7 %copy-start.1 = (f32[8,48,128]{2,1,0:T(8,128)}, f32[8,48,128]{2,1,0:T(8,128)S(1)}, u32[]{:S(2)}) copy-start(f32[8,48,128]{2,1,0:T(8,128)S(1)} %all-to-all-done.1.time_ref) | copy-start | bytes 589828

commit v7 on v4

--- a/solution.py
+++ b/solution.py
@@ -341,6 +341,7 @@
 CELL_ROWS = PAIRS * ROWS
 REST_ROW = 2 * CELL_ROWS
 RATE_ROW = 2 * REST_ROW
+VMEM_BYTES = 8 * 2**20
 BLOCK_ROWS = RATE_ROW + ROWS
 
 
@@ -768,6 +769,7 @@
         scratch_shapes=[
             pltpu.VMEM((every.shape[0] // 2, 2 * CELL_ROWS, LANES), jnp.float32)
         ],
+        compiler_params=pltpu.CompilerParams(vmem_limit_bytes=VMEM_BYTES),
     )(every, pseudo_rate, line_next.reshape(2, LANES))
     gathered = exchange_cell(packed)
     blocks = cells // 2
@@ -786,6 +788,7 @@
         in_specs=[vmem, pl.BlockSpec(memory_space=pltpu.SMEM)],
         out_specs=vmem,
         scratch_shapes=[pltpu.VMEM(size + plane, jnp.float32) for size in sizes],
+        compiler_params=pltpu.CompilerParams(vmem_limit_bytes=VMEM_BYTES),
     )(gathered, face_codes)
 
 

time: 31.6 us -> 28.6 us (0.905)
  Pallas kernels: 4 us -> 1.87 us
  blocking collectives: 27.3 us -> 25.8 us
  local copies, waits for them, and re-layouts: 0 us -> 0.69 us
    pallas_call x1, Pallas kernels: 1.95 us -> 0.28 us  [local_by_gather(): pl.pallas_call(cell_kernel, out_shape=jax.ShapeDtypeStruct((lax.axis_size...]
    all_gather x1, blocking collectives: 8.25 us -> 6.66 us  [gather_inst(): return lax.all_gather(block, 'inst', axis=0, tiled=True)]
    unnamed x0 -> x6, local copies, waits for them, and re-layouts: none -> 0.69 us
    pallas_call x1, Pallas kernels: 2.05 us -> 1.58 us  [local_by_gather(): pl.pallas_call(functools.partial(line_kernel, cells), out_shape=jax.Shape...]
where the time goes in v7:
time: 28.6 us; the launch traced here: 28.4 us
  blocking collectives  25.8 us (90%)
  Pallas kernels  1.87 us (7%)
  local copies, waits for them, and re-layouts  0.69 us (2%)
    all_to_all x1, blocking collectives, exchange_cell(): lax.all_to_all(copies, 'cell', split_axis=0, concat_axis=0, tiled=True)  19.2 us
    all_gather x1, blocking collectives, gather_inst(): return lax.all_gather(block, 'inst', axis=0, tiled=True)  6.66 us
    pallas_call x1, Pallas kernels, local_by_gather(): pl.pallas_call(functools.partial(line_kernel, cells), out_shape=jax.Shape...  1.58 us
    unnamed x6, local copies, waits for them, and re-layouts  0.69 us

profile of v7, /device:TPU:0, one launch (start us, length us, event | category | flops | bytes accessed | tf_op | source)
XLA Modules:
  0.0 28.4 jit_solution(2086183371441701207)
XLA Ops:
  0.0 0.0 copy-start
  0.0 6.7 %all_gather.3.all_ref = f32[8,6,2,256]{3,2,1,0:T(2,128)S(1)} all-gather(f32[2,6,2,256]{3,2,1,0:T(2,128)} %param.4), channel_id=1, replica_groups=mesh['inst'=4,'cell'=8] {'inst'}, dimensions={0}, use_global_device_ids=true | all-gather | bytes 122880 | tf_op jit(solution)/shard_map/all_gather | solution.py:750
  6.7 0.0 copy-start.1
  6.7 0.0 copy-done
  6.7 0.7 %copy-done.1 = s32[256]{0:T(256)S(1)} copy-done((s32[256]{0:T(256)S(1)}, s32[256]{0:T(256)}, u32[]{:S(2)}) %copy-start.1) | copy-done | bytes 1048
  7.3 0.3 %shard_map.46 = f32[8,104,128]{2,1,0:T(8,128)S(1)} custom-call(f32[8,6,2,256]{3,2,1,0:T(2,128)S(1)} %all_gather.3.all_ref, f32[2,256]{1,0:T(2,128)S(1)} %copy-done, s32[2,128]{1,0:T(2,128)S(1)} %bitcast.1), custom_call_target="tpu_custom_call" | custom-call | tf_op jit(solution)/shard_map/pallas_call | solution.py:762
  7.6 0.0 copy-start.2
  7.7 19.2 %all_to_all.5.all_ref = f32[8,104,128]{2,1,0:T(8,128)S(1)} all-to-all(f32[8,104,128]{2,1,0:T(8,128)S(1)} %shard_map.46), channel_id=1, replica_groups=mesh['inst'=4,'cell'=8] {'cell'}, dimensions={0} | all-to-all | bytes 851968 | tf_op jit(solution)/shard_map/all_to_all | solution.py:754
  26.8 0.0 copy-done.2
  26.8 1.6 %shard_map.47 = f32[2,6,2,256]{3,2,1,0:T(2,128)} custom-call(f32[8,104,128]{2,1,0:T(8,128)S(1)} %all_to_all.5.all_ref, s32[2,8]{1,0:T(2,128)S(1)} %copy-done.2), custom_call_target="tpu_custom_call" | custom-call | tf_op jit(solution)/shard_map/pallas_call | solution.py:785
Async XLA Ops:
  0.0 6.7 %copy-start = (f32[2,256]{1,0:T(2,128)S(1)}, f32[2,256]{1,0:T(2,128)}, u32[]{:S(2)}) copy-start(f32[2,256]{1,0:T(2,128)} %rate_ref.1) | copy-start | bytes 6148
  6.7 0.7 %copy-start.1 = (s32[256]{0:T(256)S(1)}, s32[256]{0:T(256)}, u32[]{:S(2)}) copy-start(s32[256]{0:T(256)} %param.6) | copy-start | bytes 3076
  7.6 19.2 %copy-start.2 = (s32[2,8]{1,0:T(2,128)S(1)}, s32[2,8]{1,0:T(2,128)}, u32[]{:S(2)}) copy-start(s32[2,8]{1,0:T(2,128)} %codes_ref.1) | copy-start | bytes 196

commit v8 on v7

--- a/solution.py
+++ b/solution.py
@@ -382,14 +382,114 @@
     return (var // 2) * ROWS + (var % 2) * 4 + inst * 2 + half
 
 
-def cell_kernel(all_ref, rate_ref, next_ref, out_ref, plane_ref):
+def cell_kernel(all_ref, rate_ref, out_ref, plane_ref):
     own_inst = lax.axis_index("inst")
     inst_count = all_ref.shape[0] // 2
     copies = out_ref.shape[0]
+    _, first_inst, _ = plane_masks()
+
+    for shift in range(inst_count):
+        pair = (own_inst - shift) & (inst_count - 1)
+        for cell in range(2):
+            for var in range(6):
+                for inst in range(2):
+                    for half in range(2):
+                        row = cell * CELL_ROWS + rows_of(var, inst, half)
+                        plane_ref[shift, pl.ds(row, 1), :] = all_ref[
+                            2 * pair + inst, var, pl.ds(cell, 1), pl.ds(half * LANES, LANES)
+                        ]
+    offsets = spectral_offsets()
+    for row in range(0, REST_ROW, ROWS):
+        same_total, other_total = None, None
+        for shift in range(inst_count):
+            plane = plane_ref[shift, pl.ds(row, ROWS), :]
+            other = jnp.where(
+                first_inst, offsets[(2 * shift + 1) % NT], offsets[(2 * shift - 1) % NT]
+            )
+            if shift > 0:
+                term = offsets[(2 * shift) % NT] * plane
+                same_total = term if same_total is None else same_total + term
+            term = other * plane
+            other_total = term if other_total is None else other_total + term
+        turned = jnp.where(
+            first_inst, pltpu.roll(other_total, 6, 0), pltpu.roll(other_total, 2, 0)
+        )
+        own = plane_ref[0, pl.ds(row, ROWS), :]
+        for copy in range(copies):
+            out_ref[copy, pl.ds(row, ROWS), :] = own
+            out_ref[copy, pl.ds(REST_ROW + row, ROWS), :] = same_total + turned
+    rates = [
+        rate_ref[pl.ds(cell, 1), pl.ds(half * LANES, LANES)]
+        for cell in range(2)
+        for half in range(2)
+    ]
+    for copy in range(copies):
+        for row, rate in enumerate(rates):
+            out_ref[copy, pl.ds(RATE_ROW + row, 1), :] = rate
+        out_ref[copy, pl.ds(RATE_ROW + 4, 4), :] = jnp.zeros((4, LANES), jnp.float32)
+
+
+def two_by_two(first, second):
+    def entry(a, b, c, d):
+        terms = [x * y for x, y in ((a, b), (c, d)) if x is not None and y is not None]
+        return None if not terms else terms[0] if len(terms) == 1 else terms[0] + terms[1]
+
+    return (
+        entry(first[0], second[0], first[1], second[2]),
+        entry(first[0], second[1], first[1], second[3]),
+        entry(first[2], second[0], first[3], second[2]),
+        entry(first[2], second[1], first[3], second[3]),
+    )
+
+
+def inverse_of(matrix):
+    reciprocal = 1.0 / (matrix[0] * matrix[3] - matrix[1] * matrix[2])
+    return (
+        matrix[3] * reciprocal,
+        -(matrix[1] * reciprocal),
+        -(matrix[2] * reciprocal),
+        matrix[0] * reciprocal,
+    )
+
+
+def less(first, second):
+    return tuple(a if b is None else a - b for a, b in zip(first, second))
+
+
+def minus(members):
+    return tuple(None if a is None else -a for a in members)
+
+
+def eliminate(centre, left, left_inverse, right, right_inverse):
+    left_factor = two_by_two(centre[0], left_inverse)
+    right_factor = two_by_two(centre[2], right_inverse)
+    sub = minus(two_by_two(left_factor, left[0]))
+    diag = less(
+        less(centre[1], two_by_two(left_factor, left[2])), two_by_two(right_factor, right[0])
+    )
+    sup = minus(two_by_two(right_factor, right[2]))
+    side = []
+    for k in range(PAIRS):
+        for row in range(2):
+            value = centre[3][row * PAIRS + k]
+            for factor, other in ((left_factor, left[3]), (right_factor, right[3])):
+                value = value - (
+                    factor[2 * row] * other[k] + factor[2 * row + 1] * other[PAIRS + k]
+                )
+            side.append((row * PAIRS + k, value))
+    return sub, diag, sup, [value for _, value in sorted(side, key=lambda item: item[0])]
+
+
+def line_kernel(
+    cells, all_ref, next_ref, codes_ref, out_ref, coef_ref, side_ref, coef2_ref, side2_ref,
+    couple_ref, diag3_ref, side3_ref,
+):
+    own_cell = lax.axis_index("cell")
     shape = (ROWS, LANES)
     lane_index = lax.broadcasted_iota(jnp.int32, shape, 1)
-    first_var, first_inst, half_index = plane_masks()
+    first_var, _, half_index = plane_masks()
     first_half = half_index == 0
+    zero = jnp.zeros(shape, jnp.float32)
 
     next_rows = [next_ref[pl.ds(half, 1), :] for half in range(2)]
     next_line = jnp.where(first_half, next_rows[0], next_rows[1])
@@ -422,138 +522,6 @@
     pick_next = picker(next_line)
     pick_prev = picker(prev_line)
 
-    for shift in range(inst_count):
-        pair = (own_inst - shift) & (inst_count - 1)
-        for cell in range(2):
-            for var in range(6):
-                for inst in range(2):
-                    for half in range(2):
-                        row = cell * CELL_ROWS + rows_of(var, inst, half)
-                        plane_ref[shift, pl.ds(row, 1), :] = all_ref[
-                            2 * pair + inst, var, pl.ds(cell, 1), pl.ds(half * LANES, LANES)
-                        ]
-    offsets = spectral_offsets()
-
-    def time_parts(cell):
-        same_total = [None] * PAIRS
-        other_total = [None] * PAIRS
-        for shift in range(inst_count):
-            same = offsets[(2 * shift) % NT]
-            other = jnp.where(
-                first_inst, offsets[(2 * shift + 1) % NT], offsets[(2 * shift - 1) % NT]
-            )
-            for k in range(PAIRS):
-                plane = plane_ref[shift, pl.ds(cell * CELL_ROWS + k * ROWS, ROWS), :]
-                if shift > 0:
-                    term = same * plane
-                    same_total[k] = term if same_total[k] is None else same_total[k] + term
-                term = other * plane
-                other_total[k] = term if other_total[k] is None else other_total[k] + term
-        return [
-            s + jnp.where(first_inst, pltpu.roll(o, 6, 0), pltpu.roll(o, 2, 0))
-            for s, o in zip(same_total, other_total)
-        ]
-
-    def flux_across(planes, velocity, pressure):
-        return [
-            planes[0] * velocity,
-            planes[1] * velocity + jnp.where(first_var, pressure, 0.0),
-            planes[2] * velocity + jnp.where(first_var, pressure * velocity, 0.0),
-        ]
-
-    for cell in range(2):
-        planes = [
-            plane_ref[0, pl.ds(cell * CELL_ROWS + k * ROWS, ROWS), :] for k in range(PAIRS)
-        ]
-        nearby = [pick_next(plane) for plane in planes]
-        _, velocity, pressure, sound = primitives(first_var, planes)
-        _, next_velocity, next_pressure, next_sound = primitives(first_var, nearby)
-        own_flux = flux_across(planes, velocity, pressure)
-        next_flux = flux_across(nearby, next_velocity, next_pressure)
-        weight = (PITCH_GAIN * 0.5) * (
-            jnp.abs(velocity) + sound + (jnp.abs(next_velocity) + next_sound)
-        )
-        time_term = time_parts(cell)
-        for k in range(PAIRS):
-            face = 0.5 * (own_flux[k] + next_flux[k]) - weight * (nearby[k] - planes[k])
-            rest = time_term[k] + (face - pick_prev(face))
-            row = cell * CELL_ROWS + k * ROWS
-            for copy in range(copies):
-                out_ref[copy, pl.ds(row, ROWS), :] = planes[k]
-                out_ref[copy, pl.ds(REST_ROW + row, ROWS), :] = rest
-    rates = [
-        rate_ref[pl.ds(cell, 1), pl.ds(half * LANES, LANES)]
-        for cell in range(2)
-        for half in range(2)
-    ]
-    for copy in range(copies):
-        for row, rate in enumerate(rates):
-            out_ref[copy, pl.ds(RATE_ROW + row, 1), :] = rate
-        out_ref[copy, pl.ds(RATE_ROW + 4, 4), :] = jnp.zeros((4, LANES), jnp.float32)
-
-
-def two_by_two(first, second):
-    def entry(a, b, c, d):
-        terms = [x * y for x, y in ((a, b), (c, d)) if x is not None and y is not None]
-        return None if not terms else terms[0] if len(terms) == 1 else terms[0] + terms[1]
-
-    return (
-        entry(first[0], second[0], first[1], second[2]),
-        entry(first[0], second[1], first[1], second[3]),
-        entry(first[2], second[0], first[3], second[2]),
-        entry(first[2], second[1], first[3], second[3]),
-    )
-
-
-def inverse_of(matrix):
-    reciprocal = 1.0 / (matrix[0] * matrix[3] - matrix[1] * matrix[2])
-    return (
-        matrix[3] * reciprocal,
-        -(matrix[1] * reciprocal),
-        -(matrix[2] * reciprocal),
-        matrix[0] * reciprocal,
-    )
-
-
-def less(first, second):
-    return tuple(a if b is None else a - b for a, b in zip(first, second))
-
-
-def minus(members):
-    return tuple(None if a is None else -a for a in members)
-
-
-def eliminate(centre, left, left_inverse, right, right_inverse):
-    left_factor = two_by_two(centre[0], left_inverse)
-    right_factor = two_by_two(centre[2], right_inverse)
-    sub = minus(two_by_two(left_factor, left[0]))
-    diag = less(
-        less(centre[1], two_by_two(left_factor, left[2])), two_by_two(right_factor, right[0])
-    )
-    sup = minus(two_by_two(right_factor, right[2]))
-    side = []
-    for k in range(PAIRS):
-        for row in range(2):
-            value = centre[3][row * PAIRS + k]
-            for factor, other in ((left_factor, left[3]), (right_factor, right[3])):
-                value = value - (
-                    factor[2 * row] * other[k] + factor[2 * row + 1] * other[PAIRS + k]
-                )
-            side.append((row * PAIRS + k, value))
-    return sub, diag, sup, [value for _, value in sorted(side, key=lambda item: item[0])]
-
-
-def line_kernel(
-    cells, all_ref, codes_ref, out_ref, coef_ref, side_ref, coef2_ref, side2_ref,
-    couple_ref, diag3_ref, side3_ref,
-):
-    own_cell = lax.axis_index("cell")
-    shape = (ROWS, LANES)
-    lane_index = lax.broadcasted_iota(jnp.int32, shape, 1)
-    first_var, _, half_index = plane_masks()
-    first_half = half_index == 0
-    zero = jnp.zeros(shape, jnp.float32)
-
     tile = half_index * (LANES // LINES_DEV) + lane_index // LINES_DEV
     codes = []
     for end in range(2):
@@ -586,9 +554,7 @@
         if cell < 0:
             return ghost(0, loaded(-1 - cell), loaded(0))
         if cell >= cells:
-            return ghost(
-                1, loaded(2 * cells - 1 - cell), loaded(cells - 1)
-            )
+            return ghost(1, loaded(2 * cells - 1 - cell), loaded(cells - 1))
         return loaded(cell)
 
     def flux_along(planes, velocity, pressure):
@@ -598,10 +564,30 @@
             planes[2] * velocity + jnp.where(first_var, pressure * velocity, 0.0),
         ]
 
-    state, pressures, radii, fluxes, steps, sensors, faces = {}, {}, {}, {}, {}, {}, {}
+    def flux_across(planes, velocity, pressure):
+        return [
+            planes[0] * velocity,
+            planes[1] * velocity + jnp.where(first_var, pressure, 0.0),
+            planes[2] * velocity + jnp.where(first_var, pressure * velocity, 0.0),
+        ]
+
+    def pitch_flux(planes, velocity_y, pressure, sound):
+        nearby = [pick_next(plane) for plane in planes]
+        _, next_velocity, next_pressure, next_sound = primitives(first_var, nearby)
+        own_flux = flux_across(planes, velocity_y, pressure)
+        next_flux = flux_across(nearby, next_velocity, next_pressure)
+        weight = (PITCH_GAIN * 0.5) * (
+            jnp.abs(velocity_y) + sound + (jnp.abs(next_velocity) + next_sound)
+        )
+        return [
+            0.5 * (a + b) - weight * (n - o)
+            for a, b, n, o in zip(own_flux, next_flux, nearby, planes)
+        ]
+
+    state, pressures, radii, fluxes, steps, rest, sensors, faces = {}, {}, {}, {}, {}, {}, {}, {}
     for cell in range(-2, cells + 2):
         planes = extended_state(cell)
-        velocity_x, _, pressure, sound = primitives(first_var, planes)
+        velocity_x, velocity_y, pressure, sound = primitives(first_var, planes)
         state[cell] = planes
         pressures[cell] = pressure
         radii[cell] = jnp.abs(velocity_x) + sound
@@ -609,6 +595,12 @@
             fluxes[cell] = flux_along(planes, velocity_x, pressure)
         if cell >= -1:
             steps[cell - 1] = [a - b for a, b in zip(planes, state[cell - 1])]
+        if 0 <= cell < cells:
+            faces_across = pitch_flux(planes, velocity_y, pressure, sound)
+            rest[cell] = [
+                time + (face - pick_prev(face))
+                for face, time in zip(faces_across, loaded(cell, REST_ROW))
+            ]
         if cell >= 0:
             twice = 2.0 * pressures[cell - 1]
             outer = pressure + pressures[cell - 2]
@@ -631,10 +623,9 @@
         if cell >= 2:
             at = cell - 2
             slot, member = at // 2 + 1, at % 2
-            rest = loaded(at, REST_ROW)
             for k in range(PAIRS):
                 side_ref[slot, member * PAIRS + k] = (
-                    faces[at - 1][k] - faces[at][k] - rest[k]
+                    faces[at - 1][k] - faces[at][k] - rest[at][k]
                 )
             below = radii[at - 1] if at > 0 else zero
             centre = radii[at]
@@ -764,13 +755,13 @@
         out_shape=jax.ShapeDtypeStruct(
             (lax.axis_size("cell"), BLOCK_ROWS, LANES), jnp.float32
         ),
-        in_specs=[vmem, vmem, vmem],
+        in_specs=[vmem, vmem],
         out_specs=vmem,
         scratch_shapes=[
             pltpu.VMEM((every.shape[0] // 2, 2 * CELL_ROWS, LANES), jnp.float32)
         ],
         compiler_params=pltpu.CompilerParams(vmem_limit_bytes=VMEM_BYTES),
-    )(every, pseudo_rate, line_next.reshape(2, LANES))
+    )(every, pseudo_rate)
     gathered = exchange_cell(packed)
     blocks = cells // 2
     sizes = [
@@ -785,11 +776,11 @@
     return pl.pallas_call(
         functools.partial(line_kernel, cells),
         out_shape=jax.ShapeDtypeStruct(state.shape, jnp.float32),
-        in_specs=[vmem, pl.BlockSpec(memory_space=pltpu.SMEM)],
+        in_specs=[vmem, vmem, pl.BlockSpec(memory_space=pltpu.SMEM)],
         out_specs=vmem,
         scratch_shapes=[pltpu.VMEM(size + plane, jnp.float32) for size in sizes],
         compiler_params=pltpu.CompilerParams(vmem_limit_bytes=VMEM_BYTES),
-    )(gathered, face_codes)
+    )(gathered, line_next.reshape(2, LANES), face_codes)
 
 
 def solution(mesh):

time: 28.6 us -> 28.7 us (level)
  no operation moved by 1% of the time
where the time goes in v8:
time: 28.7 us; the launch traced here: 28.5 us
  blocking collectives  25.8 us (90%)
  Pallas kernels  1.95 us (7%)
  local copies, waits for them, and re-layouts  0.69 us (2%)
    all_to_all x1, blocking collectives, exchange_cell(): lax.all_to_all(copies, 'cell', split_axis=0, concat_axis=0, tiled=True)  19.2 us
    all_gather x1, blocking collectives, gather_inst(): return lax.all_gather(block, 'inst', axis=0, tiled=True)  6.66 us
    pallas_call x1, Pallas kernels, local_by_gather(): pl.pallas_call(functools.partial(line_kernel, cells), out_shape=jax.Shape...  1.84 us
    unnamed x6, local copies, waits for them, and re-layouts  0.69 us

profile of v8, /device:TPU:0, one launch (start us, length us, event | category | flops | bytes accessed | tf_op | source)
XLA Modules:
  0.0 28.5 jit_solution(4842687218622028675)
XLA Ops:
  0.0 0.0 copy-start
  0.0 6.7 %all_gather.3.all_ref = f32[8,6,2,256]{3,2,1,0:T(2,128)S(1)} all-gather(f32[2,6,2,256]{3,2,1,0:T(2,128)} %param.4), channel_id=1, replica_groups=mesh['inst'=4,'cell'=8] {'inst'}, dimensions={0}, use_global_device_ids=true | all-gather | bytes 122880 | tf_op jit(solution)/shard_map/all_gather | solution.py:741
  6.7 0.0 copy-done
  6.7 0.1 shard_map.46
  6.8 0.0 copy-start.2
  6.8 19.2 %all_to_all.5.all_ref = f32[8,104,128]{2,1,0:T(8,128)S(1)} all-to-all(f32[8,104,128]{2,1,0:T(8,128)S(1)} %shard_map.46), channel_id=1, replica_groups=mesh['inst'=4,'cell'=8] {'cell'}, dimensions={0} | all-to-all | bytes 851968 | tf_op jit(solution)/shard_map/all_to_all | solution.py:745
  26.0 0.0 copy-start.1
  26.0 0.0 copy-done.2
  26.0 0.7 %copy-done.1 = s32[256]{0:T(256)S(1)} copy-done((s32[256]{0:T(256)S(1)}, s32[256]{0:T(256)}, u32[]{:S(2)}) %copy-start.1) | copy-done | bytes 1048
  26.6 1.8 %shard_map.47 = f32[2,6,2,256]{3,2,1,0:T(2,128)} custom-call(f32[8,104,128]{2,1,0:T(8,128)S(1)} %all_to_all.5.all_ref, s32[2,128]{1,0:T(2,128)S(1)} %bitcast.1, s32[2,8]{1,0:T(2,128)S(1)} %copy-done.2), custom_call_target="tpu_custom_call" | custom-call | tf_op jit(solution)/shard_map/pallas_call | solution.py:776
Async XLA Ops:
  0.0 6.7 %copy-start = (f32[2,256]{1,0:T(2,128)S(1)}, f32[2,256]{1,0:T(2,128)}, u32[]{:S(2)}) copy-start(f32[2,256]{1,0:T(2,128)} %rate_ref.1) | copy-start | bytes 6148
  6.8 19.2 %copy-start.2 = (s32[2,8]{1,0:T(2,128)S(1)}, s32[2,8]{1,0:T(2,128)}, u32[]{:S(2)}) copy-start(s32[2,8]{1,0:T(2,128)} %codes_ref.1) | copy-start | bytes 196
  26.0 0.7 %copy-start.1 = (s32[256]{0:T(256)S(1)}, s32[256]{0:T(256)}, u32[]{:S(2)}) copy-start(s32[256]{0:T(256)} %param.6) | copy-start | bytes 3076

commit v9 on v8

--- a/solution.py
+++ b/solution.py
@@ -481,9 +481,11 @@
 
 
 def line_kernel(
-    cells, all_ref, next_ref, codes_ref, out_ref, coef_ref, side_ref, coef2_ref, side2_ref,
-    couple_ref, diag3_ref, side3_ref,
+    cells, all_ref, next_ref, held_codes_ref, out_ref, coef_ref, side_ref, coef2_ref, side2_ref,
+    couple_ref, diag3_ref, side3_ref, line_ref, codes_ref, codes_sem,
 ):
+    fetch = pltpu.make_async_copy(held_codes_ref, codes_ref, codes_sem)
+    fetch.start()
     own_cell = lax.axis_index("cell")
     shape = (ROWS, LANES)
     lane_index = lax.broadcasted_iota(jnp.int32, shape, 1)
@@ -522,14 +524,6 @@
     pick_next = picker(next_line)
     pick_prev = picker(prev_line)
 
-    tile = half_index * (LANES // LINES_DEV) + lane_index // LINES_DEV
-    codes = []
-    for end in range(2):
-        plane = jnp.zeros(shape, jnp.int32)
-        for k in range(2 * LANES // LINES_DEV):
-            plane = jnp.where(tile == k, codes_ref[end, k], plane)
-        codes.append(plane)
-
     def loaded(cell, start=0):
         return [
             all_ref[cell // 2, pl.ds(start + (cell % 2) * CELL_ROWS + k * ROWS, ROWS), :]
@@ -584,10 +578,33 @@
             for a, b, n, o in zip(own_flux, next_flux, nearby, planes)
         ]
 
-    state, pressures, radii, fluxes, steps, rest, sensors, faces = {}, {}, {}, {}, {}, {}, {}, {}
+    for cell in range(cells):
+        planes = loaded(cell)
+        velocity_x, velocity_y, pressure, sound = primitives(first_var, planes)
+        line_ref[cell, 0], line_ref[cell, 1], line_ref[cell, 2] = velocity_x, pressure, sound
+        faces_across = pitch_flux(planes, velocity_y, pressure, sound)
+        times = loaded(cell, REST_ROW)
+        for k in range(PAIRS):
+            side_ref[cell // 2 + 1, (cell % 2) * PAIRS + k] = times[k] + (
+                faces_across[k] - pick_prev(faces_across[k])
+            )
+
+    fetch.wait()
+    tile = half_index * (LANES // LINES_DEV) + lane_index // LINES_DEV
+    codes = []
+    for end in range(2):
+        plane = jnp.zeros(shape, jnp.int32)
+        for k in range(2 * LANES // LINES_DEV):
+            plane = jnp.where(tile == k, codes_ref[end, k], plane)
+        codes.append(plane)
+
+    state, pressures, radii, fluxes, steps, sensors, faces = {}, {}, {}, {}, {}, {}, {}
     for cell in range(-2, cells + 2):
         planes = extended_state(cell)
-        velocity_x, velocity_y, pressure, sound = primitives(first_var, planes)
+        if 0 <= cell < cells:
+            velocity_x, pressure, sound = [line_ref[cell, k] for k in range(3)]
+        else:
+            velocity_x, _, pressure, sound = primitives(first_var, planes)
         state[cell] = planes
         pressures[cell] = pressure
         radii[cell] = jnp.abs(velocity_x) + sound
@@ -595,12 +612,6 @@
             fluxes[cell] = flux_along(planes, velocity_x, pressure)
         if cell >= -1:
             steps[cell - 1] = [a - b for a, b in zip(planes, state[cell - 1])]
-        if 0 <= cell < cells:
-            faces_across = pitch_flux(planes, velocity_y, pressure, sound)
-            rest[cell] = [
-                time + (face - pick_prev(face))
-                for face, time in zip(faces_across, loaded(cell, REST_ROW))
-            ]
         if cell >= 0:
             twice = 2.0 * pressures[cell - 1]
             outer = pressure + pressures[cell - 2]
@@ -624,9 +635,8 @@
             at = cell - 2
             slot, member = at // 2 + 1, at % 2
             for k in range(PAIRS):
-                side_ref[slot, member * PAIRS + k] = (
-                    faces[at - 1][k] - faces[at][k] - rest[at][k]
-                )
+                rest = side_ref[slot, member * PAIRS + k]
+                side_ref[slot, member * PAIRS + k] = faces[at - 1][k] - faces[at][k] - rest
             below = radii[at - 1] if at > 0 else zero
             centre = radii[at]
             above = radii[at + 1] if at < cells - 1 else zero
@@ -772,13 +782,15 @@
         (2, 2, 4),
         (2, 4),
         (2, 2 * PAIRS),
+        (cells, 3),
     ]
     return pl.pallas_call(
         functools.partial(line_kernel, cells),
         out_shape=jax.ShapeDtypeStruct(state.shape, jnp.float32),
-        in_specs=[vmem, vmem, pl.BlockSpec(memory_space=pltpu.SMEM)],
+        in_specs=[vmem, vmem, pl.BlockSpec(memory_space=pltpu.HBM)],
         out_specs=vmem,
-        scratch_shapes=[pltpu.VMEM(size + plane, jnp.float32) for size in sizes],
+        scratch_shapes=[pltpu.VMEM(size + plane, jnp.float32) for size in sizes]
+        + [pltpu.SMEM(face_codes.shape, jnp.int32), pltpu.SemaphoreType.DMA],
         compiler_params=pltpu.CompilerParams(vmem_limit_bytes=VMEM_BYTES),
     )(gathered, line_next.reshape(2, LANES), face_codes)
 

time: 28.7 us -> 28.4 us (0.990)
  Pallas kernels: 1.95 us -> 1.64 us
    pallas_call x1, Pallas kernels: 1.84 us -> 1.53 us  [local_by_gather(): pl.pallas_call(functools.partial(line_kernel, cells), out_shape=jax.Shape...]
where the time goes in v9:
time: 28.4 us; the launch traced here: 28.2 us
  blocking collectives  25.8 us (91%)
  Pallas kernels  1.64 us (6%)
  local copies, waits for them, and re-layouts  0.69 us (2%)
    all_to_all x1, blocking collectives, exchange_cell(): lax.all_to_all(copies, 'cell', split_axis=0, concat_axis=0, tiled=True)  19.2 us
    all_gather x1, blocking collectives, gather_inst(): return lax.all_gather(block, 'inst', axis=0, tiled=True)  6.66 us
    pallas_call x1, Pallas kernels, local_by_gather(): pl.pallas_call(functools.partial(line_kernel, cells), out_shape=jax.Shape...  1.53 us
    unnamed x6, local copies, waits for them, and re-layouts  0.69 us

profile of v9, /device:TPU:0, one launch (start us, length us, event | category | flops | bytes accessed | tf_op | source)
XLA Modules:
  0.0 28.2 jit_solution(1133355986426368408)
XLA Ops:
  0.0 0.0 copy-start
  0.0 6.7 %all_gather.3.all_ref = f32[8,6,2,256]{3,2,1,0:T(2,128)S(1)} all-gather(f32[2,6,2,256]{3,2,1,0:T(2,128)} %param.4), channel_id=1, replica_groups=mesh['inst'=4,'cell'=8] {'inst'}, dimensions={0}, use_global_device_ids=true | all-gather | bytes 122880 | tf_op jit(solution)/shard_map/all_gather | solution.py:751
  6.7 0.0 copy-done
  6.7 0.1 shard_map.46
  6.8 0.0 copy-start.2
  6.8 19.2 %all_to_all.5.all_ref = f32[8,104,128]{2,1,0:T(8,128)S(1)} all-to-all(f32[8,104,128]{2,1,0:T(8,128)S(1)} %shard_map.46), channel_id=1, replica_groups=mesh['inst'=4,'cell'=8] {'cell'}, dimensions={0} | all-to-all | bytes 851968 | tf_op jit(solution)/shard_map/all_to_all | solution.py:755
  26.0 0.0 copy-start.1
  26.0 0.0 copy-done.2
  26.0 0.7 %copy-done.1 = s32[256]{0:T(256)S(1)} copy-done((s32[256]{0:T(256)S(1)}, s32[256]{0:T(256)}, u32[]{:S(2)}) %copy-start.1) | copy-done | bytes 1048
  26.6 1.5 %shard_map.47 = f32[2,6,2,256]{3,2,1,0:T(2,128)} custom-call(f32[8,104,128]{2,1,0:T(8,128)S(1)} %all_to_all.5.all_ref, s32[2,128]{1,0:T(2,128)S(1)} %bitcast.1, s32[2,8]{1,0:T(2,128)S(1)} %copy-done.2), custom_call_target="tpu_custom_call" | custom-call | tf_op jit(solution)/shard_map/pallas_call | solution.py:787
Async XLA Ops:
  0.0 6.7 %copy-start = (f32[2,256]{1,0:T(2,128)S(1)}, f32[2,256]{1,0:T(2,128)}, u32[]{:S(2)}) copy-start(f32[2,256]{1,0:T(2,128)} %rate_ref.1) | copy-start | bytes 6148
  6.8 19.2 %copy-start.2 = (s32[2,8]{1,0:T(2,128)S(1)}, s32[2,8]{1,0:T(2,128)}, u32[]{:S(2)}) copy-start(s32[2,8]{1,0:T(2,128)} %held_codes_ref.1) | copy-start | bytes 196
  26.0 0.7 %copy-start.1 = (s32[256]{0:T(256)S(1)}, s32[256]{0:T(256)}, u32[]{:S(2)}) copy-start(s32[256]{0:T(256)} %param.6) | copy-start | bytes 3076

commit v10 on v9

--- a/solution.py
+++ b/solution.py
@@ -493,7 +493,9 @@
     first_half = half_index == 0
     zero = jnp.zeros(shape, jnp.float32)
 
-    next_rows = [next_ref[pl.ds(half, 1), :] for half in range(2)]
+    next_rows = [
+        next_ref[pl.ds(half * LANES, LANES)].reshape(1, LANES) for half in range(2)
+    ]
     next_line = jnp.where(first_half, next_rows[0], next_rows[1])
     column = lax.broadcasted_iota(jnp.int32, (LANES, LANES), 0)
     prev_halves = []
@@ -792,7 +794,7 @@
         scratch_shapes=[pltpu.VMEM(size + plane, jnp.float32) for size in sizes]
         + [pltpu.SMEM(face_codes.shape, jnp.int32), pltpu.SemaphoreType.DMA],
         compiler_params=pltpu.CompilerParams(vmem_limit_bytes=VMEM_BYTES),
-    )(gathered, line_next.reshape(2, LANES), face_codes)
+    )(gathered, line_next, face_codes)
 
 
 def solution(mesh):

time: 28.4 us -> 27.7 us (0.975)
  local copies, waits for them, and re-layouts: 0.69 us -> 0.02 us
    unnamed x6, local copies, waits for them, and re-layouts: 0.69 us -> 0.02 us
where the time goes in v10:
time: 27.7 us; the launch traced here: 27.5 us
  blocking collectives  25.8 us (93%)
  Pallas kernels  1.64 us (6%)
    all_to_all x1, blocking collectives, exchange_cell(): lax.all_to_all(copies, 'cell', split_axis=0, concat_axis=0, tiled=True)  19.2 us
    all_gather x1, blocking collectives, gather_inst(): return lax.all_gather(block, 'inst', axis=0, tiled=True)  6.66 us
    pallas_call x1, Pallas kernels, local_by_gather(): pl.pallas_call(functools.partial(line_kernel, cells), out_shape=jax.Shape...  1.53 us

profile of v10, /device:TPU:0, one launch (start us, length us, event | category | flops | bytes accessed | tf_op | source)
XLA Modules:
  0.0 27.5 jit_solution(7566775791685620275)
XLA Ops:
  0.0 0.0 copy-start
  0.0 6.7 %all_gather.3.all_ref = f32[8,6,2,256]{3,2,1,0:T(2,128)S(1)} all-gather(f32[2,6,2,256]{3,2,1,0:T(2,128)} %param.4), channel_id=1, replica_groups=mesh['inst'=4,'cell'=8] {'inst'}, dimensions={0}, use_global_device_ids=true | all-gather | bytes 122880 | tf_op jit(solution)/shard_map/all_gather | solution.py:753
  6.7 0.0 copy-done
  6.7 0.1 shard_map.46
  6.8 0.0 copy-start.1
  6.8 0.0 copy-start.2
  6.8 19.2 %all_to_all.5.all_ref = f32[8,104,128]{2,1,0:T(8,128)S(1)} all-to-all(f32[8,104,128]{2,1,0:T(8,128)S(1)} %shard_map.46), channel_id=1, replica_groups=mesh['inst'=4,'cell'=8] {'cell'}, dimensions={0} | all-to-all | bytes 851968 | tf_op jit(solution)/shard_map/all_to_all | solution.py:757
  26.0 0.0 copy-done.1
  26.0 0.0 copy-done.2
  26.0 1.5 %shard_map.47 = f32[2,6,2,256]{3,2,1,0:T(2,128)} custom-call(f32[8,104,128]{2,1,0:T(8,128)S(1)} %all_to_all.5.all_ref, s32[256]{0:T(256)S(1)} %copy-done.1, s32[2,8]{1,0:T(2,128)S(1)} %copy-done.2), custom_call_target="tpu_custom_call" | custom-call | tf_op jit(solution)/shard_map/pallas_call | solution.py:789
Async XLA Ops:
  0.0 6.7 %copy-start = (f32[2,256]{1,0:T(2,128)S(1)}, f32[2,256]{1,0:T(2,128)}, u32[]{:S(2)}) copy-start(f32[2,256]{1,0:T(2,128)} %rate_ref.1) | copy-start | bytes 6148
  6.8 19.2 %copy-start.1 = (s32[256]{0:T(256)S(1)}, s32[256]{0:T(256)}, u32[]{:S(2)}) copy-start(s32[256]{0:T(256)} %next_ref.1) | copy-start | bytes 3076
  6.8 19.2 %copy-start.2 = (s32[2,8]{1,0:T(2,128)S(1)}, s32[2,8]{1,0:T(2,128)}, u32[]{:S(2)}) copy-start(s32[2,8]{1,0:T(2,128)} %held_codes_ref.1) | copy-start | bytes 196

commit v11 on v0

--- a/solution.py
+++ b/solution.py
@@ -1,7 +1,11 @@
+import functools
+
 import jax
 import jax.numpy as jnp
 import numpy as np
 from jax import lax
+from jax.experimental import pallas as pl
+from jax.experimental.pallas import tpu as pltpu
 from jax.sharding import PartitionSpec as P
 
 NT = 8
@@ -291,7 +295,7 @@
     return lax.all_to_all(line_values, "cell", split_axis=2, concat_axis=3, tiled=True)
 
 
-def local(state, pseudo_rate, line_next, face_codes):
+def local_by_lines(state, pseudo_rate, line_next, face_codes):
     local_count = state.shape[0]
     tile_cells = state.shape[2]
     cell_index = lax.axis_index("cell")
@@ -331,8 +335,530 @@
     return state + update
 
 
+LANES = 128
+ROWS = 8
+PAIRS = 3
+CELL_ROWS = PAIRS * ROWS
+REST_ROW = 2 * CELL_ROWS
+RATE_ROW = 2 * REST_ROW
+VMEM_BYTES = 8 * 2**20
+BLOCK_ROWS = RATE_ROW + ROWS
+
+SIDE_ROW = 3 * CELL_ROWS
+CORRECTION_ROW = SIDE_ROW + 2 * CELL_ROWS
+MIDDLE_RATE_ROW = CORRECTION_ROW + 2 * ROWS
+MIDDLE_ROWS = MIDDLE_RATE_ROW + ROWS
+
+
+def spectral_offsets():
+    table = np.zeros(NT)
+    for offset in range(1, NT):
+        angle = np.pi * offset / NT
+        parity = -1.0 if offset % 2 == 0 else 1.0
+        table[offset] = 0.5 * OMEGA_BLADE * parity * np.cos(angle) / np.sin(angle)
+    return [float(np.float32(value)) for value in table]
+
+
+def plane_masks():
+    row_index = lax.broadcasted_iota(jnp.int32, (ROWS, LANES), 0)
+    return row_index < 4, (row_index & 2) == 0, row_index & 1
+
+
+def both(first_var, plane):
+    turned = pltpu.roll(plane, 4, 0)
+    return jnp.where(first_var, plane, turned), jnp.where(first_var, turned, plane)
+
+
+def primitives(first_var, planes):
+    density, moment_x = both(first_var, planes[0])
+    moment_y, moment_z = both(first_var, planes[1])
+    energy = jnp.where(first_var, planes[2], pltpu.roll(planes[2], 4, 0))
+    inverse = 1.0 / density
+    velocity_x = moment_x * inverse
+    velocity_y = moment_y * inverse
+    velocity_z = moment_z * inverse
+    kinetic = moment_x * velocity_x + moment_y * velocity_y + moment_z * velocity_z
+    pressure = (GAMMA_GAS - 1.0) * (energy - 0.5 * kinetic)
+    sound = jnp.sqrt(GAMMA_GAS * pressure * inverse)
+    return velocity_x, velocity_y, pressure, sound
+
+
+def rows_of(var, inst, half):
+    return (var // 2) * ROWS + (var % 2) * 4 + inst * 2 + half
+
+
+def cell_kernel(all_ref, rate_ref, out_ref, plane_ref):
+    own_inst = lax.axis_index("inst")
+    inst_count = all_ref.shape[0] // 2
+    copies = out_ref.shape[0]
+    mirrored = lax.axis_index("cell") // copies
+    _, first_inst, _ = plane_masks()
+
+    for shift in range(inst_count):
+        pair = (own_inst - shift) & (inst_count - 1)
+        for cell in range(2):
+            for var in range(6):
+                for inst in range(2):
+                    for half in range(2):
+                        row = cell * CELL_ROWS + rows_of(var, inst, half)
+                        plane_ref[shift, pl.ds(row, 1), :] = all_ref[
+                            2 * pair + inst, var, pl.ds(cell, 1), pl.ds(half * LANES, LANES)
+                        ]
+    offsets = spectral_offsets()
+    for row in range(0, REST_ROW, ROWS):
+        same_total, other_total = None, None
+        for shift in range(inst_count):
+            plane = plane_ref[shift, pl.ds(row, ROWS), :]
+            other = jnp.where(
+                first_inst, offsets[(2 * shift + 1) % NT], offsets[(2 * shift - 1) % NT]
+            )
+            if shift > 0:
+                term = offsets[(2 * shift) % NT] * plane
+                same_total = term if same_total is None else same_total + term
+            term = other * plane
+            other_total = term if other_total is None else other_total + term
+        turned = jnp.where(
+            first_inst, pltpu.roll(other_total, 6, 0), pltpu.roll(other_total, 2, 0)
+        )
+        own = plane_ref[0, pl.ds(row, ROWS), :]
+        place = jnp.bitwise_xor(row // CELL_ROWS, mirrored) * CELL_ROWS + row % CELL_ROWS
+        place = pl.multiple_of(place, ROWS)
+        for copy in range(copies):
+            out_ref[copy, pl.ds(place, ROWS), :] = own
+            out_ref[copy, pl.ds(REST_ROW + place, ROWS), :] = same_total + turned
+    rates = [
+        rate_ref[pl.ds(cell, 1), pl.ds(half * LANES, LANES)]
+        for cell in range(2)
+        for half in range(2)
+    ]
+    rates = [jnp.where(mirrored == 0, rates[k], rates[k ^ 2]) for k in range(4)]
+    for copy in range(copies):
+        for row, rate in enumerate(rates):
+            out_ref[copy, pl.ds(RATE_ROW + row, 1), :] = rate
+        out_ref[copy, pl.ds(RATE_ROW + 4, 4), :] = jnp.zeros((4, LANES), jnp.float32)
+
+
+def two_by_two(first, second):
+    def entry(a, b, c, d):
+        terms = [x * y for x, y in ((a, b), (c, d)) if x is not None and y is not None]
+        return None if not terms else terms[0] if len(terms) == 1 else terms[0] + terms[1]
+
+    return (
+        entry(first[0], second[0], first[1], second[2]),
+        entry(first[0], second[1], first[1], second[3]),
+        entry(first[2], second[0], first[3], second[2]),
+        entry(first[2], second[1], first[3], second[3]),
+    )
+
+
+def inverse_of(matrix):
+    reciprocal = 1.0 / (matrix[0] * matrix[3] - matrix[1] * matrix[2])
+    return (
+        matrix[3] * reciprocal,
+        -(matrix[1] * reciprocal),
+        -(matrix[2] * reciprocal),
+        matrix[0] * reciprocal,
+    )
+
+
+def less(first, second):
+    return tuple(a if b is None else a - b for a, b in zip(first, second))
+
+
+def minus(members):
+    return tuple(None if a is None else -a for a in members)
+
+
+def matrix_vector(matrix, low, high):
+    def row(a, b):
+        terms = [x * y for x, y in ((a, low), (b, high)) if x is not None]
+        return terms[0] if len(terms) == 1 else terms[0] + terms[1]
+
+    return row(matrix[0], matrix[1]), row(matrix[2], matrix[3])
+
+
+def apply_matrix(matrix, side):
+    parts = [matrix_vector(matrix, side[k], side[PAIRS + k]) for k in range(PAIRS)]
+    return [low for low, _ in parts] + [high for _, high in parts]
+
+
+def difference(first, second):
+    return [a - b for a, b in zip(first, second)]
+
+
+def flux_along(first_var, planes, velocity, pressure, sign):
+    normal = sign * velocity
+    return [
+        planes[0] * normal + jnp.where(first_var, 0.0, sign * pressure),
+        planes[1] * normal,
+        planes[2] * normal + jnp.where(first_var, pressure * normal, 0.0),
+    ]
+
+
+class LineCells:
+    def __init__(self, first_var, sign):
+        self.first_var, self.sign = first_var, sign
+        self.state, self.pressure, self.radius = {}, {}, {}
+        self.flux, self.step, self.sensor = {}, {}, {}
+
+    def add(self, cell, planes, velocity, pressure, sound):
+        self.state[cell], self.pressure[cell] = planes, pressure
+        self.radius[cell] = jnp.abs(velocity) + sound
+        self.flux[cell] = flux_along(self.first_var, planes, velocity, pressure, self.sign)
+        if cell - 1 in self.state:
+            self.step[cell - 1] = difference(planes, self.state[cell - 1])
+        if cell - 2 in self.state:
+            twice = 2.0 * self.pressure[cell - 1]
+            outer = pressure + self.pressure[cell - 2]
+            self.sensor[cell - 1] = jnp.abs(outer - twice) / (outer + twice)
+
+    def face(self, cell):
+        second = SENSOR_GAIN * jnp.maximum(self.sensor[cell], self.sensor[cell + 1])
+        fourth = jnp.maximum(0.0, FOURTH_GAIN - second)
+        face_radius = 0.5 * (self.radius[cell] + self.radius[cell + 1])
+        near_weight = face_radius * (second + 2.0 * fourth)
+        far_weight = face_radius * fourth
+        return [
+            0.5 * (self.flux[cell][k] + self.flux[cell + 1][k])
+            - (
+                near_weight * self.step[cell][k]
+                - far_weight * (self.step[cell + 1][k] + self.step[cell - 1][k])
+            )
+            for k in range(PAIRS)
+        ]
+
+    def near(self, cell):
+        scale = SECOND_IMPL * 0.5 + 2.0 * FOURTH_IMPL
+        return -scale * (self.radius[cell] + self.radius[cell + 1])
+
+    def far(self, cell):
+        return FOURTH_IMPL * self.radius[cell]
+
+    def middle(self, cell, rate):
+        centre, above = self.radius[cell], self.radius[cell + 1]
+        if cell == 0:
+            total, weighted = centre + (centre + above), 4.0 * centre + above
+        else:
+            below = self.radius[cell - 1]
+            total = (below + centre) + (centre + above)
+            weighted = below + 4.0 * centre + above
+        return rate * centre + SECOND_IMPL * (0.5 * total) + FOURTH_IMPL * weighted
+
+    def diagonal(self, cell, rates):
+        across = self.near(cell)
+        return (self.middle(cell, rates[0]), across, across, self.middle(cell + 1, rates[1]))
+
+    def below(self, cell):
+        return (self.far(cell - 1), self.near(cell - 1), None, self.far(cell))
+
+    def above(self, cell):
+        return (self.far(cell + 1), None, self.near(cell + 1), self.far(cell + 2))
+
+
+def rates_at(ref, index, start, first_half):
+    rows = [ref[index + (pl.ds(start + k, 1), slice(None))] for k in range(4)]
+    return [jnp.where(first_half, rows[2 * k], rows[2 * k + 1]) for k in range(2)]
+
+
+def half_kernel(
+    all_ref, next_ref, held_codes_ref, middle_ref, known_ref, spread_ref,
+    rest_ref, line_ref, codes_ref, codes_sem,
+):
+    fetch = pltpu.make_async_copy(held_codes_ref, codes_ref, codes_sem)
+    fetch.start()
+    blocks = all_ref.shape[0]
+    cells = 2 * blocks
+    mirrored = lax.axis_index("cell") // blocks
+    sign = (1 - 2 * mirrored).astype(jnp.float32)
+    shape = (ROWS, LANES)
+    lane_index = lax.broadcasted_iota(jnp.int32, shape, 1)
+    first_var, _, half_index = plane_masks()
+    first_half = half_index == 0
+    zero = jnp.zeros(shape, jnp.float32)
+
+    next_rows = [
+        next_ref[pl.ds(half * LANES, LANES)].reshape(1, LANES) for half in range(2)
+    ]
+    next_line = jnp.where(first_half, next_rows[0], next_rows[1])
+    column = lax.broadcasted_iota(jnp.int32, (LANES, LANES), 0)
+    prev_halves = []
+    for target in range(2):
+        total = None
+        for source in range(2):
+            hits = jnp.where(column + target * LANES == next_rows[source], 1.0, 0.0)
+            names = (lane_index + source * LANES).astype(jnp.float32)
+            part = lax.dot_general(
+                names, hits, (((1,), (1,)), ((), ())), preferred_element_type=jnp.float32
+            )
+            total = part if total is None else total + part
+        prev_halves.append(total)
+    prev_line = jnp.where(first_half, prev_halves[0], prev_halves[1]).astype(jnp.int32)
+
+    def picker(lines):
+        lane = lines & (LANES - 1)
+        same = (lines >> 7) == half_index
+
+        def pick(plane):
+            swapped = jnp.where(first_half, pltpu.roll(plane, 7, 0), pltpu.roll(plane, 1, 0))
+            here = jnp.take_along_axis(plane, lane, axis=1, mode="promise_in_bounds")
+            there = jnp.take_along_axis(swapped, lane, axis=1, mode="promise_in_bounds")
+            return jnp.where(same, here, there)
+
+        return pick
+
+    pick_next = picker(next_line)
+    pick_prev = picker(prev_line)
+
+    def loaded(cell, start=0):
+        return [
+            all_ref[cell // 2, pl.ds(start + (cell % 2) * CELL_ROWS + k * ROWS, ROWS), :]
+            for k in range(PAIRS)
+        ]
+
+    def flux_across(planes, velocity, pressure):
+        return [
+            planes[0] * velocity,
+            planes[1] * velocity + jnp.where(first_var, pressure, 0.0),
+            planes[2] * velocity + jnp.where(first_var, pressure * velocity, 0.0),
+        ]
+
+    def pitch_flux(planes, velocity_y, pressure, sound):
+        nearby = [pick_next(plane) for plane in planes]
+        _, next_velocity, next_pressure, next_sound = primitives(first_var, nearby)
+        own_flux = flux_across(planes, velocity_y, pressure)
+        next_flux = flux_across(nearby, next_velocity, next_pressure)
+        weight = (PITCH_GAIN * 0.5) * (
+            jnp.abs(velocity_y) + sound + (jnp.abs(next_velocity) + next_sound)
+        )
+        return [
+            0.5 * (a + b) - weight * (n - o)
+            for a, b, n, o in zip(own_flux, next_flux, nearby, planes)
+        ]
+
+    for cell in range(cells):
+        planes = loaded(cell)
+        velocity_x, velocity_y, pressure, sound = primitives(first_var, planes)
+        line_ref[cell, 0], line_ref[cell, 1], line_ref[cell, 2] = velocity_x, pressure, sound
+        faces_across = pitch_flux(planes, velocity_y, pressure, sound)
+        times = loaded(cell, REST_ROW)
+        for k in range(PAIRS):
+            rest_ref[cell, k] = times[k] + (faces_across[k] - pick_prev(faces_across[k]))
+
+    fetch.wait()
+    tile = half_index * (LANES // LINES_DEV) + lane_index // LINES_DEV
+    codes = jnp.zeros(shape, jnp.int32)
+    for k in range(2 * LANES // LINES_DEV):
+        codes = jnp.where(tile == k, codes_ref[mirrored, k], codes)
+
+    def ghost(cell):
+        planes = loaded(-1 - cell)
+        copied = loaded(0)
+        result = []
+        for k in range(PAIRS):
+            reflected = planes[k] if k else jnp.where(first_var, planes[k], -planes[k])
+            inflow = jnp.where(first_var, FREE_STATE[2 * k], FREE_STATE[2 * k + 1])
+            result.append(
+                jnp.where(codes == 0, reflected, jnp.where(codes == 1, inflow, copied[k]))
+            )
+        return result
+
+    line = LineCells(first_var, sign)
+    sides, faces, inverses, aboves = [], {}, [], []
+    for cell in range(-2, cells):
+        if cell < 0:
+            planes = ghost(cell)
+            velocity_x, _, pressure, sound = primitives(first_var, planes)
+        else:
+            planes = loaded(cell)
+            velocity_x, pressure, sound = [line_ref[cell, k] for k in range(3)]
+        line.add(cell, planes, velocity_x, pressure, sound)
+        if cell >= 1:
+            faces[cell - 2] = line.face(cell - 2)
+        if cell >= 3 and cell % 2 == 1:
+            at = cell - 3
+            block = at // 2
+            rates = rates_at(all_ref, (block,), RATE_ROW, first_half)
+            diag = line.diagonal(at, rates)
+            side = []
+            for member in range(2):
+                for k in range(PAIRS):
+                    side.append(
+                        faces[at + member - 1][k] - faces[at + member][k]
+                        - rest_ref[at + member, k]
+                    )
+            if block > 0:
+                factor = two_by_two(line.below(at), inverses[-1])
+                diag = less(diag, two_by_two(factor, aboves[-1]))
+                side = difference(side, apply_matrix(factor, sides[-1]))
+            inverses.append(inverse_of(diag))
+            aboves.append(line.above(at))
+            sides.append(side)
+
+    last = cells - 2
+    factor = two_by_two(line.below(last), inverses[-1])
+    correction = two_by_two(factor, aboves[-1])
+    side = [faces[last - 1][k] - rest_ref[last, k] for k in range(PAIRS)]
+    side += [-rest_ref[last + 1, k] for k in range(PAIRS)]
+    side = difference(side, apply_matrix(factor, sides[-1]))
+    for n in range(3):
+        for k, plane in enumerate(line.state[cells - 3 + n]):
+            middle_ref[pl.ds(n * CELL_ROWS + k * ROWS, ROWS), :] = plane
+    for n, plane in enumerate(side):
+        middle_ref[pl.ds(SIDE_ROW + n * ROWS, ROWS), :] = plane
+    for n in range(2):
+        middle_ref[pl.ds(CORRECTION_ROW + n * ROWS, ROWS), :] = jnp.where(
+            first_var, correction[2 * n], correction[2 * n + 1]
+        )
+    middle_ref[pl.ds(MIDDLE_RATE_ROW, ROWS), :] = all_ref[
+        blocks - 1, pl.ds(RATE_ROW, ROWS), :
+    ]
+
+    known, spread = [zero] * (2 * PAIRS), (zero + 1.0, zero, zero, zero + 1.0)
+    for block in range(blocks - 1, -1, -1):
+        if block < blocks - 1:
+            step = two_by_two(inverses[block], aboves[block])
+            own = apply_matrix(inverses[block], sides[block])
+            if block < blocks - 2:
+                known = difference(own, apply_matrix(step, known))
+                spread = minus(two_by_two(step, spread))
+            else:
+                known, spread = own, minus(step)
+        for n, plane in enumerate(known):
+            known_ref[block, n] = plane
+        for n, plane in enumerate(spread):
+            spread_ref[block, n] = plane
+
+
+def join_kernel(all_ref, here_ref, there_ref, known_ref, spread_ref, out_ref):
+    blocks = all_ref.shape[0]
+    own_cell = lax.axis_index("cell")
+    mirrored = own_cell // blocks
+    own_block = jnp.where(mirrored == 0, own_cell, 2 * blocks - 1 - own_cell)
+    sign = (1 - 2 * mirrored).astype(jnp.float32)
+    first_var, _, half_index = plane_masks()
+    first_half = half_index == 0
+
+    def plane_of(ref, row):
+        return ref[pl.ds(row, ROWS), :]
+
+    line = LineCells(first_var, sign)
+    for cell in range(6):
+        ref, at = (here_ref, cell) if cell < 3 else (there_ref, 5 - cell)
+        planes = [plane_of(ref, at * CELL_ROWS + k * ROWS) for k in range(PAIRS)]
+        velocity_x, _, pressure, sound = primitives(first_var, planes)
+        line.add(cell, planes, velocity_x, pressure, sound)
+    faces = {cell: line.face(cell) for cell in (1, 2, 3)}
+
+    def correction_of(ref):
+        pairs = [both(first_var, plane_of(ref, CORRECTION_ROW + n * ROWS)) for n in range(2)]
+        return [pairs[0][0], pairs[0][1], pairs[1][0], pairs[1][1]]
+
+    here_side = [plane_of(here_ref, SIDE_ROW + n * ROWS) for n in range(2 * PAIRS)]
+    there_side = [plane_of(there_ref, SIDE_ROW + n * ROWS) for n in range(2 * PAIRS)]
+    side = [here_side[k] - faces[1][k] for k in range(PAIRS)]
+    side += [here_side[PAIRS + k] + (faces[1][k] - faces[2][k]) for k in range(PAIRS)]
+    other = [there_side[PAIRS + k] + (faces[2][k] - faces[3][k]) for k in range(PAIRS)]
+    other += [there_side[k] + faces[3][k] for k in range(PAIRS)]
+    here_rates = rates_at(here_ref, (), MIDDLE_RATE_ROW, first_half)
+    there_rates = rates_at(there_ref, (), MIDDLE_RATE_ROW, first_half)
+    diag = difference(line.diagonal(1, here_rates), correction_of(here_ref))
+    other_diag = difference(line.diagonal(3, there_rates[::-1]), correction_of(there_ref)[::-1])
+    factor = two_by_two(line.above(1), inverse_of(other_diag))
+    diag = less(diag, two_by_two(factor, line.below(3)))
+    middle = apply_matrix(inverse_of(diag), difference(side, apply_matrix(factor, other)))
+    spread = [spread_ref[own_block, n] for n in range(4)]
+    moved = apply_matrix(spread, middle)
+    results = []
+    for n in range(2 * PAIRS):
+        base = all_ref[own_block, pl.ds(n * ROWS, ROWS), :]
+        results.append(base + (known_ref[own_block, n] + moved[n]))
+    for cell in range(2):
+        for k in range(PAIRS):
+            first, second = results[cell * PAIRS + k], results[(1 - cell) * PAIRS + k]
+            result = jnp.where(mirrored == 0, first, second)
+            for var in range(2):
+                for inst in range(2):
+                    for half in range(2):
+                        row = rows_of(var, inst, half)
+                        out_ref[
+                            inst, 2 * k + var, pl.ds(cell, 1), pl.ds(half * LANES, LANES)
+                        ] = result[row : row + 1]
+
+
+def share_half(copies):
+    count = lax.axis_size("cell")
+    groups = [list(range(count // 2)), list(range(count - 1, count // 2 - 1, -1))]
+    return lax.all_to_all(
+        copies, "cell", split_axis=0, concat_axis=0, tiled=True, axis_index_groups=groups
+    )
+
+
+def swap_halves(block):
+    count = lax.axis_size("cell")
+    return lax.ppermute(block, "cell", [(i, (i + count // 2) % count) for i in range(count)])
+
+
+def float_shape(*sizes):
+    return jax.ShapeDtypeStruct(sizes, jnp.float32)
+
+
+def local_by_halves(state, pseudo_rate, line_next, face_codes):
+    blocks = lax.axis_size("cell") // 2
+    cells = 2 * blocks
+    vmem = pl.BlockSpec(memory_space=pltpu.VMEM)
+    plane = (ROWS, LANES)
+    params = pltpu.CompilerParams(vmem_limit_bytes=VMEM_BYTES)
+    every = lax.all_gather(state, "inst", axis=0, tiled=True)
+    packed = pl.pallas_call(
+        cell_kernel,
+        out_shape=float_shape(blocks, BLOCK_ROWS, LANES),
+        in_specs=[vmem, vmem],
+        out_specs=vmem,
+        scratch_shapes=[pltpu.VMEM((every.shape[0] // 2, REST_ROW, LANES), jnp.float32)],
+        compiler_params=params,
+    )(every, pseudo_rate)
+    shared = share_half(packed)
+    here, known, spread = pl.pallas_call(
+        half_kernel,
+        out_shape=(
+            float_shape(MIDDLE_ROWS, LANES),
+            float_shape(blocks, 2 * PAIRS, *plane),
+            float_shape(blocks, 4, *plane),
+        ),
+        in_specs=[vmem, vmem, pl.BlockSpec(memory_space=pltpu.HBM)],
+        out_specs=(vmem, vmem, vmem),
+        scratch_shapes=[
+            pltpu.VMEM((cells, PAIRS) + plane, jnp.float32),
+            pltpu.VMEM((cells, 3) + plane, jnp.float32),
+            pltpu.SMEM(face_codes.shape, jnp.int32),
+            pltpu.SemaphoreType.DMA,
+        ],
+        compiler_params=params,
+    )(shared, line_next, face_codes)
+    there = swap_halves(here)
+    return pl.pallas_call(
+        join_kernel,
+        out_shape=float_shape(*state.shape),
+        in_specs=[vmem] * 5,
+        out_specs=vmem,
+        compiler_params=params,
+    )(shared, here, there, known, spread)
+
+
 def solution(mesh):
     placed = (P("inst", None, "cell", None), P("cell", None), P(), P())
+    inst_count, cell_count = mesh.shape["inst"], mesh.shape["cell"]
+
+    def local(state, pseudo_rate, line_next, face_codes):
+        small = (
+            state.shape == (2, 6, 2, 2 * LANES)
+            and inst_count * 2 == NT
+            and cell_count == 8
+            and face_codes.shape[1] * LINES_DEV == state.shape[3]
+        )
+        chosen = local_by_halves if small else local_by_lines
+        return chosen(state, pseudo_rate, line_next, face_codes)
+
     return jax.shard_map(
         local, mesh=mesh, in_specs=placed, out_specs=P("inst", None, "cell", None), check_vma=False
     )

time: 64.2 us -> 24.4 us (0.38)
  local copies, waits for them, and re-layouts: 19 us -> 0.02 us
  starting transfers between devices: 16.6 us -> 2.09 us
  other arithmetic: 4.36 us -> 0 us
  Pallas kernels: 0 us -> 1.51 us
  between operations: 1.35 us -> 0.03 us
  blocking collectives: 17.5 us -> 16.5 us
  matrix products: 0.92 us -> 0 us
    all_to_all x2 -> x0, starting transfers between devices: 10.5 us -> none  [the longest x1 6.96 us: local(): lax.all_to_all(stacked, 'cell', split_axis=3, concat_axis=2, tiled=True)]
    unnamed x30 -> x6, local copies, waits for them, and re-layouts: 6.25 us -> 0.02 us
    ppermute x2 -> x1, starting transfers between devices: 6.14 us -> 2.09 us  [swap_halves(): lax.ppermute(block, 'cell', [(i, (i + count // 2) % count) for i in range...]
    ppermute x2 -> x1, waiting for transfers between devices: 0.01 us -> 4.02 us  [swap_halves(): lax.ppermute(block, 'cell', [(i, (i + count // 2) % count) for i in range...]
    all_to_all x2 -> x0, waiting for transfers between devices: 3.86 us -> none  [the longest x1 3.86 us: local(): lax.all_to_all(stacked, 'cell', split_axis=3, concat_axis=2, tiled=True)]
    slice x53 -> x0, local copies, waits for them, and re-layouts: 3.5 us -> none  [the longest x24 3.35 us: pair_split(): return (shaped[..., 0, :], shaped[..., 1, :])]
    gather x4 -> x0, local copies, waits for them, and re-layouts: 3.33 us -> none  [the longest x2 1.66 us: pitch_residual(): state_next = jnp.take(cells_state, next_lines, axis=-1)]
    all_to_all x1, blocking collectives: 12.2 us -> 9.85 us  [share_half(): lax.all_to_all(copies, 'cell', split_axis=0, concat_axis=0, tiled=True, a...]
  transfers between devices with their start and end apart: 4 -> 1, of which waited for: 1 -> 1; matrix products, arithmetic and copies ran while one was open for 26% -> 0% of each run, Pallas kernels for 0% -> 0%
where the time goes in v11:
time: 24.4 us; the launch traced here: 24.2 us
  blocking collectives  16.5 us (68%)
  waiting for transfers between devices  4.02 us (16%)
  starting transfers between devices  2.09 us (9%)
  Pallas kernels  1.51 us (6%)
    all_to_all x1, blocking collectives, share_half(): lax.all_to_all(copies, 'cell', split_axis=0, concat_axis=0, tiled=True, a...  9.85 us
    all_gather x1, blocking collectives, local_by_halves(): every = lax.all_gather(state, 'inst', axis=0, tiled=True)  6.66 us
    ppermute x1, waiting for transfers between devices, swap_halves(): lax.ppermute(block, 'cell', [(i, (i + count // 2) % count) for i in range...  4.02 us
    ppermute x1, starting transfers between devices, swap_halves(): lax.ppermute(block, 'cell', [(i, (i + count // 2) % count) for i in range...  2.09 us
    pallas_call x1, Pallas kernels, local_by_halves(): pl.pallas_call(join_kernel, out_shape=float_shape(*state.shape), in_specs...  0.71 us
    pallas_call x1, Pallas kernels, local_by_halves(): pl.pallas_call(half_kernel, out_shape=(float_shape(MIDDLE_ROWS, LANES), f...  0.7 us
  transfers between devices with their start and end apart: 1, of which 1 were waited for; matrix products, arithmetic and copies ran while one was open for 0% of the time, Pallas kernels for 0%

profile of v11, /device:TPU:0, one launch (start us, length us, event | category | flops | bytes accessed | tf_op | source)
XLA Modules:
  0.0 24.2 jit_solution(2987031622034844747)
XLA Ops:
  0.0 0.0 copy-start
  0.0 6.7 %all_gather.3.all_ref = f32[8,6,2,256]{3,2,1,0:T(2,128)S(1)} all-gather(f32[2,6,2,256]{3,2,1,0:T(2,128)} %param.4), channel_id=1, replica_groups=mesh['inst'=4,'cell'=8] {'inst'}, dimensions={0}, use_global_device_ids=true | all-gather | bytes 122880 | tf_op jit(solution)/shard_map/all_gather | solution.py:811
  6.7 0.0 copy-done
  6.7 0.1 shard_map.46
  6.8 0.0 copy-start.1
  6.8 0.0 copy-start.2
  6.8 9.8 %all_to_all.5.all_ref = f32[4,104,128]{2,1,0:T(8,128)S(1)} all-to-all(f32[4,104,128]{2,1,0:T(8,128)S(1)} %shard_map.46), channel_id=1, replica_groups={{0,1,2,3},{7,6,5,4},{8,9,10,11},{15,14,13,12},{16,17,18,19},{23,22,21,2..., dimensions={0} | all-to-all | bytes 425984 | tf_op jit(solution)/shard_map/all_to_all | solution.py:791
  16.6 0.0 copy-done.1
  16.6 0.0 copy-done.2
  16.6 0.7 %shard_map.47 = (f32[144,128]{1,0:T(8,128)S(1)}, f32[4,6,8,128]{3,2,1,0:T(8,128)S(1)}, f32[4,4,8,128]{3,2,1,0:T(8,128)S(1)}) custom-call(f32[4,104,128]{2,1,0:T(8,128)S(1)} %all_to_all.5.all_ref, s32[256]{0:T(256)S(1)} %copy-done.1, s32[2,8]{1,0:T(2,128)S(1)} %copy-done.2), custom_call_target="tpu_custom_call" | custom-call | tf_op jit(solution)/shard_map/pallas_call | solution.py:821
  17.4 2.1 %collective-permute-start = (f32[144,128]{1,0:T(8,128)S(1)}, f32[144,128]{1,0:T(8,128)S(1)}, u32[]{:S(2)}, u32[]{:S(2)}) collective-permute-start(f32[144,128]{1,0:T(8,128)S(1)} %get-tuple-element.8.here_ref), channel_id=1, source_target_pairs={{0,4},{1,5},{2,6},{3,7},{4,0},{5,1},{6,2},{7,3},{8,12},{9,13},{10,... | collective-permute-start | bytes 221192 | tf_op jit(solution)/shard_map/ppermute | solution.py:798
  19.5 4.0 %collective-permute-done.there_ref = f32[144,128]{1,0:T(8,128)S(1)} collective-permute-done((f32[144,128]{1,0:T(8,128)S(1)}, f32[144,128]{1,0:T(8,128)S(1)}, u32[]{:S(2)}, u32[]{:S(2)}) %collective-permute-start) | collective-permute-done | bytes 73760 | tf_op jit(solution)/shard_map/ppermute | solution.py:798
  23.5 0.7 %shard_map.48 = f32[2,6,2,256]{3,2,1,0:T(2,128)} custom-call(f32[4,104,128]{2,1,0:T(8,128)S(1)} %all_to_all.5.all_ref, f32[144,128]{1,0:T(8,128)S(1)} %get-tuple-element.8.here_ref, f32[144,128]{1,0:T(8,128)S(1)} %collective-permute-done.there_ref, f32[4,6,8,128]{3,2,1,0:T(8,128)S(1)} %get-tuple-element.9.known_ref, ...), custom_call_target="tpu_custom_call" | custom-call | tf_op jit(solution)/shard_map/pallas_call | solution.py:839
Async XLA Ops:
  0.0 6.7 %copy-start = (f32[2,256]{1,0:T(2,128)S(1)}, f32[2,256]{1,0:T(2,128)}, u32[]{:S(2)}) copy-start(f32[2,256]{1,0:T(2,128)} %rate_ref.1) | copy-start | bytes 6148
  6.8 9.9 %copy-start.1 = (s32[256]{0:T(256)S(1)}, s32[256]{0:T(256)}, u32[]{:S(2)}) copy-start(s32[256]{0:T(256)} %next_ref.1) | copy-start | bytes 3076
  6.8 9.9 %copy-start.2 = (s32[2,8]{1,0:T(2,128)S(1)}, s32[2,8]{1,0:T(2,128)}, u32[]{:S(2)}) copy-start(s32[2,8]{1,0:T(2,128)} %held_codes_ref.1) | copy-start | bytes 196
  17.4 6.1 %collective-permute-start = (f32[144,128]{1,0:T(8,128)S(1)}, f32[144,128]{1,0:T(8,128)S(1)}, u32[]{:S(2)}, u32[]{:S(2)}) collective-permute-start(f32[144,128]{1,0:T(8,128)S(1)} %get-tuple-element.8.here_ref), channel_id=1, source_target_pairs={{0,4},{1,5},{2,6},{3,7},{4,0},{5,1},{6,2},{7,3},{8,12},{9,13},{10,... | collective-permute-start | bytes 221192 | tf_op jit(solution)/shard_map/ppermute | solution.py:798

commit v12 on v11

--- a/solution.py
+++ b/solution.py
@@ -346,8 +346,8 @@
 
 SIDE_ROW = 3 * CELL_ROWS
 CORRECTION_ROW = SIDE_ROW + 2 * CELL_ROWS
-MIDDLE_RATE_ROW = CORRECTION_ROW + 2 * ROWS
-MIDDLE_ROWS = MIDDLE_RATE_ROW + ROWS
+MIDDLE_ROWS = CORRECTION_ROW + 2 * ROWS
+BLOCK_PLANES = 4 + 3 + 2 * PAIRS
 
 
 def spectral_offsets():
@@ -542,7 +542,8 @@
             below = self.radius[cell - 1]
             total = (below + centre) + (centre + above)
             weighted = below + 4.0 * centre + above
-        return rate * centre + SECOND_IMPL * (0.5 * total) + FOURTH_IMPL * weighted
+        result = SECOND_IMPL * (0.5 * total) + FOURTH_IMPL * weighted
+        return result if rate is None else rate * centre + result
 
     def diagonal(self, cell, rates):
         across = self.near(cell)
@@ -561,8 +562,8 @@
 
 
 def half_kernel(
-    all_ref, next_ref, held_codes_ref, middle_ref, known_ref, spread_ref,
-    rest_ref, line_ref, codes_ref, codes_sem,
+    all_ref, next_ref, held_codes_ref, middle_ref, blocks_ref, rest_ref, line_ref,
+    codes_ref, codes_sem,
 ):
     fetch = pltpu.make_async_copy(held_codes_ref, codes_ref, codes_sem)
     fetch.start()
@@ -696,7 +697,11 @@
 
     last = cells - 2
     factor = two_by_two(line.below(last), inverses[-1])
-    correction = two_by_two(factor, aboves[-1])
+    correction = list(two_by_two(factor, aboves[-1]))
+    rates = rates_at(all_ref, (blocks - 1,), RATE_ROW, first_half)
+    for member in range(2):
+        centre = line.radius[last + member]
+        correction[3 * member] = correction[3 * member] - rates[member] * centre
     side = [faces[last - 1][k] - rest_ref[last, k] for k in range(PAIRS)]
     side += [-rest_ref[last + 1, k] for k in range(PAIRS)]
     side = difference(side, apply_matrix(factor, sides[-1]))
@@ -709,34 +714,41 @@
         middle_ref[pl.ds(CORRECTION_ROW + n * ROWS, ROWS), :] = jnp.where(
             first_var, correction[2 * n], correction[2 * n + 1]
         )
-    middle_ref[pl.ds(MIDDLE_RATE_ROW, ROWS), :] = all_ref[
-        blocks - 1, pl.ds(RATE_ROW, ROWS), :
-    ]
-
+    for block in range(blocks - 1):
+        kept = [*inverses[block], aboves[block][0], *aboves[block][2:], *sides[block]]
+        for n, plane in enumerate(kept):
+            blocks_ref[block, n] = plane
+
+
+def spread_kernel(all_ref, blocks_ref, known_ref, spread_ref, table_ref):
+    blocks = all_ref.shape[0]
+    own_cell = lax.axis_index("cell")
+    own_block = jnp.where(own_cell < blocks, own_cell, 2 * blocks - 1 - own_cell)
+    zero = jnp.zeros((ROWS, LANES), jnp.float32)
     known, spread = [zero] * (2 * PAIRS), (zero + 1.0, zero, zero, zero + 1.0)
     for block in range(blocks - 1, -1, -1):
         if block < blocks - 1:
-            step = two_by_two(inverses[block], aboves[block])
-            own = apply_matrix(inverses[block], sides[block])
+            kept = [blocks_ref[block, n] for n in range(BLOCK_PLANES)]
+            inverse, above, side = kept[:4], (kept[4], None, kept[5], kept[6]), kept[7:]
+            step = two_by_two(inverse, above)
+            own = apply_matrix(inverse, side)
             if block < blocks - 2:
                 known = difference(own, apply_matrix(step, known))
                 spread = minus(two_by_two(step, spread))
             else:
                 known, spread = own, minus(step)
-        for n, plane in enumerate(known):
-            known_ref[block, n] = plane
-        for n, plane in enumerate(spread):
-            spread_ref[block, n] = plane
-
-
-def join_kernel(all_ref, here_ref, there_ref, known_ref, spread_ref, out_ref):
-    blocks = all_ref.shape[0]
-    own_cell = lax.axis_index("cell")
-    mirrored = own_cell // blocks
-    own_block = jnp.where(mirrored == 0, own_cell, 2 * blocks - 1 - own_cell)
+        for n, plane in enumerate(known + list(spread)):
+            table_ref[block, n] = plane
+    for n in range(2 * PAIRS):
+        known_ref[n] = all_ref[own_block, pl.ds(n * ROWS, ROWS), :] + table_ref[own_block, n]
+    for n in range(4):
+        spread_ref[n] = table_ref[own_block, 2 * PAIRS + n]
+
+
+def join_kernel(here_ref, there_ref, known_ref, spread_ref, out_ref):
+    mirrored = lax.axis_index("cell") // (lax.axis_size("cell") // 2)
     sign = (1 - 2 * mirrored).astype(jnp.float32)
-    first_var, _, half_index = plane_masks()
-    first_half = half_index == 0
+    first_var, _, _ = plane_masks()
 
     def plane_of(ref, row):
         return ref[pl.ds(row, ROWS), :]
@@ -759,19 +771,14 @@
     side += [here_side[PAIRS + k] + (faces[1][k] - faces[2][k]) for k in range(PAIRS)]
     other = [there_side[PAIRS + k] + (faces[2][k] - faces[3][k]) for k in range(PAIRS)]
     other += [there_side[k] + faces[3][k] for k in range(PAIRS)]
-    here_rates = rates_at(here_ref, (), MIDDLE_RATE_ROW, first_half)
-    there_rates = rates_at(there_ref, (), MIDDLE_RATE_ROW, first_half)
-    diag = difference(line.diagonal(1, here_rates), correction_of(here_ref))
-    other_diag = difference(line.diagonal(3, there_rates[::-1]), correction_of(there_ref)[::-1])
+    no_rates = (None, None)
+    diag = difference(line.diagonal(1, no_rates), correction_of(here_ref))
+    other_diag = difference(line.diagonal(3, no_rates), correction_of(there_ref)[::-1])
     factor = two_by_two(line.above(1), inverse_of(other_diag))
     diag = less(diag, two_by_two(factor, line.below(3)))
     middle = apply_matrix(inverse_of(diag), difference(side, apply_matrix(factor, other)))
-    spread = [spread_ref[own_block, n] for n in range(4)]
-    moved = apply_matrix(spread, middle)
-    results = []
-    for n in range(2 * PAIRS):
-        base = all_ref[own_block, pl.ds(n * ROWS, ROWS), :]
-        results.append(base + (known_ref[own_block, n] + moved[n]))
+    moved = apply_matrix([spread_ref[n] for n in range(4)], middle)
+    results = [known_ref[n] + moved[n] for n in range(2 * PAIRS)]
     for cell in range(2):
         for k in range(PAIRS):
             first, second = results[cell * PAIRS + k], results[(1 - cell) * PAIRS + k]
@@ -818,15 +825,14 @@
         compiler_params=params,
     )(every, pseudo_rate)
     shared = share_half(packed)
-    here, known, spread = pl.pallas_call(
+    here, eliminated = pl.pallas_call(
         half_kernel,
         out_shape=(
             float_shape(MIDDLE_ROWS, LANES),
-            float_shape(blocks, 2 * PAIRS, *plane),
-            float_shape(blocks, 4, *plane),
+            float_shape(blocks - 1, BLOCK_PLANES, *plane),
         ),
         in_specs=[vmem, vmem, pl.BlockSpec(memory_space=pltpu.HBM)],
-        out_specs=(vmem, vmem, vmem),
+        out_specs=(vmem, vmem),
         scratch_shapes=[
             pltpu.VMEM((cells, PAIRS) + plane, jnp.float32),
             pltpu.VMEM((cells, 3) + plane, jnp.float32),
@@ -836,13 +842,22 @@
         compiler_params=params,
     )(shared, line_next, face_codes)
     there = swap_halves(here)
+    known, spread = pl.pallas_call(
+        spread_kernel,
+        out_shape=(float_shape(2 * PAIRS, *plane), float_shape(4, *plane)),
+        in_specs=[vmem, vmem],
+        out_specs=(vmem, vmem),
+        scratch_shapes=[pltpu.VMEM((blocks, 2 * PAIRS + 4) + plane, jnp.float32)],
+        compiler_params=params,
+        cost_estimate=pl.CostEstimate(flops=10**6, bytes_accessed=10**6, transcendentals=0),
+    )(shared, eliminated)
     return pl.pallas_call(
         join_kernel,
         out_shape=float_shape(*state.shape),
-        in_specs=[vmem] * 5,
+        in_specs=[vmem] * 4,
         out_specs=vmem,
         compiler_params=params,
-    )(shared, here, there, known, spread)
+    )(here, there, known, spread)
 
 
 def solution(mesh):

time: 24.4 us -> 24.3 us (level)
  no operation moved by 1% of the time
where the time goes in v12:
time: 24.3 us; the launch traced here: 24.1 us
  blocking collectives  16.5 us (68%)
  waiting for transfers between devices  3.89 us (16%)
  starting transfers between devices  2.09 us (9%)
  Pallas kernels  1.53 us (6%)
    all_to_all x1, blocking collectives, share_half(): lax.all_to_all(copies, 'cell', split_axis=0, concat_axis=0, tiled=True, a...  9.85 us
    all_gather x1, blocking collectives, local_by_halves(): every = lax.all_gather(state, 'inst', axis=0, tiled=True)  6.66 us
    ppermute x1, waiting for transfers between devices, swap_halves(): lax.ppermute(block, 'cell', [(i, (i + count // 2) % count) for i in range...  3.89 us
    ppermute x1, starting transfers between devices, swap_halves(): lax.ppermute(block, 'cell', [(i, (i + count // 2) % count) for i in range...  2.09 us
    pallas_call x1, Pallas kernels, local_by_halves(): pl.pallas_call(join_kernel, out_shape=float_shape(*state.shape), in_specs...  0.7 us
    pallas_call x1, Pallas kernels, local_by_halves(): pl.pallas_call(half_kernel, out_shape=(float_shape(MIDDLE_ROWS, LANES), f...  0.69 us
  transfers between devices with their start and end apart: 1, of which 1 were waited for; matrix products, arithmetic and copies ran while one was open for 0% of the time, Pallas kernels for 0%

profile of v12, /device:TPU:0, one launch (start us, length us, event | category | flops | bytes accessed | tf_op | source)
XLA Modules:
  0.0 24.1 jit_solution(5416732290288277623)
XLA Ops:
  0.0 0.0 copy-start
  0.0 6.7 %all_gather.3.all_ref = f32[8,6,2,256]{3,2,1,0:T(2,128)S(1)} all-gather(f32[2,6,2,256]{3,2,1,0:T(2,128)} %param.4), channel_id=1, replica_groups=mesh['inst'=4,'cell'=8] {'inst'}, dimensions={0}, use_global_device_ids=true | all-gather | bytes 122880 | tf_op jit(solution)/shard_map/all_gather | solution.py:818
  6.7 0.0 copy-done
  6.7 0.1 shard_map.46
  6.8 0.0 copy-start.1
  6.8 0.0 copy-start.2
  6.8 9.8 %all_to_all.5.all_ref = f32[4,104,128]{2,1,0:T(8,128)S(1)} all-to-all(f32[4,104,128]{2,1,0:T(8,128)S(1)} %shard_map.46), channel_id=1, replica_groups={{0,1,2,3},{7,6,5,4},{8,9,10,11},{15,14,13,12},{16,17,18,19},{23,22,21,2..., dimensions={0} | all-to-all | bytes 425984 | tf_op jit(solution)/shard_map/all_to_all | solution.py:798
  16.6 0.0 copy-done.1
  16.6 0.0 copy-done.2
  16.6 0.7 %shard_map.47 = (f32[136,128]{1,0:T(8,128)S(1)}, f32[3,13,8,128]{3,2,1,0:T(8,128)S(1)}) custom-call(f32[4,104,128]{2,1,0:T(8,128)S(1)} %all_to_all.5.all_ref, s32[256]{0:T(256)S(1)} %copy-done.1, s32[2,8]{1,0:T(2,128)S(1)} %copy-done.2), custom_call_target="tpu_custom_call" | custom-call | tf_op jit(solution)/shard_map/pallas_call | solution.py:828
  17.3 2.1 %collective-permute-start = (f32[136,128]{1,0:T(8,128)S(1)}, f32[136,128]{1,0:T(8,128)S(1)}, u32[]{:S(2)}, u32[]{:S(2)}) collective-permute-start(f32[136,128]{1,0:T(8,128)S(1)} %get-tuple-element.9.here_ref), channel_id=1, source_target_pairs={{0,4},{1,5},{2,6},{3,7},{4,0},{5,1},{6,2},{7,3},{8,12},{9,13},{10,... | collective-permute-start | bytes 208904 | tf_op jit(solution)/shard_map/ppermute | solution.py:805
  19.5 3.9 %collective-permute-done.there_ref = f32[136,128]{1,0:T(8,128)S(1)} collective-permute-done((f32[136,128]{1,0:T(8,128)S(1)}, f32[136,128]{1,0:T(8,128)S(1)}, u32[]{:S(2)}, u32[]{:S(2)}) %collective-permute-start) | collective-permute-done | bytes 69664 | tf_op jit(solution)/shard_map/ppermute | solution.py:805
  23.4 0.7 %shard_map.49 = f32[2,6,2,256]{3,2,1,0:T(2,128)} custom-call(f32[136,128]{1,0:T(8,128)S(1)} %get-tuple-element.9.here_ref, f32[136,128]{1,0:T(8,128)S(1)} %collective-permute-done.there_ref, f32[6,8,128]{2,1,0:T(8,128)S(1)} %get-tuple-element.11.known_ref, f32[4,8,128]{2,1,0:T(8,128)S(1)} %get-tuple-element.12.spread_ref), custom_call_target="tpu_custom_call" | custom-call | tf_op jit(solution)/shard_map/pallas_call | solution.py:854
  (1 shorter events, 0.0 us)
Async XLA Ops:
  0.0 6.7 %copy-start = (f32[2,256]{1,0:T(2,128)S(1)}, f32[2,256]{1,0:T(2,128)}, u32[]{:S(2)}) copy-start(f32[2,256]{1,0:T(2,128)} %rate_ref.1) | copy-start | bytes 6148
  6.8 9.9 %copy-start.1 = (s32[256]{0:T(256)S(1)}, s32[256]{0:T(256)}, u32[]{:S(2)}) copy-start(s32[256]{0:T(256)} %next_ref.1) | copy-start | bytes 3076
  6.8 9.9 %copy-start.2 = (s32[2,8]{1,0:T(2,128)S(1)}, s32[2,8]{1,0:T(2,128)}, u32[]{:S(2)}) copy-start(s32[2,8]{1,0:T(2,128)} %held_codes_ref.1) | copy-start | bytes 196
  17.3 6.0 %collective-permute-start = (f32[136,128]{1,0:T(8,128)S(1)}, f32[136,128]{1,0:T(8,128)S(1)}, u32[]{:S(2)}, u32[]{:S(2)}) collective-permute-start(f32[136,128]{1,0:T(8,128)S(1)} %get-tuple-element.9.here_ref), channel_id=1, source_target_pairs={{0,4},{1,5},{2,6},{3,7},{4,0},{5,1},{6,2},{7,3},{8,12},{9,13},{10,... | collective-permute-start | bytes 208904 | tf_op jit(solution)/shard_map/ppermute | solution.py:805

commit v13 on v12

--- a/solution.py
+++ b/solution.py
@@ -562,11 +562,8 @@
 
 
 def half_kernel(
-    all_ref, next_ref, held_codes_ref, middle_ref, blocks_ref, rest_ref, line_ref,
-    codes_ref, codes_sem,
+    all_ref, next_ref, codes_ref, middle_ref, blocks_ref, rest_ref, line_ref,
 ):
-    fetch = pltpu.make_async_copy(held_codes_ref, codes_ref, codes_sem)
-    fetch.start()
     blocks = all_ref.shape[0]
     cells = 2 * blocks
     mirrored = lax.axis_index("cell") // blocks
@@ -645,11 +642,11 @@
         for k in range(PAIRS):
             rest_ref[cell, k] = times[k] + (faces_across[k] - pick_prev(faces_across[k]))
 
-    fetch.wait()
     tile = half_index * (LANES // LINES_DEV) + lane_index // LINES_DEV
+    end_codes = jnp.where(mirrored == 0, codes_ref[pl.ds(0, 1), :], codes_ref[pl.ds(1, 1), :])
     codes = jnp.zeros(shape, jnp.int32)
     for k in range(2 * LANES // LINES_DEV):
-        codes = jnp.where(tile == k, codes_ref[mirrored, k], codes)
+        codes = jnp.where(tile == k, jnp.broadcast_to(end_codes[:, k : k + 1], shape), codes)
 
     def ghost(cell):
         planes = loaded(-1 - cell)
@@ -831,13 +828,11 @@
             float_shape(MIDDLE_ROWS, LANES),
             float_shape(blocks - 1, BLOCK_PLANES, *plane),
         ),
-        in_specs=[vmem, vmem, pl.BlockSpec(memory_space=pltpu.HBM)],
+        in_specs=[vmem, vmem, vmem],
         out_specs=(vmem, vmem),
         scratch_shapes=[
             pltpu.VMEM((cells, PAIRS) + plane, jnp.float32),
             pltpu.VMEM((cells, 3) + plane, jnp.float32),
-            pltpu.SMEM(face_codes.shape, jnp.int32),
-            pltpu.SemaphoreType.DMA,
         ],
         compiler_params=params,
     )(shared, line_next, face_codes)

time: 24.3 us -> 23.9 us (0.984)
  Pallas kernels: 1.53 us -> 1.18 us
    pallas_call x1, Pallas kernels: 0.69 us -> 0.34 us  [local_by_halves(): pl.pallas_call(half_kernel, out_shape=(float_shape(MIDDLE_ROWS, LANES), f...]
where the time goes in v13:
time: 23.9 us; the launch traced here: 23.7 us
  blocking collectives  16.5 us (69%)
  waiting for transfers between devices  3.89 us (16%)
  starting transfers between devices  2.09 us (9%)
  Pallas kernels  1.18 us (5%)
    all_to_all x1, blocking collectives, share_half(): lax.all_to_all(copies, 'cell', split_axis=0, concat_axis=0, tiled=True, a...  9.85 us
    all_gather x1, blocking collectives, local_by_halves(): every = lax.all_gather(state, 'inst', axis=0, tiled=True)  6.66 us
    ppermute x1, waiting for transfers between devices, swap_halves(): lax.ppermute(block, 'cell', [(i, (i + count // 2) % count) for i in range...  3.89 us
    ppermute x1, starting transfers between devices, swap_halves(): lax.ppermute(block, 'cell', [(i, (i + count // 2) % count) for i in range...  2.09 us
    pallas_call x1, Pallas kernels, local_by_halves(): pl.pallas_call(join_kernel, out_shape=float_shape(*state.shape), in_specs...  0.7 us
  transfers between devices with their start and end apart: 1, of which 1 were waited for; matrix products, arithmetic and copies ran while one was open for 0% of the time, Pallas kernels for 0%

profile of v13, /device:TPU:0, one launch (start us, length us, event | category | flops | bytes accessed | tf_op | source)
XLA Modules:
  0.0 23.7 jit_solution(4965773384641270532)
XLA Ops:
  0.0 0.0 copy-start
  0.0 6.7 %all_gather.3.all_ref = f32[8,6,2,256]{3,2,1,0:T(2,128)S(1)} all-gather(f32[2,6,2,256]{3,2,1,0:T(2,128)} %param.4), channel_id=1, replica_groups=mesh['inst'=4,'cell'=8] {'inst'}, dimensions={0}, use_global_device_ids=true | all-gather | bytes 122880 | tf_op jit(solution)/shard_map/all_gather | solution.py:815
  6.7 0.0 copy-done
  6.7 0.1 shard_map.46
  6.8 0.0 copy-start.1
  6.8 0.0 copy-start.2
  6.8 9.8 %all_to_all.5.all_ref = f32[4,104,128]{2,1,0:T(8,128)S(1)} all-to-all(f32[4,104,128]{2,1,0:T(8,128)S(1)} %shard_map.46), channel_id=1, replica_groups={{0,1,2,3},{7,6,5,4},{8,9,10,11},{15,14,13,12},{16,17,18,19},{23,22,21,2..., dimensions={0} | all-to-all | bytes 425984 | tf_op jit(solution)/shard_map/all_to_all | solution.py:795
  16.6 0.0 copy-done.1
  16.6 0.0 copy-done.2
  16.6 0.3 %shard_map.47 = (f32[136,128]{1,0:T(8,128)S(1)}, f32[3,13,8,128]{3,2,1,0:T(8,128)S(1)}) custom-call(f32[4,104,128]{2,1,0:T(8,128)S(1)} %all_to_all.5.all_ref, s32[256]{0:T(256)S(1)} %copy-done.1, s32[2,8]{1,0:T(2,128)S(1)} %copy-done.2), custom_call_target="tpu_custom_call" | custom-call | tf_op jit(solution)/shard_map/pallas_call | solution.py:825
  17.0 2.1 %collective-permute-start = (f32[136,128]{1,0:T(8,128)S(1)}, f32[136,128]{1,0:T(8,128)S(1)}, u32[]{:S(2)}, u32[]{:S(2)}) collective-permute-start(f32[136,128]{1,0:T(8,128)S(1)} %get-tuple-element.9.here_ref), channel_id=1, source_target_pairs={{0,4},{1,5},{2,6},{3,7},{4,0},{5,1},{6,2},{7,3},{8,12},{9,13},{10,... | collective-permute-start | bytes 208904 | tf_op jit(solution)/shard_map/ppermute | solution.py:802
  19.1 3.9 %collective-permute-done.there_ref = f32[136,128]{1,0:T(8,128)S(1)} collective-permute-done((f32[136,128]{1,0:T(8,128)S(1)}, f32[136,128]{1,0:T(8,128)S(1)}, u32[]{:S(2)}, u32[]{:S(2)}) %collective-permute-start) | collective-permute-done | bytes 69664 | tf_op jit(solution)/shard_map/ppermute | solution.py:802
  23.0 0.7 %shard_map.49 = f32[2,6,2,256]{3,2,1,0:T(2,128)} custom-call(f32[136,128]{1,0:T(8,128)S(1)} %get-tuple-element.9.here_ref, f32[136,128]{1,0:T(8,128)S(1)} %collective-permute-done.there_ref, f32[6,8,128]{2,1,0:T(8,128)S(1)} %get-tuple-element.11.known_ref, f32[4,8,128]{2,1,0:T(8,128)S(1)} %get-tuple-element.12.spread_ref), custom_call_target="tpu_custom_call" | custom-call | tf_op jit(solution)/shard_map/pallas_call | solution.py:849
  (1 shorter events, 0.0 us)
Async XLA Ops:
  0.0 6.7 %copy-start = (f32[2,256]{1,0:T(2,128)S(1)}, f32[2,256]{1,0:T(2,128)}, u32[]{:S(2)}) copy-start(f32[2,256]{1,0:T(2,128)} %rate_ref.1) | copy-start | bytes 6148
  6.8 9.9 %copy-start.1 = (s32[256]{0:T(256)S(1)}, s32[256]{0:T(256)}, u32[]{:S(2)}) copy-start(s32[256]{0:T(256)} %next_ref.1) | copy-start | bytes 3076
  6.8 9.9 %copy-start.2 = (s32[2,8]{1,0:T(2,128)S(1)}, s32[2,8]{1,0:T(2,128)}, u32[]{:S(2)}) copy-start(s32[2,8]{1,0:T(2,128)} %codes_ref.1) | copy-start | bytes 196
  17.0 6.0 %collective-permute-start = (f32[136,128]{1,0:T(8,128)S(1)}, f32[136,128]{1,0:T(8,128)S(1)}, u32[]{:S(2)}, u32[]{:S(2)}) collective-permute-start(f32[136,128]{1,0:T(8,128)S(1)} %get-tuple-element.9.here_ref), channel_id=1, source_target_pairs={{0,4},{1,5},{2,6},{3,7},{4,0},{5,1},{6,2},{7,3},{8,12},{9,13},{10,... | collective-permute-start | bytes 208904 | tf_op jit(solution)/shard_map/ppermute | solution.py:802

commit v14 on v13

--- a/solution.py
+++ b/solution.py
@@ -339,8 +339,7 @@
 ROWS = 8
 PAIRS = 3
 CELL_ROWS = PAIRS * ROWS
-REST_ROW = 2 * CELL_ROWS
-RATE_ROW = 2 * REST_ROW
+RATE_ROW = 2 * CELL_ROWS
 VMEM_BYTES = 8 * 2**20
 BLOCK_ROWS = RATE_ROW + ROWS
 
@@ -387,55 +386,33 @@
     return (var // 2) * ROWS + (var % 2) * 4 + inst * 2 + half
 
 
-def cell_kernel(all_ref, rate_ref, out_ref, plane_ref):
-    own_inst = lax.axis_index("inst")
-    inst_count = all_ref.shape[0] // 2
-    copies = out_ref.shape[0]
-    mirrored = lax.axis_index("cell") // copies
-    _, first_inst, _ = plane_masks()
-
-    for shift in range(inst_count):
-        pair = (own_inst - shift) & (inst_count - 1)
-        for cell in range(2):
-            for var in range(6):
-                for inst in range(2):
-                    for half in range(2):
-                        row = cell * CELL_ROWS + rows_of(var, inst, half)
-                        plane_ref[shift, pl.ds(row, 1), :] = all_ref[
-                            2 * pair + inst, var, pl.ds(cell, 1), pl.ds(half * LANES, LANES)
-                        ]
-    offsets = spectral_offsets()
-    for row in range(0, REST_ROW, ROWS):
-        same_total, other_total = None, None
-        for shift in range(inst_count):
-            plane = plane_ref[shift, pl.ds(row, ROWS), :]
-            other = jnp.where(
-                first_inst, offsets[(2 * shift + 1) % NT], offsets[(2 * shift - 1) % NT]
-            )
-            if shift > 0:
-                term = offsets[(2 * shift) % NT] * plane
-                same_total = term if same_total is None else same_total + term
-            term = other * plane
-            other_total = term if other_total is None else other_total + term
-        turned = jnp.where(
-            first_inst, pltpu.roll(other_total, 6, 0), pltpu.roll(other_total, 2, 0)
-        )
-        own = plane_ref[0, pl.ds(row, ROWS), :]
-        place = jnp.bitwise_xor(row // CELL_ROWS, mirrored) * CELL_ROWS + row % CELL_ROWS
-        place = pl.multiple_of(place, ROWS)
-        for copy in range(copies):
-            out_ref[copy, pl.ds(place, ROWS), :] = own
-            out_ref[copy, pl.ds(REST_ROW + place, ROWS), :] = same_total + turned
+def pack_kernel(state_ref, rate_ref, out_ref):
+    mirrored = lax.axis_index("cell") // (lax.axis_size("cell") // 2)
+    for cell in range(2):
+        place = pl.multiple_of(jnp.bitwise_xor(cell, mirrored) * CELL_ROWS, ROWS)
+        for k in range(PAIRS):
+            rows = [
+                state_ref[inst, 2 * k + var, pl.ds(cell, 1), pl.ds(half * LANES, LANES)]
+                for var in range(2)
+                for inst in range(2)
+                for half in range(2)
+            ]
+            for row, values in enumerate(rows):
+                out_ref[0, pl.ds(place + (k * ROWS + row), 1), :] = values
     rates = [
         rate_ref[pl.ds(cell, 1), pl.ds(half * LANES, LANES)]
         for cell in range(2)
         for half in range(2)
     ]
-    rates = [jnp.where(mirrored == 0, rates[k], rates[k ^ 2]) for k in range(4)]
-    for copy in range(copies):
-        for row, rate in enumerate(rates):
-            out_ref[copy, pl.ds(RATE_ROW + row, 1), :] = rate
-        out_ref[copy, pl.ds(RATE_ROW + 4, 4), :] = jnp.zeros((4, LANES), jnp.float32)
+    for row in range(4):
+        out_ref[0, pl.ds(RATE_ROW + row, 1), :] = jnp.where(
+            mirrored == 0, rates[row], rates[row ^ 2]
+        )
+    out_ref[0, pl.ds(RATE_ROW + 4, 4), :] = jnp.zeros((4, LANES), jnp.float32)
+    for row in range(0, BLOCK_ROWS, ROWS):
+        values = out_ref[0, pl.ds(row, ROWS), :]
+        for copy in range(1, out_ref.shape[0]):
+            out_ref[copy, pl.ds(row, ROWS), :] = values
 
 
 def two_by_two(first, second):
@@ -564,13 +541,14 @@
 def half_kernel(
     all_ref, next_ref, codes_ref, middle_ref, blocks_ref, rest_ref, line_ref,
 ):
-    blocks = all_ref.shape[0]
+    own_inst = lax.axis_index("inst")
+    inst_count, blocks = all_ref.shape[:2]
     cells = 2 * blocks
     mirrored = lax.axis_index("cell") // blocks
     sign = (1 - 2 * mirrored).astype(jnp.float32)
     shape = (ROWS, LANES)
     lane_index = lax.broadcasted_iota(jnp.int32, shape, 1)
-    first_var, _, half_index = plane_masks()
+    first_var, first_inst, half_index = plane_masks()
     first_half = half_index == 0
     zero = jnp.zeros(shape, jnp.float32)
 
@@ -607,11 +585,36 @@
     pick_next = picker(next_line)
     pick_prev = picker(prev_line)
 
-    def loaded(cell, start=0):
+    def loaded(cell, inst=own_inst):
         return [
-            all_ref[cell // 2, pl.ds(start + (cell % 2) * CELL_ROWS + k * ROWS, ROWS), :]
+            all_ref[inst, cell // 2, pl.ds((cell % 2) * CELL_ROWS + k * ROWS, ROWS), :]
             for k in range(PAIRS)
         ]
+
+    offsets = spectral_offsets()
+
+    def time_parts(cell):
+        pairs = [
+            loaded(cell, (own_inst - shift) & (inst_count - 1)) for shift in range(inst_count)
+        ]
+        result = []
+        for k in range(PAIRS):
+            same_total, other_total = None, None
+            for shift in range(inst_count):
+                plane = pairs[shift][k]
+                other = jnp.where(
+                    first_inst, offsets[(2 * shift + 1) % NT], offsets[(2 * shift - 1) % NT]
+                )
+                if shift > 0:
+                    term = offsets[(2 * shift) % NT] * plane
+                    same_total = term if same_total is None else same_total + term
+                term = other * plane
+                other_total = term if other_total is None else other_total + term
+            turned = jnp.where(
+                first_inst, pltpu.roll(other_total, 6, 0), pltpu.roll(other_total, 2, 0)
+            )
+            result.append(same_total + turned)
+        return result
 
     def flux_across(planes, velocity, pressure):
         return [
@@ -638,7 +641,7 @@
         velocity_x, velocity_y, pressure, sound = primitives(first_var, planes)
         line_ref[cell, 0], line_ref[cell, 1], line_ref[cell, 2] = velocity_x, pressure, sound
         faces_across = pitch_flux(planes, velocity_y, pressure, sound)
-        times = loaded(cell, REST_ROW)
+        times = time_parts(cell)
         for k in range(PAIRS):
             rest_ref[cell, k] = times[k] + (faces_across[k] - pick_prev(faces_across[k]))
 
@@ -675,7 +678,7 @@
         if cell >= 3 and cell % 2 == 1:
             at = cell - 3
             block = at // 2
-            rates = rates_at(all_ref, (block,), RATE_ROW, first_half)
+            rates = rates_at(all_ref, (own_inst, block), RATE_ROW, first_half)
             diag = line.diagonal(at, rates)
             side = []
             for member in range(2):
@@ -695,7 +698,7 @@
     last = cells - 2
     factor = two_by_two(line.below(last), inverses[-1])
     correction = list(two_by_two(factor, aboves[-1]))
-    rates = rates_at(all_ref, (blocks - 1,), RATE_ROW, first_half)
+    rates = rates_at(all_ref, (own_inst, blocks - 1), RATE_ROW, first_half)
     for member in range(2):
         centre = line.radius[last + member]
         correction[3 * member] = correction[3 * member] - rates[member] * centre
@@ -718,7 +721,8 @@
 
 
 def spread_kernel(all_ref, blocks_ref, known_ref, spread_ref, table_ref):
-    blocks = all_ref.shape[0]
+    own_inst = lax.axis_index("inst")
+    blocks = all_ref.shape[1]
     own_cell = lax.axis_index("cell")
     own_block = jnp.where(own_cell < blocks, own_cell, 2 * blocks - 1 - own_cell)
     zero = jnp.zeros((ROWS, LANES), jnp.float32)
@@ -737,7 +741,8 @@
         for n, plane in enumerate(known + list(spread)):
             table_ref[block, n] = plane
     for n in range(2 * PAIRS):
-        known_ref[n] = all_ref[own_block, pl.ds(n * ROWS, ROWS), :] + table_ref[own_block, n]
+        base = all_ref[own_inst, own_block, pl.ds(n * ROWS, ROWS), :]
+        known_ref[n] = base + table_ref[own_block, n]
     for n in range(4):
         spread_ref[n] = table_ref[own_block, 2 * PAIRS + n]
 
@@ -790,10 +795,12 @@
 
 
 def share_half(copies):
-    count = lax.axis_size("cell")
-    groups = [list(range(count // 2)), list(range(count - 1, count // 2 - 1, -1))]
+    insts, count = lax.axis_size("inst"), lax.axis_size("cell")
+    halves = [range(count // 2), range(count - 1, count // 2 - 1, -1)]
+    groups = [[inst * count + cell for inst in range(insts) for cell in half] for half in halves]
     return lax.all_to_all(
-        copies, "cell", split_axis=0, concat_axis=0, tiled=True, axis_index_groups=groups
+        copies, ("inst", "cell"), split_axis=0, concat_axis=0, tiled=True,
+        axis_index_groups=groups,
     )
 
 
@@ -812,16 +819,15 @@
     vmem = pl.BlockSpec(memory_space=pltpu.VMEM)
     plane = (ROWS, LANES)
     params = pltpu.CompilerParams(vmem_limit_bytes=VMEM_BYTES)
-    every = lax.all_gather(state, "inst", axis=0, tiled=True)
+    insts = lax.axis_size("inst")
     packed = pl.pallas_call(
-        cell_kernel,
-        out_shape=float_shape(blocks, BLOCK_ROWS, LANES),
+        pack_kernel,
+        out_shape=float_shape(insts * blocks, BLOCK_ROWS, LANES),
         in_specs=[vmem, vmem],
         out_specs=vmem,
-        scratch_shapes=[pltpu.VMEM((every.shape[0] // 2, REST_ROW, LANES), jnp.float32)],
         compiler_params=params,
-    )(every, pseudo_rate)
-    shared = share_half(packed)
+    )(state, pseudo_rate)
+    shared = share_half(packed).reshape(insts, blocks, BLOCK_ROWS, LANES)
     here, eliminated = pl.pallas_call(
         half_kernel,
         out_shape=(

time: 23.9 us -> 25 us (1.046)
  local copies, waits for them, and re-layouts: 0.02 us -> 2.1 us
  blocking collectives: 16.5 us -> 14.7 us
  waiting for transfers between devices: 3.89 us -> 5.23 us
  starting transfers between devices: 2.09 us -> 1.55 us
    all_gather x1 -> x0, blocking collectives: 6.66 us -> none  [local_by_halves(): every = lax.all_gather(state, 'inst', axis=0, tiled=True)]
    all_to_all x1, blocking collectives: 9.85 us -> 14.7 us  [share_half(): lax.all_to_all(copies, ('inst', 'cell'), split_axis=0, concat_axis=0, til...]
    unnamed x6 -> x8, local copies, waits for them, and re-layouts: 0.02 us -> 2.1 us
    ppermute x1, waiting for transfers between devices: 3.89 us -> 5.23 us  [swap_halves(): lax.ppermute(block, 'cell', [(i, (i + count // 2) % count) for i in range...]
    ppermute x1, starting transfers between devices: 2.09 us -> 1.55 us  [swap_halves(): lax.ppermute(block, 'cell', [(i, (i + count // 2) % count) for i in range...]
where the time goes in v14:
time: 25 us; the launch traced here: 24.8 us
  blocking collectives  14.7 us (59%)
  waiting for transfers between devices  5.23 us (21%)
  local copies, waits for them, and re-layouts  2.1 us (8%)
  starting transfers between devices  1.55 us (6%)
  Pallas kernels  1.16 us (5%)
    all_to_all x1, blocking collectives, share_half(): lax.all_to_all(copies, ('inst', 'cell'), split_axis=0, concat_axis=0, til...  14.7 us
    ppermute x1, waiting for transfers between devices, swap_halves(): lax.ppermute(block, 'cell', [(i, (i + count // 2) % count) for i in range...  5.23 us
    unnamed x8, local copies, waits for them, and re-layouts  2.1 us
    ppermute x1, starting transfers between devices, swap_halves(): lax.ppermute(block, 'cell', [(i, (i + count // 2) % count) for i in range...  1.55 us
    pallas_call x1, Pallas kernels, local_by_halves(): pl.pallas_call(join_kernel, out_shape=float_shape(*state.shape), in_specs...  0.7 us
  transfers between devices with their start and end apart: 1, of which 1 were waited for; matrix products, arithmetic and copies ran while one was open for 0% of the time, Pallas kernels for 0%

profile of v14, /device:TPU:0, one launch (start us, length us, event | category | flops | bytes accessed | tf_op | source)
XLA Modules:
  0.0 24.8 jit_solution(10154254280230855346)
XLA Ops:
  0.0 0.0 copy-start
  0.0 0.7 %copy-done = f32[2,6,2,256]{3,2,1,0:T(2,128)S(1)} copy-done((f32[2,6,2,256]{3,2,1,0:T(2,128)S(1)}, f32[2,6,2,256]{3,2,1,0:T(2,128)}, u32[]{:S(2)}) %copy-start) | copy-done | bytes 24600
  0.7 0.0 copy-start.1
  0.7 0.7 %copy-done.1 = f32[2,256]{1,0:T(2,128)S(1)} copy-done((f32[2,256]{1,0:T(2,128)S(1)}, f32[2,256]{1,0:T(2,128)}, u32[]{:S(2)}) %copy-start.1) | copy-done | bytes 2072
  1.4 0.1 shard_map.46
  1.5 0.0 copy-start.3
  1.5 14.7 %all_to_all.5 = f32[16,56,128]{2,1,0:T(8,128)S(1)} all-to-all(f32[16,56,128]{2,1,0:T(8,128)S(1)} %shard_map.46), channel_id=1, replica_groups={{0,1,2,3,8,9,10,11,16,17,18,19,24,25,26,27},{7,6,5,4,15,14,13,12,23,22,..., dimensions={0} | all-to-all | bytes 917504 | tf_op jit(solution)/shard_map/all_to_all | solution.py:801
  16.2 0.0 copy-start.2
  16.2 0.0 copy-done.3
  16.2 0.7 %copy-done.2 = s32[256]{0:T(256)S(1)} copy-done((s32[256]{0:T(256)S(1)}, s32[256]{0:T(256)}, u32[]{:S(2)}) %copy-start.2) | copy-done | bytes 1048
  16.9 0.4 %shard_map.47 = (f32[136,128]{1,0:T(8,128)S(1)}, f32[3,13,8,128]{3,2,1,0:T(8,128)S(1)}) custom-call(f32[4,4,56,128]{3,2,1,0:T(8,128)S(1)} %bitcast.1, s32[256]{0:T(256)S(1)} %copy-done.2, s32[2,8]{1,0:T(2,128)S(1)} %copy-done.3), custom_call_target="tpu_custom_call" | custom-call | tf_op jit(solution)/shard_map/pallas_call | solution.py:831
  17.3 1.5 %collective-permute-start = (f32[136,128]{1,0:T(8,128)S(1)}, f32[136,128]{1,0:T(8,128)S(1)}, u32[]{:S(2)}, u32[]{:S(2)}) collective-permute-start(f32[136,128]{1,0:T(8,128)S(1)} %get-tuple-element.9.here_ref), channel_id=1, source_target_pairs={{0,4},{1,5},{2,6},{3,7},{4,0},{5,1},{6,2},{7,3},{8,12},{9,13},{10,... | collective-permute-start | bytes 208904 | tf_op jit(solution)/shard_map/ppermute | solution.py:809
  18.9 5.2 %collective-permute-done.there_ref = f32[136,128]{1,0:T(8,128)S(1)} collective-permute-done((f32[136,128]{1,0:T(8,128)S(1)}, f32[136,128]{1,0:T(8,128)S(1)}, u32[]{:S(2)}, u32[]{:S(2)}) %collective-permute-start) | collective-permute-done | bytes 69664 | tf_op jit(solution)/shard_map/ppermute | solution.py:809
  24.1 0.7 %shard_map.49 = f32[2,6,2,256]{3,2,1,0:T(2,128)} custom-call(f32[136,128]{1,0:T(8,128)S(1)} %get-tuple-element.9.here_ref, f32[136,128]{1,0:T(8,128)S(1)} %collective-permute-done.there_ref, f32[6,8,128]{2,1,0:T(8,128)S(1)} %get-tuple-element.11.known_ref, f32[4,8,128]{2,1,0:T(8,128)S(1)} %get-tuple-element.12.spread_ref), custom_call_target="tpu_custom_call" | custom-call | tf_op jit(solution)/shard_map/pallas_call | solution.py:855
  (1 shorter events, 0.0 us)
Async XLA Ops:
  0.0 0.7 %copy-start = (f32[2,6,2,256]{3,2,1,0:T(2,128)S(1)}, f32[2,6,2,256]{3,2,1,0:T(2,128)}, u32[]{:S(2)}) copy-start(f32[2,6,2,256]{3,2,1,0:T(2,128)} %state_ref.1) | copy-start | bytes 73732
  0.7 0.7 %copy-start.1 = (f32[2,256]{1,0:T(2,128)S(1)}, f32[2,256]{1,0:T(2,128)}, u32[]{:S(2)}) copy-start(f32[2,256]{1,0:T(2,128)} %rate_ref.1) | copy-start | bytes 6148
  1.5 14.7 %copy-start.3 = (s32[2,8]{1,0:T(2,128)S(1)}, s32[2,8]{1,0:T(2,128)}, u32[]{:S(2)}) copy-start(s32[2,8]{1,0:T(2,128)} %codes_ref.1) | copy-start | bytes 196
  16.2 0.7 %copy-start.2 = (s32[256]{0:T(256)S(1)}, s32[256]{0:T(256)}, u32[]{:S(2)}) copy-start(s32[256]{0:T(256)} %next_ref.1) | copy-start | bytes 3076
  17.3 6.8 %collective-permute-start = (f32[136,128]{1,0:T(8,128)S(1)}, f32[136,128]{1,0:T(8,128)S(1)}, u32[]{:S(2)}, u32[]{:S(2)}) collective-permute-start(f32[136,128]{1,0:T(8,128)S(1)} %get-tuple-element.9.here_ref), channel_id=1, source_target_pairs={{0,4},{1,5},{2,6},{3,7},{4,0},{5,1},{6,2},{7,3},{8,12},{9,13},{10,... | collective-permute-start | bytes 208904 | tf_op jit(solution)/shard_map/ppermute | solution.py:809

commit v15 on v14

--- a/solution.py
+++ b/solution.py
@@ -386,7 +386,25 @@
     return (var // 2) * ROWS + (var % 2) * 4 + inst * 2 + half
 
 
-def pack_kernel(state_ref, rate_ref, out_ref):
+def pack_kernel(
+    held_state_ref, held_rate_ref, held_next_ref, held_codes_ref, out_ref, next_ref, codes_ref,
+    state_ref, rate_ref, sems,
+):
+    copies = [
+        pltpu.make_async_copy(source, target, sems.at[k])
+        for k, (source, target) in enumerate(
+            (
+                (held_state_ref, state_ref),
+                (held_rate_ref, rate_ref),
+                (held_next_ref, next_ref),
+                (held_codes_ref, codes_ref),
+            )
+        )
+    ]
+    for copy in copies:
+        copy.start()
+    for copy in copies:
+        copy.wait()
     mirrored = lax.axis_index("cell") // (lax.axis_size("cell") // 2)
     for cell in range(2):
         place = pl.multiple_of(jnp.bitwise_xor(cell, mirrored) * CELL_ROWS, ROWS)
@@ -820,13 +838,26 @@
     plane = (ROWS, LANES)
     params = pltpu.CompilerParams(vmem_limit_bytes=VMEM_BYTES)
     insts = lax.axis_size("inst")
-    packed = pl.pallas_call(
+    held = [
+        pltpu.with_memory_space_constraint(array, pltpu.HBM)
+        for array in (state, pseudo_rate, line_next, face_codes)
+    ]
+    packed, next_here, codes_here = pl.pallas_call(
         pack_kernel,
-        out_shape=float_shape(insts * blocks, BLOCK_ROWS, LANES),
-        in_specs=[vmem, vmem],
-        out_specs=vmem,
+        out_shape=(
+            float_shape(insts * blocks, BLOCK_ROWS, LANES),
+            jax.ShapeDtypeStruct(line_next.shape, jnp.int32),
+            jax.ShapeDtypeStruct(face_codes.shape, jnp.int32),
+        ),
+        in_specs=[pl.BlockSpec(memory_space=pltpu.HBM)] * 4,
+        out_specs=(vmem, vmem, vmem),
+        scratch_shapes=[
+            pltpu.VMEM(state.shape, jnp.float32),
+            pltpu.VMEM(pseudo_rate.shape, jnp.float32),
+            pltpu.SemaphoreType.DMA((4,)),
+        ],
         compiler_params=params,
-    )(state, pseudo_rate)
+    )(*held)
     shared = share_half(packed).reshape(insts, blocks, BLOCK_ROWS, LANES)
     here, eliminated = pl.pallas_call(
         half_kernel,
@@ -841,7 +872,7 @@
             pltpu.VMEM((cells, 3) + plane, jnp.float32),
         ],
         compiler_params=params,
-    )(shared, line_next, face_codes)
+    )(shared, next_here, codes_here)
     there = swap_halves(here)
     known, spread = pl.pallas_call(
         spread_kernel,

time: 25 us -> 23.7 us (0.948)
  local copies, waits for them, and re-layouts: 2.1 us -> 0 us
  Pallas kernels: 1.16 us -> 1.94 us
    unnamed x8 -> x0, local copies, waits for them, and re-layouts: 2.1 us -> none
    pallas_call x1, Pallas kernels: 0.06 us -> 0.83 us  [local_by_halves(): pl.pallas_call(pack_kernel, out_shape=(float_shape(insts * blocks, BLOCK_...]
where the time goes in v15:
time: 23.7 us; the launch traced here: 23.5 us
  blocking collectives  14.7 us (62%)
  waiting for transfers between devices  5.23 us (22%)
  Pallas kernels  1.94 us (8%)
  starting transfers between devices  1.55 us (7%)
    all_to_all x1, blocking collectives, share_half(): lax.all_to_all(copies, ('inst', 'cell'), split_axis=0, concat_axis=0, til...  14.7 us
    ppermute x1, waiting for transfers between devices, swap_halves(): lax.ppermute(block, 'cell', [(i, (i + count // 2) % count) for i in range...  5.23 us
    ppermute x1, starting transfers between devices, swap_halves(): lax.ppermute(block, 'cell', [(i, (i + count // 2) % count) for i in range...  1.55 us
    pallas_call x1, Pallas kernels, local_by_halves(): pl.pallas_call(pack_kernel, out_shape=(float_shape(insts * blocks, BLOCK_...  0.83 us
    pallas_call x1, Pallas kernels, local_by_halves(): pl.pallas_call(join_kernel, out_shape=float_shape(*state.shape), in_specs...  0.7 us
  transfers between devices with their start and end apart: 1, of which 1 were waited for; matrix products, arithmetic and copies ran while one was open for 0% of the time, Pallas kernels for 0%

profile of v15, /device:TPU:0, one launch (start us, length us, event | category | flops | bytes accessed | tf_op | source)
XLA Modules:
  0.0 23.5 jit_solution(14651506256850442415)
XLA Ops:
  0.0 0.8 %shard_map.46 = (f32[16,56,128]{2,1,0:T(8,128)S(1)}, s32[256]{0:T(256)S(1)}, s32[2,8]{1,0:T(2,128)S(1)}) custom-call(f32[2,6,2,256]{3,2,1,0:T(2,128)} %held_state_ref.1, f32[2,256]{1,0:T(2,128)} %held_rate_ref.1, s32[256]{0:T(256)} %held_next_ref.1, s32[2,8]{1,0:T(2,128)} %held_codes_ref.1), custom_call_target="tpu_custom_call" | custom-call | tf_op jit(solution)/shard_map/pallas_call | solution.py:845
  0.8 14.7 %all_to_all.5 = f32[16,56,128]{2,1,0:T(8,128)S(1)} all-to-all(f32[16,56,128]{2,1,0:T(8,128)S(1)} %get-tuple-element.12), channel_id=1, replica_groups={{0,1,2,3,8,9,10,11,16,17,18,19,24,25,26,27},{7,6,5,4,15,14,13,12,23,22,..., dimensions={0} | all-to-all | bytes 917504 | tf_op jit(solution)/shard_map/all_to_all | solution.py:819
  15.6 0.4 %shard_map.47 = (f32[136,128]{1,0:T(8,128)S(1)}, f32[3,13,8,128]{3,2,1,0:T(8,128)S(1)}) custom-call(f32[4,4,56,128]{3,2,1,0:T(8,128)S(1)} %bitcast.1, s32[256]{0:T(256)S(1)} %get-tuple-element.13.next_ref, s32[2,8]{1,0:T(2,128)S(1)} %get-tuple-element.14.codes_ref), custom_call_target="tpu_custom_call" | custom-call | tf_op jit(solution)/shard_map/pallas_call | solution.py:862
  15.9 1.5 %collective-permute-start = (f32[136,128]{1,0:T(8,128)S(1)}, f32[136,128]{1,0:T(8,128)S(1)}, u32[]{:S(2)}, u32[]{:S(2)}) collective-permute-start(f32[136,128]{1,0:T(8,128)S(1)} %get-tuple-element.15.here_ref), channel_id=1, source_target_pairs={{0,4},{1,5},{2,6},{3,7},{4,0},{5,1},{6,2},{7,3},{8,12},{9,13},{10,... | collective-permute-start | bytes 208904 | tf_op jit(solution)/shard_map/ppermute | solution.py:827
  17.5 5.2 %collective-permute-done.there_ref = f32[136,128]{1,0:T(8,128)S(1)} collective-permute-done((f32[136,128]{1,0:T(8,128)S(1)}, f32[136,128]{1,0:T(8,128)S(1)}, u32[]{:S(2)}, u32[]{:S(2)}) %collective-permute-start) | collective-permute-done | bytes 69664 | tf_op jit(solution)/shard_map/ppermute | solution.py:827
  22.7 0.7 %shard_map.49 = f32[2,6,2,256]{3,2,1,0:T(2,128)} custom-call(f32[136,128]{1,0:T(8,128)S(1)} %get-tuple-element.15.here_ref, f32[136,128]{1,0:T(8,128)S(1)} %collective-permute-done.there_ref, f32[6,8,128]{2,1,0:T(8,128)S(1)} %get-tuple-element.17.known_ref, f32[4,8,128]{2,1,0:T(8,128)S(1)} %get-tuple-element.18.spread_ref), custom_call_target="tpu_custom_call" | custom-call | tf_op jit(solution)/shard_map/pallas_call | solution.py:886
  (1 shorter events, 0.0 us)
Async XLA Ops:
  15.9 6.8 %collective-permute-start = (f32[136,128]{1,0:T(8,128)S(1)}, f32[136,128]{1,0:T(8,128)S(1)}, u32[]{:S(2)}, u32[]{:S(2)}) collective-permute-start(f32[136,128]{1,0:T(8,128)S(1)} %get-tuple-element.15.here_ref), channel_id=1, source_target_pairs={{0,4},{1,5},{2,6},{3,7},{4,0},{5,1},{6,2},{7,3},{8,12},{9,13},{10,... | collective-permute-start | bytes 208904 | tf_op jit(solution)/shard_map/ppermute | solution.py:827

commit v16 on v15

--- a/solution.py
+++ b/solution.py
@@ -765,10 +765,13 @@
         spread_ref[n] = table_ref[own_block, 2 * PAIRS + n]
 
 
-def join_kernel(here_ref, there_ref, known_ref, spread_ref, out_ref):
+def join_kernel(here_ref, first_ref, second_ref, known_ref, spread_ref, out_ref, there_ref):
     mirrored = lax.axis_index("cell") // (lax.axis_size("cell") // 2)
     sign = (1 - 2 * mirrored).astype(jnp.float32)
     first_var, _, _ = plane_masks()
+    for row in range(0, MIDDLE_ROWS, ROWS):
+        rows = pl.ds(row, ROWS)
+        there_ref[rows, :] = first_ref[rows, :] + second_ref[rows, :]
 
     def plane_of(ref, row):
         return ref[pl.ds(row, ROWS), :]
@@ -823,8 +826,13 @@
 
 
 def swap_halves(block):
-    count = lax.axis_size("cell")
-    return lax.ppermute(block, "cell", [(i, (i + count // 2) % count) for i in range(count)])
+    half = lax.axis_size("cell") // 2
+    results = []
+    for start in (half // 2, 0):
+        ups = [(cell, cell + half) for cell in range(start, start + half // 2)]
+        pairs = ups + [(target, source) for source, target in ups]
+        results.append(lax.ppermute(block, "cell", pairs))
+    return results
 
 
 def float_shape(*sizes):
@@ -873,7 +881,7 @@
         ],
         compiler_params=params,
     )(shared, next_here, codes_here)
-    there = swap_halves(here)
+    first, second = swap_halves(here)
     known, spread = pl.pallas_call(
         spread_kernel,
         out_shape=(float_shape(2 * PAIRS, *plane), float_shape(4, *plane)),
@@ -886,10 +894,11 @@
     return pl.pallas_call(
         join_kernel,
         out_shape=float_shape(*state.shape),
-        in_specs=[vmem] * 4,
+        in_specs=[vmem] * 5,
         out_specs=vmem,
+        scratch_shapes=[pltpu.VMEM((MIDDLE_ROWS, LANES), jnp.float32)],
         compiler_params=params,
-    )(here, there, known, spread)
+    )(here, first, second, known, spread)
 
 
 def solution(mesh):

time: 23.7 us -> 25.5 us (1.076)
  starting transfers between devices: 1.55 us -> 4.06 us
  waiting for transfers between devices: 5.23 us -> 4.53 us
    ppermute x1 -> x2, starting transfers between devices: 1.55 us -> 4.06 us  [swap_halves(): results.append(lax.ppermute(block, 'cell', pairs))]
    ppermute x1 -> x2, waiting for transfers between devices: 5.23 us -> 4.53 us  [swap_halves(): results.append(lax.ppermute(block, 'cell', pairs))]
  transfers between devices with their start and end apart: 1 -> 2, of which waited for: 1 -> 1; matrix products, arithmetic and copies ran while one was open for 0% -> 0% of each run, Pallas kernels for 0% -> 0%
where the time goes in v16:
time: 25.5 us; the launch traced here: 25.3 us
  blocking collectives  14.7 us (58%)
  waiting for transfers between devices  4.53 us (18%)
  starting transfers between devices  4.06 us (16%)
  Pallas kernels  1.95 us (8%)
    all_to_all x1, blocking collectives, share_half(): lax.all_to_all(copies, ('inst', 'cell'), split_axis=0, concat_axis=0, til...  14.7 us
    ppermute x2, waiting for transfers between devices, swap_halves(): results.append(lax.ppermute(block, 'cell', pairs))  4.53 us
    ppermute x2, starting transfers between devices, swap_halves(): results.append(lax.ppermute(block, 'cell', pairs))  4.06 us
    pallas_call x1, Pallas kernels, local_by_halves(): pl.pallas_call(pack_kernel, out_shape=(float_shape(insts * blocks, BLOCK_...  0.83 us
    pallas_call x1, Pallas kernels, local_by_halves(): pl.pallas_call(join_kernel, out_shape=float_shape(*state.shape), in_specs...  0.71 us
  transfers between devices with their start and end apart: 2, of which 1 were waited for; matrix products, arithmetic and copies ran while one was open for 0% of the time, Pallas kernels for 0%

profile of v16, /device:TPU:0, one launch (start us, length us, event | category | flops | bytes accessed | tf_op | source)
XLA Modules:
  0.0 25.3 jit_solution(2874239860842482682)
XLA Ops:
  0.0 0.8 %shard_map.46 = (f32[16,56,128]{2,1,0:T(8,128)S(1)}, s32[256]{0:T(256)S(1)}, s32[2,8]{1,0:T(2,128)S(1)}) custom-call(f32[2,6,2,256]{3,2,1,0:T(2,128)} %held_state_ref.1, f32[2,256]{1,0:T(2,128)} %held_rate_ref.1, s32[256]{0:T(256)} %held_next_ref.1, s32[2,8]{1,0:T(2,128)} %held_codes_ref.1), custom_call_target="tpu_custom_call" | custom-call | tf_op jit(solution)/shard_map/pallas_call | solution.py:853
  0.8 14.7 %all_to_all.5 = f32[16,56,128]{2,1,0:T(8,128)S(1)} all-to-all(f32[16,56,128]{2,1,0:T(8,128)S(1)} %get-tuple-element.12), channel_id=1, replica_groups={{0,1,2,3,8,9,10,11,16,17,18,19,24,25,26,27},{7,6,5,4,15,14,13,12,23,22,..., dimensions={0} | all-to-all | bytes 917504 | tf_op jit(solution)/shard_map/all_to_all | solution.py:822
  15.6 0.4 %shard_map.47 = (f32[136,128]{1,0:T(8,128)S(1)}, f32[3,13,8,128]{3,2,1,0:T(8,128)S(1)}) custom-call(f32[4,4,56,128]{3,2,1,0:T(8,128)S(1)} %bitcast.1, s32[256]{0:T(256)S(1)} %get-tuple-element.13.next_ref, s32[2,8]{1,0:T(2,128)S(1)} %get-tuple-element.14.codes_ref), custom_call_target="tpu_custom_call" | custom-call | tf_op jit(solution)/shard_map/pallas_call | solution.py:870
  15.9 3.4 %collective-permute-start.1 = (f32[136,128]{1,0:T(8,128)S(1)}, f32[136,128]{1,0:T(8,128)S(1)}, u32[]{:S(2)}, u32[]{:S(2)}) collective-permute-start(f32[136,128]{1,0:T(8,128)S(1)} %get-tuple-element.15.here_ref), channel_id=1, source_target_pairs={{0,4},{1,5},{4,0},{5,1},{8,12},{9,13},{12,8},{13,9},{16,20},{17,21... | collective-permute-start | bytes 208904 | tf_op jit(solution)/shard_map/ppermute | solution.py:834
  19.3 0.7 %collective-permute-start = (f32[136,128]{1,0:T(8,128)S(1)}, f32[136,128]{1,0:T(8,128)S(1)}, u32[]{:S(2)}, u32[]{:S(2)}) collective-permute-start(f32[136,128]{1,0:T(8,128)S(1)} %get-tuple-element.15.here_ref), channel_id=1, source_target_pairs={{2,6},{3,7},{6,2},{7,3},{10,14},{11,15},{14,10},{15,11},{18,22},{1... | collective-permute-start | bytes 208904 | tf_op jit(solution)/shard_map/ppermute | solution.py:834
  20.0 4.5 %collective-permute-done.1.second_ref = f32[136,128]{1,0:T(8,128)S(1)} collective-permute-done((f32[136,128]{1,0:T(8,128)S(1)}, f32[136,128]{1,0:T(8,128)S(1)}, u32[]{:S(2)}, u32[]{:S(2)}) %collective-permute-start.1) | collective-permute-done | bytes 69664 | tf_op jit(solution)/shard_map/ppermute | solution.py:834
  24.6 0.0 collective-permute-done.first_ref
  24.6 0.7 %shard_map.49 = f32[2,6,2,256]{3,2,1,0:T(2,128)} custom-call(f32[136,128]{1,0:T(8,128)S(1)} %get-tuple-element.15.here_ref, f32[136,128]{1,0:T(8,128)S(1)} %collective-permute-done.first_ref, f32[136,128]{1,0:T(8,128)S(1)} %collective-permute-done.1.second_ref, f32[6,8,128]{2,1,0:T(8,128)S(1)} %get-tuple-element.17.known_ref, ...), custom_call_target="tpu_custom_call" | custom-call | tf_op jit(solution)/shard_map/pallas_call | solution.py:894
  (1 shorter events, 0.0 us)
Async XLA Ops:
  15.9 8.6 %collective-permute-start.1 = (f32[136,128]{1,0:T(8,128)S(1)}, f32[136,128]{1,0:T(8,128)S(1)}, u32[]{:S(2)}, u32[]{:S(2)}) collective-permute-start(f32[136,128]{1,0:T(8,128)S(1)} %get-tuple-element.15.here_ref), channel_id=1, source_target_pairs={{0,4},{1,5},{4,0},{5,1},{8,12},{9,13},{12,8},{13,9},{16,20},{17,21... | collective-permute-start | bytes 208904 | tf_op jit(solution)/shard_map/ppermute | solution.py:834
  19.3 5.2 %collective-permute-start = (f32[136,128]{1,0:T(8,128)S(1)}, f32[136,128]{1,0:T(8,128)S(1)}, u32[]{:S(2)}, u32[]{:S(2)}) collective-permute-start(f32[136,128]{1,0:T(8,128)S(1)} %get-tuple-element.15.here_ref), channel_id=1, source_target_pairs={{2,6},{3,7},{6,2},{7,3},{10,14},{11,15},{14,10},{15,11},{18,22},{1... | collective-permute-start | bytes 208904 | tf_op jit(solution)/shard_map/ppermute | solution.py:834

commit v17 on v15

--- a/solution.py
+++ b/solution.py
@@ -346,7 +346,7 @@
 SIDE_ROW = 3 * CELL_ROWS
 CORRECTION_ROW = SIDE_ROW + 2 * CELL_ROWS
 MIDDLE_ROWS = CORRECTION_ROW + 2 * ROWS
-BLOCK_PLANES = 4 + 3 + 2 * PAIRS
+FIXED_ROWS = 3 * CELL_ROWS + 2 * ROWS
 
 
 def spectral_offsets():
@@ -433,6 +433,40 @@
             out_ref[copy, pl.ds(row, ROWS), :] = values
 
 
+def turn_insts(first_inst, plane):
+    return jnp.where(first_inst, pltpu.roll(plane, 6, 0), pltpu.roll(plane, 2, 0))
+
+
+def time_weights(first_inst, shift):
+    offsets = spectral_offsets()
+    other = jnp.where(
+        first_inst, offsets[(2 * shift + 1) % NT], offsets[(2 * shift - 1) % NT]
+    )
+    return offsets[(2 * shift) % NT], other
+
+
+def cell_rows(cell, k):
+    return pl.ds((cell % 2) * CELL_ROWS + k * ROWS, ROWS)
+
+
+def partner_kernel(all_ref, out_ref):
+    own_inst = lax.axis_index("inst")
+    own_y, core = own_inst >> 1, own_inst & 1
+    _, first_inst, _ = plane_masks()
+    one, three = time_weights(first_inst, 1), time_weights(first_inst, 3)
+    near = [jnp.where(core == 0, a, b) for a, b in zip(one, three)]
+    away = [jnp.where(core == 0, b, a) for a, b in zip(one, three)]
+    for cell in range(2 * all_ref.shape[1]):
+        for k in range(PAIRS):
+            here = all_ref[own_y, cell // 2, cell_rows(cell, k), :]
+            there = all_ref[1 - own_y, cell // 2, cell_rows(cell, k), :]
+            out_ref[pl.ds(cell * CELL_ROWS + k * ROWS, ROWS), :] = (
+                near[0] * here
+                + away[0] * there
+                + turn_insts(first_inst, near[1] * here + away[1] * there)
+            )
+
+
 def two_by_two(first, second):
     def entry(a, b, c, d):
         terms = [x * y for x, y in ((a, b), (c, d)) if x is not None and y is not None]
@@ -557,10 +591,10 @@
 
 
 def half_kernel(
-    all_ref, next_ref, codes_ref, middle_ref, blocks_ref, rest_ref, line_ref,
+    all_ref, next_ref, codes_ref, partial_ref, factor_ref, blocks_ref, fixed_ref, line_ref,
 ):
-    own_inst = lax.axis_index("inst")
-    inst_count, blocks = all_ref.shape[:2]
+    own_y = lax.axis_index("inst") >> 1
+    blocks = all_ref.shape[1]
     cells = 2 * blocks
     mirrored = lax.axis_index("cell") // blocks
     sign = (1 - 2 * mirrored).astype(jnp.float32)
@@ -603,36 +637,17 @@
     pick_next = picker(next_line)
     pick_prev = picker(prev_line)
 
-    def loaded(cell, inst=own_inst):
+    def loaded(cell, place=own_y):
+        return [all_ref[place, cell // 2, cell_rows(cell, k), :] for k in range(PAIRS)]
+
+    own_weights, away_weights = time_weights(first_inst, 0), time_weights(first_inst, 2)
+
+    def own_time_parts(planes, cell):
         return [
-            all_ref[inst, cell // 2, pl.ds((cell % 2) * CELL_ROWS + k * ROWS, ROWS), :]
-            for k in range(PAIRS)
+            away_weights[0] * away
+            + turn_insts(first_inst, own_weights[1] * own + away_weights[1] * away)
+            for own, away in zip(planes, loaded(cell, 1 - own_y))
         ]
-
-    offsets = spectral_offsets()
-
-    def time_parts(cell):
-        pairs = [
-            loaded(cell, (own_inst - shift) & (inst_count - 1)) for shift in range(inst_count)
-        ]
-        result = []
-        for k in range(PAIRS):
-            same_total, other_total = None, None
-            for shift in range(inst_count):
-                plane = pairs[shift][k]
-                other = jnp.where(
-                    first_inst, offsets[(2 * shift + 1) % NT], offsets[(2 * shift - 1) % NT]
-                )
-                if shift > 0:
-                    term = offsets[(2 * shift) % NT] * plane
-                    same_total = term if same_total is None else same_total + term
-                term = other * plane
-                other_total = term if other_total is None else other_total + term
-            turned = jnp.where(
-                first_inst, pltpu.roll(other_total, 6, 0), pltpu.roll(other_total, 2, 0)
-            )
-            result.append(same_total + turned)
-        return result
 
     def flux_across(planes, velocity, pressure):
         return [
@@ -659,9 +674,9 @@
         velocity_x, velocity_y, pressure, sound = primitives(first_var, planes)
         line_ref[cell, 0], line_ref[cell, 1], line_ref[cell, 2] = velocity_x, pressure, sound
         faces_across = pitch_flux(planes, velocity_y, pressure, sound)
-        times = time_parts(cell)
+        times = own_time_parts(planes, cell)
         for k in range(PAIRS):
-            rest_ref[cell, k] = times[k] + (faces_across[k] - pick_prev(faces_across[k]))
+            partial_ref[cell, k] = -(times[k] + (faces_across[k] - pick_prev(faces_across[k])))
 
     tile = half_index * (LANES // LINES_DEV) + lane_index // LINES_DEV
     end_codes = jnp.where(mirrored == 0, codes_ref[pl.ds(0, 1), :], codes_ref[pl.ds(1, 1), :])
@@ -682,7 +697,7 @@
         return result
 
     line = LineCells(first_var, sign)
-    sides, faces, inverses, aboves = [], {}, [], []
+    faces, inverses, aboves = {}, [], []
     for cell in range(-2, cells):
         if cell < 0:
             planes = ghost(cell)
@@ -693,53 +708,73 @@
         line.add(cell, planes, velocity_x, pressure, sound)
         if cell >= 1:
             faces[cell - 2] = line.face(cell - 2)
+        if cell >= 2:
+            at = cell - 2
+            for k in range(PAIRS):
+                partial_ref[at, k] = partial_ref[at, k] + (faces[at - 1][k] - faces[at][k])
         if cell >= 3 and cell % 2 == 1:
             at = cell - 3
             block = at // 2
-            rates = rates_at(all_ref, (own_inst, block), RATE_ROW, first_half)
+            rates = rates_at(all_ref, (own_y, block), RATE_ROW, first_half)
             diag = line.diagonal(at, rates)
-            side = []
-            for member in range(2):
-                for k in range(PAIRS):
-                    side.append(
-                        faces[at + member - 1][k] - faces[at + member][k]
-                        - rest_ref[at + member, k]
-                    )
             if block > 0:
                 factor = two_by_two(line.below(at), inverses[-1])
                 diag = less(diag, two_by_two(factor, aboves[-1]))
-                side = difference(side, apply_matrix(factor, sides[-1]))
+                for n in range(4):
+                    factor_ref[block - 1, n] = factor[n]
             inverses.append(inverse_of(diag))
             aboves.append(line.above(at))
-            sides.append(side)
+            kept = [*inverses[-1], aboves[-1][0], *aboves[-1][2:]]
+            for n, plane in enumerate(kept):
+                blocks_ref[block, n] = plane
 
     last = cells - 2
+    for k in range(PAIRS):
+        partial_ref[last, k] = partial_ref[last, k] + faces[last - 1][k]
     factor = two_by_two(line.below(last), inverses[-1])
+    for n in range(4):
+        factor_ref[blocks - 2, n] = factor[n]
     correction = list(two_by_two(factor, aboves[-1]))
-    rates = rates_at(all_ref, (own_inst, blocks - 1), RATE_ROW, first_half)
+    rates = rates_at(all_ref, (own_y, blocks - 1), RATE_ROW, first_half)
     for member in range(2):
         centre = line.radius[last + member]
         correction[3 * member] = correction[3 * member] - rates[member] * centre
-    side = [faces[last - 1][k] - rest_ref[last, k] for k in range(PAIRS)]
-    side += [-rest_ref[last + 1, k] for k in range(PAIRS)]
-    side = difference(side, apply_matrix(factor, sides[-1]))
     for n in range(3):
         for k, plane in enumerate(line.state[cells - 3 + n]):
-            middle_ref[pl.ds(n * CELL_ROWS + k * ROWS, ROWS), :] = plane
-    for n, plane in enumerate(side):
-        middle_ref[pl.ds(SIDE_ROW + n * ROWS, ROWS), :] = plane
+            fixed_ref[pl.ds(n * CELL_ROWS + k * ROWS, ROWS), :] = plane
     for n in range(2):
-        middle_ref[pl.ds(CORRECTION_ROW + n * ROWS, ROWS), :] = jnp.where(
+        fixed_ref[pl.ds(SIDE_ROW + n * ROWS, ROWS), :] = jnp.where(
             first_var, correction[2 * n], correction[2 * n + 1]
         )
-    for block in range(blocks - 1):
-        kept = [*inverses[block], aboves[block][0], *aboves[block][2:], *sides[block]]
-        for n, plane in enumerate(kept):
-            blocks_ref[block, n] = plane
-
-
-def spread_kernel(all_ref, blocks_ref, known_ref, spread_ref, table_ref):
-    own_inst = lax.axis_index("inst")
+
+
+def reduce_kernel(partial_ref, time_ref, factor_ref, fixed_ref, middle_ref, sides_ref):
+    blocks = partial_ref.shape[0] // 2
+    side = None
+    for block in range(blocks):
+        own = []
+        for cell in (2 * block, 2 * block + 1):
+            for k in range(PAIRS):
+                time = time_ref[pl.ds(cell * CELL_ROWS + k * ROWS, ROWS), :]
+                own.append(partial_ref[cell, k] - time)
+        if block > 0:
+            factor = [factor_ref[block - 1, n] for n in range(4)]
+            own = difference(own, apply_matrix(factor, side))
+        side = own
+        for n, plane in enumerate(side):
+            if block < blocks - 1:
+                sides_ref[block, n] = plane
+            else:
+                middle_ref[pl.ds(SIDE_ROW + n * ROWS, ROWS), :] = plane
+    for row in range(0, SIDE_ROW, ROWS):
+        middle_ref[pl.ds(row, ROWS), :] = fixed_ref[pl.ds(row, ROWS), :]
+    for n in range(2):
+        rows = fixed_ref[pl.ds(SIDE_ROW + n * ROWS, ROWS), :]
+        middle_ref[pl.ds(CORRECTION_ROW + n * ROWS, ROWS), :] = rows
+
+
+def spread_kernel(all_ref, blocks_ref, sides_ref, known_ref, spread_ref, table_ref):
+    own_y = lax.axis_index("inst") >> 1
     blocks = all_ref.shape[1]
     own_cell = lax.axis_index("cell")
     own_block = jnp.where(own_cell < blocks, own_cell, 2 * blocks - 1 - own_cell)
@@ -747,8 +782,9 @@
     known, spread = [zero] * (2 * PAIRS), (zero + 1.0, zero, zero, zero + 1.0)
     for block in range(blocks - 1, -1, -1):
         if block < blocks - 1:
-            kept = [blocks_ref[block, n] for n in range(BLOCK_PLANES)]
-            inverse, above, side = kept[:4], (kept[4], None, kept[5], kept[6]), kept[7:]
+            kept = [blocks_ref[block, n] for n in range(7)]
+            inverse, above = kept[:4], (kept[4], None, kept[5], kept[6])
+            side = [sides_ref[block, n] for n in range(2 * PAIRS)]
             step = two_by_two(inverse, above)
             own = apply_matrix(inverse, side)
             if block < blocks - 2:
@@ -759,7 +795,7 @@
         for n, plane in enumerate(known + list(spread)):
             table_ref[block, n] = plane
     for n in range(2 * PAIRS):
-        base = all_ref[own_inst, own_block, pl.ds(n * ROWS, ROWS), :]
+        base = all_ref[own_y, own_block, pl.ds(n * ROWS, ROWS), :]
         known_ref[n] = base + table_ref[own_block, n]
     for n in range(4):
         spread_ref[n] = table_ref[own_block, 2 * PAIRS + n]
@@ -815,11 +851,20 @@
 def share_half(copies):
     insts, count = lax.axis_size("inst"), lax.axis_size("cell")
     halves = [range(count // 2), range(count - 1, count // 2 - 1, -1)]
-    groups = [[inst * count + cell for inst in range(insts) for cell in half] for half in halves]
+    groups = [
+        [inst * count + cell for inst in range(core, insts, 2) for cell in half]
+        for core in range(2)
+        for half in halves
+    ]
     return lax.all_to_all(
         copies, ("inst", "cell"), split_axis=0, concat_axis=0, tiled=True,
         axis_index_groups=groups,
     )
+
+
+def swap_cores(block):
+    pairs = [(inst, inst ^ 1) for inst in range(lax.axis_size("inst"))]
+    return lax.ppermute(block, "inst", pairs)
 
 
 def swap_halves(block):
@@ -837,7 +882,7 @@
     vmem = pl.BlockSpec(memory_space=pltpu.VMEM)
     plane = (ROWS, LANES)
     params = pltpu.CompilerParams(vmem_limit_bytes=VMEM_BYTES)
-    insts = lax.axis_size("inst")
+    places = lax.axis_size("inst") // 2
     held = [
         pltpu.with_memory_space_constraint(array, pltpu.HBM)
         for array in (state, pseudo_rate, line_next, face_codes)
@@ -845,7 +890,7 @@
     packed, next_here, codes_here = pl.pallas_call(
         pack_kernel,
         out_shape=(
-            float_shape(insts * blocks, BLOCK_ROWS, LANES),
+            float_shape(places * blocks, BLOCK_ROWS, LANES),
             jax.ShapeDtypeStruct(line_next.shape, jnp.int32),
             jax.ShapeDtypeStruct(face_codes.shape, jnp.int32),
         ),
@@ -858,31 +903,50 @@
         ],
         compiler_params=params,
     )(*held)
-    shared = share_half(packed).reshape(insts, blocks, BLOCK_ROWS, LANES)
-    here, eliminated = pl.pallas_call(
+    shared = share_half(packed).reshape(places, blocks, BLOCK_ROWS, LANES)
+    for_partner = pl.pallas_call(
+        partner_kernel,
+        out_shape=float_shape(cells * CELL_ROWS, LANES),
+        in_specs=[vmem],
+        out_specs=vmem,
+        compiler_params=params,
+    )(shared)
+    from_partner = swap_cores(for_partner)
+    beside = pl.CostEstimate(flops=10**6, bytes_accessed=10**6, transcendentals=0)
+    partial, factors, eliminated, fixed = pl.pallas_call(
         half_kernel,
         out_shape=(
+            float_shape(cells, PAIRS, *plane),
+            float_shape(blocks - 1, 4, *plane),
+            float_shape(blocks - 1, 7, *plane),
+            float_shape(FIXED_ROWS, LANES),
+        ),
+        in_specs=[vmem] * 3,
+        out_specs=(vmem,) * 4,
+        scratch_shapes=[pltpu.VMEM((cells, 3) + plane, jnp.float32)],
+        compiler_params=params,
+        cost_estimate=beside,
+    )(shared, next_here, codes_here)
+    here, sides = pl.pallas_call(
+        reduce_kernel,
+        out_shape=(
             float_shape(MIDDLE_ROWS, LANES),
-            float_shape(blocks - 1, BLOCK_PLANES, *plane),
+            float_shape(blocks - 1, 2 * PAIRS, *plane),
         ),
-        in_specs=[vmem, vmem, vmem],
+        in_specs=[vmem] * 4,
         out_specs=(vmem, vmem),
-        scratch_shapes=[
-            pltpu.VMEM((cells, PAIRS) + plane, jnp.float32),
-            pltpu.VMEM((cells, 3) + plane, jnp.float32),
-        ],
         compiler_params=params,
-    )(shared, next_here, codes_here)
+    )(partial, from_partner, factors, fixed)
     there = swap_halves(here)
     known, spread = pl.pallas_call(
         spread_kernel,
         out_shape=(float_shape(2 * PAIRS, *plane), float_shape(4, *plane)),
-        in_specs=[vmem, vmem],
+        in_specs=[vmem] * 3,
         out_specs=(vmem, vmem),
         scratch_shapes=[pltpu.VMEM((blocks, 2 * PAIRS + 4) + plane, jnp.float32)],
         compiler_params=params,
-        cost_estimate=pl.CostEstimate(flops=10**6, bytes_accessed=10**6, transcendentals=0),
-    )(shared, eliminated)
+        cost_estimate=beside,
+    )(shared, eliminated, sides)
     return pl.pallas_call(
         join_kernel,
         out_shape=float_shape(*state.shape),

time: 23.7 us -> 22.3 us (0.941)
  blocking collectives: 14.7 us -> 12.8 us
  waiting for transfers between devices: 5.23 us -> 6.43 us
  starting transfers between devices: 1.55 us -> 0.92 us
    all_to_all x1, blocking collectives: 14.7 us -> 12.8 us  [share_half(): lax.all_to_all(copies, ('inst', 'cell'), split_axis=0, concat_axis=0, til...]
    ppermute x0 -> x1, waiting for transfers between devices: none -> 0.94 us  [swap_cores(): return lax.ppermute(block, 'inst', pairs)]
    ppermute x1, starting transfers between devices: 1.55 us -> 0.85 us  [swap_halves(): lax.ppermute(block, 'cell', [(i, (i + count // 2) % count) for i in range...]
    ppermute x1, waiting for transfers between devices: 5.23 us -> 5.5 us  [swap_halves(): lax.ppermute(block, 'cell', [(i, (i + count // 2) % count) for i in range...]
    pallas_call x2 -> x4, Pallas kernels: 1.2 us -> 1.24 us  [the longest x1 0.82 us: local_by_halves(): pl.pallas_call(pack_kernel, out_shape=(float_shape(places * blocks, BLOCK...]
  transfers between devices with their start and end apart: 1 -> 2, of which waited for: 1 -> 2; matrix products, arithmetic and copies ran while one was open for 0% -> 0% of each run, Pallas kernels for 0% -> 2%
where the time goes in v17:
time: 22.3 us; the launch traced here: 22.1 us
  blocking collectives  12.8 us (57%)
  waiting for transfers between devices  6.43 us (29%)
  Pallas kernels  1.98 us (9%)
  starting transfers between devices  0.92 us (4%)
    all_to_all x1, blocking collectives, share_half(): lax.all_to_all(copies, ('inst', 'cell'), split_axis=0, concat_axis=0, til...  12.8 us
    ppermute x1, waiting for transfers between devices, swap_halves(): lax.ppermute(block, 'cell', [(i, (i + count // 2) % count) for i in range...  5.5 us
    ppermute x1, waiting for transfers between devices, swap_cores(): return lax.ppermute(block, 'inst', pairs)  0.94 us
    ppermute x1, starting transfers between devices, swap_halves(): lax.ppermute(block, 'cell', [(i, (i + count // 2) % count) for i in range...  0.85 us
    pallas_call x1, Pallas kernels, local_by_halves(): pl.pallas_call(pack_kernel, out_shape=(float_shape(places * blocks, BLOCK...  0.82 us
    pallas_call x1, Pallas kernels, local_by_halves(): pl.pallas_call(join_kernel, out_shape=float_shape(*state.shape), in_specs...  0.7 us
  transfers between devices with their start and end apart: 2, of which 2 were waited for; matrix products, arithmetic and copies ran while one was open for 0% of the time, Pallas kernels for 2%

profile of v17, /device:TPU:0, one launch (start us, length us, event | category | flops | bytes accessed | tf_op | source)
XLA Modules:
  0.0 22.1 jit_solution(16546625043738406009)
XLA Ops:
  0.0 0.8 %shard_map.46 = (f32[8,56,128]{2,1,0:T(8,128)S(1)}, s32[256]{0:T(256)S(1)}, s32[2,8]{1,0:T(2,128)S(1)}) custom-call(f32[2,6,2,256]{3,2,1,0:T(2,128)} %held_state_ref.1, f32[2,256]{1,0:T(2,128)} %held_rate_ref.1, s32[256]{0:T(256)} %held_next_ref.1, s32[2,8]{1,0:T(2,128)} %held_codes_ref.1), custom_call_target="tpu_custom_call" | custom-call | tf_op jit(solution)/shard_map/pallas_call | solution.py:890
  0.8 12.8 %all_to_all.5 = f32[8,56,128]{2,1,0:T(8,128)S(1)} all-to-all(f32[8,56,128]{2,1,0:T(8,128)S(1)} %get-tuple-element.16), channel_id=1, replica_groups={{0,1,2,3,16,17,18,19},{7,6,5,4,23,22,21,20},{8,9,10,11,24,25,26,27},{15..., dimensions={0} | all-to-all | bytes 458752 | tf_op jit(solution)/shard_map/all_to_all | solution.py:859
  13.6 0.1 collective-permute-start
  13.7 0.4 %shard_map.47 = (f32[8,3,8,128]{3,2,1,0:T(8,128)S(1)}, f32[3,4,8,128]{3,2,1,0:T(8,128)S(1)}, f32[3,7,8,128]{3,2,1,0:T(8,128)S(1)}, f32[88,128]{1,0:T(8,128)S(1)}) custom-call(f32[2,4,56,128]{3,2,1,0:T(8,128)S(1)} %bitcast.2, s32[256]{0:T(256)S(1)} %get-tuple-element.17.next_ref, s32[2,8]{1,0:T(2,128)S(1)} %get-tuple-element.18.codes_ref), custom_call_target="tpu_custom_call" | custom-call | flops 1000000 | bytes 1000000 | tf_op jit(solution)/shard_map/pallas_call | solution.py:916
  14.1 0.9 %collective-permute-done.time_ref = f32[192,128]{1,0:T(8,128)S(1)} collective-permute-done((f32[192,128]{1,0:T(8,128)S(1)}, f32[192,128]{1,0:T(8,128)S(1)}, u32[]{:S(2)}, u32[]{:S(2)}) %collective-permute-start) | collective-permute-done | bytes 98336 | tf_op jit(solution)/shard_map/ppermute | solution.py:867
  15.0 0.9 %collective-permute-start.1 = (f32[136,128]{1,0:T(8,128)S(1)}, f32[136,128]{1,0:T(8,128)S(1)}, u32[]{:S(2)}, u32[]{:S(2)}) collective-permute-start(f32[136,128]{1,0:T(8,128)S(1)} %get-tuple-element.22.here_ref), channel_id=1, source_target_pairs={{0,4},{1,5},{2,6},{3,7},{4,0},{5,1},{6,2},{7,3},{8,12},{9,13},{10,... | collective-permute-start | bytes 208904 | tf_op jit(solution)/shard_map/ppermute | solution.py:872
  15.9 5.5 %collective-permute-done.1.there_ref = f32[136,128]{1,0:T(8,128)S(1)} collective-permute-done((f32[136,128]{1,0:T(8,128)S(1)}, f32[136,128]{1,0:T(8,128)S(1)}, u32[]{:S(2)}, u32[]{:S(2)}) %collective-permute-start.1) | collective-permute-done | bytes 69664 | tf_op jit(solution)/shard_map/ppermute | solution.py:872
  21.4 0.7 %shard_map.51 = f32[2,6,2,256]{3,2,1,0:T(2,128)} custom-call(f32[136,128]{1,0:T(8,128)S(1)} %get-tuple-element.22.here_ref, f32[136,128]{1,0:T(8,128)S(1)} %collective-permute-done.1.there_ref, f32[6,8,128]{2,1,0:T(8,128)S(1)} %get-tuple-element.25.known_ref, f32[4,8,128]{2,1,0:T(8,128)S(1)} %get-tuple-element.26.spread_ref), custom_call_target="tpu_custom_call" | custom-call | tf_op jit(solution)/shard_map/pallas_call | solution.py:950
  (3 shorter events, 0.1 us)
Async XLA Ops:
  13.6 1.4 %collective-permute-start = (f32[192,128]{1,0:T(8,128)S(1)}, f32[192,128]{1,0:T(8,128)S(1)}, u32[]{:S(2)}, u32[]{:S(2)}) collective-permute-start(f32[192,128]{1,0:T(8,128)S(1)} %shard_map.48), channel_id=1, source_target_pairs={{0,8},{8,0},{16,24},{24,16},{1,9},{9,1},{17,25},{25,17},{2,10},{10... | collective-permute-start | bytes 294920 | tf_op jit(solution)/shard_map/ppermute | solution.py:867
  15.0 6.4 %collective-permute-start.1 = (f32[136,128]{1,0:T(8,128)S(1)}, f32[136,128]{1,0:T(8,128)S(1)}, u32[]{:S(2)}, u32[]{:S(2)}) collective-permute-start(f32[136,128]{1,0:T(8,128)S(1)} %get-tuple-element.22.here_ref), channel_id=1, source_target_pairs={{0,4},{1,5},{2,6},{3,7},{4,0},{5,1},{6,2},{7,3},{8,12},{9,13},{10,... | collective-permute-start | bytes 208904 | tf_op jit(solution)/shard_map/ppermute | solution.py:872

commit v18 on v17

--- a/solution.py
+++ b/solution.py
@@ -343,10 +343,8 @@
 VMEM_BYTES = 8 * 2**20
 BLOCK_ROWS = RATE_ROW + ROWS
 
-SIDE_ROW = 3 * CELL_ROWS
-CORRECTION_ROW = SIDE_ROW + 2 * CELL_ROWS
-MIDDLE_ROWS = CORRECTION_ROW + 2 * ROWS
-FIXED_ROWS = 3 * CELL_ROWS + 2 * ROWS
+CORRECTION_ROW = 3 * CELL_ROWS
+FIXED_ROWS = CORRECTION_ROW + 2 * ROWS
 
 
 def spectral_offsets():
@@ -743,12 +741,12 @@
         for k, plane in enumerate(line.state[cells - 3 + n]):
             fixed_ref[pl.ds(n * CELL_ROWS + k * ROWS, ROWS), :] = plane
     for n in range(2):
-        fixed_ref[pl.ds(SIDE_ROW + n * ROWS, ROWS), :] = jnp.where(
+        fixed_ref[pl.ds(CORRECTION_ROW + n * ROWS, ROWS), :] = jnp.where(
             first_var, correction[2 * n], correction[2 * n + 1]
         )
 
 
-def reduce_kernel(partial_ref, time_ref, factor_ref, fixed_ref, middle_ref, sides_ref):
+def reduce_kernel(partial_ref, time_ref, factor_ref, middle_ref, sides_ref):
     blocks = partial_ref.shape[0] // 2
     side = None
     for block in range(blocks):
@@ -765,12 +763,7 @@
             if block < blocks - 1:
                 sides_ref[block, n] = plane
             else:
-                middle_ref[pl.ds(SIDE_ROW + n * ROWS, ROWS), :] = plane
-    for row in range(0, SIDE_ROW, ROWS):
-        middle_ref[pl.ds(row, ROWS), :] = fixed_ref[pl.ds(row, ROWS), :]
-    for n in range(2):
-        rows = fixed_ref[pl.ds(SIDE_ROW + n * ROWS, ROWS), :]
-        middle_ref[pl.ds(CORRECTION_ROW + n * ROWS, ROWS), :] = rows
+                middle_ref[pl.ds(n * ROWS, ROWS), :] = plane
 
 
 def spread_kernel(all_ref, blocks_ref, sides_ref, known_ref, spread_ref, table_ref):
@@ -801,7 +794,9 @@
         spread_ref[n] = table_ref[own_block, 2 * PAIRS + n]
 
 
-def join_kernel(here_ref, there_ref, known_ref, spread_ref, out_ref):
+def join_kernel(
+    here_ref, there_ref, here_side_ref, there_side_ref, known_ref, spread_ref, out_ref
+):
     mirrored = lax.axis_index("cell") // (lax.axis_size("cell") // 2)
     sign = (1 - 2 * mirrored).astype(jnp.float32)
     first_var, _, _ = plane_masks()
@@ -821,8 +816,8 @@
         pairs = [both(first_var, plane_of(ref, CORRECTION_ROW + n * ROWS)) for n in range(2)]
         return [pairs[0][0], pairs[0][1], pairs[1][0], pairs[1][1]]
 
-    here_side = [plane_of(here_ref, SIDE_ROW + n * ROWS) for n in range(2 * PAIRS)]
-    there_side = [plane_of(there_ref, SIDE_ROW + n * ROWS) for n in range(2 * PAIRS)]
+    here_side = [plane_of(here_side_ref, n * ROWS) for n in range(2 * PAIRS)]
+    there_side = [plane_of(there_side_ref, n * ROWS) for n in range(2 * PAIRS)]
     side = [here_side[k] - faces[1][k] for k in range(PAIRS)]
     side += [here_side[PAIRS + k] + (faces[1][k] - faces[2][k]) for k in range(PAIRS)]
     other = [there_side[PAIRS + k] + (faces[2][k] - faces[3][k]) for k in range(PAIRS)]
@@ -913,7 +908,7 @@
     )(shared)
     from_partner = swap_cores(for_partner)
     beside = pl.CostEstimate(flops=10**6, bytes_accessed=10**6, transcendentals=0)
-    partial, factors, eliminated, fixed = pl.pallas_call(
+    partial, factors, eliminated, here = pl.pallas_call(
         half_kernel,
         out_shape=(
             float_shape(cells, PAIRS, *plane),
@@ -927,17 +922,18 @@
         compiler_params=params,
         cost_estimate=beside,
     )(shared, next_here, codes_here)
-    here, sides = pl.pallas_call(
+    there = swap_halves(here)
+    here_side, sides = pl.pallas_call(
         reduce_kernel,
         out_shape=(
-            float_shape(MIDDLE_ROWS, LANES),
+            float_shape(2 * CELL_ROWS, LANES),
             float_shape(blocks - 1, 2 * PAIRS, *plane),
         ),
-        in_specs=[vmem] * 4,
+        in_specs=[vmem] * 3,
         out_specs=(vmem, vmem),
         compiler_params=params,
-    )(partial, from_partner, factors, fixed)
-    there = swap_halves(here)
+    )(partial, from_partner, factors)
+    there_side = swap_halves(here_side)
     known, spread = pl.pallas_call(
         spread_kernel,
         out_shape=(float_shape(2 * PAIRS, *plane), float_shape(4, *plane)),
@@ -950,10 +946,10 @@
     return pl.pallas_call(
         join_kernel,
         out_shape=float_shape(*state.shape),
-        in_specs=[vmem] * 4,
+        in_specs=[vmem] * 6,
         out_specs=vmem,
         compiler_params=params,
-    )(here, there, known, spread)
+    )(here, there, here_side, there_side, known, spread)
 
 
 def solution(mesh):

time: 22.3 us -> 21.7 us (0.973)
  waiting for transfers between devices: 6.43 us -> 3.69 us
  starting transfers between devices: 0.92 us -> 3.05 us
    ppermute x1 -> x2, starting transfers between devices: 0.85 us -> 2.97 us  [swap_halves(): lax.ppermute(block, 'cell', [(i, (i + count // 2) % count) for i in range...]
    ppermute x1 -> x2, waiting for transfers between devices: 5.5 us -> 3.61 us  [swap_halves(): lax.ppermute(block, 'cell', [(i, (i + count // 2) % count) for i in range...]
    ppermute x1, waiting for transfers between devices: 0.94 us -> 0.08 us  [swap_cores(): return lax.ppermute(block, 'inst', pairs)]
  transfers between devices with their start and end apart: 2 -> 3, of which waited for: 2 -> 3; matrix products, arithmetic and copies ran while one was open for 0% -> 0% of each run, Pallas kernels for 2% -> 2%
where the time goes in v18:
time: 21.7 us; the launch traced here: 21.5 us
  blocking collectives  12.8 us (59%)
  waiting for transfers between devices  3.69 us (17%)
  starting transfers between devices  3.05 us (14%)
  Pallas kernels  1.97 us (9%)
    all_to_all x1, blocking collectives, share_half(): lax.all_to_all(copies, ('inst', 'cell'), split_axis=0, concat_axis=0, til...  12.8 us
    ppermute x2, waiting for transfers between devices, swap_halves(): lax.ppermute(block, 'cell', [(i, (i + count // 2) % count) for i in range...  3.61 us
    ppermute x2, starting transfers between devices, swap_halves(): lax.ppermute(block, 'cell', [(i, (i + count // 2) % count) for i in range...  2.97 us
    pallas_call x1, Pallas kernels, local_by_halves(): pl.pallas_call(pack_kernel, out_shape=(float_shape(places * blocks, BLOCK...  0.82 us
    pallas_call x1, Pallas kernels, local_by_halves(): pl.pallas_call(join_kernel, out_shape=float_shape(*state.shape), in_specs...  0.7 us
  transfers between devices with their start and end apart: 3, of which 3 were waited for; matrix products, arithmetic and copies ran while one was open for 0% of the time, Pallas kernels for 2%

profile of v18, /device:TPU:0, one launch (start us, length us, event | category | flops | bytes accessed | tf_op | source)
XLA Modules:
  0.0 21.5 jit_solution(17851300223106694116)
XLA Ops:
  0.0 0.8 %shard_map.46 = (f32[8,56,128]{2,1,0:T(8,128)S(1)}, s32[256]{0:T(256)S(1)}, s32[2,8]{1,0:T(2,128)S(1)}) custom-call(f32[2,6,2,256]{3,2,1,0:T(2,128)} %held_state_ref.1, f32[2,256]{1,0:T(2,128)} %held_rate_ref.1, s32[256]{0:T(256)} %held_next_ref.1, s32[2,8]{1,0:T(2,128)} %held_codes_ref.1), custom_call_target="tpu_custom_call" | custom-call | tf_op jit(solution)/shard_map/pallas_call | solution.py:885
  0.8 12.8 %all_to_all.5 = f32[8,56,128]{2,1,0:T(8,128)S(1)} all-to-all(f32[8,56,128]{2,1,0:T(8,128)S(1)} %get-tuple-element.16), channel_id=1, replica_groups={{0,1,2,3,16,17,18,19},{7,6,5,4,23,22,21,20},{8,9,10,11,24,25,26,27},{15..., dimensions={0} | all-to-all | bytes 458752 | tf_op jit(solution)/shard_map/all_to_all | solution.py:854
  13.6 0.1 collective-permute-start.1
  13.7 0.4 %shard_map.47 = (f32[8,3,8,128]{3,2,1,0:T(8,128)S(1)}, f32[3,4,8,128]{3,2,1,0:T(8,128)S(1)}, f32[3,7,8,128]{3,2,1,0:T(8,128)S(1)}, f32[88,128]{1,0:T(8,128)S(1)}) custom-call(f32[2,4,56,128]{3,2,1,0:T(8,128)S(1)} %bitcast.2, s32[256]{0:T(256)S(1)} %get-tuple-element.17.next_ref, s32[2,8]{1,0:T(2,128)S(1)} %get-tuple-element.18.codes_ref), custom_call_target="tpu_custom_call" | custom-call | flops 1000000 | bytes 1000000 | tf_op jit(solution)/shard_map/pallas_call | solution.py:911
  14.1 0.9 %collective-permute-start = (f32[88,128]{1,0:T(8,128)S(1)}, f32[88,128]{1,0:T(8,128)S(1)}, u32[]{:S(2)}, u32[]{:S(2)}) collective-permute-start(f32[88,128]{1,0:T(8,128)S(1)} %get-tuple-element.19.here_ref), channel_id=1, source_target_pairs={{0,4},{1,5},{2,6},{3,7},{4,0},{5,1},{6,2},{7,3},{8,12},{9,13},{10,... | collective-permute-start | bytes 135176 | tf_op jit(solution)/shard_map/ppermute | solution.py:867
  14.9 0.1 collective-permute-done.1.time_ref
  15.0 2.1 %collective-permute-start.2 = (f32[48,128]{1,0:T(8,128)S(1)}, f32[48,128]{1,0:T(8,128)S(1)}, u32[]{:S(2)}, u32[]{:S(2)}) collective-permute-start(f32[48,128]{1,0:T(8,128)S(1)} %get-tuple-element.22.here_side_ref), channel_id=1, source_target_pairs={{0,4},{1,5},{2,6},{3,7},{4,0},{5,1},{6,2},{7,3},{8,12},{9,13},{10,... | collective-permute-start | bytes 73736 | tf_op jit(solution)/shard_map/ppermute | solution.py:867
  17.2 2.9 %collective-permute-done.there_ref = f32[88,128]{1,0:T(8,128)S(1)} collective-permute-done((f32[88,128]{1,0:T(8,128)S(1)}, f32[88,128]{1,0:T(8,128)S(1)}, u32[]{:S(2)}, u32[]{:S(2)}) %collective-permute-start) | collective-permute-done | bytes 45088 | tf_op jit(solution)/shard_map/ppermute | solution.py:867
  20.1 0.8 %collective-permute-done.2.there_side_ref = f32[48,128]{1,0:T(8,128)S(1)} collective-permute-done((f32[48,128]{1,0:T(8,128)S(1)}, f32[48,128]{1,0:T(8,128)S(1)}, u32[]{:S(2)}, u32[]{:S(2)}) %collective-permute-start.2) | collective-permute-done | bytes 24608 | tf_op jit(solution)/shard_map/ppermute | solution.py:867
  20.8 0.7 %shard_map.51 = f32[2,6,2,256]{3,2,1,0:T(2,128)} custom-call(f32[88,128]{1,0:T(8,128)S(1)} %get-tuple-element.19.here_ref, f32[88,128]{1,0:T(8,128)S(1)} %collective-permute-done.there_ref, f32[48,128]{1,0:T(8,128)S(1)} %get-tuple-element.22.here_side_ref, f32[48,128]{1,0:T(8,128)S(1)} %collective-permute-done.2.there_side_ref, ...), custom_call_target="tpu_custom_call" | custom-call | tf_op jit(solution)/shard_map/pallas_call | solution.py:946
  (3 shorter events, 0.1 us)
Async XLA Ops:
  13.6 1.4 %collective-permute-start.1 = (f32[192,128]{1,0:T(8,128)S(1)}, f32[192,128]{1,0:T(8,128)S(1)}, u32[]{:S(2)}, u32[]{:S(2)}) collective-permute-start(f32[192,128]{1,0:T(8,128)S(1)} %shard_map.48), channel_id=1, source_target_pairs={{0,8},{8,0},{16,24},{24,16},{1,9},{9,1},{17,25},{25,17},{2,10},{10... | collective-permute-start | bytes 294920 | tf_op jit(solution)/shard_map/ppermute | solution.py:862
  14.1 6.0 %collective-permute-start = (f32[88,128]{1,0:T(8,128)S(1)}, f32[88,128]{1,0:T(8,128)S(1)}, u32[]{:S(2)}, u32[]{:S(2)}) collective-permute-start(f32[88,128]{1,0:T(8,128)S(1)} %get-tuple-element.19.here_ref), channel_id=1, source_target_pairs={{0,4},{1,5},{2,6},{3,7},{4,0},{5,1},{6,2},{7,3},{8,12},{9,13},{10,... | collective-permute-start | bytes 135176 | tf_op jit(solution)/shard_map/ppermute | solution.py:867
  15.0 5.8 %collective-permute-start.2 = (f32[48,128]{1,0:T(8,128)S(1)}, f32[48,128]{1,0:T(8,128)S(1)}, u32[]{:S(2)}, u32[]{:S(2)}) collective-permute-start(f32[48,128]{1,0:T(8,128)S(1)} %get-tuple-element.22.here_side_ref), channel_id=1, source_target_pairs={{0,4},{1,5},{2,6},{3,7},{4,0},{5,1},{6,2},{7,3},{8,12},{9,13},{10,... | collective-permute-start | bytes 73736 | tf_op jit(solution)/shard_map/ppermute | solution.py:867

commit v19 on v18

--- a/solution.py
+++ b/solution.py
@@ -343,8 +343,9 @@
 VMEM_BYTES = 8 * 2**20
 BLOCK_ROWS = RATE_ROW + ROWS
 
-CORRECTION_ROW = 3 * CELL_ROWS
-FIXED_ROWS = CORRECTION_ROW + 2 * ROWS
+MIDDLE_CELLS = 3
+CORRECTION_ROW = 2 * CELL_ROWS
+SIDE_ROWS = CORRECTION_ROW + 2 * ROWS
 
 
 def spectral_offsets():
@@ -447,14 +448,19 @@
     return pl.ds((cell % 2) * CELL_ROWS + k * ROWS, ROWS)
 
 
-def partner_kernel(all_ref, out_ref):
+def partner_kernel(all_ref, out_ref, middle_ref):
     own_inst = lax.axis_index("inst")
     own_y, core = own_inst >> 1, own_inst & 1
     _, first_inst, _ = plane_masks()
     one, three = time_weights(first_inst, 1), time_weights(first_inst, 3)
     near = [jnp.where(core == 0, a, b) for a, b in zip(one, three)]
     away = [jnp.where(core == 0, b, a) for a, b in zip(one, three)]
-    for cell in range(2 * all_ref.shape[1]):
+    cells = 2 * all_ref.shape[1]
+    for cell in range(cells - MIDDLE_CELLS, cells):
+        for k in range(PAIRS):
+            row = (cell - (cells - MIDDLE_CELLS)) * CELL_ROWS + k * ROWS
+            middle_ref[pl.ds(row, ROWS), :] = all_ref[own_y, cell // 2, cell_rows(cell, k), :]
+    for cell in range(cells):
         for k in range(PAIRS):
             here = all_ref[own_y, cell // 2, cell_rows(cell, k), :]
             there = all_ref[1 - own_y, cell // 2, cell_rows(cell, k), :]
@@ -589,7 +595,8 @@
 
 
 def half_kernel(
-    all_ref, next_ref, codes_ref, partial_ref, factor_ref, blocks_ref, fixed_ref, line_ref,
+    all_ref, next_ref, codes_ref, partial_ref, factor_ref, blocks_ref, correction_ref,
+    line_ref,
 ):
     own_y = lax.axis_index("inst") >> 1
     blocks = all_ref.shape[1]
@@ -737,16 +744,15 @@
     for member in range(2):
         centre = line.radius[last + member]
         correction[3 * member] = correction[3 * member] - rates[member] * centre
-    for n in range(3):
-        for k, plane in enumerate(line.state[cells - 3 + n]):
-            fixed_ref[pl.ds(n * CELL_ROWS + k * ROWS, ROWS), :] = plane
     for n in range(2):
-        fixed_ref[pl.ds(CORRECTION_ROW + n * ROWS, ROWS), :] = jnp.where(
+        correction_ref[pl.ds(n * ROWS, ROWS), :] = jnp.where(
             first_var, correction[2 * n], correction[2 * n + 1]
         )
 
 
-def reduce_kernel(partial_ref, time_ref, factor_ref, middle_ref, sides_ref):
+def reduce_kernel(partial_ref, time_ref, factor_ref, correction_ref, middle_ref, sides_ref):
+    for row in range(0, 2 * ROWS, ROWS):
+        middle_ref[pl.ds(CORRECTION_ROW + row, ROWS), :] = correction_ref[pl.ds(row, ROWS), :]
     blocks = partial_ref.shape[0] // 2
     side = None
     for block in range(blocks):
@@ -823,8 +829,8 @@
     other = [there_side[PAIRS + k] + (faces[2][k] - faces[3][k]) for k in range(PAIRS)]
     other += [there_side[k] + faces[3][k] for k in range(PAIRS)]
     no_rates = (None, None)
-    diag = difference(line.diagonal(1, no_rates), correction_of(here_ref))
-    other_diag = difference(line.diagonal(3, no_rates), correction_of(there_ref)[::-1])
+    diag = difference(line.diagonal(1, no_rates), correction_of(here_side_ref))
+    other_diag = difference(line.diagonal(3, no_rates), correction_of(there_side_ref)[::-1])
     factor = two_by_two(line.above(1), inverse_of(other_diag))
     diag = less(diag, two_by_two(factor, line.below(3)))
     middle = apply_matrix(inverse_of(diag), difference(side, apply_matrix(factor, other)))
@@ -899,22 +905,26 @@
         compiler_params=params,
     )(*held)
     shared = share_half(packed).reshape(places, blocks, BLOCK_ROWS, LANES)
-    for_partner = pl.pallas_call(
+    for_partner, here = pl.pallas_call(
         partner_kernel,
-        out_shape=float_shape(cells * CELL_ROWS, LANES),
+        out_shape=(
+            float_shape(cells * CELL_ROWS, LANES),
+            float_shape(MIDDLE_CELLS * CELL_ROWS, LANES),
+        ),
         in_specs=[vmem],
-        out_specs=vmem,
+        out_specs=(vmem, vmem),
         compiler_params=params,
     )(shared)
     from_partner = swap_cores(for_partner)
+    there = swap_halves(here)
     beside = pl.CostEstimate(flops=10**6, bytes_accessed=10**6, transcendentals=0)
-    partial, factors, eliminated, here = pl.pallas_call(
+    partial, factors, eliminated, correction = pl.pallas_call(
         half_kernel,
         out_shape=(
             float_shape(cells, PAIRS, *plane),
             float_shape(blocks - 1, 4, *plane),
             float_shape(blocks - 1, 7, *plane),
-            float_shape(FIXED_ROWS, LANES),
+            float_shape(2 * ROWS, LANES),
         ),
         in_specs=[vmem] * 3,
         out_specs=(vmem,) * 4,
@@ -922,17 +932,16 @@
         compiler_params=params,
         cost_estimate=beside,
     )(shared, next_here, codes_here)
-    there = swap_halves(here)
     here_side, sides = pl.pallas_call(
         reduce_kernel,
         out_shape=(
-            float_shape(2 * CELL_ROWS, LANES),
+            float_shape(SIDE_ROWS, LANES),
             float_shape(blocks - 1, 2 * PAIRS, *plane),
         ),
-        in_specs=[vmem] * 3,
+        in_specs=[vmem] * 4,
         out_specs=(vmem, vmem),
         compiler_params=params,
-    )(partial, from_partner, factors)
+    )(partial, from_partner, factors, correction)
     there_side = swap_halves(here_side)
     known, spread = pl.pallas_call(
         spread_kernel,

time: 21.7 us -> 21 us (0.968)
  waiting for transfers between devices: 3.69 us -> 2.92 us
    ppermute x2, waiting for transfers between devices: 3.61 us -> 2.84 us  [swap_halves(): lax.ppermute(block, 'cell', [(i, (i + count // 2) % count) for i in range...]
where the time goes in v19:
time: 21 us; the launch traced here: 20.8 us
  blocking collectives  12.8 us (61%)
  starting transfers between devices  3.06 us (15%)
  waiting for transfers between devices  2.92 us (14%)
  Pallas kernels  1.98 us (9%)
    all_to_all x1, blocking collectives, share_half(): lax.all_to_all(copies, ('inst', 'cell'), split_axis=0, concat_axis=0, til...  12.8 us
    ppermute x2, starting transfers between devices, swap_halves(): lax.ppermute(block, 'cell', [(i, (i + count // 2) % count) for i in range...  2.99 us
    ppermute x2, waiting for transfers between devices, swap_halves(): lax.ppermute(block, 'cell', [(i, (i + count // 2) % count) for i in range...  2.84 us
    pallas_call x1, Pallas kernels, local_by_halves(): pl.pallas_call(pack_kernel, out_shape=(float_shape(places * blocks, BLOCK...  0.82 us
    pallas_call x1, Pallas kernels, local_by_halves(): pl.pallas_call(join_kernel, out_shape=float_shape(*state.shape), in_specs...  0.7 us
  transfers between devices with their start and end apart: 3, of which 3 were waited for; matrix products, arithmetic and copies ran while one was open for 0% of the time, Pallas kernels for 2%

profile of v19, /device:TPU:0, one launch (start us, length us, event | category | flops | bytes accessed | tf_op | source)
XLA Modules:
  0.0 20.8 jit_solution(7618491186125622889)
XLA Ops:
  0.0 0.8 %shard_map.46 = (f32[8,56,128]{2,1,0:T(8,128)S(1)}, s32[256]{0:T(256)S(1)}, s32[2,8]{1,0:T(2,128)S(1)}) custom-call(f32[2,6,2,256]{3,2,1,0:T(2,128)} %held_state_ref.1, f32[2,256]{1,0:T(2,128)} %held_rate_ref.1, s32[256]{0:T(256)} %held_next_ref.1, s32[2,8]{1,0:T(2,128)} %held_codes_ref.1), custom_call_target="tpu_custom_call" | custom-call | tf_op jit(solution)/shard_map/pallas_call | solution.py:891
  0.8 12.8 %all_to_all.5 = f32[8,56,128]{2,1,0:T(8,128)S(1)} all-to-all(f32[8,56,128]{2,1,0:T(8,128)S(1)} %get-tuple-element.18), channel_id=1, replica_groups={{0,1,2,3,16,17,18,19},{7,6,5,4,23,22,21,20},{8,9,10,11,24,25,26,27},{15..., dimensions={0} | all-to-all | bytes 458752 | tf_op jit(solution)/shard_map/all_to_all | solution.py:860
  13.6 0.1 collective-permute-start.1
  13.7 0.9 %collective-permute-start = (f32[72,128]{1,0:T(8,128)S(1)}, f32[72,128]{1,0:T(8,128)S(1)}, u32[]{:S(2)}, u32[]{:S(2)}) collective-permute-start(f32[72,128]{1,0:T(8,128)S(1)} %get-tuple-element.19.here_ref), channel_id=1, source_target_pairs={{0,4},{1,5},{2,6},{3,7},{4,0},{5,1},{6,2},{7,3},{8,12},{9,13},{10,... | collective-permute-start | bytes 110600 | tf_op jit(solution)/shard_map/ppermute | solution.py:873
  14.6 0.4 %shard_map.48 = (f32[8,3,8,128]{3,2,1,0:T(8,128)S(1)}, f32[3,4,8,128]{3,2,1,0:T(8,128)S(1)}, f32[3,7,8,128]{3,2,1,0:T(8,128)S(1)}, f32[16,128]{1,0:T(8,128)S(1)}) custom-call(f32[2,4,56,128]{3,2,1,0:T(8,128)S(1)} %bitcast.2, s32[256]{0:T(256)S(1)} %get-tuple-element.20.next_ref, s32[2,8]{1,0:T(2,128)S(1)} %get-tuple-element.21.codes_ref), custom_call_target="tpu_custom_call" | custom-call | flops 1000000 | bytes 1000000 | tf_op jit(solution)/shard_map/pallas_call | solution.py:921
  14.9 0.1 collective-permute-done.1.time_ref
  15.0 2.1 %collective-permute-start.2 = (f32[64,128]{1,0:T(8,128)S(1)}, f32[64,128]{1,0:T(8,128)S(1)}, u32[]{:S(2)}, u32[]{:S(2)}) collective-permute-start(f32[64,128]{1,0:T(8,128)S(1)} %get-tuple-element.26.here_side_ref), channel_id=1, source_target_pairs={{0,4},{1,5},{2,6},{3,7},{4,0},{5,1},{6,2},{7,3},{8,12},{9,13},{10,... | collective-permute-start | bytes 98312 | tf_op jit(solution)/shard_map/ppermute | solution.py:873
  17.2 1.9 %collective-permute-done.there_ref = f32[72,128]{1,0:T(8,128)S(1)} collective-permute-done((f32[72,128]{1,0:T(8,128)S(1)}, f32[72,128]{1,0:T(8,128)S(1)}, u32[]{:S(2)}, u32[]{:S(2)}) %collective-permute-start) | collective-permute-done | bytes 36896 | tf_op jit(solution)/shard_map/ppermute | solution.py:873
  19.1 0.9 %collective-permute-done.2.there_side_ref = f32[64,128]{1,0:T(8,128)S(1)} collective-permute-done((f32[64,128]{1,0:T(8,128)S(1)}, f32[64,128]{1,0:T(8,128)S(1)}, u32[]{:S(2)}, u32[]{:S(2)}) %collective-permute-start.2) | collective-permute-done | bytes 32800 | tf_op jit(solution)/shard_map/ppermute | solution.py:873
  20.1 0.7 %shard_map.51 = f32[2,6,2,256]{3,2,1,0:T(2,128)} custom-call(f32[72,128]{1,0:T(8,128)S(1)} %get-tuple-element.19.here_ref, f32[72,128]{1,0:T(8,128)S(1)} %collective-permute-done.there_ref, f32[64,128]{1,0:T(8,128)S(1)} %get-tuple-element.26.here_side_ref, f32[64,128]{1,0:T(8,128)S(1)} %collective-permute-done.2.there_side_ref, ...), custom_call_target="tpu_custom_call" | custom-call | tf_op jit(solution)/shard_map/pallas_call | solution.py:955
  (3 shorter events, 0.1 us)
Async XLA Ops:
  13.6 1.4 %collective-permute-start.1 = (f32[192,128]{1,0:T(8,128)S(1)}, f32[192,128]{1,0:T(8,128)S(1)}, u32[]{:S(2)}, u32[]{:S(2)}) collective-permute-start(f32[192,128]{1,0:T(8,128)S(1)} %get-tuple-element.23), channel_id=1, source_target_pairs={{0,8},{8,0},{16,24},{24,16},{1,9},{9,1},{17,25},{25,17},{2,10},{10... | collective-permute-start | bytes 294920 | tf_op jit(solution)/shard_map/ppermute | solution.py:868
  13.7 5.4 %collective-permute-start = (f32[72,128]{1,0:T(8,128)S(1)}, f32[72,128]{1,0:T(8,128)S(1)}, u32[]{:S(2)}, u32[]{:S(2)}) collective-permute-start(f32[72,128]{1,0:T(8,128)S(1)} %get-tuple-element.19.here_ref), channel_id=1, source_target_pairs={{0,4},{1,5},{2,6},{3,7},{4,0},{5,1},{6,2},{7,3},{8,12},{9,13},{10,... | collective-permute-start | bytes 110600 | tf_op jit(solution)/shard_map/ppermute | solution.py:873
  15.0 5.0 %collective-permute-start.2 = (f32[64,128]{1,0:T(8,128)S(1)}, f32[64,128]{1,0:T(8,128)S(1)}, u32[]{:S(2)}, u32[]{:S(2)}) collective-permute-start(f32[64,128]{1,0:T(8,128)S(1)} %get-tuple-element.26.here_side_ref), channel_id=1, source_target_pairs={{0,4},{1,5},{2,6},{3,7},{4,0},{5,1},{6,2},{7,3},{8,12},{9,13},{10,... | collective-permute-start | bytes 98312 | tf_op jit(solution)/shard_map/ppermute | solution.py:873

commit v20 on v19

--- a/solution.py
+++ b/solution.py
@@ -800,16 +800,19 @@
         spread_ref[n] = table_ref[own_block, 2 * PAIRS + n]
 
 
-def join_kernel(
-    here_ref, there_ref, here_side_ref, there_side_ref, known_ref, spread_ref, out_ref
-):
+def plane_of(ref, row):
+    return ref[pl.ds(row, ROWS), :]
+
+
+def correction_of(first_var, ref):
+    pairs = [both(first_var, plane_of(ref, CORRECTION_ROW + n * ROWS)) for n in range(2)]
+    return [pairs[0][0], pairs[0][1], pairs[1][0], pairs[1][1]]
+
+
+def middle_kernel(here_ref, there_ref, here_side_ref, side_ref, other_ref, matrix_ref):
     mirrored = lax.axis_index("cell") // (lax.axis_size("cell") // 2)
     sign = (1 - 2 * mirrored).astype(jnp.float32)
     first_var, _, _ = plane_masks()
-
-    def plane_of(ref, row):
-        return ref[pl.ds(row, ROWS), :]
-
     line = LineCells(first_var, sign)
     for cell in range(6):
         ref, at = (here_ref, cell) if cell < 3 else (there_ref, 5 - cell)
@@ -817,22 +820,38 @@
         velocity_x, _, pressure, sound = primitives(first_var, planes)
         line.add(cell, planes, velocity_x, pressure, sound)
     faces = {cell: line.face(cell) for cell in (1, 2, 3)}
-
-    def correction_of(ref):
-        pairs = [both(first_var, plane_of(ref, CORRECTION_ROW + n * ROWS)) for n in range(2)]
-        return [pairs[0][0], pairs[0][1], pairs[1][0], pairs[1][1]]
-
-    here_side = [plane_of(here_side_ref, n * ROWS) for n in range(2 * PAIRS)]
-    there_side = [plane_of(there_side_ref, n * ROWS) for n in range(2 * PAIRS)]
-    side = [here_side[k] - faces[1][k] for k in range(PAIRS)]
-    side += [here_side[PAIRS + k] + (faces[1][k] - faces[2][k]) for k in range(PAIRS)]
-    other = [there_side[PAIRS + k] + (faces[2][k] - faces[3][k]) for k in range(PAIRS)]
-    other += [there_side[k] + faces[3][k] for k in range(PAIRS)]
+    for k in range(PAIRS):
+        side_ref[k] = plane_of(here_side_ref, k * ROWS) - faces[1][k]
+        side_ref[PAIRS + k] = plane_of(here_side_ref, (PAIRS + k) * ROWS) + (
+            faces[1][k] - faces[2][k]
+        )
+        other_ref[k] = faces[2][k] - faces[3][k]
+        other_ref[PAIRS + k] = faces[3][k]
     no_rates = (None, None)
-    diag = difference(line.diagonal(1, no_rates), correction_of(here_side_ref))
-    other_diag = difference(line.diagonal(3, no_rates), correction_of(there_side_ref)[::-1])
-    factor = two_by_two(line.above(1), inverse_of(other_diag))
-    diag = less(diag, two_by_two(factor, line.below(3)))
+    diag = difference(line.diagonal(1, no_rates), correction_of(first_var, here_side_ref))
+    above, below = line.above(1), line.below(3)
+    kept = [*diag, *line.diagonal(3, no_rates), above[0], *above[2:], *below[:2], below[3]]
+    for n, plane in enumerate(kept):
+        matrix_ref[n] = plane
+
+
+def join_kernel(
+    side_ref, other_ref, matrix_ref, there_side_ref, known_ref, spread_ref, out_ref
+):
+    mirrored = lax.axis_index("cell") // (lax.axis_size("cell") // 2)
+    first_var, _, _ = plane_masks()
+    kept = [matrix_ref[n] for n in range(14)]
+    diag, other_diag = kept[:4], kept[4:8]
+    above, below = (kept[8], None, kept[9], kept[10]), (kept[11], kept[12], None, kept[13])
+    other_diag = difference(other_diag, correction_of(first_var, there_side_ref)[::-1])
+    other = []
+    for member in range(2):
+        for k in range(PAIRS):
+            there = plane_of(there_side_ref, ((1 - member) * PAIRS + k) * ROWS)
+            other.append(there + other_ref[member * PAIRS + k])
+    factor = two_by_two(above, inverse_of(other_diag))
+    diag = less(diag, two_by_two(factor, below))
+    side = [side_ref[n] for n in range(2 * PAIRS)]
     middle = apply_matrix(inverse_of(diag), difference(side, apply_matrix(factor, other)))
     moved = apply_matrix([spread_ref[n] for n in range(4)], middle)
     results = [known_ref[n] + moved[n] for n in range(2 * PAIRS)]
@@ -952,13 +971,25 @@
         compiler_params=params,
         cost_estimate=beside,
     )(shared, eliminated, sides)
+    side, other, matrices = pl.pallas_call(
+        middle_kernel,
+        out_shape=(
+            float_shape(2 * PAIRS, *plane),
+            float_shape(2 * PAIRS, *plane),
+            float_shape(14, *plane),
+        ),
+        in_specs=[vmem] * 3,
+        out_specs=(vmem,) * 3,
+        compiler_params=params,
+        cost_estimate=beside,
+    )(here, there, here_side)
     return pl.pallas_call(
         join_kernel,
         out_shape=float_shape(*state.shape),
         in_specs=[vmem] * 6,
         out_specs=vmem,
         compiler_params=params,
-    )(here, there, here_side, there_side, known, spread)
+    )(side, other, matrices, there_side, known, spread)
 
 
 def solution(mesh):

time: 21 us -> 20.9 us (level)
  no operation moved by 1% of the time
where the time goes in v20:
time: 20.9 us; the launch traced here: 20.7 us
  blocking collectives  12.8 us (61%)
  starting transfers between devices  3.06 us (15%)
  waiting for transfers between devices  2.85 us (14%)
  Pallas kernels  2 us (10%)
    all_to_all x1, blocking collectives, share_half(): lax.all_to_all(copies, ('inst', 'cell'), split_axis=0, concat_axis=0, til...  12.8 us
    ppermute x2, starting transfers between devices, swap_halves(): lax.ppermute(block, 'cell', [(i, (i + count // 2) % count) for i in range...  2.99 us
    ppermute x2, waiting for transfers between devices, swap_halves(): lax.ppermute(block, 'cell', [(i, (i + count // 2) % count) for i in range...  2.77 us
    pallas_call x1, Pallas kernels, local_by_halves(): pl.pallas_call(pack_kernel, out_shape=(float_shape(places * blocks, BLOCK...  0.82 us
    pallas_call x1, Pallas kernels, local_by_halves(): pl.pallas_call(join_kernel, out_shape=float_shape(*state.shape), in_specs...  0.66 us
  transfers between devices with their start and end apart: 3, of which 3 were waited for; matrix products, arithmetic and copies ran while one was open for 0% of the time, Pallas kernels for 2%

profile of v20, /device:TPU:0, one launch (start us, length us, event | category | flops | bytes accessed | tf_op | source)
XLA Modules:
  0.0 20.7 jit_solution(15881180245571599260)
XLA Ops:
  0.0 0.8 %shard_map.46 = (f32[8,56,128]{2,1,0:T(8,128)S(1)}, s32[256]{0:T(256)S(1)}, s32[2,8]{1,0:T(2,128)S(1)}) custom-call(f32[2,6,2,256]{3,2,1,0:T(2,128)} %held_state_ref.1, f32[2,256]{1,0:T(2,128)} %held_rate_ref.1, s32[256]{0:T(256)} %held_next_ref.1, s32[2,8]{1,0:T(2,128)} %held_codes_ref.1), custom_call_target="tpu_custom_call" | custom-call | tf_op jit(solution)/shard_map/pallas_call | solution.py:910
  0.8 12.8 %all_to_all.5 = f32[8,56,128]{2,1,0:T(8,128)S(1)} all-to-all(f32[8,56,128]{2,1,0:T(8,128)S(1)} %get-tuple-element.21), channel_id=1, replica_groups={{0,1,2,3,16,17,18,19},{7,6,5,4,23,22,21,20},{8,9,10,11,24,25,26,27},{15..., dimensions={0} | all-to-all | bytes 458752 | tf_op jit(solution)/shard_map/all_to_all | solution.py:879
  13.6 0.1 collective-permute-start.1
  13.7 0.9 %collective-permute-start = (f32[72,128]{1,0:T(8,128)S(1)}, f32[72,128]{1,0:T(8,128)S(1)}, u32[]{:S(2)}, u32[]{:S(2)}) collective-permute-start(f32[72,128]{1,0:T(8,128)S(1)} %get-tuple-element.22.here_ref), channel_id=1, source_target_pairs={{0,4},{1,5},{2,6},{3,7},{4,0},{5,1},{6,2},{7,3},{8,12},{9,13},{10,... | collective-permute-start | bytes 110600 | tf_op jit(solution)/shard_map/ppermute | solution.py:892
  14.6 0.4 %shard_map.48 = (f32[8,3,8,128]{3,2,1,0:T(8,128)S(1)}, f32[3,4,8,128]{3,2,1,0:T(8,128)S(1)}, f32[3,7,8,128]{3,2,1,0:T(8,128)S(1)}, f32[16,128]{1,0:T(8,128)S(1)}) custom-call(f32[2,4,56,128]{3,2,1,0:T(8,128)S(1)} %bitcast.2, s32[256]{0:T(256)S(1)} %get-tuple-element.23.next_ref, s32[2,8]{1,0:T(2,128)S(1)} %get-tuple-element.24.codes_ref), custom_call_target="tpu_custom_call" | custom-call | flops 1000000 | bytes 1000000 | tf_op jit(solution)/shard_map/pallas_call | solution.py:940
  14.9 0.1 collective-permute-done.1.time_ref
  15.0 2.1 %collective-permute-start.2 = (f32[64,128]{1,0:T(8,128)S(1)}, f32[64,128]{1,0:T(8,128)S(1)}, u32[]{:S(2)}, u32[]{:S(2)}) collective-permute-start(f32[64,128]{1,0:T(8,128)S(1)} %get-tuple-element.29.here_side_ref), channel_id=1, source_target_pairs={{0,4},{1,5},{2,6},{3,7},{4,0},{5,1},{6,2},{7,3},{8,12},{9,13},{10,... | collective-permute-start | bytes 98312 | tf_op jit(solution)/shard_map/ppermute | solution.py:892
  17.2 1.9 %collective-permute-done.there_ref = f32[72,128]{1,0:T(8,128)S(1)} collective-permute-done((f32[72,128]{1,0:T(8,128)S(1)}, f32[72,128]{1,0:T(8,128)S(1)}, u32[]{:S(2)}, u32[]{:S(2)}) %collective-permute-start) | collective-permute-done | bytes 36896 | tf_op jit(solution)/shard_map/ppermute | solution.py:892
  19.1 0.1 shard_map.50
  19.2 0.9 %collective-permute-done.2.there_side_ref = f32[64,128]{1,0:T(8,128)S(1)} collective-permute-done((f32[64,128]{1,0:T(8,128)S(1)}, f32[64,128]{1,0:T(8,128)S(1)}, u32[]{:S(2)}, u32[]{:S(2)}) %collective-permute-start.2) | collective-permute-done | bytes 32800 | tf_op jit(solution)/shard_map/ppermute | solution.py:892
  20.1 0.7 %shard_map.52 = f32[2,6,2,256]{3,2,1,0:T(2,128)} custom-call(f32[6,8,128]{2,1,0:T(8,128)S(1)} %get-tuple-element.30.side_ref, f32[6,8,128]{2,1,0:T(8,128)S(1)} %get-tuple-element.31.other_ref, f32[14,8,128]{2,1,0:T(8,128)S(1)} %get-tuple-element.32.matrix_ref, f32[64,128]{1,0:T(8,128)S(1)} %collective-permute-done.2.there_side_ref, ...), custom_call_target="tpu_custom_call" | custom-call | tf_op jit(solution)/shard_map/pallas_call | solution.py:986
  (3 shorter events, 0.1 us)
Async XLA Ops:
  13.6 1.4 %collective-permute-start.1 = (f32[192,128]{1,0:T(8,128)S(1)}, f32[192,128]{1,0:T(8,128)S(1)}, u32[]{:S(2)}, u32[]{:S(2)}) collective-permute-start(f32[192,128]{1,0:T(8,128)S(1)} %get-tuple-element.26), channel_id=1, source_target_pairs={{0,8},{8,0},{16,24},{24,16},{1,9},{9,1},{17,25},{25,17},{2,10},{10... | collective-permute-start | bytes 294920 | tf_op jit(solution)/shard_map/ppermute | solution.py:887
  13.7 5.4 %collective-permute-start = (f32[72,128]{1,0:T(8,128)S(1)}, f32[72,128]{1,0:T(8,128)S(1)}, u32[]{:S(2)}, u32[]{:S(2)}) collective-permute-start(f32[72,128]{1,0:T(8,128)S(1)} %get-tuple-element.22.here_ref), channel_id=1, source_target_pairs={{0,4},{1,5},{2,6},{3,7},{4,0},{5,1},{6,2},{7,3},{8,12},{9,13},{10,... | collective-permute-start | bytes 110600 | tf_op jit(solution)/shard_map/ppermute | solution.py:892
  15.0 5.0 %collective-permute-start.2 = (f32[64,128]{1,0:T(8,128)S(1)}, f32[64,128]{1,0:T(8,128)S(1)}, u32[]{:S(2)}, u32[]{:S(2)}) collective-permute-start(f32[64,128]{1,0:T(8,128)S(1)} %get-tuple-element.29.here_side_ref), channel_id=1, source_target_pairs={{0,4},{1,5},{2,6},{3,7},{4,0},{5,1},{6,2},{7,3},{8,12},{9,13},{10,... | collective-permute-start | bytes 98312 | tf_op jit(solution)/shard_map/ppermute | solution.py:892

commit v21 on v20

--- a/solution.py
+++ b/solution.py
@@ -339,9 +339,10 @@
 ROWS = 8
 PAIRS = 3
 CELL_ROWS = PAIRS * ROWS
-RATE_ROW = 2 * CELL_ROWS
+TILE = 4
+STATE_TILES = 2 * CELL_ROWS // TILE
+BLOCK_TILES = STATE_TILES + 1
 VMEM_BYTES = 8 * 2**20
-BLOCK_ROWS = RATE_ROW + ROWS
 
 MIDDLE_CELLS = 3
 CORRECTION_ROW = 2 * CELL_ROWS
@@ -406,30 +407,27 @@
         copy.wait()
     mirrored = lax.axis_index("cell") // (lax.axis_size("cell") // 2)
     for cell in range(2):
-        place = pl.multiple_of(jnp.bitwise_xor(cell, mirrored) * CELL_ROWS, ROWS)
-        for k in range(PAIRS):
-            rows = [
-                state_ref[inst, 2 * k + var, pl.ds(cell, 1), pl.ds(half * LANES, LANES)]
-                for var in range(2)
-                for inst in range(2)
-                for half in range(2)
-            ]
-            for row, values in enumerate(rows):
-                out_ref[0, pl.ds(place + (k * ROWS + row), 1), :] = values
+        place = jnp.bitwise_xor(cell, mirrored) * (CELL_ROWS // TILE)
+        for var in range(6):
+            for inst in range(2):
+                for half in range(2):
+                    row = rows_of(var, inst, half)
+                    out_ref[0, place + row // TILE, pl.ds(row % TILE, 1), :] = state_ref[
+                        inst, var, pl.ds(cell, 1), pl.ds(half * LANES, LANES)
+                    ]
     rates = [
         rate_ref[pl.ds(cell, 1), pl.ds(half * LANES, LANES)]
         for cell in range(2)
         for half in range(2)
     ]
     for row in range(4):
-        out_ref[0, pl.ds(RATE_ROW + row, 1), :] = jnp.where(
+        out_ref[0, STATE_TILES, pl.ds(row, 1), :] = jnp.where(
             mirrored == 0, rates[row], rates[row ^ 2]
         )
-    out_ref[0, pl.ds(RATE_ROW + 4, 4), :] = jnp.zeros((4, LANES), jnp.float32)
-    for row in range(0, BLOCK_ROWS, ROWS):
-        values = out_ref[0, pl.ds(row, ROWS), :]
+    for tile in range(BLOCK_TILES):
+        values = out_ref[0, tile]
         for copy in range(1, out_ref.shape[0]):
-            out_ref[copy, pl.ds(row, ROWS), :] = values
+            out_ref[copy, tile] = values
 
 
 def turn_insts(first_inst, plane):
@@ -444,8 +442,13 @@
     return offsets[(2 * shift) % NT], other
 
 
-def cell_rows(cell, k):
-    return pl.ds((cell % 2) * CELL_ROWS + k * ROWS, ROWS)
+def block_plane(ref, place, block, n):
+    tiles = ref[place, block, pl.ds(2 * n, 2), :, :]
+    return tiles.reshape(ROWS, LANES)
+
+
+def cell_plane(ref, place, cell, k):
+    return block_plane(ref, place, cell // 2, (cell % 2) * PAIRS + k)
 
 
 def partner_kernel(all_ref, out_ref, middle_ref):
@@ -459,11 +462,11 @@
     for cell in range(cells - MIDDLE_CELLS, cells):
         for k in range(PAIRS):
             row = (cell - (cells - MIDDLE_CELLS)) * CELL_ROWS + k * ROWS
-            middle_ref[pl.ds(row, ROWS), :] = all_ref[own_y, cell // 2, cell_rows(cell, k), :]
+            middle_ref[pl.ds(row, ROWS), :] = cell_plane(all_ref, own_y, cell, k)
     for cell in range(cells):
         for k in range(PAIRS):
-            here = all_ref[own_y, cell // 2, cell_rows(cell, k), :]
-            there = all_ref[1 - own_y, cell // 2, cell_rows(cell, k), :]
+            here = cell_plane(all_ref, own_y, cell, k)
+            there = cell_plane(all_ref, 1 - own_y, cell, k)
             out_ref[pl.ds(cell * CELL_ROWS + k * ROWS, ROWS), :] = (
                 near[0] * here
                 + away[0] * there
@@ -589,8 +592,8 @@
         return (self.far(cell + 1), None, self.near(cell + 1), self.far(cell + 2))
 
 
-def rates_at(ref, index, start, first_half):
-    rows = [ref[index + (pl.ds(start + k, 1), slice(None))] for k in range(4)]
+def rates_at(ref, place, block, first_half):
+    rows = [ref[place, block, STATE_TILES, pl.ds(k, 1), :] for k in range(4)]
     return [jnp.where(first_half, rows[2 * k], rows[2 * k + 1]) for k in range(2)]
 
 
@@ -643,7 +646,7 @@
     pick_prev = picker(prev_line)
 
     def loaded(cell, place=own_y):
-        return [all_ref[place, cell // 2, cell_rows(cell, k), :] for k in range(PAIRS)]
+        return [cell_plane(all_ref, place, cell, k) for k in range(PAIRS)]
 
     own_weights, away_weights = time_weights(first_inst, 0), time_weights(first_inst, 2)
 
@@ -720,7 +723,7 @@
         if cell >= 3 and cell % 2 == 1:
             at = cell - 3
             block = at // 2
-            rates = rates_at(all_ref, (own_y, block), RATE_ROW, first_half)
+            rates = rates_at(all_ref, own_y, block, first_half)
             diag = line.diagonal(at, rates)
             if block > 0:
                 factor = two_by_two(line.below(at), inverses[-1])
@@ -740,7 +743,7 @@
     for n in range(4):
         factor_ref[blocks - 2, n] = factor[n]
     correction = list(two_by_two(factor, aboves[-1]))
-    rates = rates_at(all_ref, (own_y, blocks - 1), RATE_ROW, first_half)
+    rates = rates_at(all_ref, own_y, blocks - 1, first_half)
     for member in range(2):
         centre = line.radius[last + member]
         correction[3 * member] = correction[3 * member] - rates[member] * centre
@@ -794,7 +797,7 @@
         for n, plane in enumerate(known + list(spread)):
             table_ref[block, n] = plane
     for n in range(2 * PAIRS):
-        base = all_ref[own_y, own_block, pl.ds(n * ROWS, ROWS), :]
+        base = block_plane(all_ref, own_y, own_block, n)
         known_ref[n] = base + table_ref[own_block, n]
     for n in range(4):
         spread_ref[n] = table_ref[own_block, 2 * PAIRS + n]
@@ -910,7 +913,7 @@
     packed, next_here, codes_here = pl.pallas_call(
         pack_kernel,
         out_shape=(
-            float_shape(places * blocks, BLOCK_ROWS, LANES),
+            float_shape(places * blocks, BLOCK_TILES, TILE, LANES),
             jax.ShapeDtypeStruct(line_next.shape, jnp.int32),
             jax.ShapeDtypeStruct(face_codes.shape, jnp.int32),
         ),
@@ -923,7 +926,7 @@
         ],
         compiler_params=params,
     )(*held)
-    shared = share_half(packed).reshape(places, blocks, BLOCK_ROWS, LANES)
+    shared = share_half(packed).reshape(places, blocks, BLOCK_TILES, TILE, LANES)
     for_partner, here = pl.pallas_call(
         partner_kernel,
         out_shape=(

time: 20.9 us -> 20.9 us (level)
  transfers between devices with their start and end apart: 3 -> 3, of which waited for: 3 -> 2; matrix products, arithmetic and copies ran while one was open for 0% -> 0% of each run, Pallas kernels for 2% -> 3%
where the time goes in v21:
time: 20.9 us; the launch traced here: 20.7 us
  blocking collectives  12.7 us (61%)
  starting transfers between devices  3.13 us (15%)
  waiting for transfers between devices  2.74 us (13%)
  Pallas kernels  2.13 us (10%)
    all_to_all x1, blocking collectives, share_half(): lax.all_to_all(copies, ('inst', 'cell'), split_axis=0, concat_axis=0, til...  12.7 us
    ppermute x2, starting transfers between devices, swap_halves(): lax.ppermute(block, 'cell', [(i, (i + count // 2) % count) for i in range...  3.06 us
    ppermute x2, waiting for transfers between devices, swap_halves(): lax.ppermute(block, 'cell', [(i, (i + count // 2) % count) for i in range...  2.73 us
    pallas_call x1, Pallas kernels, local_by_halves(): pl.pallas_call(pack_kernel, out_shape=(float_shape(places * blocks, BLOCK...  0.83 us
    pallas_call x1, Pallas kernels, local_by_halves(): pl.pallas_call(join_kernel, out_shape=float_shape(*state.shape), in_specs...  0.66 us
    pallas_call x1, Pallas kernels, local_by_halves(): pl.pallas_call(half_kernel, out_shape=(float_shape(cells, PAIRS, *plane),...  0.45 us
  transfers between devices with their start and end apart: 3, of which 2 were waited for; matrix products, arithmetic and copies ran while one was open for 0% of the time, Pallas kernels for 3%

profile of v21, /device:TPU:0, one launch (start us, length us, event | category | flops | bytes accessed | tf_op | source)
XLA Modules:
  0.0 20.7 jit_solution(12411632182144268781)
XLA Ops:
  0.0 0.8 %shard_map.46 = (f32[8,13,4,128]{3,2,1,0:T(4,128)S(1)}, s32[256]{0:T(256)S(1)}, s32[2,8]{1,0:T(2,128)S(1)}) custom-call(f32[2,6,2,256]{3,2,1,0:T(2,128)} %held_state_ref.1, f32[2,256]{1,0:T(2,128)} %held_rate_ref.1, s32[256]{0:T(256)} %held_next_ref.1, s32[2,8]{1,0:T(2,128)} %held_codes_ref.1), custom_call_target="tpu_custom_call" | custom-call | tf_op jit(solution)/shard_map/pallas_call | solution.py:913
  0.8 12.7 %all_to_all.5 = f32[8,13,4,128]{3,2,1,0:T(4,128)S(1)} all-to-all(f32[8,13,4,128]{3,2,1,0:T(4,128)S(1)} %get-tuple-element.21), channel_id=1, replica_groups={{0,1,2,3,16,17,18,19},{7,6,5,4,23,22,21,20},{8,9,10,11,24,25,26,27},{15..., dimensions={0} | all-to-all | bytes 425984 | tf_op jit(solution)/shard_map/all_to_all | solution.py:882
  13.5 0.1 shard_map.47
  13.6 0.1 collective-permute-start.1
  13.7 0.9 %collective-permute-start = (f32[72,128]{1,0:T(8,128)S(1)}, f32[72,128]{1,0:T(8,128)S(1)}, u32[]{:S(2)}, u32[]{:S(2)}) collective-permute-start(f32[72,128]{1,0:T(8,128)S(1)} %get-tuple-element.22.here_ref), channel_id=1, source_target_pairs={{0,4},{1,5},{2,6},{3,7},{4,0},{5,1},{6,2},{7,3},{8,12},{9,13},{10,... | collective-permute-start | bytes 110600 | tf_op jit(solution)/shard_map/ppermute | solution.py:895
  14.5 0.4 %shard_map.48 = (f32[8,3,8,128]{3,2,1,0:T(8,128)S(1)}, f32[3,4,8,128]{3,2,1,0:T(8,128)S(1)}, f32[3,7,8,128]{3,2,1,0:T(8,128)S(1)}, f32[16,128]{1,0:T(8,128)S(1)}) custom-call(f32[2,4,13,4,128]{4,3,2,1,0:T(4,128)S(1)} %bitcast.2, s32[256]{0:T(256)S(1)} %get-tuple-element.23.next_ref, s32[2,8]{1,0:T(2,128)S(1)} %get-tuple-element.24.codes_ref), custom_call_target="tpu_custom_call" | custom-call | flops 1000000 | bytes 1000000 | tf_op jit(solution)/shard_map/pallas_call | solution.py:943
  15.0 0.0 collective-permute-done.1.time_ref
  15.0 2.2 %collective-permute-start.2 = (f32[64,128]{1,0:T(8,128)S(1)}, f32[64,128]{1,0:T(8,128)S(1)}, u32[]{:S(2)}, u32[]{:S(2)}) collective-permute-start(f32[64,128]{1,0:T(8,128)S(1)} %get-tuple-element.29.here_side_ref), channel_id=1, source_target_pairs={{0,4},{1,5},{2,6},{3,7},{4,0},{5,1},{6,2},{7,3},{8,12},{9,13},{10,... | collective-permute-start | bytes 98312 | tf_op jit(solution)/shard_map/ppermute | solution.py:895
  17.3 1.8 %collective-permute-done.there_ref = f32[72,128]{1,0:T(8,128)S(1)} collective-permute-done((f32[72,128]{1,0:T(8,128)S(1)}, f32[72,128]{1,0:T(8,128)S(1)}, u32[]{:S(2)}, u32[]{:S(2)}) %collective-permute-start) | collective-permute-done | bytes 36896 | tf_op jit(solution)/shard_map/ppermute | solution.py:895
  19.1 0.1 shard_map.50
  19.2 0.9 %collective-permute-done.2.there_side_ref = f32[64,128]{1,0:T(8,128)S(1)} collective-permute-done((f32[64,128]{1,0:T(8,128)S(1)}, f32[64,128]{1,0:T(8,128)S(1)}, u32[]{:S(2)}, u32[]{:S(2)}) %collective-permute-start.2) | collective-permute-done | bytes 32800 | tf_op jit(solution)/shard_map/ppermute | solution.py:895
  20.1 0.7 %shard_map.52 = f32[2,6,2,256]{3,2,1,0:T(2,128)} custom-call(f32[6,8,128]{2,1,0:T(8,128)S(1)} %get-tuple-element.30.side_ref, f32[6,8,128]{2,1,0:T(8,128)S(1)} %get-tuple-element.31.other_ref, f32[14,8,128]{2,1,0:T(8,128)S(1)} %get-tuple-element.32.matrix_ref, f32[64,128]{1,0:T(8,128)S(1)} %collective-permute-done.2.there_side_ref, ...), custom_call_target="tpu_custom_call" | custom-call | tf_op jit(solution)/shard_map/pallas_call | solution.py:989
  (2 shorter events, 0.1 us)
Async XLA Ops:
  13.6 1.4 %collective-permute-start.1 = (f32[192,128]{1,0:T(8,128)S(1)}, f32[192,128]{1,0:T(8,128)S(1)}, u32[]{:S(2)}, u32[]{:S(2)}) collective-permute-start(f32[192,128]{1,0:T(8,128)S(1)} %get-tuple-element.26), channel_id=1, source_target_pairs={{0,8},{8,0},{16,24},{24,16},{1,9},{9,1},{17,25},{25,17},{2,10},{10... | collective-permute-start | bytes 294920 | tf_op jit(solution)/shard_map/ppermute | solution.py:890
  13.7 5.4 %collective-permute-start = (f32[72,128]{1,0:T(8,128)S(1)}, f32[72,128]{1,0:T(8,128)S(1)}, u32[]{:S(2)}, u32[]{:S(2)}) collective-permute-start(f32[72,128]{1,0:T(8,128)S(1)} %get-tuple-element.22.here_ref), channel_id=1, source_target_pairs={{0,4},{1,5},{2,6},{3,7},{4,0},{5,1},{6,2},{7,3},{8,12},{9,13},{10,... | collective-permute-start | bytes 110600 | tf_op jit(solution)/shard_map/ppermute | solution.py:895
  15.0 5.0 %collective-permute-start.2 = (f32[64,128]{1,0:T(8,128)S(1)}, f32[64,128]{1,0:T(8,128)S(1)}, u32[]{:S(2)}, u32[]{:S(2)}) collective-permute-start(f32[64,128]{1,0:T(8,128)S(1)} %get-tuple-element.29.here_side_ref), channel_id=1, source_target_pairs={{0,4},{1,5},{2,6},{3,7},{4,0},{5,1},{6,2},{7,3},{8,12},{9,13},{10,... | collective-permute-start | bytes 98312 | tf_op jit(solution)/shard_map/ppermute | solution.py:895

commit v22 on v20

--- a/solution.py
+++ b/solution.py
@@ -444,8 +444,12 @@
     return offsets[(2 * shift) % NT], other
 
 
-def cell_rows(cell, k):
-    return pl.ds((cell % 2) * CELL_ROWS + k * ROWS, ROWS)
+def at_block(ref, y, block):
+    return ref.at[ref.shape[0] - 1 - y, ref.shape[1] - 1 - block]
+
+
+def cell_plane(ref, y, cell, k):
+    return at_block(ref, y, cell // 2)[pl.ds((cell % 2) * CELL_ROWS + k * ROWS, ROWS), :]
 
 
 def partner_kernel(all_ref, out_ref, middle_ref):
@@ -459,11 +463,11 @@
     for cell in range(cells - MIDDLE_CELLS, cells):
         for k in range(PAIRS):
             row = (cell - (cells - MIDDLE_CELLS)) * CELL_ROWS + k * ROWS
-            middle_ref[pl.ds(row, ROWS), :] = all_ref[own_y, cell // 2, cell_rows(cell, k), :]
+            middle_ref[pl.ds(row, ROWS), :] = cell_plane(all_ref, own_y, cell, k)
     for cell in range(cells):
         for k in range(PAIRS):
-            here = all_ref[own_y, cell // 2, cell_rows(cell, k), :]
-            there = all_ref[1 - own_y, cell // 2, cell_rows(cell, k), :]
+            here = cell_plane(all_ref, own_y, cell, k)
+            there = cell_plane(all_ref, 1 - own_y, cell, k)
             out_ref[pl.ds(cell * CELL_ROWS + k * ROWS, ROWS), :] = (
                 near[0] * here
                 + away[0] * there
@@ -589,8 +593,8 @@
         return (self.far(cell + 1), None, self.near(cell + 1), self.far(cell + 2))
 
 
-def rates_at(ref, index, start, first_half):
-    rows = [ref[index + (pl.ds(start + k, 1), slice(None))] for k in range(4)]
+def rates_at(ref, y, block, first_half):
+    rows = [at_block(ref, y, block)[pl.ds(RATE_ROW + k, 1), :] for k in range(4)]
     return [jnp.where(first_half, rows[2 * k], rows[2 * k + 1]) for k in range(2)]
 
 
@@ -642,8 +646,8 @@
     pick_next = picker(next_line)
     pick_prev = picker(prev_line)
 
-    def loaded(cell, place=own_y):
-        return [all_ref[place, cell // 2, cell_rows(cell, k), :] for k in range(PAIRS)]
+    def loaded(cell, y=own_y):
+        return [cell_plane(all_ref, y, cell, k) for k in range(PAIRS)]
 
     own_weights, away_weights = time_weights(first_inst, 0), time_weights(first_inst, 2)
 
@@ -720,7 +724,7 @@
         if cell >= 3 and cell % 2 == 1:
             at = cell - 3
             block = at // 2
-            rates = rates_at(all_ref, (own_y, block), RATE_ROW, first_half)
+            rates = rates_at(all_ref, own_y, block, first_half)
             diag = line.diagonal(at, rates)
             if block > 0:
                 factor = two_by_two(line.below(at), inverses[-1])
@@ -740,7 +744,7 @@
     for n in range(4):
         factor_ref[blocks - 2, n] = factor[n]
     correction = list(two_by_two(factor, aboves[-1]))
-    rates = rates_at(all_ref, (own_y, blocks - 1), RATE_ROW, first_half)
+    rates = rates_at(all_ref, own_y, blocks - 1, first_half)
     for member in range(2):
         centre = line.radius[last + member]
         correction[3 * member] = correction[3 * member] - rates[member] * centre
@@ -794,7 +798,7 @@
         for n, plane in enumerate(known + list(spread)):
             table_ref[block, n] = plane
     for n in range(2 * PAIRS):
-        base = all_ref[own_y, own_block, pl.ds(n * ROWS, ROWS), :]
+        base = at_block(all_ref, own_y, own_block)[pl.ds(n * ROWS, ROWS), :]
         known_ref[n] = base + table_ref[own_block, n]
     for n in range(4):
         spread_ref[n] = table_ref[own_block, 2 * PAIRS + n]
@@ -870,9 +874,9 @@
 
 def share_half(copies):
     insts, count = lax.axis_size("inst"), lax.axis_size("cell")
-    halves = [range(count // 2), range(count - 1, count // 2 - 1, -1)]
+    halves = [range(count // 2 - 1, -1, -1), range(count // 2, count)]
     groups = [
-        [inst * count + cell for inst in range(core, insts, 2) for cell in half]
+        [inst * count + cell for inst in range(insts - 2 + core, -1, -2) for cell in half]
         for core in range(2)
         for half in halves
     ]

time: 20.9 us -> 22 us (1.053)
  blocking collectives: 12.8 us -> 10.9 us
  starting transfers between devices: 3.06 us -> 4.59 us
  waiting for transfers between devices: 2.85 us -> 4.2 us
    all_to_all x1, blocking collectives: 12.8 us -> 10.9 us  [share_half(): lax.all_to_all(copies, ('inst', 'cell'), split_axis=0, concat_axis=0, til...]
    ppermute x2, starting transfers between devices: 2.99 us -> 4.52 us  [swap_halves(): lax.ppermute(block, 'cell', [(i, (i + count // 2) % count) for i in range...]
    ppermute x2, waiting for transfers between devices: 2.77 us -> 4.2 us  [swap_halves(): lax.ppermute(block, 'cell', [(i, (i + count // 2) % count) for i in range...]
  transfers between devices with their start and end apart: 3 -> 3, of which waited for: 3 -> 2; matrix products, arithmetic and copies ran while one was open for 0% -> 0% of each run, Pallas kernels for 2% -> 2%
where the time goes in v22:
time: 22 us; the launch traced here: 21.8 us
  blocking collectives  10.9 us (50%)
  starting transfers between devices  4.59 us (21%)
  waiting for transfers between devices  4.2 us (19%)
  Pallas kernels  2 us (9%)
    all_to_all x1, blocking collectives, share_half(): lax.all_to_all(copies, ('inst', 'cell'), split_axis=0, concat_axis=0, til...  10.9 us
    ppermute x2, starting transfers between devices, swap_halves(): lax.ppermute(block, 'cell', [(i, (i + count // 2) % count) for i in range...  4.52 us
    ppermute x2, waiting for transfers between devices, swap_halves(): lax.ppermute(block, 'cell', [(i, (i + count // 2) % count) for i in range...  4.2 us
    pallas_call x1, Pallas kernels, local_by_halves(): pl.pallas_call(pack_kernel, out_shape=(float_shape(places * blocks, BLOCK...  0.82 us
    pallas_call x1, Pallas kernels, local_by_halves(): pl.pallas_call(join_kernel, out_shape=float_shape(*state.shape), in_specs...  0.66 us
  transfers between devices with their start and end apart: 3, of which 2 were waited for; matrix products, arithmetic and copies ran while one was open for 0% of the time, Pallas kernels for 2%

profile of v22, /device:TPU:0, one launch (start us, length us, event | category | flops | bytes accessed | tf_op | source)
XLA Modules:
  0.0 21.8 jit_solution(1630456074920526199)
XLA Ops:
  0.0 0.8 %shard_map.46 = (f32[8,56,128]{2,1,0:T(8,128)S(1)}, s32[256]{0:T(256)S(1)}, s32[2,8]{1,0:T(2,128)S(1)}) custom-call(f32[2,6,2,256]{3,2,1,0:T(2,128)} %held_state_ref.1, f32[2,256]{1,0:T(2,128)} %held_rate_ref.1, s32[256]{0:T(256)} %held_next_ref.1, s32[2,8]{1,0:T(2,128)} %held_codes_ref.1), custom_call_target="tpu_custom_call" | custom-call | tf_op jit(solution)/shard_map/pallas_call | solution.py:914
  0.8 10.9 %all_to_all.5 = f32[8,56,128]{2,1,0:T(8,128)S(1)} all-to-all(f32[8,56,128]{2,1,0:T(8,128)S(1)} %get-tuple-element.21), channel_id=1, replica_groups={{19,18,17,16,3,2,1,0},{20,21,22,23,4,5,6,7},{27,26,25,24,11,10,9,8},{28..., dimensions={0} | all-to-all | bytes 458752 | tf_op jit(solution)/shard_map/all_to_all | solution.py:883
  11.8 0.1 collective-permute-start.1
  11.9 3.6 %collective-permute-start = (f32[72,128]{1,0:T(8,128)S(1)}, f32[72,128]{1,0:T(8,128)S(1)}, u32[]{:S(2)}, u32[]{:S(2)}) collective-permute-start(f32[72,128]{1,0:T(8,128)S(1)} %get-tuple-element.22.here_ref), channel_id=1, source_target_pairs={{0,4},{1,5},{2,6},{3,7},{4,0},{5,1},{6,2},{7,3},{8,12},{9,13},{10,... | collective-permute-start | bytes 110600 | tf_op jit(solution)/shard_map/ppermute | solution.py:896
  15.5 0.3 %shard_map.48 = (f32[8,3,8,128]{3,2,1,0:T(8,128)S(1)}, f32[3,4,8,128]{3,2,1,0:T(8,128)S(1)}, f32[3,7,8,128]{3,2,1,0:T(8,128)S(1)}, f32[16,128]{1,0:T(8,128)S(1)}) custom-call(f32[2,4,56,128]{3,2,1,0:T(8,128)S(1)} %bitcast.2, s32[256]{0:T(256)S(1)} %get-tuple-element.23.next_ref, s32[2,8]{1,0:T(2,128)S(1)} %get-tuple-element.24.codes_ref), custom_call_target="tpu_custom_call" | custom-call | flops 1000000 | bytes 1000000 | tf_op jit(solution)/shard_map/pallas_call | solution.py:944
  15.8 0.0 collective-permute-done.1.time_ref
  15.9 0.9 %collective-permute-start.2 = (f32[64,128]{1,0:T(8,128)S(1)}, f32[64,128]{1,0:T(8,128)S(1)}, u32[]{:S(2)}, u32[]{:S(2)}) collective-permute-start(f32[64,128]{1,0:T(8,128)S(1)} %get-tuple-element.29.here_side_ref), channel_id=1, source_target_pairs={{0,4},{1,5},{2,6},{3,7},{4,0},{5,1},{6,2},{7,3},{8,12},{9,13},{10,... | collective-permute-start | bytes 98312 | tf_op jit(solution)/shard_map/ppermute | solution.py:896
  16.8 1.5 %collective-permute-done.there_ref = f32[72,128]{1,0:T(8,128)S(1)} collective-permute-done((f32[72,128]{1,0:T(8,128)S(1)}, f32[72,128]{1,0:T(8,128)S(1)}, u32[]{:S(2)}, u32[]{:S(2)}) %collective-permute-start) | collective-permute-done | bytes 36896 | tf_op jit(solution)/shard_map/ppermute | solution.py:896
  18.3 0.1 shard_map.50
  18.4 2.7 %collective-permute-done.2.there_side_ref = f32[64,128]{1,0:T(8,128)S(1)} collective-permute-done((f32[64,128]{1,0:T(8,128)S(1)}, f32[64,128]{1,0:T(8,128)S(1)}, u32[]{:S(2)}, u32[]{:S(2)}) %collective-permute-start.2) | collective-permute-done | bytes 32800 | tf_op jit(solution)/shard_map/ppermute | solution.py:896
  21.1 0.7 %shard_map.52 = f32[2,6,2,256]{3,2,1,0:T(2,128)} custom-call(f32[6,8,128]{2,1,0:T(8,128)S(1)} %get-tuple-element.30.side_ref, f32[6,8,128]{2,1,0:T(8,128)S(1)} %get-tuple-element.31.other_ref, f32[14,8,128]{2,1,0:T(8,128)S(1)} %get-tuple-element.32.matrix_ref, f32[64,128]{1,0:T(8,128)S(1)} %collective-permute-done.2.there_side_ref, ...), custom_call_target="tpu_custom_call" | custom-call | tf_op jit(solution)/shard_map/pallas_call | solution.py:990
  (3 shorter events, 0.1 us)
Async XLA Ops:
  11.8 4.0 %collective-permute-start.1 = (f32[192,128]{1,0:T(8,128)S(1)}, f32[192,128]{1,0:T(8,128)S(1)}, u32[]{:S(2)}, u32[]{:S(2)}) collective-permute-start(f32[192,128]{1,0:T(8,128)S(1)} %get-tuple-element.26), channel_id=1, source_target_pairs={{0,8},{8,0},{16,24},{24,16},{1,9},{9,1},{17,25},{25,17},{2,10},{10... | collective-permute-start | bytes 294920 | tf_op jit(solution)/shard_map/ppermute | solution.py:891
  11.9 6.5 %collective-permute-start = (f32[72,128]{1,0:T(8,128)S(1)}, f32[72,128]{1,0:T(8,128)S(1)}, u32[]{:S(2)}, u32[]{:S(2)}) collective-permute-start(f32[72,128]{1,0:T(8,128)S(1)} %get-tuple-element.22.here_ref), channel_id=1, source_target_pairs={{0,4},{1,5},{2,6},{3,7},{4,0},{5,1},{6,2},{7,3},{8,12},{9,13},{10,... | collective-permute-start | bytes 110600 | tf_op jit(solution)/shard_map/ppermute | solution.py:896
  15.9 5.2 %collective-permute-start.2 = (f32[64,128]{1,0:T(8,128)S(1)}, f32[64,128]{1,0:T(8,128)S(1)}, u32[]{:S(2)}, u32[]{:S(2)}) collective-permute-start(f32[64,128]{1,0:T(8,128)S(1)} %get-tuple-element.29.here_side_ref), channel_id=1, source_target_pairs={{0,4},{1,5},{2,6},{3,7},{4,0},{5,1},{6,2},{7,3},{8,12},{9,13},{10,... | collective-permute-start | bytes 98312 | tf_op jit(solution)/shard_map/ppermute | solution.py:896

commit v23 on v22

--- a/solution.py
+++ b/solution.py
@@ -445,7 +445,10 @@
 
 
 def at_block(ref, y, block):
-    return ref.at[ref.shape[0] - 1 - y, ref.shape[1] - 1 - block]
+    blocks = ref.shape[1]
+    mirrored = lax.axis_index("cell") // blocks
+    place = mirrored * block + (1 - mirrored) * (blocks - 1 - block)
+    return ref.at[ref.shape[0] - 1 - y, place]
 
 
 def cell_plane(ref, y, cell, k):
@@ -874,7 +877,7 @@
 
 def share_half(copies):
     insts, count = lax.axis_size("inst"), lax.axis_size("cell")
-    halves = [range(count // 2 - 1, -1, -1), range(count // 2, count)]
+    halves = [range(count // 2 - 1, -1, -1), range(count - 1, count // 2 - 1, -1)]
     groups = [
         [inst * count + cell for inst in range(insts - 2 + core, -1, -2) for cell in half]
         for core in range(2)

time: 22 us -> 20.8 us (0.945)
  starting transfers between devices: 4.59 us -> 3.65 us
  waiting for transfers between devices: 4.2 us -> 3.98 us
    ppermute x2, starting transfers between devices: 4.52 us -> 3.58 us  [swap_halves(): lax.ppermute(block, 'cell', [(i, (i + count // 2) % count) for i in range...]
where the time goes in v23:
time: 20.8 us; the launch traced here: 20.6 us
  blocking collectives  10.9 us (52%)
  waiting for transfers between devices  3.98 us (19%)
  starting transfers between devices  3.65 us (18%)
  Pallas kernels  2 us (10%)
    all_to_all x1, blocking collectives, share_half(): lax.all_to_all(copies, ('inst', 'cell'), split_axis=0, concat_axis=0, til...  10.9 us
    ppermute x2, waiting for transfers between devices, swap_halves(): lax.ppermute(block, 'cell', [(i, (i + count // 2) % count) for i in range...  3.98 us
    ppermute x2, starting transfers between devices, swap_halves(): lax.ppermute(block, 'cell', [(i, (i + count // 2) % count) for i in range...  3.58 us
    pallas_call x1, Pallas kernels, local_by_halves(): pl.pallas_call(pack_kernel, out_shape=(float_shape(places * blocks, BLOCK...  0.82 us
    pallas_call x1, Pallas kernels, local_by_halves(): pl.pallas_call(join_kernel, out_shape=float_shape(*state.shape), in_specs...  0.66 us
  transfers between devices with their start and end apart: 3, of which 2 were waited for; matrix products, arithmetic and copies ran while one was open for 0% of the time, Pallas kernels for 2%

profile of v23, /device:TPU:0, one launch (start us, length us, event | category | flops | bytes accessed | tf_op | source)
XLA Modules:
  0.0 20.6 jit_solution(6174798071166343467)
XLA Ops:
  0.0 0.8 %shard_map.46 = (f32[8,56,128]{2,1,0:T(8,128)S(1)}, s32[256]{0:T(256)S(1)}, s32[2,8]{1,0:T(2,128)S(1)}) custom-call(f32[2,6,2,256]{3,2,1,0:T(2,128)} %held_state_ref.1, f32[2,256]{1,0:T(2,128)} %held_rate_ref.1, s32[256]{0:T(256)} %held_next_ref.1, s32[2,8]{1,0:T(2,128)} %held_codes_ref.1), custom_call_target="tpu_custom_call" | custom-call | tf_op jit(solution)/shard_map/pallas_call | solution.py:917
  0.8 10.9 %all_to_all.5 = f32[8,56,128]{2,1,0:T(8,128)S(1)} all-to-all(f32[8,56,128]{2,1,0:T(8,128)S(1)} %get-tuple-element.21), channel_id=1, replica_groups={{19,18,17,16,3,2,1,0},{23,22,21,20,7,6,5,4},{27,26,25,24,11,10,9,8},{31..., dimensions={0} | all-to-all | bytes 458752 | tf_op jit(solution)/shard_map/all_to_all | solution.py:886
  11.8 0.1 collective-permute-start.1
  11.9 2.7 %collective-permute-start = (f32[72,128]{1,0:T(8,128)S(1)}, f32[72,128]{1,0:T(8,128)S(1)}, u32[]{:S(2)}, u32[]{:S(2)}) collective-permute-start(f32[72,128]{1,0:T(8,128)S(1)} %get-tuple-element.22.here_ref), channel_id=1, source_target_pairs={{0,4},{1,5},{2,6},{3,7},{4,0},{5,1},{6,2},{7,3},{8,12},{9,13},{10,... | collective-permute-start | bytes 110600 | tf_op jit(solution)/shard_map/ppermute | solution.py:899
  14.5 0.3 %shard_map.48 = (f32[8,3,8,128]{3,2,1,0:T(8,128)S(1)}, f32[3,4,8,128]{3,2,1,0:T(8,128)S(1)}, f32[3,7,8,128]{3,2,1,0:T(8,128)S(1)}, f32[16,128]{1,0:T(8,128)S(1)}) custom-call(f32[2,4,56,128]{3,2,1,0:T(8,128)S(1)} %bitcast.2, s32[256]{0:T(256)S(1)} %get-tuple-element.23.next_ref, s32[2,8]{1,0:T(2,128)S(1)} %get-tuple-element.24.codes_ref), custom_call_target="tpu_custom_call" | custom-call | flops 1000000 | bytes 1000000 | tf_op jit(solution)/shard_map/pallas_call | solution.py:947
  14.9 0.0 collective-permute-done.1.time_ref
  14.9 0.9 %collective-permute-start.2 = (f32[64,128]{1,0:T(8,128)S(1)}, f32[64,128]{1,0:T(8,128)S(1)}, u32[]{:S(2)}, u32[]{:S(2)}) collective-permute-start(f32[64,128]{1,0:T(8,128)S(1)} %get-tuple-element.29.here_side_ref), channel_id=1, source_target_pairs={{0,4},{1,5},{2,6},{3,7},{4,0},{5,1},{6,2},{7,3},{8,12},{9,13},{10,... | collective-permute-start | bytes 98312 | tf_op jit(solution)/shard_map/ppermute | solution.py:899
  15.9 1.7 %collective-permute-done.there_ref = f32[72,128]{1,0:T(8,128)S(1)} collective-permute-done((f32[72,128]{1,0:T(8,128)S(1)}, f32[72,128]{1,0:T(8,128)S(1)}, u32[]{:S(2)}, u32[]{:S(2)}) %collective-permute-start) | collective-permute-done | bytes 36896 | tf_op jit(solution)/shard_map/ppermute | solution.py:899
  17.6 0.1 shard_map.50
  17.7 2.3 %collective-permute-done.2.there_side_ref = f32[64,128]{1,0:T(8,128)S(1)} collective-permute-done((f32[64,128]{1,0:T(8,128)S(1)}, f32[64,128]{1,0:T(8,128)S(1)}, u32[]{:S(2)}, u32[]{:S(2)}) %collective-permute-start.2) | collective-permute-done | bytes 32800 | tf_op jit(solution)/shard_map/ppermute | solution.py:899
  19.9 0.7 %shard_map.52 = f32[2,6,2,256]{3,2,1,0:T(2,128)} custom-call(f32[6,8,128]{2,1,0:T(8,128)S(1)} %get-tuple-element.30.side_ref, f32[6,8,128]{2,1,0:T(8,128)S(1)} %get-tuple-element.31.other_ref, f32[14,8,128]{2,1,0:T(8,128)S(1)} %get-tuple-element.32.matrix_ref, f32[64,128]{1,0:T(8,128)S(1)} %collective-permute-done.2.there_side_ref, ...), custom_call_target="tpu_custom_call" | custom-call | tf_op jit(solution)/shard_map/pallas_call | solution.py:993
  (3 shorter events, 0.1 us)
Async XLA Ops:
  11.8 3.1 %collective-permute-start.1 = (f32[192,128]{1,0:T(8,128)S(1)}, f32[192,128]{1,0:T(8,128)S(1)}, u32[]{:S(2)}, u32[]{:S(2)}) collective-permute-start(f32[192,128]{1,0:T(8,128)S(1)} %get-tuple-element.26), channel_id=1, source_target_pairs={{0,8},{8,0},{16,24},{24,16},{1,9},{9,1},{17,25},{25,17},{2,10},{10... | collective-permute-start | bytes 294920 | tf_op jit(solution)/shard_map/ppermute | solution.py:894
  11.9 5.7 %collective-permute-start = (f32[72,128]{1,0:T(8,128)S(1)}, f32[72,128]{1,0:T(8,128)S(1)}, u32[]{:S(2)}, u32[]{:S(2)}) collective-permute-start(f32[72,128]{1,0:T(8,128)S(1)} %get-tuple-element.22.here_ref), channel_id=1, source_target_pairs={{0,4},{1,5},{2,6},{3,7},{4,0},{5,1},{6,2},{7,3},{8,12},{9,13},{10,... | collective-permute-start | bytes 110600 | tf_op jit(solution)/shard_map/ppermute | solution.py:899
  14.9 5.0 %collective-permute-start.2 = (f32[64,128]{1,0:T(8,128)S(1)}, f32[64,128]{1,0:T(8,128)S(1)}, u32[]{:S(2)}, u32[]{:S(2)}) collective-permute-start(f32[64,128]{1,0:T(8,128)S(1)} %get-tuple-element.29.here_side_ref), channel_id=1, source_target_pairs={{0,4},{1,5},{2,6},{3,7},{4,0},{5,1},{6,2},{7,3},{8,12},{9,13},{10,... | collective-permute-start | bytes 98312 | tf_op jit(solution)/shard_map/ppermute | solution.py:899

commit v24 on v17

--- a/solution.py
+++ b/solution.py
@@ -445,8 +445,15 @@
     return offsets[(2 * shift) % NT], other
 
 
-def cell_rows(cell, k):
-    return pl.ds((cell % 2) * CELL_ROWS + k * ROWS, ROWS)
+def at_block(ref, y, block):
+    blocks = ref.shape[1]
+    mirrored = lax.axis_index("cell") // blocks
+    place = mirrored * block + (1 - mirrored) * (blocks - 1 - block)
+    return ref.at[ref.shape[0] - 1 - y, place]
+
+
+def cell_plane(ref, y, cell, k):
+    return at_block(ref, y, cell // 2)[pl.ds((cell % 2) * CELL_ROWS + k * ROWS, ROWS), :]
 
 
 def partner_kernel(all_ref, out_ref):
@@ -458,8 +465,8 @@
     away = [jnp.where(core == 0, b, a) for a, b in zip(one, three)]
     for cell in range(2 * all_ref.shape[1]):
         for k in range(PAIRS):
-            here = all_ref[own_y, cell // 2, cell_rows(cell, k), :]
-            there = all_ref[1 - own_y, cell // 2, cell_rows(cell, k), :]
+            here = cell_plane(all_ref, own_y, cell, k)
+            there = cell_plane(all_ref, 1 - own_y, cell, k)
             out_ref[pl.ds(cell * CELL_ROWS + k * ROWS, ROWS), :] = (
                 near[0] * here
                 + away[0] * there
@@ -585,8 +592,8 @@
         return (self.far(cell + 1), None, self.near(cell + 1), self.far(cell + 2))
 
 
-def rates_at(ref, index, start, first_half):
-    rows = [ref[index + (pl.ds(start + k, 1), slice(None))] for k in range(4)]
+def rates_at(ref, y, block, first_half):
+    rows = [at_block(ref, y, block)[pl.ds(RATE_ROW + k, 1), :] for k in range(4)]
     return [jnp.where(first_half, rows[2 * k], rows[2 * k + 1]) for k in range(2)]
 
 
@@ -637,8 +644,8 @@
     pick_next = picker(next_line)
     pick_prev = picker(prev_line)
 
-    def loaded(cell, place=own_y):
-        return [all_ref[place, cell // 2, cell_rows(cell, k), :] for k in range(PAIRS)]
+    def loaded(cell, y=own_y):
+        return [cell_plane(all_ref, y, cell, k) for k in range(PAIRS)]
 
     own_weights, away_weights = time_weights(first_inst, 0), time_weights(first_inst, 2)
 
@@ -715,7 +722,7 @@
         if cell >= 3 and cell % 2 == 1:
             at = cell - 3
             block = at // 2
-            rates = rates_at(all_ref, (own_y, block), RATE_ROW, first_half)
+            rates = rates_at(all_ref, own_y, block, first_half)
             diag = line.diagonal(at, rates)
             if block > 0:
                 factor = two_by_two(line.below(at), inverses[-1])
@@ -735,7 +742,7 @@
     for n in range(4):
         factor_ref[blocks - 2, n] = factor[n]
     correction = list(two_by_two(factor, aboves[-1]))
-    rates = rates_at(all_ref, (own_y, blocks - 1), RATE_ROW, first_half)
+    rates = rates_at(all_ref, own_y, blocks - 1, first_half)
     for member in range(2):
         centre = line.radius[last + member]
         correction[3 * member] = correction[3 * member] - rates[member] * centre
@@ -795,7 +802,7 @@
         for n, plane in enumerate(known + list(spread)):
             table_ref[block, n] = plane
     for n in range(2 * PAIRS):
-        base = all_ref[own_y, own_block, pl.ds(n * ROWS, ROWS), :]
+        base = at_block(all_ref, own_y, own_block)[pl.ds(n * ROWS, ROWS), :]
         known_ref[n] = base + table_ref[own_block, n]
     for n in range(4):
         spread_ref[n] = table_ref[own_block, 2 * PAIRS + n]
@@ -850,9 +857,9 @@
 
 def share_half(copies):
     insts, count = lax.axis_size("inst"), lax.axis_size("cell")
-    halves = [range(count // 2), range(count - 1, count // 2 - 1, -1)]
+    halves = [range(count // 2 - 1, -1, -1), range(count - 1, count // 2 - 1, -1)]
     groups = [
-        [inst * count + cell for inst in range(core, insts, 2) for cell in half]
+        [inst * count + cell for inst in range(insts - 2 + core, -1, -2) for cell in half]
         for core in range(2)
         for half in halves
     ]

time: 22.3 us -> 20.8 us (0.933)
  blocking collectives: 12.8 us -> 10.9 us
  starting transfers between devices: 0.92 us -> 2.73 us
  waiting for transfers between devices: 6.43 us -> 4.94 us
    all_to_all x1, blocking collectives: 12.8 us -> 10.9 us  [share_half(): lax.all_to_all(copies, ('inst', 'cell'), split_axis=0, concat_axis=0, til...]
    ppermute x1, starting transfers between devices: 0.85 us -> 2.65 us  [swap_halves(): lax.ppermute(block, 'cell', [(i, (i + count // 2) % count) for i in range...]
    ppermute x1, waiting for transfers between devices: 5.5 us -> 4 us  [swap_halves(): lax.ppermute(block, 'cell', [(i, (i + count // 2) % count) for i in range...]
where the time goes in v24:
time: 20.8 us; the launch traced here: 20.6 us
  blocking collectives  10.9 us (52%)
  waiting for transfers between devices  4.94 us (24%)
  starting transfers between devices  2.73 us (13%)
  Pallas kernels  1.98 us (10%)
    all_to_all x1, blocking collectives, share_half(): lax.all_to_all(copies, ('inst', 'cell'), split_axis=0, concat_axis=0, til...  10.9 us
    ppermute x1, waiting for transfers between devices, swap_halves(): lax.ppermute(block, 'cell', [(i, (i + count // 2) % count) for i in range...  4 us
    ppermute x1, starting transfers between devices, swap_halves(): lax.ppermute(block, 'cell', [(i, (i + count // 2) % count) for i in range...  2.65 us
    ppermute x1, waiting for transfers between devices, swap_cores(): return lax.ppermute(block, 'inst', pairs)  0.94 us
    pallas_call x1, Pallas kernels, local_by_halves(): pl.pallas_call(pack_kernel, out_shape=(float_shape(places * blocks, BLOCK...  0.82 us
    pallas_call x1, Pallas kernels, local_by_halves(): pl.pallas_call(join_kernel, out_shape=float_shape(*state.shape), in_specs...  0.7 us
  transfers between devices with their start and end apart: 2, of which 2 were waited for; matrix products, arithmetic and copies ran while one was open for 0% of the time, Pallas kernels for 2%

profile of v24, /device:TPU:0, one launch (start us, length us, event | category | flops | bytes accessed | tf_op | source)
XLA Modules:
  0.0 20.6 jit_solution(15807248798228223051)
XLA Ops:
  0.0 0.8 %shard_map.46 = (f32[8,56,128]{2,1,0:T(8,128)S(1)}, s32[256]{0:T(256)S(1)}, s32[2,8]{1,0:T(2,128)S(1)}) custom-call(f32[2,6,2,256]{3,2,1,0:T(2,128)} %held_state_ref.1, f32[2,256]{1,0:T(2,128)} %held_rate_ref.1, s32[256]{0:T(256)} %held_next_ref.1, s32[2,8]{1,0:T(2,128)} %held_codes_ref.1), custom_call_target="tpu_custom_call" | custom-call | tf_op jit(solution)/shard_map/pallas_call | solution.py:897
  0.8 10.9 %all_to_all.5 = f32[8,56,128]{2,1,0:T(8,128)S(1)} all-to-all(f32[8,56,128]{2,1,0:T(8,128)S(1)} %get-tuple-element.16), channel_id=1, replica_groups={{19,18,17,16,3,2,1,0},{23,22,21,20,7,6,5,4},{27,26,25,24,11,10,9,8},{31..., dimensions={0} | all-to-all | bytes 458752 | tf_op jit(solution)/shard_map/all_to_all | solution.py:866
  11.8 0.1 collective-permute-start
  11.9 0.4 %shard_map.47 = (f32[8,3,8,128]{3,2,1,0:T(8,128)S(1)}, f32[3,4,8,128]{3,2,1,0:T(8,128)S(1)}, f32[3,7,8,128]{3,2,1,0:T(8,128)S(1)}, f32[88,128]{1,0:T(8,128)S(1)}) custom-call(f32[2,4,56,128]{3,2,1,0:T(8,128)S(1)} %bitcast.2, s32[256]{0:T(256)S(1)} %get-tuple-element.17.next_ref, s32[2,8]{1,0:T(2,128)S(1)} %get-tuple-element.18.codes_ref), custom_call_target="tpu_custom_call" | custom-call | flops 1000000 | bytes 1000000 | tf_op jit(solution)/shard_map/pallas_call | solution.py:923
  12.2 0.9 %collective-permute-done.time_ref = f32[192,128]{1,0:T(8,128)S(1)} collective-permute-done((f32[192,128]{1,0:T(8,128)S(1)}, f32[192,128]{1,0:T(8,128)S(1)}, u32[]{:S(2)}, u32[]{:S(2)}) %collective-permute-start) | collective-permute-done | bytes 98336 | tf_op jit(solution)/shard_map/ppermute | solution.py:874
  13.2 2.7 %collective-permute-start.1 = (f32[136,128]{1,0:T(8,128)S(1)}, f32[136,128]{1,0:T(8,128)S(1)}, u32[]{:S(2)}, u32[]{:S(2)}) collective-permute-start(f32[136,128]{1,0:T(8,128)S(1)} %get-tuple-element.22.here_ref), channel_id=1, source_target_pairs={{0,4},{1,5},{2,6},{3,7},{4,0},{5,1},{6,2},{7,3},{8,12},{9,13},{10,... | collective-permute-start | bytes 208904 | tf_op jit(solution)/shard_map/ppermute | solution.py:879
  15.9 4.0 %collective-permute-done.1.there_ref = f32[136,128]{1,0:T(8,128)S(1)} collective-permute-done((f32[136,128]{1,0:T(8,128)S(1)}, f32[136,128]{1,0:T(8,128)S(1)}, u32[]{:S(2)}, u32[]{:S(2)}) %collective-permute-start.1) | collective-permute-done | bytes 69664 | tf_op jit(solution)/shard_map/ppermute | solution.py:879
  19.9 0.7 %shard_map.51 = f32[2,6,2,256]{3,2,1,0:T(2,128)} custom-call(f32[136,128]{1,0:T(8,128)S(1)} %get-tuple-element.22.here_ref, f32[136,128]{1,0:T(8,128)S(1)} %collective-permute-done.1.there_ref, f32[6,8,128]{2,1,0:T(8,128)S(1)} %get-tuple-element.25.known_ref, f32[4,8,128]{2,1,0:T(8,128)S(1)} %get-tuple-element.26.spread_ref), custom_call_target="tpu_custom_call" | custom-call | tf_op jit(solution)/shard_map/pallas_call | solution.py:957
  (3 shorter events, 0.1 us)
Async XLA Ops:
  11.8 1.4 %collective-permute-start = (f32[192,128]{1,0:T(8,128)S(1)}, f32[192,128]{1,0:T(8,128)S(1)}, u32[]{:S(2)}, u32[]{:S(2)}) collective-permute-start(f32[192,128]{1,0:T(8,128)S(1)} %shard_map.48), channel_id=1, source_target_pairs={{0,8},{8,0},{16,24},{24,16},{1,9},{9,1},{17,25},{25,17},{2,10},{10... | collective-permute-start | bytes 294920 | tf_op jit(solution)/shard_map/ppermute | solution.py:874
  13.2 6.7 %collective-permute-start.1 = (f32[136,128]{1,0:T(8,128)S(1)}, f32[136,128]{1,0:T(8,128)S(1)}, u32[]{:S(2)}, u32[]{:S(2)}) collective-permute-start(f32[136,128]{1,0:T(8,128)S(1)} %get-tuple-element.22.here_ref), channel_id=1, source_target_pairs={{0,4},{1,5},{2,6},{3,7},{4,0},{5,1},{6,2},{7,3},{8,12},{9,13},{10,... | collective-permute-start | bytes 208904 | tf_op jit(solution)/shard_map/ppermute | solution.py:879

commit v25 on v23

--- a/solution.py
+++ b/solution.py
@@ -455,7 +455,7 @@
     return at_block(ref, y, cell // 2)[pl.ds((cell % 2) * CELL_ROWS + k * ROWS, ROWS), :]
 
 
-def partner_kernel(all_ref, out_ref, middle_ref):
+def partner_kernel(all_ref, out_ref):
     own_inst = lax.axis_index("inst")
     own_y, core = own_inst >> 1, own_inst & 1
     _, first_inst, _ = plane_masks()
@@ -463,10 +463,6 @@
     near = [jnp.where(core == 0, a, b) for a, b in zip(one, three)]
     away = [jnp.where(core == 0, b, a) for a, b in zip(one, three)]
     cells = 2 * all_ref.shape[1]
-    for cell in range(cells - MIDDLE_CELLS, cells):
-        for k in range(PAIRS):
-            row = (cell - (cells - MIDDLE_CELLS)) * CELL_ROWS + k * ROWS
-            middle_ref[pl.ds(row, ROWS), :] = cell_plane(all_ref, own_y, cell, k)
     for cell in range(cells):
         for k in range(PAIRS):
             here = cell_plane(all_ref, own_y, cell, k)
@@ -599,6 +595,35 @@
 def rates_at(ref, y, block, first_half):
     rows = [at_block(ref, y, block)[pl.ds(RATE_ROW + k, 1), :] for k in range(4)]
     return [jnp.where(first_half, rows[2 * k], rows[2 * k + 1]) for k in range(2)]
+
+
+def near_half_kernel(all_ref, next_ref, codes_ref, *refs):
+    *results, middle_ref, line_ref = refs
+    own_y = lax.axis_index("inst") >> 1
+    cells = 2 * all_ref.shape[1]
+    for cell in range(cells - MIDDLE_CELLS, cells):
+        for k in range(PAIRS):
+            row = (cell - (cells - MIDDLE_CELLS)) * CELL_ROWS + k * ROWS
+            middle_ref[pl.ds(row, ROWS), :] = cell_plane(all_ref, own_y, cell, k)
+
+    @pl.when(lax.axis_index("cell") < all_ref.shape[1])
+    def _():
+        half_kernel(all_ref, next_ref, codes_ref, *results, line_ref)
+
+
+def far_half_kernel(all_ref, next_ref, codes_ref, *refs):
+    *refs, line_ref = refs
+    given, results = refs[: len(refs) // 2], refs[len(refs) // 2 :]
+    far = lax.axis_index("cell") >= all_ref.shape[1]
+
+    @pl.when(far)
+    def _():
+        half_kernel(all_ref, next_ref, codes_ref, *results, line_ref)
+
+    @pl.when(jnp.logical_not(far))
+    def _():
+        for source, target in zip(given, results):
+            target[...] = source[...]
 
 
 def half_kernel(
@@ -931,33 +956,42 @@
         compiler_params=params,
     )(*held)
     shared = share_half(packed).reshape(places, blocks, BLOCK_ROWS, LANES)
-    for_partner, here = pl.pallas_call(
+    for_partner = pl.pallas_call(
         partner_kernel,
-        out_shape=(
-            float_shape(cells * CELL_ROWS, LANES),
-            float_shape(MIDDLE_CELLS * CELL_ROWS, LANES),
-        ),
+        out_shape=float_shape(cells * CELL_ROWS, LANES),
         in_specs=[vmem],
-        out_specs=(vmem, vmem),
+        out_specs=vmem,
         compiler_params=params,
     )(shared)
     from_partner = swap_cores(for_partner)
+    beside = pl.CostEstimate(flops=10**6, bytes_accessed=10**6, transcendentals=0)
+    kinds = (
+        float_shape(cells, PAIRS, *plane),
+        float_shape(blocks - 1, 4, *plane),
+        float_shape(blocks - 1, 7, *plane),
+        float_shape(2 * ROWS, LANES),
+    )
+    line_scratch = [pltpu.VMEM((cells, 3) + plane, jnp.float32)]
+    arguments = (shared, next_here, codes_here)
+    *near, here = pl.pallas_call(
+        near_half_kernel,
+        out_shape=kinds + (float_shape(MIDDLE_CELLS * CELL_ROWS, LANES),),
+        in_specs=[vmem] * 3,
+        out_specs=(vmem,) * 5,
+        scratch_shapes=line_scratch,
+        compiler_params=params,
+    )(*arguments)
     there = swap_halves(here)
-    beside = pl.CostEstimate(flops=10**6, bytes_accessed=10**6, transcendentals=0)
     partial, factors, eliminated, correction = pl.pallas_call(
-        half_kernel,
-        out_shape=(
-            float_shape(cells, PAIRS, *plane),
-            float_shape(blocks - 1, 4, *plane),
-            float_shape(blocks - 1, 7, *plane),
-            float_shape(2 * ROWS, LANES),
-        ),
-        in_specs=[vmem] * 3,
+        far_half_kernel,
+        out_shape=kinds,
+        in_specs=[vmem] * 7,
         out_specs=(vmem,) * 4,
-        scratch_shapes=[pltpu.VMEM((cells, 3) + plane, jnp.float32)],
+        scratch_shapes=line_scratch,
+        input_output_aliases={3 + n: n for n in range(4)},
         compiler_params=params,
         cost_estimate=beside,
-    )(shared, next_here, codes_here)
+    )(*arguments, *near)
     here_side, sides = pl.pallas_call(
         reduce_kernel,
         out_shape=(

time: 20.8 us -> 20.5 us (0.986)
  waiting for transfers between devices: 3.98 us -> 3.68 us
    ppermute x2, waiting for transfers between devices: 3.98 us -> 3.68 us  [swap_halves(): lax.ppermute(block, 'cell', [(i, (i + count // 2) % count) for i in range...]
    pallas_call x2 -> x3, Pallas kernels: 0.39 us -> 0.44 us  [the longest x1 0.37 us: local_by_halves(): pl.pallas_call(near_half_kernel, out_shape=kinds + (float_shape(MIDDLE_CE...]
  transfers between devices with their start and end apart: 3 -> 3, of which waited for: 2 -> 2; matrix products, arithmetic and copies ran while one was open for 0% -> 0% of each run, Pallas kernels for 2% -> 3%
where the time goes in v25:
time: 20.5 us; the launch traced here: 20.3 us
  blocking collectives  10.9 us (53%)
  waiting for transfers between devices  3.68 us (18%)
  starting transfers between devices  3.59 us (18%)
  Pallas kernels  2.05 us (10%)
    all_to_all x1, blocking collectives, share_half(): lax.all_to_all(copies, ('inst', 'cell'), split_axis=0, concat_axis=0, til...  10.9 us
    ppermute x2, waiting for transfers between devices, swap_halves(): lax.ppermute(block, 'cell', [(i, (i + count // 2) % count) for i in range...  3.68 us
    ppermute x2, starting transfers between devices, swap_halves(): lax.ppermute(block, 'cell', [(i, (i + count // 2) % count) for i in range...  3.52 us
    pallas_call x1, Pallas kernels, local_by_halves(): pl.pallas_call(pack_kernel, out_shape=(float_shape(places * blocks, BLOCK...  0.82 us
    pallas_call x1, Pallas kernels, local_by_halves(): pl.pallas_call(join_kernel, out_shape=float_shape(*state.shape), in_specs...  0.66 us
  transfers between devices with their start and end apart: 3, of which 2 were waited for; matrix products, arithmetic and copies ran while one was open for 0% of the time, Pallas kernels for 3%

profile of v25, /device:TPU:0, one launch (start us, length us, event | category | flops | bytes accessed | tf_op | source)
XLA Modules:
  0.0 20.3 jit_solution(5341865569360945025)
XLA Ops:
  0.0 0.8 %shard_map.46 = (f32[8,56,128]{2,1,0:T(8,128)S(1)}, s32[256]{0:T(256)S(1)}, s32[2,8]{1,0:T(2,128)S(1)}) custom-call(f32[2,6,2,256]{3,2,1,0:T(2,128)} %held_state_ref.1, f32[2,256]{1,0:T(2,128)} %held_rate_ref.1, s32[256]{0:T(256)} %held_next_ref.1, s32[2,8]{1,0:T(2,128)} %held_codes_ref.1), custom_call_target="tpu_custom_call" | custom-call | tf_op jit(solution)/shard_map/pallas_call | solution.py:942
  0.8 10.9 %all_to_all.5 = f32[8,56,128]{2,1,0:T(8,128)S(1)} all-to-all(f32[8,56,128]{2,1,0:T(8,128)S(1)} %get-tuple-element.24), channel_id=1, replica_groups={{19,18,17,16,3,2,1,0},{23,22,21,20,7,6,5,4},{27,26,25,24,11,10,9,8},{31..., dimensions={0} | all-to-all | bytes 458752 | tf_op jit(solution)/shard_map/all_to_all | solution.py:911
  11.8 0.1 collective-permute-start.1
  11.9 0.4 %shard_map.47 = (f32[8,3,8,128]{3,2,1,0:T(8,128)S(1)}, f32[3,4,8,128]{3,2,1,0:T(8,128)S(1)}, f32[3,7,8,128]{3,2,1,0:T(8,128)S(1)}, f32[16,128]{1,0:T(8,128)S(1)}, f32[72,128]{1,0:T(8,128)S(1)}) custom-call(f32[2,4,56,128]{3,2,1,0:T(8,128)S(1)} %bitcast.2, s32[256]{0:T(256)S(1)} %get-tuple-element.25.next_ref, s32[2,8]{1,0:T(2,128)S(1)} %get-tuple-element.26.codes_ref), custom_call_target="tpu_custom_call" | custom-call | tf_op jit(solution)/shard_map/pallas_call | solution.py:976
  12.3 2.3 %collective-permute-start = (f32[72,128]{1,0:T(8,128)S(1)}, f32[72,128]{1,0:T(8,128)S(1)}, u32[]{:S(2)}, u32[]{:S(2)}) collective-permute-start(f32[72,128]{1,0:T(8,128)S(1)} %get-tuple-element.27.here_ref), channel_id=1, source_target_pairs={{0,4},{1,5},{2,6},{3,7},{4,0},{5,1},{6,2},{7,3},{8,12},{9,13},{10,... | collective-permute-start | bytes 110600 | tf_op jit(solution)/shard_map/ppermute | solution.py:924
  14.6 0.0 collective-permute-done.1.time_ref
  14.6 1.2 %collective-permute-start.2 = (f32[64,128]{1,0:T(8,128)S(1)}, f32[64,128]{1,0:T(8,128)S(1)}, u32[]{:S(2)}, u32[]{:S(2)}) collective-permute-start(f32[64,128]{1,0:T(8,128)S(1)} %get-tuple-element.35.here_side_ref), channel_id=1, source_target_pairs={{0,4},{1,5},{2,6},{3,7},{4,0},{5,1},{6,2},{7,3},{8,12},{9,13},{10,... | collective-permute-start | bytes 98312 | tf_op jit(solution)/shard_map/ppermute | solution.py:924
  15.9 2.1 %collective-permute-done.there_ref = f32[72,128]{1,0:T(8,128)S(1)} collective-permute-done((f32[72,128]{1,0:T(8,128)S(1)}, f32[72,128]{1,0:T(8,128)S(1)}, u32[]{:S(2)}, u32[]{:S(2)}) %collective-permute-start) | collective-permute-done | bytes 36896 | tf_op jit(solution)/shard_map/ppermute | solution.py:924
  18.0 0.1 shard_map.51
  18.0 1.6 %collective-permute-done.2.there_side_ref = f32[64,128]{1,0:T(8,128)S(1)} collective-permute-done((f32[64,128]{1,0:T(8,128)S(1)}, f32[64,128]{1,0:T(8,128)S(1)}, u32[]{:S(2)}, u32[]{:S(2)}) %collective-permute-start.2) | collective-permute-done | bytes 32800 | tf_op jit(solution)/shard_map/ppermute | solution.py:924
  19.6 0.7 %shard_map.53 = f32[2,6,2,256]{3,2,1,0:T(2,128)} custom-call(f32[6,8,128]{2,1,0:T(8,128)S(1)} %get-tuple-element.36.side_ref, f32[6,8,128]{2,1,0:T(8,128)S(1)} %get-tuple-element.37.other_ref, f32[14,8,128]{2,1,0:T(8,128)S(1)} %get-tuple-element.38.matrix_ref, f32[64,128]{1,0:T(8,128)S(1)} %collective-permute-done.2.there_side_ref, ...), custom_call_target="tpu_custom_call" | custom-call | tf_op jit(solution)/shard_map/pallas_call | solution.py:1027
  (4 shorter events, 0.1 us)
Async XLA Ops:
  11.8 2.8 %collective-permute-start.1 = (f32[192,128]{1,0:T(8,128)S(1)}, f32[192,128]{1,0:T(8,128)S(1)}, u32[]{:S(2)}, u32[]{:S(2)}) collective-permute-start(f32[192,128]{1,0:T(8,128)S(1)} %shard_map.49), channel_id=1, source_target_pairs={{0,8},{8,0},{16,24},{24,16},{1,9},{9,1},{17,25},{25,17},{2,10},{10... | collective-permute-start | bytes 294920 | tf_op jit(solution)/shard_map/ppermute | solution.py:919
  12.3 5.7 %collective-permute-start = (f32[72,128]{1,0:T(8,128)S(1)}, f32[72,128]{1,0:T(8,128)S(1)}, u32[]{:S(2)}, u32[]{:S(2)}) collective-permute-start(f32[72,128]{1,0:T(8,128)S(1)} %get-tuple-element.27.here_ref), channel_id=1, source_target_pairs={{0,4},{1,5},{2,6},{3,7},{4,0},{5,1},{6,2},{7,3},{8,12},{9,13},{10,... | collective-permute-start | bytes 110600 | tf_op jit(solution)/shard_map/ppermute | solution.py:924
  14.6 5.0 %collective-permute-start.2 = (f32[64,128]{1,0:T(8,128)S(1)}, f32[64,128]{1,0:T(8,128)S(1)}, u32[]{:S(2)}, u32[]{:S(2)}) collective-permute-start(f32[64,128]{1,0:T(8,128)S(1)} %get-tuple-element.35.here_side_ref), channel_id=1, source_target_pairs={{0,4},{1,5},{2,6},{3,7},{4,0},{5,1},{6,2},{7,3},{8,12},{9,13},{10,... | collective-permute-start | bytes 98312 | tf_op jit(solution)/shard_map/ppermute | solution.py:924

commit v26 on v25

--- a/solution.py
+++ b/solution.py
@@ -444,33 +444,36 @@
     return offsets[(2 * shift) % NT], other
 
 
-def at_block(ref, y, block):
+def select_weights(core, first_inst, first_shift, second_shift):
+    first, second = time_weights(first_inst, first_shift), time_weights(first_inst, second_shift)
+    return [jnp.where(core == 0, a, b) for a, b in zip(first, second)]
+
+
+def at_block(ref, core, block):
     blocks = ref.shape[1]
     mirrored = lax.axis_index("cell") // blocks
     place = mirrored * block + (1 - mirrored) * (blocks - 1 - block)
-    return ref.at[ref.shape[0] - 1 - y, place]
-
-
-def cell_plane(ref, y, cell, k):
-    return at_block(ref, y, cell // 2)[pl.ds((cell % 2) * CELL_ROWS + k * ROWS, ROWS), :]
+    return ref.at[ref.shape[0] - 1 - core, place]
+
+
+def cell_plane(ref, core, cell, k):
+    return at_block(ref, core, cell // 2)[pl.ds((cell % 2) * CELL_ROWS + k * ROWS, ROWS), :]
 
 
 def partner_kernel(all_ref, out_ref):
-    own_inst = lax.axis_index("inst")
-    own_y, core = own_inst >> 1, own_inst & 1
+    core = lax.axis_index("inst") & 1
     _, first_inst, _ = plane_masks()
-    one, three = time_weights(first_inst, 1), time_weights(first_inst, 3)
-    near = [jnp.where(core == 0, a, b) for a, b in zip(one, three)]
-    away = [jnp.where(core == 0, b, a) for a, b in zip(one, three)]
+    own_weights = time_weights(first_inst, 2)
+    other_weights = select_weights(core, first_inst, 1, 3)
     cells = 2 * all_ref.shape[1]
     for cell in range(cells):
         for k in range(PAIRS):
-            here = cell_plane(all_ref, own_y, cell, k)
-            there = cell_plane(all_ref, 1 - own_y, cell, k)
+            own = cell_plane(all_ref, core, cell, k)
+            other = cell_plane(all_ref, 1 - core, cell, k)
             out_ref[pl.ds(cell * CELL_ROWS + k * ROWS, ROWS), :] = (
-                near[0] * here
-                + away[0] * there
-                + turn_insts(first_inst, near[1] * here + away[1] * there)
+                own_weights[0] * own
+                + other_weights[0] * other
+                + turn_insts(first_inst, own_weights[1] * own + other_weights[1] * other)
             )
 
 
@@ -592,19 +595,19 @@
         return (self.far(cell + 1), None, self.near(cell + 1), self.far(cell + 2))
 
 
-def rates_at(ref, y, block, first_half):
-    rows = [at_block(ref, y, block)[pl.ds(RATE_ROW + k, 1), :] for k in range(4)]
+def rates_at(ref, core, block, first_half):
+    rows = [at_block(ref, core, block)[pl.ds(RATE_ROW + k, 1), :] for k in range(4)]
     return [jnp.where(first_half, rows[2 * k], rows[2 * k + 1]) for k in range(2)]
 
 
 def near_half_kernel(all_ref, next_ref, codes_ref, *refs):
     *results, middle_ref, line_ref = refs
-    own_y = lax.axis_index("inst") >> 1
+    core = lax.axis_index("inst") & 1
     cells = 2 * all_ref.shape[1]
     for cell in range(cells - MIDDLE_CELLS, cells):
         for k in range(PAIRS):
             row = (cell - (cells - MIDDLE_CELLS)) * CELL_ROWS + k * ROWS
-            middle_ref[pl.ds(row, ROWS), :] = cell_plane(all_ref, own_y, cell, k)
+            middle_ref[pl.ds(row, ROWS), :] = cell_plane(all_ref, core, cell, k)
 
     @pl.when(lax.axis_index("cell") < all_ref.shape[1])
     def _():
@@ -630,7 +633,7 @@
     all_ref, next_ref, codes_ref, partial_ref, factor_ref, blocks_ref, correction_ref,
     line_ref,
 ):
-    own_y = lax.axis_index("inst") >> 1
+    core = lax.axis_index("inst") & 1
     blocks = all_ref.shape[1]
     cells = 2 * blocks
     mirrored = lax.axis_index("cell") // blocks
@@ -674,16 +677,17 @@
     pick_next = picker(next_line)
     pick_prev = picker(prev_line)
 
-    def loaded(cell, y=own_y):
-        return [cell_plane(all_ref, y, cell, k) for k in range(PAIRS)]
-
-    own_weights, away_weights = time_weights(first_inst, 0), time_weights(first_inst, 2)
-
-    def own_time_parts(planes, cell):
+    def loaded(cell, of_core=core):
+        return [cell_plane(all_ref, of_core, cell, k) for k in range(PAIRS)]
+
+    own_weights = time_weights(first_inst, 0)
+    other_weights = select_weights(core, first_inst, 3, 1)
+
+    def chip_time_parts(planes, cell):
         return [
-            away_weights[0] * away
-            + turn_insts(first_inst, own_weights[1] * own + away_weights[1] * away)
-            for own, away in zip(planes, loaded(cell, 1 - own_y))
+            other_weights[0] * other
+            + turn_insts(first_inst, own_weights[1] * own + other_weights[1] * other)
+            for own, other in zip(planes, loaded(cell, 1 - core))
         ]
 
     def flux_across(planes, velocity, pressure):
@@ -711,7 +715,7 @@
         velocity_x, velocity_y, pressure, sound = primitives(first_var, planes)
         line_ref[cell, 0], line_ref[cell, 1], line_ref[cell, 2] = velocity_x, pressure, sound
         faces_across = pitch_flux(planes, velocity_y, pressure, sound)
-        times = own_time_parts(planes, cell)
+        times = chip_time_parts(planes, cell)
         for k in range(PAIRS):
             partial_ref[cell, k] = -(times[k] + (faces_across[k] - pick_prev(faces_across[k])))
 
@@ -752,7 +756,7 @@
         if cell >= 3 and cell % 2 == 1:
             at = cell - 3
             block = at // 2
-            rates = rates_at(all_ref, own_y, block, first_half)
+            rates = rates_at(all_ref, core, block, first_half)
             diag = line.diagonal(at, rates)
             if block > 0:
                 factor = two_by_two(line.below(at), inverses[-1])
@@ -772,7 +776,7 @@
     for n in range(4):
         factor_ref[blocks - 2, n] = factor[n]
     correction = list(two_by_two(factor, aboves[-1]))
-    rates = rates_at(all_ref, own_y, blocks - 1, first_half)
+    rates = rates_at(all_ref, core, blocks - 1, first_half)
     for member in range(2):
         centre = line.radius[last + member]
         correction[3 * member] = correction[3 * member] - rates[member] * centre
@@ -805,7 +809,7 @@
 
 
 def spread_kernel(all_ref, blocks_ref, sides_ref, known_ref, spread_ref, table_ref):
-    own_y = lax.axis_index("inst") >> 1
+    core = lax.axis_index("inst") & 1
     blocks = all_ref.shape[1]
     own_cell = lax.axis_index("cell")
     own_block = jnp.where(own_cell < blocks, own_cell, 2 * blocks - 1 - own_cell)
@@ -826,7 +830,7 @@
         for n, plane in enumerate(known + list(spread)):
             table_ref[block, n] = plane
     for n in range(2 * PAIRS):
-        base = at_block(all_ref, own_y, own_block)[pl.ds(n * ROWS, ROWS), :]
+        base = at_block(all_ref, core, own_block)[pl.ds(n * ROWS, ROWS), :]
         known_ref[n] = base + table_ref[own_block, n]
     for n in range(4):
         spread_ref[n] = table_ref[own_block, 2 * PAIRS + n]
@@ -904,8 +908,8 @@
     insts, count = lax.axis_size("inst"), lax.axis_size("cell")
     halves = [range(count // 2 - 1, -1, -1), range(count - 1, count // 2 - 1, -1)]
     groups = [
-        [inst * count + cell for inst in range(insts - 2 + core, -1, -2) for cell in half]
-        for core in range(2)
+        [inst * count + cell for inst in (first + 1, first) for cell in half]
+        for first in range(0, insts, 2)
         for half in halves
     ]
     return lax.all_to_all(
@@ -914,8 +918,8 @@
     )
 
 
-def swap_cores(block):
-    pairs = [(inst, inst ^ 1) for inst in range(lax.axis_size("inst"))]
+def swap_sides(block):
+    pairs = [(inst, inst ^ 2) for inst in range(lax.axis_size("inst"))]
     return lax.ppermute(block, "inst", pairs)
 
 
@@ -963,7 +967,7 @@
         out_specs=vmem,
         compiler_params=params,
     )(shared)
-    from_partner = swap_cores(for_partner)
+    from_partner = swap_sides(for_partner)
     beside = pl.CostEstimate(flops=10**6, bytes_accessed=10**6, transcendentals=0)
     kinds = (
         float_shape(cells, PAIRS, *plane),

time: 20.5 us -> 21 us (1.024)
  starting transfers between devices: 3.59 us -> 6.48 us
  blocking collectives: 10.9 us -> 9.72 us
  waiting for transfers between devices: 3.68 us -> 2.58 us
    ppermute x2, waiting for transfers between devices: 3.68 us -> 2.11 us  [swap_halves(): lax.ppermute(block, 'cell', [(i, (i + count // 2) % count) for i in range...]
    ppermute x1, starting transfers between devices: 0.07 us -> 1.58 us  [swap_sides(): return lax.ppermute(block, 'inst', pairs)]
    ppermute x2, starting transfers between devices: 3.52 us -> 4.9 us  [swap_halves(): lax.ppermute(block, 'cell', [(i, (i + count // 2) % count) for i in range...]
    all_to_all x1, blocking collectives: 10.9 us -> 9.72 us  [share_half(): lax.all_to_all(copies, ('inst', 'cell'), split_axis=0, concat_axis=0, til...]
    ppermute x1, waiting for transfers between devices: 0.01 us -> 0.47 us  [swap_sides(): return lax.ppermute(block, 'inst', pairs)]
  transfers between devices with their start and end apart: 3 -> 3, of which waited for: 2 -> 2; matrix products, arithmetic and copies ran while one was open for 0% -> 0% of each run, Pallas kernels for 3% -> 2%
where the time goes in v26:
time: 21 us; the launch traced here: 20.8 us
  blocking collectives  9.72 us (46%)
  starting transfers between devices  6.48 us (31%)
  waiting for transfers between devices  2.58 us (12%)
  Pallas kernels  2.03 us (10%)
    all_to_all x1, blocking collectives, share_half(): lax.all_to_all(copies, ('inst', 'cell'), split_axis=0, concat_axis=0, til...  9.72 us
    ppermute x2, starting transfers between devices, swap_halves(): lax.ppermute(block, 'cell', [(i, (i + count // 2) % count) for i in range...  4.9 us
    ppermute x2, waiting for transfers between devices, swap_halves(): lax.ppermute(block, 'cell', [(i, (i + count // 2) % count) for i in range...  2.11 us
    ppermute x1, starting transfers between devices, swap_sides(): return lax.ppermute(block, 'inst', pairs)  1.58 us
    pallas_call x1, Pallas kernels, local_by_halves(): pl.pallas_call(pack_kernel, out_shape=(float_shape(places * blocks, BLOCK...  0.82 us
    pallas_call x1, Pallas kernels, local_by_halves(): pl.pallas_call(join_kernel, out_shape=float_shape(*state.shape), in_specs...  0.66 us
    ppermute x1, waiting for transfers between devices, swap_sides(): return lax.ppermute(block, 'inst', pairs)  0.47 us
  transfers between devices with their start and end apart: 3, of which 2 were waited for; matrix products, arithmetic and copies ran while one was open for 0% of the time, Pallas kernels for 2%

profile of v26, /device:TPU:0, one launch (start us, length us, event | category | flops | bytes accessed | tf_op | source)
XLA Modules:
  0.0 20.8 jit_solution(8375420068082042750)
XLA Ops:
  0.0 0.8 %shard_map.46 = (f32[8,56,128]{2,1,0:T(8,128)S(1)}, s32[256]{0:T(256)S(1)}, s32[2,8]{1,0:T(2,128)S(1)}) custom-call(f32[2,6,2,256]{3,2,1,0:T(2,128)} %held_state_ref.1, f32[2,256]{1,0:T(2,128)} %held_rate_ref.1, s32[256]{0:T(256)} %held_next_ref.1, s32[2,8]{1,0:T(2,128)} %held_codes_ref.1), custom_call_target="tpu_custom_call" | custom-call | tf_op jit(solution)/shard_map/pallas_call | solution.py:946
  0.8 9.7 %all_to_all.5 = f32[8,56,128]{2,1,0:T(8,128)S(1)} all-to-all(f32[8,56,128]{2,1,0:T(8,128)S(1)} %get-tuple-element.24), channel_id=1, replica_groups={{11,10,9,8,3,2,1,0},{15,14,13,12,7,6,5,4},{27,26,25,24,19,18,17,16},{31..., dimensions={0} | all-to-all | bytes 458752 | tf_op jit(solution)/shard_map/all_to_all | solution.py:915
  10.6 1.6 %collective-permute-start.1 = (f32[192,128]{1,0:T(8,128)S(1)}, f32[192,128]{1,0:T(8,128)S(1)}, u32[]{:S(2)}, u32[]{:S(2)}) collective-permute-start(f32[192,128]{1,0:T(8,128)S(1)} %shard_map.49), channel_id=1, source_target_pairs={{0,16},{8,24},{16,0},{24,8},{1,17},{9,25},{17,1},{25,9},{2,18},{10... | collective-permute-start | bytes 294920 | tf_op jit(solution)/shard_map/ppermute | solution.py:923
  12.2 0.4 %shard_map.47 = (f32[8,3,8,128]{3,2,1,0:T(8,128)S(1)}, f32[3,4,8,128]{3,2,1,0:T(8,128)S(1)}, f32[3,7,8,128]{3,2,1,0:T(8,128)S(1)}, f32[16,128]{1,0:T(8,128)S(1)}, f32[72,128]{1,0:T(8,128)S(1)}) custom-call(f32[2,4,56,128]{3,2,1,0:T(8,128)S(1)} %bitcast.2, s32[256]{0:T(256)S(1)} %get-tuple-element.25.next_ref, s32[2,8]{1,0:T(2,128)S(1)} %get-tuple-element.26.codes_ref), custom_call_target="tpu_custom_call" | custom-call | tf_op jit(solution)/shard_map/pallas_call | solution.py:980
  12.5 2.2 %collective-permute-start = (f32[72,128]{1,0:T(8,128)S(1)}, f32[72,128]{1,0:T(8,128)S(1)}, u32[]{:S(2)}, u32[]{:S(2)}) collective-permute-start(f32[72,128]{1,0:T(8,128)S(1)} %get-tuple-element.27.here_ref), channel_id=1, source_target_pairs={{0,4},{1,5},{2,6},{3,7},{4,0},{5,1},{6,2},{7,3},{8,12},{9,13},{10,... | collective-permute-start | bytes 110600 | tf_op jit(solution)/shard_map/ppermute | solution.py:928
  14.8 0.5 %collective-permute-done.1.time_ref = f32[192,128]{1,0:T(8,128)S(1)} collective-permute-done((f32[192,128]{1,0:T(8,128)S(1)}, f32[192,128]{1,0:T(8,128)S(1)}, u32[]{:S(2)}, u32[]{:S(2)}) %collective-permute-start.1) | collective-permute-done | bytes 98336 | tf_op jit(solution)/shard_map/ppermute | solution.py:923
  15.3 2.7 %collective-permute-start.2 = (f32[64,128]{1,0:T(8,128)S(1)}, f32[64,128]{1,0:T(8,128)S(1)}, u32[]{:S(2)}, u32[]{:S(2)}) collective-permute-start(f32[64,128]{1,0:T(8,128)S(1)} %get-tuple-element.35.here_side_ref), channel_id=1, source_target_pairs={{0,4},{1,5},{2,6},{3,7},{4,0},{5,1},{6,2},{7,3},{8,12},{9,13},{10,... | collective-permute-start | bytes 98312 | tf_op jit(solution)/shard_map/ppermute | solution.py:928
  18.0 0.0 collective-permute-done.there_ref
  18.0 0.1 shard_map.51
  18.1 2.1 %collective-permute-done.2.there_side_ref = f32[64,128]{1,0:T(8,128)S(1)} collective-permute-done((f32[64,128]{1,0:T(8,128)S(1)}, f32[64,128]{1,0:T(8,128)S(1)}, u32[]{:S(2)}, u32[]{:S(2)}) %collective-permute-start.2) | collective-permute-done | bytes 32800 | tf_op jit(solution)/shard_map/ppermute | solution.py:928
  20.2 0.7 %shard_map.53 = f32[2,6,2,256]{3,2,1,0:T(2,128)} custom-call(f32[6,8,128]{2,1,0:T(8,128)S(1)} %get-tuple-element.36.side_ref, f32[6,8,128]{2,1,0:T(8,128)S(1)} %get-tuple-element.37.other_ref, f32[14,8,128]{2,1,0:T(8,128)S(1)} %get-tuple-element.38.matrix_ref, f32[64,128]{1,0:T(8,128)S(1)} %collective-permute-done.2.there_side_ref, ...), custom_call_target="tpu_custom_call" | custom-call | tf_op jit(solution)/shard_map/pallas_call | solution.py:1031
  (4 shorter events, 0.1 us)
Async XLA Ops:
  10.6 4.7 %collective-permute-start.1 = (f32[192,128]{1,0:T(8,128)S(1)}, f32[192,128]{1,0:T(8,128)S(1)}, u32[]{:S(2)}, u32[]{:S(2)}) collective-permute-start(f32[192,128]{1,0:T(8,128)S(1)} %shard_map.49), channel_id=1, source_target_pairs={{0,16},{8,24},{16,0},{24,8},{1,17},{9,25},{17,1},{25,9},{2,18},{10... | collective-permute-start | bytes 294920 | tf_op jit(solution)/shard_map/ppermute | solution.py:923
  12.5 5.5 %collective-permute-start = (f32[72,128]{1,0:T(8,128)S(1)}, f32[72,128]{1,0:T(8,128)S(1)}, u32[]{:S(2)}, u32[]{:S(2)}) collective-permute-start(f32[72,128]{1,0:T(8,128)S(1)} %get-tuple-element.27.here_ref), channel_id=1, source_target_pairs={{0,4},{1,5},{2,6},{3,7},{4,0},{5,1},{6,2},{7,3},{8,12},{9,13},{10,... | collective-permute-start | bytes 110600 | tf_op jit(solution)/shard_map/ppermute | solution.py:928
  15.3 4.9 %collective-permute-start.2 = (f32[64,128]{1,0:T(8,128)S(1)}, f32[64,128]{1,0:T(8,128)S(1)}, u32[]{:S(2)}, u32[]{:S(2)}) collective-permute-start(f32[64,128]{1,0:T(8,128)S(1)} %get-tuple-element.35.here_side_ref), channel_id=1, source_target_pairs={{0,4},{1,5},{2,6},{3,7},{4,0},{5,1},{6,2},{7,3},{8,12},{9,13},{10,... | collective-permute-start | bytes 98312 | tf_op jit(solution)/shard_map/ppermute | solution.py:928

commit v27 on v25

--- a/solution.py
+++ b/solution.py
@@ -343,9 +343,11 @@
 VMEM_BYTES = 8 * 2**20
 BLOCK_ROWS = RATE_ROW + ROWS
 
-MIDDLE_CELLS = 3
+MIDDLE_CELLS = 2
+ROUND_CELLS = 4
 CORRECTION_ROW = 2 * CELL_ROWS
-SIDE_ROWS = CORRECTION_ROW + 2 * ROWS
+THIRD_ROW = CORRECTION_ROW + 2 * ROWS
+SIDE_ROWS = THIRD_ROW + CELL_ROWS
 
 
 def spectral_offsets():
@@ -598,13 +600,20 @@
 
 
 def near_half_kernel(all_ref, next_ref, codes_ref, *refs):
-    *results, middle_ref, line_ref = refs
+    *results, middle_ref, round_ref, third_ref, line_ref = refs
     own_y = lax.axis_index("inst") >> 1
     cells = 2 * all_ref.shape[1]
     for cell in range(cells - MIDDLE_CELLS, cells):
         for k in range(PAIRS):
             row = (cell - (cells - MIDDLE_CELLS)) * CELL_ROWS + k * ROWS
             middle_ref[pl.ds(row, ROWS), :] = cell_plane(all_ref, own_y, cell, k)
+    for cell in range(ROUND_CELLS):
+        for k in range(PAIRS):
+            plane = cell_plane(all_ref, own_y, cells - 1 - cell, k)
+            round_ref[pl.ds(cell * CELL_ROWS + k * ROWS, ROWS), :] = plane
+    for k in range(PAIRS):
+        third = cell_plane(all_ref, own_y, cells - MIDDLE_CELLS - 1, k)
+        third_ref[pl.ds(k * ROWS, ROWS), :] = third
 
     @pl.when(lax.axis_index("cell") < all_ref.shape[1])
     def _():
@@ -782,7 +791,12 @@
         )
 
 
-def reduce_kernel(partial_ref, time_ref, factor_ref, correction_ref, middle_ref, sides_ref):
+def reduce_kernel(
+    partial_ref, time_ref, factor_ref, correction_ref, here_ref, third_ref, middle_ref, sides_ref,
+    again_ref,
+):
+    again_ref[...] = here_ref[...]
+    middle_ref[pl.ds(THIRD_ROW, CELL_ROWS), :] = third_ref[...]
     for row in range(0, 2 * ROWS, ROWS):
         middle_ref[pl.ds(CORRECTION_ROW + row, ROWS), :] = correction_ref[pl.ds(row, ROWS), :]
     blocks = partial_ref.shape[0] // 2
@@ -841,14 +855,32 @@
     return [pairs[0][0], pairs[0][1], pairs[1][0], pairs[1][1]]
 
 
-def middle_kernel(here_ref, there_ref, here_side_ref, side_ref, other_ref, matrix_ref):
-    mirrored = lax.axis_index("cell") // (lax.axis_size("cell") // 2)
+def middle_kernel(
+    here_ref, first_ref, second_ref, here_side_ref, there_side_ref, side_ref, other_ref, matrix_ref
+):
+    own_cell, count = lax.axis_index("cell"), lax.axis_size("cell")
+    mirrored = own_cell // (count // 2)
+    outer = jnp.logical_or(own_cell < count // 4, own_cell >= count - count // 4)
     sign = (1 - 2 * mirrored).astype(jnp.float32)
     first_var, _, _ = plane_masks()
     line = LineCells(first_var, sign)
     for cell in range(6):
-        ref, at = (here_ref, cell) if cell < 3 else (there_ref, 5 - cell)
-        planes = [plane_of(ref, at * CELL_ROWS + k * ROWS) for k in range(PAIRS)]
+        at = cell if cell < 3 else 5 - cell
+        rows = [(at - 1) * CELL_ROWS + k * ROWS for k in range(PAIRS)]
+        if at == 0:
+            ref = here_side_ref if cell < 3 else there_side_ref
+            planes = [plane_of(ref, THIRD_ROW + k * ROWS) for k in range(PAIRS)]
+        elif cell < 3:
+            planes = [plane_of(here_ref, row) for row in rows]
+        else:
+            planes = [
+                jnp.where(
+                    outer,
+                    plane_of(first_ref, (2 - at) * CELL_ROWS + k * ROWS),
+                    plane_of(second_ref, row),
+                )
+                for k, row in enumerate(rows)
+            ]
         velocity_x, _, pressure, sound = primitives(first_var, planes)
         line.add(cell, planes, velocity_x, pressure, sound)
     faces = {cell: line.face(cell) for cell in (1, 2, 3)}
@@ -857,8 +889,10 @@
         side_ref[PAIRS + k] = plane_of(here_side_ref, (PAIRS + k) * ROWS) + (
             faces[1][k] - faces[2][k]
         )
-        other_ref[k] = faces[2][k] - faces[3][k]
-        other_ref[PAIRS + k] = faces[3][k]
+        other_ref[k] = plane_of(there_side_ref, (PAIRS + k) * ROWS) + (
+            faces[2][k] - faces[3][k]
+        )
+        other_ref[PAIRS + k] = plane_of(there_side_ref, k * ROWS) + faces[3][k]
     no_rates = (None, None)
     diag = difference(line.diagonal(1, no_rates), correction_of(first_var, here_side_ref))
     above, below = line.above(1), line.below(3)
@@ -876,11 +910,7 @@
     diag, other_diag = kept[:4], kept[4:8]
     above, below = (kept[8], None, kept[9], kept[10]), (kept[11], kept[12], None, kept[13])
     other_diag = difference(other_diag, correction_of(first_var, there_side_ref)[::-1])
-    other = []
-    for member in range(2):
-        for k in range(PAIRS):
-            there = plane_of(there_side_ref, ((1 - member) * PAIRS + k) * ROWS)
-            other.append(there + other_ref[member * PAIRS + k])
+    other = [other_ref[n] for n in range(2 * PAIRS)]
     factor = two_by_two(above, inverse_of(other_diag))
     diag = less(diag, two_by_two(factor, below))
     side = [side_ref[n] for n in range(2 * PAIRS)]
@@ -922,6 +952,16 @@
 def swap_halves(block):
     count = lax.axis_size("cell")
     return lax.ppermute(block, "cell", [(i, (i + count // 2) % count) for i in range(count)])
+
+
+def pass_round(block, back):
+    width = lax.axis_size("cell") // 4
+    steps = [(2, 0), (0, 1), (1, 3), (3, 2)]
+    pairs = [
+        (source * width + i, target * width + i) for source, target in steps for i in range(width)
+    ]
+    pairs = [(target, source) for source, target in pairs] if back else pairs
+    return lax.ppermute(block, "cell", pairs)
 
 
 def float_shape(*sizes):
@@ -973,15 +1013,20 @@
     )
     line_scratch = [pltpu.VMEM((cells, 3) + plane, jnp.float32)]
     arguments = (shared, next_here, codes_here)
-    *near, here = pl.pallas_call(
+    *near, here, for_round, third = pl.pallas_call(
         near_half_kernel,
-        out_shape=kinds + (float_shape(MIDDLE_CELLS * CELL_ROWS, LANES),),
+        out_shape=kinds
+        + (
+            float_shape(MIDDLE_CELLS * CELL_ROWS, LANES),
+            float_shape(ROUND_CELLS * CELL_ROWS, LANES),
+            float_shape(CELL_ROWS, LANES),
+        ),
         in_specs=[vmem] * 3,
-        out_specs=(vmem,) * 5,
+        out_specs=(vmem,) * 7,
         scratch_shapes=line_scratch,
         compiler_params=params,
     )(*arguments)
-    there = swap_halves(here)
+    there_first = pass_round(for_round, False)
     partial, factors, eliminated, correction = pl.pallas_call(
         far_half_kernel,
         out_shape=kinds,
@@ -992,17 +1037,19 @@
         compiler_params=params,
         cost_estimate=beside,
     )(*arguments, *near)
-    here_side, sides = pl.pallas_call(
+    here_side, sides, here_again = pl.pallas_call(
         reduce_kernel,
         out_shape=(
             float_shape(SIDE_ROWS, LANES),
             float_shape(blocks - 1, 2 * PAIRS, *plane),
+            float_shape(MIDDLE_CELLS * CELL_ROWS, LANES),
         ),
-        in_specs=[vmem] * 4,
-        out_specs=(vmem, vmem),
+        in_specs=[vmem] * 6,
+        out_specs=(vmem,) * 3,
         compiler_params=params,
-    )(partial, from_partner, factors, correction)
+    )(partial, from_partner, factors, correction, here, third)
     there_side = swap_halves(here_side)
+    there_second = pass_round(here_again, True)
     known, spread = pl.pallas_call(
         spread_kernel,
         out_shape=(float_shape(2 * PAIRS, *plane), float_shape(4, *plane)),
@@ -1019,11 +1066,10 @@
             float_shape(2 * PAIRS, *plane),
             float_shape(14, *plane),
         ),
-        in_specs=[vmem] * 3,
+        in_specs=[vmem] * 5,
         out_specs=(vmem,) * 3,
         compiler_params=params,
-        cost_estimate=beside,
-    )(here, there, here_side)
+    )(here, there_first, there_second, here_side, there_side)
     return pl.pallas_call(
         join_kernel,
         out_shape=float_shape(*state.shape),

time: 20.5 us -> 20.6 us (level)
  starting transfers between devices: 3.59 us -> 4.26 us
  waiting for transfers between devices: 3.68 us -> 3.12 us
    ppermute x2 -> x1, waiting for transfers between devices: 3.68 us -> 0.01 us  [swap_halves(): lax.ppermute(block, 'cell', [(i, (i + count // 2) % count) for i in range...]
    ppermute x0 -> x2, waiting for transfers between devices: none -> 3.12 us  [pass_round(): return lax.ppermute(block, 'cell', pairs)]
    ppermute x0 -> x2, starting transfers between devices: none -> 1.88 us  [pass_round(): return lax.ppermute(block, 'cell', pairs)]
    ppermute x2 -> x1, starting transfers between devices: 3.52 us -> 2.31 us  [swap_halves(): lax.ppermute(block, 'cell', [(i, (i + count // 2) % count) for i in range...]
  transfers between devices with their start and end apart: 3 -> 4, of which waited for: 2 -> 2; matrix products, arithmetic and copies ran while one was open for 0% -> 0% of each run, Pallas kernels for 3% -> 2%
where the time goes in v27:
time: 20.6 us; the launch traced here: 20.4 us
  blocking collectives  10.9 us (53%)
  starting transfers between devices  4.26 us (21%)
  waiting for transfers between devices  3.12 us (15%)
  Pallas kernels  2.05 us (10%)
    all_to_all x1, blocking collectives, share_half(): lax.all_to_all(copies, ('inst', 'cell'), split_axis=0, concat_axis=0, til...  10.9 us
    ppermute x2, waiting for transfers between devices, pass_round(): return lax.ppermute(block, 'cell', pairs)  3.12 us
    ppermute x1, starting transfers between devices, swap_halves(): lax.ppermute(block, 'cell', [(i, (i + count // 2) % count) for i in range...  2.31 us
    ppermute x2, starting transfers between devices, pass_round(): return lax.ppermute(block, 'cell', pairs)  1.88 us
    pallas_call x1, Pallas kernels, local_by_halves(): pl.pallas_call(pack_kernel, out_shape=(float_shape(places * blocks, BLOCK...  0.82 us
    pallas_call x1, Pallas kernels, local_by_halves(): pl.pallas_call(join_kernel, out_shape=float_shape(*state.shape), in_specs...  0.66 us
  transfers between devices with their start and end apart: 4, of which 2 were waited for; matrix products, arithmetic and copies ran while one was open for 0% of the time, Pallas kernels for 2%

profile of v27, /device:TPU:0, one launch (start us, length us, event | category | flops | bytes accessed | tf_op | source)
XLA Modules:
  0.0 20.4 jit_solution(458855507680738677)
XLA Ops:
  0.0 0.8 %shard_map.46 = (f32[8,56,128]{2,1,0:T(8,128)S(1)}, s32[256]{0:T(256)S(1)}, s32[2,8]{1,0:T(2,128)S(1)}) custom-call(f32[2,6,2,256]{3,2,1,0:T(2,128)} %held_state_ref.1, f32[2,256]{1,0:T(2,128)} %held_rate_ref.1, s32[256]{0:T(256)} %held_next_ref.1, s32[2,8]{1,0:T(2,128)} %held_codes_ref.1), custom_call_target="tpu_custom_call" | custom-call | tf_op jit(solution)/shard_map/pallas_call | solution.py:982
  0.8 10.9 %all_to_all.5 = f32[8,56,128]{2,1,0:T(8,128)S(1)} all-to-all(f32[8,56,128]{2,1,0:T(8,128)S(1)} %get-tuple-element.27), channel_id=1, replica_groups={{19,18,17,16,3,2,1,0},{23,22,21,20,7,6,5,4},{27,26,25,24,11,10,9,8},{31..., dimensions={0} | all-to-all | bytes 458752 | tf_op jit(solution)/shard_map/all_to_all | solution.py:941
  11.8 0.1 collective-permute-start.1
  11.9 0.4 %shard_map.47 = (f32[8,3,8,128]{3,2,1,0:T(8,128)S(1)}, f32[3,4,8,128]{3,2,1,0:T(8,128)S(1)}, f32[3,7,8,128]{3,2,1,0:T(8,128)S(1)}, f32[16,128]{1,0:T(8,128)S(1)}...) custom-call(f32[2,4,56,128]{3,2,1,0:T(8,128)S(1)} %bitcast.2, ...), custom_call_target="tpu_custom_call" | custom-call | tf_op jit(solution)/shard_map/pallas_call | solution.py:1016
  12.3 1.2 %collective-permute-start = (f32[96,128]{1,0:T(8,128)S(1)}, f32[96,128]{1,0:T(8,128)S(1)}, u32[]{:S(2)}, u32[]{:S(2)}) collective-permute-start(f32[96,128]{1,0:T(8,128)S(1)} %get-tuple-element.31), channel_id=1, source_target_pairs={{4,0},{5,1},{0,2},{1,3},{2,6},{3,7},{6,4},{7,5},{12,8},{13,9},{8,1... | collective-permute-start | bytes 147464 | tf_op jit(solution)/shard_map/ppermute | solution.py:964
  13.5 0.0 collective-permute-done.1.time_ref
  13.5 2.3 %collective-permute-start.3 = (f32[88,128]{1,0:T(8,128)S(1)}, f32[88,128]{1,0:T(8,128)S(1)}, u32[]{:S(2)}, u32[]{:S(2)}) collective-permute-start(f32[88,128]{1,0:T(8,128)S(1)} %get-tuple-element.41.here_side_ref), channel_id=1, source_target_pairs={{0,4},{1,5},{2,6},{3,7},{4,0},{5,1},{6,2},{7,3},{8,12},{9,13},{10,... | collective-permute-start | bytes 135176 | tf_op jit(solution)/shard_map/ppermute | solution.py:954
  15.9 0.7 %collective-permute-start.2 = (f32[48,128]{1,0:T(8,128)S(1)}, f32[48,128]{1,0:T(8,128)S(1)}, u32[]{:S(2)}, u32[]{:S(2)}) collective-permute-start(f32[48,128]{1,0:T(8,128)S(1)} %get-tuple-element.40), channel_id=1, source_target_pairs={{0,4},{1,5},{2,0},{3,1},{6,2},{7,3},{4,6},{5,7},{8,12},{9,13},{10,... | collective-permute-start | bytes 73736 | tf_op jit(solution)/shard_map/ppermute | solution.py:964
  16.6 0.9 %collective-permute-done.first_ref = f32[96,128]{1,0:T(8,128)S(1)} collective-permute-done((f32[96,128]{1,0:T(8,128)S(1)}, f32[96,128]{1,0:T(8,128)S(1)}, u32[]{:S(2)}, u32[]{:S(2)}) %collective-permute-start) | collective-permute-done | bytes 49184 | tf_op jit(solution)/shard_map/ppermute | solution.py:964
  17.4 2.2 %collective-permute-done.2.second_ref = f32[48,128]{1,0:T(8,128)S(1)} collective-permute-done((f32[48,128]{1,0:T(8,128)S(1)}, f32[48,128]{1,0:T(8,128)S(1)}, u32[]{:S(2)}, u32[]{:S(2)}) %collective-permute-start.2) | collective-permute-done | bytes 24608 | tf_op jit(solution)/shard_map/ppermute | solution.py:964
  19.7 0.0 collective-permute-done.3.there_side_ref
  19.7 0.1 shard_map.51
  19.8 0.7 %shard_map.53 = f32[2,6,2,256]{3,2,1,0:T(2,128)} custom-call(f32[6,8,128]{2,1,0:T(8,128)S(1)} %get-tuple-element.42.side_ref, f32[6,8,128]{2,1,0:T(8,128)S(1)} %get-tuple-element.43.other_ref, f32[14,8,128]{2,1,0:T(8,128)S(1)} %get-tuple-element.44.matrix_ref, f32[88,128]{1,0:T(8,128)S(1)} %collective-permute-done.3.there_side_ref, ...), custom_call_target="tpu_custom_call" | custom-call | tf_op jit(solution)/shard_map/pallas_call | solution.py:1073
  (4 shorter events, 0.1 us)
Async XLA Ops:
  11.8 1.7 %collective-permute-start.1 = (f32[192,128]{1,0:T(8,128)S(1)}, f32[192,128]{1,0:T(8,128)S(1)}, u32[]{:S(2)}, u32[]{:S(2)}) collective-permute-start(f32[192,128]{1,0:T(8,128)S(1)} %shard_map.49), channel_id=1, source_target_pairs={{0,8},{8,0},{16,24},{24,16},{1,9},{9,1},{17,25},{25,17},{2,10},{10... | collective-permute-start | bytes 294920 | tf_op jit(solution)/shard_map/ppermute | solution.py:949
  12.3 5.2 %collective-permute-start = (f32[96,128]{1,0:T(8,128)S(1)}, f32[96,128]{1,0:T(8,128)S(1)}, u32[]{:S(2)}, u32[]{:S(2)}) collective-permute-start(f32[96,128]{1,0:T(8,128)S(1)} %get-tuple-element.31), channel_id=1, source_target_pairs={{4,0},{5,1},{0,2},{1,3},{2,6},{3,7},{6,4},{7,5},{12,8},{13,9},{8,1... | collective-permute-start | bytes 147464 | tf_op jit(solution)/shard_map/ppermute | solution.py:964
  13.5 6.1 %collective-permute-start.3 = (f32[88,128]{1,0:T(8,128)S(1)}, f32[88,128]{1,0:T(8,128)S(1)}, u32[]{:S(2)}, u32[]{:S(2)}) collective-permute-start(f32[88,128]{1,0:T(8,128)S(1)} %get-tuple-element.41.here_side_ref), channel_id=1, source_target_pairs={{0,4},{1,5},{2,6},{3,7},{4,0},{5,1},{6,2},{7,3},{8,12},{9,13},{10,... | collective-permute-start | bytes 135176 | tf_op jit(solution)/shard_map/ppermute | solution.py:954
  15.9 3.8 %collective-permute-start.2 = (f32[48,128]{1,0:T(8,128)S(1)}, f32[48,128]{1,0:T(8,128)S(1)}, u32[]{:S(2)}, u32[]{:S(2)}) collective-permute-start(f32[48,128]{1,0:T(8,128)S(1)} %get-tuple-element.40), channel_id=1, source_target_pairs={{0,4},{1,5},{2,0},{3,1},{6,2},{7,3},{4,6},{5,7},{8,12},{9,13},{10,... | collective-permute-start | bytes 73736 | tf_op jit(solution)/shard_map/ppermute | solution.py:964

commit v28 on v27

--- a/solution.py
+++ b/solution.py
@@ -954,14 +954,16 @@
     return lax.ppermute(block, "cell", [(i, (i + count // 2) % count) for i in range(count)])
 
 
-def pass_round(block, back):
+def pass_round(block, steps):
     width = lax.axis_size("cell") // 4
-    steps = [(2, 0), (0, 1), (1, 3), (3, 2)]
     pairs = [
         (source * width + i, target * width + i) for source, target in steps for i in range(width)
     ]
-    pairs = [(target, source) for source, target in pairs] if back else pairs
     return lax.ppermute(block, "cell", pairs)
+
+
+FIRST_ROUND = ((2, 0), (0, 1), (1, 3), (3, 2))
+SECOND_ROUND = ((3, 1), (1, 2), (2, 3), (0, 0))
 
 
 def float_shape(*sizes):
@@ -1026,7 +1028,7 @@
         scratch_shapes=line_scratch,
         compiler_params=params,
     )(*arguments)
-    there_first = pass_round(for_round, False)
+    there_first = pass_round(for_round, FIRST_ROUND)
     partial, factors, eliminated, correction = pl.pallas_call(
         far_half_kernel,
         out_shape=kinds,
@@ -1049,7 +1051,7 @@
         compiler_params=params,
     )(partial, from_partner, factors, correction, here, third)
     there_side = swap_halves(here_side)
-    there_second = pass_round(here_again, True)
+    there_second = pass_round(here_again, SECOND_ROUND)
     known, spread = pl.pallas_call(
         spread_kernel,
         out_shape=(float_shape(2 * PAIRS, *plane), float_shape(4, *plane)),

time: 20.6 us -> 21.8 us (1.058)
  the two profiles are of different devices: /device:TPU:0 before, /device:TPU:10 now
where the time goes in v28:
time: 21.8 us; the launch traced here: 21.6 us
  blocking collectives  9.34 us (43%)
  starting transfers between devices  5.57 us (26%)
  waiting for transfers between devices  4.57 us (21%)
  Pallas kernels  2.05 us (9%)
    all_to_all x1, blocking collectives, share_half(): lax.all_to_all(copies, ('inst', 'cell'), split_axis=0, concat_axis=0, til...  9.34 us
    ppermute x2, waiting for transfers between devices, pass_round(): return lax.ppermute(block, 'cell', pairs)  4.56 us
    ppermute x2, starting transfers between devices, pass_round(): return lax.ppermute(block, 'cell', pairs)  4.29 us
    ppermute x1, starting transfers between devices, swap_halves(): lax.ppermute(block, 'cell', [(i, (i + count // 2) % count) for i in range...  1.22 us
    pallas_call x1, Pallas kernels, local_by_halves(): pl.pallas_call(pack_kernel, out_shape=(float_shape(places * blocks, BLOCK...  0.82 us
    pallas_call x1, Pallas kernels, local_by_halves(): pl.pallas_call(join_kernel, out_shape=float_shape(*state.shape), in_specs...  0.66 us
  transfers between devices with their start and end apart: 4, of which 1 were waited for; matrix products, arithmetic and copies ran while one was open for 0% of the time, Pallas kernels for 2%

profile of v28, /device:TPU:10, one launch (start us, length us, event | category | flops | bytes accessed | tf_op | source)
XLA Modules:
  0.0 21.6 jit_solution(14689071112926402840)
XLA Ops:
  0.0 0.8 %shard_map.46 = (f32[8,56,128]{2,1,0:T(8,128)S(1)}, s32[256]{0:T(256)S(1)}, s32[2,8]{1,0:T(2,128)S(1)}) custom-call(f32[2,6,2,256]{3,2,1,0:T(2,128)} %held_state_ref.1, f32[2,256]{1,0:T(2,128)} %held_rate_ref.1, s32[256]{0:T(256)} %held_next_ref.1, s32[2,8]{1,0:T(2,128)} %held_codes_ref.1), custom_call_target="tpu_custom_call" | custom-call | tf_op jit(solution)/shard_map/pallas_call | solution.py:984
  0.8 9.3 %all_to_all.5 = f32[8,56,128]{2,1,0:T(8,128)S(1)} all-to-all(f32[8,56,128]{2,1,0:T(8,128)S(1)} %get-tuple-element.27), channel_id=1, replica_groups={{19,18,17,16,3,2,1,0},{23,22,21,20,7,6,5,4},{27,26,25,24,11,10,9,8},{31..., dimensions={0} | all-to-all | bytes 458752 | tf_op jit(solution)/shard_map/all_to_all | solution.py:941
  10.2 0.1 collective-permute-start.1
  10.3 0.4 %shard_map.47 = (f32[8,3,8,128]{3,2,1,0:T(8,128)S(1)}, f32[3,4,8,128]{3,2,1,0:T(8,128)S(1)}, f32[3,7,8,128]{3,2,1,0:T(8,128)S(1)}, f32[16,128]{1,0:T(8,128)S(1)}...) custom-call(f32[2,4,56,128]{3,2,1,0:T(8,128)S(1)} %bitcast.2, ...), custom_call_target="tpu_custom_call" | custom-call | tf_op jit(solution)/shard_map/pallas_call | solution.py:1018
  10.7 2.3 %collective-permute-start = (f32[96,128]{1,0:T(8,128)S(1)}, f32[96,128]{1,0:T(8,128)S(1)}, u32[]{:S(2)}, u32[]{:S(2)}) collective-permute-start(f32[96,128]{1,0:T(8,128)S(1)} %get-tuple-element.31), channel_id=1, source_target_pairs={{4,0},{5,1},{0,2},{1,3},{2,6},{3,7},{6,4},{7,5},{12,8},{13,9},{8,1... | collective-permute-start | bytes 147464 | tf_op jit(solution)/shard_map/ppermute | solution.py:962
  13.0 0.0 collective-permute-done.1.time_ref
  13.0 1.2 %collective-permute-start.3 = (f32[88,128]{1,0:T(8,128)S(1)}, f32[88,128]{1,0:T(8,128)S(1)}, u32[]{:S(2)}, u32[]{:S(2)}) collective-permute-start(f32[88,128]{1,0:T(8,128)S(1)} %get-tuple-element.41.here_side_ref), channel_id=1, source_target_pairs={{0,4},{1,5},{2,6},{3,7},{4,0},{5,1},{6,2},{7,3},{8,12},{9,13},{10,... | collective-permute-start | bytes 135176 | tf_op jit(solution)/shard_map/ppermute | solution.py:954
  14.3 2.0 %collective-permute-start.2 = (f32[48,128]{1,0:T(8,128)S(1)}, f32[48,128]{1,0:T(8,128)S(1)}, u32[]{:S(2)}, u32[]{:S(2)}) collective-permute-start(f32[48,128]{1,0:T(8,128)S(1)} %get-tuple-element.40), channel_id=1, source_target_pairs={{6,2},{7,3},{2,4},{3,5},{4,6},{5,7},{0,0},{1,1},{14,10},{15,11},{1... | collective-permute-start | bytes 73736 | tf_op jit(solution)/shard_map/ppermute | solution.py:962
  16.3 0.0 collective-permute-done.first_ref
  16.3 4.6 %collective-permute-done.2.second_ref = f32[48,128]{1,0:T(8,128)S(1)} collective-permute-done((f32[48,128]{1,0:T(8,128)S(1)}, f32[48,128]{1,0:T(8,128)S(1)}, u32[]{:S(2)}, u32[]{:S(2)}) %collective-permute-start.2) | collective-permute-done | bytes 24608 | tf_op jit(solution)/shard_map/ppermute | solution.py:962
  20.9 0.0 collective-permute-done.3.there_side_ref
  20.9 0.1 shard_map.51
  20.9 0.7 %shard_map.53 = f32[2,6,2,256]{3,2,1,0:T(2,128)} custom-call(f32[6,8,128]{2,1,0:T(8,128)S(1)} %get-tuple-element.42.side_ref, f32[6,8,128]{2,1,0:T(8,128)S(1)} %get-tuple-element.43.other_ref, f32[14,8,128]{2,1,0:T(8,128)S(1)} %get-tuple-element.44.matrix_ref, f32[88,128]{1,0:T(8,128)S(1)} %collective-permute-done.3.there_side_ref, ...), custom_call_target="tpu_custom_call" | custom-call | tf_op jit(solution)/shard_map/pallas_call | solution.py:1075
  (4 shorter events, 0.1 us)
Async XLA Ops:
  10.2 2.8 %collective-permute-start.1 = (f32[192,128]{1,0:T(8,128)S(1)}, f32[192,128]{1,0:T(8,128)S(1)}, u32[]{:S(2)}, u32[]{:S(2)}) collective-permute-start(f32[192,128]{1,0:T(8,128)S(1)} %shard_map.49), channel_id=1, source_target_pairs={{0,8},{8,0},{16,24},{24,16},{1,9},{9,1},{17,25},{25,17},{2,10},{10... | collective-permute-start | bytes 294920 | tf_op jit(solution)/shard_map/ppermute | solution.py:949
  10.7 5.6 %collective-permute-start = (f32[96,128]{1,0:T(8,128)S(1)}, f32[96,128]{1,0:T(8,128)S(1)}, u32[]{:S(2)}, u32[]{:S(2)}) collective-permute-start(f32[96,128]{1,0:T(8,128)S(1)} %get-tuple-element.31), channel_id=1, source_target_pairs={{4,0},{5,1},{0,2},{1,3},{2,6},{3,7},{6,4},{7,5},{12,8},{13,9},{8,1... | collective-permute-start | bytes 147464 | tf_op jit(solution)/shard_map/ppermute | solution.py:962
  13.0 7.8 %collective-permute-start.3 = (f32[88,128]{1,0:T(8,128)S(1)}, f32[88,128]{1,0:T(8,128)S(1)}, u32[]{:S(2)}, u32[]{:S(2)}) collective-permute-start(f32[88,128]{1,0:T(8,128)S(1)} %get-tuple-element.41.here_side_ref), channel_id=1, source_target_pairs={{0,4},{1,5},{2,6},{3,7},{4,0},{5,1},{6,2},{7,3},{8,12},{9,13},{10,... | collective-permute-start | bytes 135176 | tf_op jit(solution)/shard_map/ppermute | solution.py:954
  14.3 6.6 %collective-permute-start.2 = (f32[48,128]{1,0:T(8,128)S(1)}, f32[48,128]{1,0:T(8,128)S(1)}, u32[]{:S(2)}, u32[]{:S(2)}) collective-permute-start(f32[48,128]{1,0:T(8,128)S(1)} %get-tuple-element.40), channel_id=1, source_target_pairs={{6,2},{7,3},{2,4},{3,5},{4,6},{5,7},{0,0},{1,1},{14,10},{15,11},{1... | collective-permute-start | bytes 73736 | tf_op jit(solution)/shard_map/ppermute | solution.py:962

commit v29 on v28

--- a/solution.py
+++ b/solution.py
@@ -957,7 +957,9 @@
 def pass_round(block, steps):
     width = lax.axis_size("cell") // 4
     pairs = [
-        (source * width + i, target * width + i) for source, target in steps for i in range(width)
+        (source * width + i, target * width + (i + (source == target)) % width)
+        for source, target in steps
+        for i in range(width)
     ]
     return lax.ppermute(block, "cell", pairs)
 

time: 21.8 us -> 20.6 us (0.945)
  the two profiles are of different devices: /device:TPU:10 before, /device:TPU:0 now
where the time goes in v29:
time: 20.6 us; the launch traced here: 20.4 us
  blocking collectives  10.9 us (53%)
  starting transfers between devices  5.06 us (25%)
  waiting for transfers between devices  2.32 us (11%)
  Pallas kernels  2.05 us (10%)
    all_to_all x1, blocking collectives, share_half(): lax.all_to_all(copies, ('inst', 'cell'), split_axis=0, concat_axis=0, til...  10.9 us
    ppermute x2, starting transfers between devices, pass_round(): return lax.ppermute(block, 'cell', pairs)  2.67 us
    ppermute x2, waiting for transfers between devices, pass_round(): return lax.ppermute(block, 'cell', pairs)  2.32 us
    ppermute x1, starting transfers between devices, swap_halves(): lax.ppermute(block, 'cell', [(i, (i + count // 2) % count) for i in range...  2.31 us
    pallas_call x1, Pallas kernels, local_by_halves(): pl.pallas_call(pack_kernel, out_shape=(float_shape(places * blocks, BLOCK...  0.82 us
    pallas_call x1, Pallas kernels, local_by_halves(): pl.pallas_call(join_kernel, out_shape=float_shape(*state.shape), in_specs...  0.66 us
  transfers between devices with their start and end apart: 4, of which 2 were waited for; matrix products, arithmetic and copies ran while one was open for 0% of the time, Pallas kernels for 2%

profile of v29, /device:TPU:0, one launch (start us, length us, event | category | flops | bytes accessed | tf_op | source)
XLA Modules:
  0.0 20.4 jit_solution(7716922288164205162)
XLA Ops:
  0.0 0.8 %shard_map.46 = (f32[8,56,128]{2,1,0:T(8,128)S(1)}, s32[256]{0:T(256)S(1)}, s32[2,8]{1,0:T(2,128)S(1)}) custom-call(f32[2,6,2,256]{3,2,1,0:T(2,128)} %held_state_ref.1, f32[2,256]{1,0:T(2,128)} %held_rate_ref.1, s32[256]{0:T(256)} %held_next_ref.1, s32[2,8]{1,0:T(2,128)} %held_codes_ref.1), custom_call_target="tpu_custom_call" | custom-call | tf_op jit(solution)/shard_map/pallas_call | solution.py:986
  0.8 10.9 %all_to_all.5 = f32[8,56,128]{2,1,0:T(8,128)S(1)} all-to-all(f32[8,56,128]{2,1,0:T(8,128)S(1)} %get-tuple-element.27), channel_id=1, replica_groups={{19,18,17,16,3,2,1,0},{23,22,21,20,7,6,5,4},{27,26,25,24,11,10,9,8},{31..., dimensions={0} | all-to-all | bytes 458752 | tf_op jit(solution)/shard_map/all_to_all | solution.py:941
  11.8 0.1 collective-permute-start.1
  11.9 0.4 %shard_map.47 = (f32[8,3,8,128]{3,2,1,0:T(8,128)S(1)}, f32[3,4,8,128]{3,2,1,0:T(8,128)S(1)}, f32[3,7,8,128]{3,2,1,0:T(8,128)S(1)}, f32[16,128]{1,0:T(8,128)S(1)}...) custom-call(f32[2,4,56,128]{3,2,1,0:T(8,128)S(1)} %bitcast.2, ...), custom_call_target="tpu_custom_call" | custom-call | tf_op jit(solution)/shard_map/pallas_call | solution.py:1020
  12.3 1.2 %collective-permute-start = (f32[96,128]{1,0:T(8,128)S(1)}, f32[96,128]{1,0:T(8,128)S(1)}, u32[]{:S(2)}, u32[]{:S(2)}) collective-permute-start(f32[96,128]{1,0:T(8,128)S(1)} %get-tuple-element.31), channel_id=1, source_target_pairs={{4,0},{5,1},{0,2},{1,3},{2,6},{3,7},{6,4},{7,5},{12,8},{13,9},{8,1... | collective-permute-start | bytes 147464 | tf_op jit(solution)/shard_map/ppermute | solution.py:964
  13.5 0.0 collective-permute-done.1.time_ref
  13.5 2.3 %collective-permute-start.3 = (f32[88,128]{1,0:T(8,128)S(1)}, f32[88,128]{1,0:T(8,128)S(1)}, u32[]{:S(2)}, u32[]{:S(2)}) collective-permute-start(f32[88,128]{1,0:T(8,128)S(1)} %get-tuple-element.41.here_side_ref), channel_id=1, source_target_pairs={{0,4},{1,5},{2,6},{3,7},{4,0},{5,1},{6,2},{7,3},{8,12},{9,13},{10,... | collective-permute-start | bytes 135176 | tf_op jit(solution)/shard_map/ppermute | solution.py:954
  15.9 1.5 %collective-permute-start.2 = (f32[48,128]{1,0:T(8,128)S(1)}, f32[48,128]{1,0:T(8,128)S(1)}, u32[]{:S(2)}, u32[]{:S(2)}) collective-permute-start(f32[48,128]{1,0:T(8,128)S(1)} %get-tuple-element.40), channel_id=1, source_target_pairs={{6,2},{7,3},{2,4},{3,5},{4,6},{5,7},{0,1},{1,0},{14,10},{15,11},{1... | collective-permute-start | bytes 73736 | tf_op jit(solution)/shard_map/ppermute | solution.py:964
  17.4 0.1 collective-permute-done.first_ref
  17.4 2.2 %collective-permute-done.2.second_ref = f32[48,128]{1,0:T(8,128)S(1)} collective-permute-done((f32[48,128]{1,0:T(8,128)S(1)}, f32[48,128]{1,0:T(8,128)S(1)}, u32[]{:S(2)}, u32[]{:S(2)}) %collective-permute-start.2) | collective-permute-done | bytes 24608 | tf_op jit(solution)/shard_map/ppermute | solution.py:964
  19.7 0.0 collective-permute-done.3.there_side_ref
  19.7 0.1 shard_map.51
  19.8 0.7 %shard_map.53 = f32[2,6,2,256]{3,2,1,0:T(2,128)} custom-call(f32[6,8,128]{2,1,0:T(8,128)S(1)} %get-tuple-element.42.side_ref, f32[6,8,128]{2,1,0:T(8,128)S(1)} %get-tuple-element.43.other_ref, f32[14,8,128]{2,1,0:T(8,128)S(1)} %get-tuple-element.44.matrix_ref, f32[88,128]{1,0:T(8,128)S(1)} %collective-permute-done.3.there_side_ref, ...), custom_call_target="tpu_custom_call" | custom-call | tf_op jit(solution)/shard_map/pallas_call | solution.py:1077
  (4 shorter events, 0.1 us)
Async XLA Ops:
  11.8 1.7 %collective-permute-start.1 = (f32[192,128]{1,0:T(8,128)S(1)}, f32[192,128]{1,0:T(8,128)S(1)}, u32[]{:S(2)}, u32[]{:S(2)}) collective-permute-start(f32[192,128]{1,0:T(8,128)S(1)} %shard_map.49), channel_id=1, source_target_pairs={{0,8},{8,0},{16,24},{24,16},{1,9},{9,1},{17,25},{25,17},{2,10},{10... | collective-permute-start | bytes 294920 | tf_op jit(solution)/shard_map/ppermute | solution.py:949
  12.3 5.2 %collective-permute-start = (f32[96,128]{1,0:T(8,128)S(1)}, f32[96,128]{1,0:T(8,128)S(1)}, u32[]{:S(2)}, u32[]{:S(2)}) collective-permute-start(f32[96,128]{1,0:T(8,128)S(1)} %get-tuple-element.31), channel_id=1, source_target_pairs={{4,0},{5,1},{0,2},{1,3},{2,6},{3,7},{6,4},{7,5},{12,8},{13,9},{8,1... | collective-permute-start | bytes 147464 | tf_op jit(solution)/shard_map/ppermute | solution.py:964
  13.5 6.1 %collective-permute-start.3 = (f32[88,128]{1,0:T(8,128)S(1)}, f32[88,128]{1,0:T(8,128)S(1)}, u32[]{:S(2)}, u32[]{:S(2)}) collective-permute-start(f32[88,128]{1,0:T(8,128)S(1)} %get-tuple-element.41.here_side_ref), channel_id=1, source_target_pairs={{0,4},{1,5},{2,6},{3,7},{4,0},{5,1},{6,2},{7,3},{8,12},{9,13},{10,... | collective-permute-start | bytes 135176 | tf_op jit(solution)/shard_map/ppermute | solution.py:954
  15.9 3.8 %collective-permute-start.2 = (f32[48,128]{1,0:T(8,128)S(1)}, f32[48,128]{1,0:T(8,128)S(1)}, u32[]{:S(2)}, u32[]{:S(2)}) collective-permute-start(f32[48,128]{1,0:T(8,128)S(1)} %get-tuple-element.40), channel_id=1, source_target_pairs={{6,2},{7,3},{2,4},{3,5},{4,6},{5,7},{0,1},{1,0},{14,10},{15,11},{1... | collective-permute-start | bytes 73736 | tf_op jit(solution)/shard_map/ppermute | solution.py:964

commit v30 on v29

--- a/solution.py
+++ b/solution.py
@@ -955,13 +955,18 @@
 
 
 def pass_round(block, steps):
-    width = lax.axis_size("cell") // 4
+    insts, count = lax.axis_size("inst"), lax.axis_size("cell")
+    width = count // 4
     pairs = [
-        (source * width + i, target * width + (i + (source == target)) % width)
+        (
+            inst * count + source * width + i,
+            (inst ^ (source == target)) * count + target * width + i,
+        )
+        for inst in range(insts)
         for source, target in steps
         for i in range(width)
     ]
-    return lax.ppermute(block, "cell", pairs)
+    return lax.ppermute(block, ("inst", "cell"), pairs)
 
 
 FIRST_ROUND = ((2, 0), (0, 1), (1, 3), (3, 2))

time: 20.6 us -> 19.9 us (0.966)
  the two profiles are of different devices: /device:TPU:0 before, /device:TPU:10 now
where the time goes in v30:
time: 19.9 us; the launch traced here: 19.7 us
  blocking collectives  9.34 us (47%)
  waiting for transfers between devices  4.6 us (23%)
  starting transfers between devices  3.68 us (18%)
  Pallas kernels  2.05 us (10%)
    all_to_all x1, blocking collectives, share_half(): lax.all_to_all(copies, ('inst', 'cell'), split_axis=0, concat_axis=0, til...  9.34 us
    ppermute x2, waiting for transfers between devices, pass_round(): return lax.ppermute(block, ('inst', 'cell'), pairs)  4.6 us
    ppermute x2, starting transfers between devices, pass_round(): return lax.ppermute(block, ('inst', 'cell'), pairs)  2.39 us
    ppermute x1, starting transfers between devices, swap_halves(): lax.ppermute(block, 'cell', [(i, (i + count // 2) % count) for i in range...  1.22 us
    pallas_call x1, Pallas kernels, local_by_halves(): pl.pallas_call(pack_kernel, out_shape=(float_shape(places * blocks, BLOCK...  0.82 us
    pallas_call x1, Pallas kernels, local_by_halves(): pl.pallas_call(join_kernel, out_shape=float_shape(*state.shape), in_specs...  0.66 us
  transfers between devices with their start and end apart: 4, of which 2 were waited for; matrix products, arithmetic and copies ran while one was open for 0% of the time, Pallas kernels for 2%

profile of v30, /device:TPU:10, one launch (start us, length us, event | category | flops | bytes accessed | tf_op | source)
XLA Modules:
  0.0 19.7 jit_solution(15786659546793685601)
XLA Ops:
  0.0 0.8 %shard_map.46 = (f32[8,56,128]{2,1,0:T(8,128)S(1)}, s32[256]{0:T(256)S(1)}, s32[2,8]{1,0:T(2,128)S(1)}) custom-call(f32[2,6,2,256]{3,2,1,0:T(2,128)} %held_state_ref.1, f32[2,256]{1,0:T(2,128)} %held_rate_ref.1, s32[256]{0:T(256)} %held_next_ref.1, s32[2,8]{1,0:T(2,128)} %held_codes_ref.1), custom_call_target="tpu_custom_call" | custom-call | tf_op jit(solution)/shard_map/pallas_call | solution.py:991
  0.8 9.3 %all_to_all.5 = f32[8,56,128]{2,1,0:T(8,128)S(1)} all-to-all(f32[8,56,128]{2,1,0:T(8,128)S(1)} %get-tuple-element.27), channel_id=1, replica_groups={{19,18,17,16,3,2,1,0},{23,22,21,20,7,6,5,4},{27,26,25,24,11,10,9,8},{31..., dimensions={0} | all-to-all | bytes 458752 | tf_op jit(solution)/shard_map/all_to_all | solution.py:941
  10.2 0.1 collective-permute-start.1
  10.3 0.4 %shard_map.47 = (f32[8,3,8,128]{3,2,1,0:T(8,128)S(1)}, f32[3,4,8,128]{3,2,1,0:T(8,128)S(1)}, f32[3,7,8,128]{3,2,1,0:T(8,128)S(1)}, f32[16,128]{1,0:T(8,128)S(1)}...) custom-call(f32[2,4,56,128]{3,2,1,0:T(8,128)S(1)} %bitcast.2, ...), custom_call_target="tpu_custom_call" | custom-call | tf_op jit(solution)/shard_map/pallas_call | solution.py:1025
  10.7 2.3 %collective-permute-start = (f32[96,128]{1,0:T(8,128)S(1)}, f32[96,128]{1,0:T(8,128)S(1)}, u32[]{:S(2)}, u32[]{:S(2)}) collective-permute-start(f32[96,128]{1,0:T(8,128)S(1)} %get-tuple-element.31), channel_id=1, source_target_pairs={{4,0},{5,1},{0,2},{1,3},{2,6},{3,7},{6,4},{7,5},{12,8},{13,9},{8,1... | collective-permute-start | bytes 147464 | tf_op jit(solution)/shard_map/ppermute | solution.py:969
  13.0 0.0 collective-permute-done.1.time_ref
  13.0 1.2 %collective-permute-start.3 = (f32[88,128]{1,0:T(8,128)S(1)}, f32[88,128]{1,0:T(8,128)S(1)}, u32[]{:S(2)}, u32[]{:S(2)}) collective-permute-start(f32[88,128]{1,0:T(8,128)S(1)} %get-tuple-element.41.here_side_ref), channel_id=1, source_target_pairs={{0,4},{1,5},{2,6},{3,7},{4,0},{5,1},{6,2},{7,3},{8,12},{9,13},{10,... | collective-permute-start | bytes 135176 | tf_op jit(solution)/shard_map/ppermute | solution.py:954
  14.3 0.1 collective-permute-start.2
  14.4 0.5 %collective-permute-done.first_ref = f32[96,128]{1,0:T(8,128)S(1)} collective-permute-done((f32[96,128]{1,0:T(8,128)S(1)}, f32[96,128]{1,0:T(8,128)S(1)}, u32[]{:S(2)}, u32[]{:S(2)}) %collective-permute-start) | collective-permute-done | bytes 49184 | tf_op jit(solution)/shard_map/ppermute | solution.py:969
  14.8 4.1 %collective-permute-done.2.second_ref = f32[48,128]{1,0:T(8,128)S(1)} collective-permute-done((f32[48,128]{1,0:T(8,128)S(1)}, f32[48,128]{1,0:T(8,128)S(1)}, u32[]{:S(2)}, u32[]{:S(2)}) %collective-permute-start.2) | collective-permute-done | bytes 24608 | tf_op jit(solution)/shard_map/ppermute | solution.py:969
  19.0 0.0 collective-permute-done.3.there_side_ref
  19.0 0.1 shard_map.51
  19.1 0.7 %shard_map.53 = f32[2,6,2,256]{3,2,1,0:T(2,128)} custom-call(f32[6,8,128]{2,1,0:T(8,128)S(1)} %get-tuple-element.42.side_ref, f32[6,8,128]{2,1,0:T(8,128)S(1)} %get-tuple-element.43.other_ref, f32[14,8,128]{2,1,0:T(8,128)S(1)} %get-tuple-element.44.matrix_ref, f32[88,128]{1,0:T(8,128)S(1)} %collective-permute-done.3.there_side_ref, ...), custom_call_target="tpu_custom_call" | custom-call | tf_op jit(solution)/shard_map/pallas_call | solution.py:1082
  (4 shorter events, 0.1 us)
Async XLA Ops:
  10.2 2.8 %collective-permute-start.1 = (f32[192,128]{1,0:T(8,128)S(1)}, f32[192,128]{1,0:T(8,128)S(1)}, u32[]{:S(2)}, u32[]{:S(2)}) collective-permute-start(f32[192,128]{1,0:T(8,128)S(1)} %shard_map.49), channel_id=1, source_target_pairs={{0,8},{8,0},{16,24},{24,16},{1,9},{9,1},{17,25},{25,17},{2,10},{10... | collective-permute-start | bytes 294920 | tf_op jit(solution)/shard_map/ppermute | solution.py:949
  10.7 4.2 %collective-permute-start = (f32[96,128]{1,0:T(8,128)S(1)}, f32[96,128]{1,0:T(8,128)S(1)}, u32[]{:S(2)}, u32[]{:S(2)}) collective-permute-start(f32[96,128]{1,0:T(8,128)S(1)} %get-tuple-element.31), channel_id=1, source_target_pairs={{4,0},{5,1},{0,2},{1,3},{2,6},{3,7},{6,4},{7,5},{12,8},{13,9},{8,1... | collective-permute-start | bytes 147464 | tf_op jit(solution)/shard_map/ppermute | solution.py:969
  13.0 5.9 %collective-permute-start.3 = (f32[88,128]{1,0:T(8,128)S(1)}, f32[88,128]{1,0:T(8,128)S(1)}, u32[]{:S(2)}, u32[]{:S(2)}) collective-permute-start(f32[88,128]{1,0:T(8,128)S(1)} %get-tuple-element.41.here_side_ref), channel_id=1, source_target_pairs={{0,4},{1,5},{2,6},{3,7},{4,0},{5,1},{6,2},{7,3},{8,12},{9,13},{10,... | collective-permute-start | bytes 135176 | tf_op jit(solution)/shard_map/ppermute | solution.py:954
  14.3 4.7 %collective-permute-start.2 = (f32[48,128]{1,0:T(8,128)S(1)}, f32[48,128]{1,0:T(8,128)S(1)}, u32[]{:S(2)}, u32[]{:S(2)}) collective-permute-start(f32[48,128]{1,0:T(8,128)S(1)} %get-tuple-element.40), channel_id=1, source_target_pairs={{6,2},{7,3},{2,4},{3,5},{4,6},{5,7},{0,8},{1,9},{14,10},{15,11},{1... | collective-permute-start | bytes 73736 | tf_op jit(solution)/shard_map/ppermute | solution.py:969

commit v31 on v30

--- a/solution.py
+++ b/solution.py
@@ -343,11 +343,11 @@
 VMEM_BYTES = 8 * 2**20
 BLOCK_ROWS = RATE_ROW + ROWS
 
-MIDDLE_CELLS = 2
-ROUND_CELLS = 4
+MIDDLE_CELLS = (1, 0, 2)
+MIDDLE_ROWS = 3 * CELL_ROWS
+SECOND_ROWS = MIDDLE_ROWS - ROWS
 CORRECTION_ROW = 2 * CELL_ROWS
-THIRD_ROW = CORRECTION_ROW + 2 * ROWS
-SIDE_ROWS = THIRD_ROW + CELL_ROWS
+SIDE_ROWS = CORRECTION_ROW + 3 * ROWS
 
 
 def spectral_offsets():
@@ -600,20 +600,13 @@
 
 
 def near_half_kernel(all_ref, next_ref, codes_ref, *refs):
-    *results, middle_ref, round_ref, third_ref, line_ref = refs
+    *results, middle_ref, line_ref = refs
     own_y = lax.axis_index("inst") >> 1
     cells = 2 * all_ref.shape[1]
-    for cell in range(cells - MIDDLE_CELLS, cells):
+    for n, back in enumerate(MIDDLE_CELLS):
         for k in range(PAIRS):
-            row = (cell - (cells - MIDDLE_CELLS)) * CELL_ROWS + k * ROWS
-            middle_ref[pl.ds(row, ROWS), :] = cell_plane(all_ref, own_y, cell, k)
-    for cell in range(ROUND_CELLS):
-        for k in range(PAIRS):
-            plane = cell_plane(all_ref, own_y, cells - 1 - cell, k)
-            round_ref[pl.ds(cell * CELL_ROWS + k * ROWS, ROWS), :] = plane
-    for k in range(PAIRS):
-        third = cell_plane(all_ref, own_y, cells - MIDDLE_CELLS - 1, k)
-        third_ref[pl.ds(k * ROWS, ROWS), :] = third
+            plane = cell_plane(all_ref, own_y, cells - 1 - back, k)
+            middle_ref[pl.ds(n * CELL_ROWS + k * ROWS, ROWS), :] = plane
 
     @pl.when(lax.axis_index("cell") < all_ref.shape[1])
     def _():
@@ -792,11 +785,10 @@
 
 
 def reduce_kernel(
-    partial_ref, time_ref, factor_ref, correction_ref, here_ref, third_ref, middle_ref, sides_ref,
-    again_ref,
+    partial_ref, time_ref, factor_ref, correction_ref, here_ref, middle_ref, sides_ref, again_ref
 ):
-    again_ref[...] = here_ref[...]
-    middle_ref[pl.ds(THIRD_ROW, CELL_ROWS), :] = third_ref[...]
+    again_ref[...] = here_ref[pl.ds(0, SECOND_ROWS), :]
+    middle_ref[pl.ds(SIDE_ROWS - ROWS, ROWS), :] = here_ref[pl.ds(SECOND_ROWS, ROWS), :]
     for row in range(0, 2 * ROWS, ROWS):
         middle_ref[pl.ds(CORRECTION_ROW + row, ROWS), :] = correction_ref[pl.ds(row, ROWS), :]
     blocks = partial_ref.shape[0] // 2
@@ -865,22 +857,17 @@
     first_var, _, _ = plane_masks()
     line = LineCells(first_var, sign)
     for cell in range(6):
-        at = cell if cell < 3 else 5 - cell
-        rows = [(at - 1) * CELL_ROWS + k * ROWS for k in range(PAIRS)]
-        if at == 0:
-            ref = here_side_ref if cell < 3 else there_side_ref
-            planes = [plane_of(ref, THIRD_ROW + k * ROWS) for k in range(PAIRS)]
-        elif cell < 3:
-            planes = [plane_of(here_ref, row) for row in rows]
-        else:
-            planes = [
-                jnp.where(
-                    outer,
-                    plane_of(first_ref, (2 - at) * CELL_ROWS + k * ROWS),
-                    plane_of(second_ref, row),
-                )
-                for k, row in enumerate(rows)
-            ]
+        at = (2, 0, 1)[cell if cell < 3 else 5 - cell]
+        planes = []
+        for k in range(PAIRS):
+            row = at * CELL_ROWS + k * ROWS
+            if cell < 3:
+                planes.append(plane_of(here_ref, row))
+            elif row < SECOND_ROWS:
+                first, second = plane_of(first_ref, row), plane_of(second_ref, row)
+                planes.append(jnp.where(outer, first, second))
+            else:
+                planes.append(plane_of(there_side_ref, SIDE_ROWS - ROWS))
         velocity_x, _, pressure, sound = primitives(first_var, planes)
         line.add(cell, planes, velocity_x, pressure, sound)
     faces = {cell: line.face(cell) for cell in (1, 2, 3)}
@@ -1022,20 +1009,16 @@
     )
     line_scratch = [pltpu.VMEM((cells, 3) + plane, jnp.float32)]
     arguments = (shared, next_here, codes_here)
-    *near, here, for_round, third = pl.pallas_call(
+    *near, here = pl.pallas_call(
         near_half_kernel,
         out_shape=kinds
-        + (
-            float_shape(MIDDLE_CELLS * CELL_ROWS, LANES),
-            float_shape(ROUND_CELLS * CELL_ROWS, LANES),
-            float_shape(CELL_ROWS, LANES),
-        ),
+        + (float_shape(MIDDLE_ROWS, LANES),),
         in_specs=[vmem] * 3,
-        out_specs=(vmem,) * 7,
+        out_specs=(vmem,) * 5,
         scratch_shapes=line_scratch,
         compiler_params=params,
     )(*arguments)
-    there_first = pass_round(for_round, FIRST_ROUND)
+    there_first = pass_round(here, FIRST_ROUND)
     partial, factors, eliminated, correction = pl.pallas_call(
         far_half_kernel,
         out_shape=kinds,
@@ -1051,12 +1034,12 @@
         out_shape=(
             float_shape(SIDE_ROWS, LANES),
             float_shape(blocks - 1, 2 * PAIRS, *plane),
-            float_shape(MIDDLE_CELLS * CELL_ROWS, LANES),
+            float_shape(SECOND_ROWS, LANES),
         ),
-        in_specs=[vmem] * 6,
+        in_specs=[vmem] * 5,
         out_specs=(vmem,) * 3,
         compiler_params=params,
-    )(partial, from_partner, factors, correction, here, third)
+    )(partial, from_partner, factors, correction, here)
     there_side = swap_halves(here_side)
     there_second = pass_round(here_again, SECOND_ROUND)
     known, spread = pl.pallas_call(

time: 19.9 us -> 20 us (level)
  no operation moved by 1% of the time
where the time goes in v31:
time: 20 us; the launch traced here: 19.8 us
  blocking collectives  9.34 us (47%)
  waiting for transfers between devices  4.7 us (24%)
  starting transfers between devices  3.68 us (18%)
  Pallas kernels  2.04 us (10%)
    all_to_all x1, blocking collectives, share_half(): lax.all_to_all(copies, ('inst', 'cell'), split_axis=0, concat_axis=0, til...  9.34 us
    ppermute x2, waiting for transfers between devices, pass_round(): return lax.ppermute(block, ('inst', 'cell'), pairs)  4.7 us
    ppermute x2, starting transfers between devices, pass_round(): return lax.ppermute(block, ('inst', 'cell'), pairs)  2.39 us
    ppermute x1, starting transfers between devices, swap_halves(): lax.ppermute(block, 'cell', [(i, (i + count // 2) % count) for i in range...  1.22 us
    pallas_call x1, Pallas kernels, local_by_halves(): pl.pallas_call(pack_kernel, out_shape=(float_shape(places * blocks, BLOCK...  0.82 us
    pallas_call x1, Pallas kernels, local_by_halves(): pl.pallas_call(join_kernel, out_shape=float_shape(*state.shape), in_specs...  0.66 us
  transfers between devices with their start and end apart: 4, of which 2 were waited for; matrix products, arithmetic and copies ran while one was open for 0% of the time, Pallas kernels for 2%

profile of v31, /device:TPU:10, one launch (start us, length us, event | category | flops | bytes accessed | tf_op | source)
XLA Modules:
  0.0 19.8 jit_solution(13338135454734096694)
XLA Ops:
  0.0 0.8 %shard_map.46 = (f32[8,56,128]{2,1,0:T(8,128)S(1)}, s32[256]{0:T(256)S(1)}, s32[2,8]{1,0:T(2,128)S(1)}) custom-call(f32[2,6,2,256]{3,2,1,0:T(2,128)} %held_state_ref.1, f32[2,256]{1,0:T(2,128)} %held_rate_ref.1, s32[256]{0:T(256)} %held_next_ref.1, s32[2,8]{1,0:T(2,128)} %held_codes_ref.1), custom_call_target="tpu_custom_call" | custom-call | tf_op jit(solution)/shard_map/pallas_call | solution.py:978
  0.8 9.3 %all_to_all.5 = f32[8,56,128]{2,1,0:T(8,128)S(1)} all-to-all(f32[8,56,128]{2,1,0:T(8,128)S(1)} %get-tuple-element.25), channel_id=1, replica_groups={{19,18,17,16,3,2,1,0},{23,22,21,20,7,6,5,4},{27,26,25,24,11,10,9,8},{31..., dimensions={0} | all-to-all | bytes 458752 | tf_op jit(solution)/shard_map/all_to_all | solution.py:928
  10.2 0.1 collective-permute-start.1
  10.3 0.4 %shard_map.47 = (f32[8,3,8,128]{3,2,1,0:T(8,128)S(1)}, f32[3,4,8,128]{3,2,1,0:T(8,128)S(1)}, f32[3,7,8,128]{3,2,1,0:T(8,128)S(1)}, f32[16,128]{1,0:T(8,128)S(1)}, f32[72,128]{1,0:T(8,128)S(1)}) custom-call(f32[2,4,56,128]{3,2,1,0:T(8,128)S(1)} %bitcast.2, s32[256]{0:T(256)S(1)} %get-tuple-element.26.next_ref, s32[2,8]{1,0:T(2,128)S(1)} %get-tuple-element.27.codes_ref), custom_call_target="tpu_custom_call" | custom-call | tf_op jit(solution)/shard_map/pallas_call | solution.py:1012
  10.7 2.3 %collective-permute-start = (f32[72,128]{1,0:T(8,128)S(1)}, f32[72,128]{1,0:T(8,128)S(1)}, u32[]{:S(2)}, u32[]{:S(2)}) collective-permute-start(f32[72,128]{1,0:T(8,128)S(1)} %get-tuple-element.28.here_ref), channel_id=1, source_target_pairs={{4,0},{5,1},{0,2},{1,3},{2,6},{3,7},{6,4},{7,5},{12,8},{13,9},{8,1... | collective-permute-start | bytes 110600 | tf_op jit(solution)/shard_map/ppermute | solution.py:956
  13.0 0.0 collective-permute-done.1.time_ref
  13.0 1.2 %collective-permute-start.3 = (f32[72,128]{1,0:T(8,128)S(1)}, f32[72,128]{1,0:T(8,128)S(1)}, u32[]{:S(2)}, u32[]{:S(2)}) collective-permute-start(f32[72,128]{1,0:T(8,128)S(1)} %get-tuple-element.37.here_side_ref), channel_id=1, source_target_pairs={{0,4},{1,5},{2,6},{3,7},{4,0},{5,1},{6,2},{7,3},{8,12},{9,13},{10,... | collective-permute-start | bytes 110600 | tf_op jit(solution)/shard_map/ppermute | solution.py:941
  14.3 0.1 collective-permute-start.2
  14.4 0.3 %collective-permute-done.first_ref = f32[72,128]{1,0:T(8,128)S(1)} collective-permute-done((f32[72,128]{1,0:T(8,128)S(1)}, f32[72,128]{1,0:T(8,128)S(1)}, u32[]{:S(2)}, u32[]{:S(2)}) %collective-permute-start) | collective-permute-done | bytes 36896 | tf_op jit(solution)/shard_map/ppermute | solution.py:956
  14.7 4.4 %collective-permute-done.2.second_ref = f32[64,128]{1,0:T(8,128)S(1)} collective-permute-done((f32[64,128]{1,0:T(8,128)S(1)}, f32[64,128]{1,0:T(8,128)S(1)}, u32[]{:S(2)}, u32[]{:S(2)}) %collective-permute-start.2) | collective-permute-done | bytes 32800 | tf_op jit(solution)/shard_map/ppermute | solution.py:956
  19.1 0.0 collective-permute-done.3.there_side_ref
  19.1 0.1 shard_map.51
  19.2 0.7 %shard_map.53 = f32[2,6,2,256]{3,2,1,0:T(2,128)} custom-call(f32[6,8,128]{2,1,0:T(8,128)S(1)} %get-tuple-element.38.side_ref, f32[6,8,128]{2,1,0:T(8,128)S(1)} %get-tuple-element.39.other_ref, f32[14,8,128]{2,1,0:T(8,128)S(1)} %get-tuple-element.40.matrix_ref, f32[72,128]{1,0:T(8,128)S(1)} %collective-permute-done.3.there_side_ref, ...), custom_call_target="tpu_custom_call" | custom-call | tf_op jit(solution)/shard_map/pallas_call | solution.py:1065
  (4 shorter events, 0.1 us)
Async XLA Ops:
  10.2 2.8 %collective-permute-start.1 = (f32[192,128]{1,0:T(8,128)S(1)}, f32[192,128]{1,0:T(8,128)S(1)}, u32[]{:S(2)}, u32[]{:S(2)}) collective-permute-start(f32[192,128]{1,0:T(8,128)S(1)} %shard_map.49), channel_id=1, source_target_pairs={{0,8},{8,0},{16,24},{24,16},{1,9},{9,1},{17,25},{25,17},{2,10},{10... | collective-permute-start | bytes 294920 | tf_op jit(solution)/shard_map/ppermute | solution.py:936
  10.7 4.0 %collective-permute-start = (f32[72,128]{1,0:T(8,128)S(1)}, f32[72,128]{1,0:T(8,128)S(1)}, u32[]{:S(2)}, u32[]{:S(2)}) collective-permute-start(f32[72,128]{1,0:T(8,128)S(1)} %get-tuple-element.28.here_ref), channel_id=1, source_target_pairs={{4,0},{5,1},{0,2},{1,3},{2,6},{3,7},{6,4},{7,5},{12,8},{13,9},{8,1... | collective-permute-start | bytes 110600 | tf_op jit(solution)/shard_map/ppermute | solution.py:956
  13.0 6.0 %collective-permute-start.3 = (f32[72,128]{1,0:T(8,128)S(1)}, f32[72,128]{1,0:T(8,128)S(1)}, u32[]{:S(2)}, u32[]{:S(2)}) collective-permute-start(f32[72,128]{1,0:T(8,128)S(1)} %get-tuple-element.37.here_side_ref), channel_id=1, source_target_pairs={{0,4},{1,5},{2,6},{3,7},{4,0},{5,1},{6,2},{7,3},{8,12},{9,13},{10,... | collective-permute-start | bytes 110600 | tf_op jit(solution)/shard_map/ppermute | solution.py:941
  14.3 4.8 %collective-permute-start.2 = (f32[64,128]{1,0:T(8,128)S(1)}, f32[64,128]{1,0:T(8,128)S(1)}, u32[]{:S(2)}, u32[]{:S(2)}) collective-permute-start(f32[64,128]{1,0:T(8,128)S(1)} %get-tuple-element.36), channel_id=1, source_target_pairs={{6,2},{7,3},{2,4},{3,5},{4,6},{5,7},{0,8},{1,9},{14,10},{15,11},{1... | collective-permute-start | bytes 98312 | tf_op jit(solution)/shard_map/ppermute | solution.py:956

commit v32 on v31

--- a/solution.py
+++ b/solution.py
@@ -852,7 +852,7 @@
 ):
     own_cell, count = lax.axis_index("cell"), lax.axis_size("cell")
     mirrored = own_cell // (count // 2)
-    outer = jnp.logical_or(own_cell < count // 4, own_cell >= count - count // 4)
+    early = (own_cell // (count // 4)) % 2 == 0
     sign = (1 - 2 * mirrored).astype(jnp.float32)
     first_var, _, _ = plane_masks()
     line = LineCells(first_var, sign)
@@ -865,7 +865,7 @@
                 planes.append(plane_of(here_ref, row))
             elif row < SECOND_ROWS:
                 first, second = plane_of(first_ref, row), plane_of(second_ref, row)
-                planes.append(jnp.where(outer, first, second))
+                planes.append(jnp.where(early, first, second))
             else:
                 planes.append(plane_of(there_side_ref, SIDE_ROWS - ROWS))
         velocity_x, _, pressure, sound = primitives(first_var, planes)
@@ -956,8 +956,8 @@
     return lax.ppermute(block, ("inst", "cell"), pairs)
 
 
-FIRST_ROUND = ((2, 0), (0, 1), (1, 3), (3, 2))
-SECOND_ROUND = ((3, 1), (1, 2), (2, 3), (0, 0))
+FIRST_ROUND = ((2, 0), (0, 1), (1, 2), (3, 3))
+SECOND_ROUND = ((3, 1), (1, 3), (0, 0), (2, 2))
 
 
 def float_shape(*sizes):

time: 20 us -> 20 us (level)
  starting transfers between devices: 3.68 us -> 4.48 us
  waiting for transfers between devices: 4.7 us -> 3.9 us
    ppermute x1, starting transfers between devices: 1.22 us -> 2.11 us  [swap_halves(): lax.ppermute(block, 'cell', [(i, (i + count // 2) % count) for i in range...]
    ppermute x2, waiting for transfers between devices: 4.7 us -> 3.89 us  [pass_round(): return lax.ppermute(block, ('inst', 'cell'), pairs)]
  transfers between devices with their start and end apart: 4 -> 4, of which waited for: 2 -> 1; matrix products, arithmetic and copies ran while one was open for 0% -> 0% of each run, Pallas kernels for 2% -> 2%
where the time goes in v32:
time: 20 us; the launch traced here: 19.8 us
  blocking collectives  9.34 us (47%)
  starting transfers between devices  4.48 us (22%)
  waiting for transfers between devices  3.9 us (20%)
  Pallas kernels  2.04 us (10%)
    all_to_all x1, blocking collectives, share_half(): lax.all_to_all(copies, ('inst', 'cell'), split_axis=0, concat_axis=0, til...  9.34 us
    ppermute x2, waiting for transfers between devices, pass_round(): return lax.ppermute(block, ('inst', 'cell'), pairs)  3.89 us
    ppermute x2, starting transfers between devices, pass_round(): return lax.ppermute(block, ('inst', 'cell'), pairs)  2.3 us
    ppermute x1, starting transfers between devices, swap_halves(): lax.ppermute(block, 'cell', [(i, (i + count // 2) % count) for i in range...  2.11 us
    pallas_call x1, Pallas kernels, local_by_halves(): pl.pallas_call(pack_kernel, out_shape=(float_shape(places * blocks, BLOCK...  0.82 us
    pallas_call x1, Pallas kernels, local_by_halves(): pl.pallas_call(join_kernel, out_shape=float_shape(*state.shape), in_specs...  0.66 us
  transfers between devices with their start and end apart: 4, of which 1 were waited for; matrix products, arithmetic and copies ran while one was open for 0% of the time, Pallas kernels for 2%

profile of v32, /device:TPU:10, one launch (start us, length us, event | category | flops | bytes accessed | tf_op | source)
XLA Modules:
  0.0 19.8 jit_solution(6486575702345755509)
XLA Ops:
  0.0 0.8 %shard_map.46 = (f32[8,56,128]{2,1,0:T(8,128)S(1)}, s32[256]{0:T(256)S(1)}, s32[2,8]{1,0:T(2,128)S(1)}) custom-call(f32[2,6,2,256]{3,2,1,0:T(2,128)} %held_state_ref.1, f32[2,256]{1,0:T(2,128)} %held_rate_ref.1, s32[256]{0:T(256)} %held_next_ref.1, s32[2,8]{1,0:T(2,128)} %held_codes_ref.1), custom_call_target="tpu_custom_call" | custom-call | tf_op jit(solution)/shard_map/pallas_call | solution.py:978
  0.8 9.3 %all_to_all.5 = f32[8,56,128]{2,1,0:T(8,128)S(1)} all-to-all(f32[8,56,128]{2,1,0:T(8,128)S(1)} %get-tuple-element.25), channel_id=1, replica_groups={{19,18,17,16,3,2,1,0},{23,22,21,20,7,6,5,4},{27,26,25,24,11,10,9,8},{31..., dimensions={0} | all-to-all | bytes 458752 | tf_op jit(solution)/shard_map/all_to_all | solution.py:928
  10.2 0.1 collective-permute-start.1
  10.3 0.4 %shard_map.47 = (f32[8,3,8,128]{3,2,1,0:T(8,128)S(1)}, f32[3,4,8,128]{3,2,1,0:T(8,128)S(1)}, f32[3,7,8,128]{3,2,1,0:T(8,128)S(1)}, f32[16,128]{1,0:T(8,128)S(1)}, f32[72,128]{1,0:T(8,128)S(1)}) custom-call(f32[2,4,56,128]{3,2,1,0:T(8,128)S(1)} %bitcast.2, s32[256]{0:T(256)S(1)} %get-tuple-element.26.next_ref, s32[2,8]{1,0:T(2,128)S(1)} %get-tuple-element.27.codes_ref), custom_call_target="tpu_custom_call" | custom-call | tf_op jit(solution)/shard_map/pallas_call | solution.py:1012
  10.7 1.4 %collective-permute-start = (f32[72,128]{1,0:T(8,128)S(1)}, f32[72,128]{1,0:T(8,128)S(1)}, u32[]{:S(2)}, u32[]{:S(2)}) collective-permute-start(f32[72,128]{1,0:T(8,128)S(1)} %get-tuple-element.28.here_ref), channel_id=1, source_target_pairs={{4,0},{5,1},{0,2},{1,3},{2,4},{3,5},{6,14},{7,15},{12,8},{13,9},{8... | collective-permute-start | bytes 110600 | tf_op jit(solution)/shard_map/ppermute | solution.py:956
  12.1 0.0 collective-permute-done.1.time_ref
  12.2 2.1 %collective-permute-start.3 = (f32[72,128]{1,0:T(8,128)S(1)}, f32[72,128]{1,0:T(8,128)S(1)}, u32[]{:S(2)}, u32[]{:S(2)}) collective-permute-start(f32[72,128]{1,0:T(8,128)S(1)} %get-tuple-element.37.here_side_ref), channel_id=1, source_target_pairs={{0,4},{1,5},{2,6},{3,7},{4,0},{5,1},{6,2},{7,3},{8,12},{9,13},{10,... | collective-permute-start | bytes 110600 | tf_op jit(solution)/shard_map/ppermute | solution.py:941
  14.3 0.9 %collective-permute-start.2 = (f32[64,128]{1,0:T(8,128)S(1)}, f32[64,128]{1,0:T(8,128)S(1)}, u32[]{:S(2)}, u32[]{:S(2)}) collective-permute-start(f32[64,128]{1,0:T(8,128)S(1)} %get-tuple-element.36), channel_id=1, source_target_pairs={{6,2},{7,3},{2,6},{3,7},{0,8},{1,9},{4,12},{5,13},{14,10},{15,11},... | collective-permute-start | bytes 98312 | tf_op jit(solution)/shard_map/ppermute | solution.py:956
  15.2 0.0 collective-permute-done.first_ref
  15.2 3.9 %collective-permute-done.2.second_ref = f32[64,128]{1,0:T(8,128)S(1)} collective-permute-done((f32[64,128]{1,0:T(8,128)S(1)}, f32[64,128]{1,0:T(8,128)S(1)}, u32[]{:S(2)}, u32[]{:S(2)}) %collective-permute-start.2) | collective-permute-done | bytes 32800 | tf_op jit(solution)/shard_map/ppermute | solution.py:956
  19.1 0.0 collective-permute-done.3.there_side_ref
  19.1 0.1 shard_map.51
  19.2 0.7 %shard_map.53 = f32[2,6,2,256]{3,2,1,0:T(2,128)} custom-call(f32[6,8,128]{2,1,0:T(8,128)S(1)} %get-tuple-element.38.side_ref, f32[6,8,128]{2,1,0:T(8,128)S(1)} %get-tuple-element.39.other_ref, f32[14,8,128]{2,1,0:T(8,128)S(1)} %get-tuple-element.40.matrix_ref, f32[72,128]{1,0:T(8,128)S(1)} %collective-permute-done.3.there_side_ref, ...), custom_call_target="tpu_custom_call" | custom-call | tf_op jit(solution)/shard_map/pallas_call | solution.py:1065
  (4 shorter events, 0.1 us)
Async XLA Ops:
  10.2 1.9 %collective-permute-start.1 = (f32[192,128]{1,0:T(8,128)S(1)}, f32[192,128]{1,0:T(8,128)S(1)}, u32[]{:S(2)}, u32[]{:S(2)}) collective-permute-start(f32[192,128]{1,0:T(8,128)S(1)} %shard_map.49), channel_id=1, source_target_pairs={{0,8},{8,0},{16,24},{24,16},{1,9},{9,1},{17,25},{25,17},{2,10},{10... | collective-permute-start | bytes 294920 | tf_op jit(solution)/shard_map/ppermute | solution.py:936
  10.7 4.5 %collective-permute-start = (f32[72,128]{1,0:T(8,128)S(1)}, f32[72,128]{1,0:T(8,128)S(1)}, u32[]{:S(2)}, u32[]{:S(2)}) collective-permute-start(f32[72,128]{1,0:T(8,128)S(1)} %get-tuple-element.28.here_ref), channel_id=1, source_target_pairs={{4,0},{5,1},{0,2},{1,3},{2,4},{3,5},{6,14},{7,15},{12,8},{13,9},{8... | collective-permute-start | bytes 110600 | tf_op jit(solution)/shard_map/ppermute | solution.py:956
  12.2 6.9 %collective-permute-start.3 = (f32[72,128]{1,0:T(8,128)S(1)}, f32[72,128]{1,0:T(8,128)S(1)}, u32[]{:S(2)}, u32[]{:S(2)}) collective-permute-start(f32[72,128]{1,0:T(8,128)S(1)} %get-tuple-element.37.here_side_ref), channel_id=1, source_target_pairs={{0,4},{1,5},{2,6},{3,7},{4,0},{5,1},{6,2},{7,3},{8,12},{9,13},{10,... | collective-permute-start | bytes 110600 | tf_op jit(solution)/shard_map/ppermute | solution.py:941
  14.3 4.8 %collective-permute-start.2 = (f32[64,128]{1,0:T(8,128)S(1)}, f32[64,128]{1,0:T(8,128)S(1)}, u32[]{:S(2)}, u32[]{:S(2)}) collective-permute-start(f32[64,128]{1,0:T(8,128)S(1)} %get-tuple-element.36), channel_id=1, source_target_pairs={{6,2},{7,3},{2,6},{3,7},{0,8},{1,9},{4,12},{5,13},{14,10},{15,11},... | collective-permute-start | bytes 98312 | tf_op jit(solution)/shard_map/ppermute | solution.py:956

commit v33 on v30

--- a/solution.py
+++ b/solution.py
@@ -446,11 +446,21 @@
     return offsets[(2 * shift) % NT], other
 
 
+NEAR_ORDER = ((1, 3), (1, 2), (1, 1), (1, 0), (0, 3), (0, 2), (0, 1), (0, 0))
+FAR_ORDER = ((1, 3), (1, 2), (1, 0), (1, 1), (0, 2), (0, 0), (0, 1), (0, 3))
+
+
 def at_block(ref, y, block):
-    blocks = ref.shape[1]
-    mirrored = lax.axis_index("cell") // blocks
-    place = mirrored * block + (1 - mirrored) * (blocks - 1 - block)
-    return ref.at[ref.shape[0] - 1 - y, place]
+    blocks = ref.shape[0] // 2
+    near = lax.axis_index("cell") < blocks
+    place = 0
+    for n, (near_at, far_at) in enumerate(zip(NEAR_ORDER, FAR_ORDER)):
+        for at, in_half in ((near_at, near), (far_at, jnp.logical_not(near))):
+            if isinstance(block, int) and at[1] != block:
+                continue
+            here = jnp.logical_and(in_half, jnp.logical_and(y == at[0], block == at[1]))
+            place = place + n * here.astype(jnp.int32)
+    return ref.at[place]
 
 
 def cell_plane(ref, y, cell, k):
@@ -464,7 +474,7 @@
     one, three = time_weights(first_inst, 1), time_weights(first_inst, 3)
     near = [jnp.where(core == 0, a, b) for a, b in zip(one, three)]
     away = [jnp.where(core == 0, b, a) for a, b in zip(one, three)]
-    cells = 2 * all_ref.shape[1]
+    cells = 2 * (all_ref.shape[0] // 2)
     for cell in range(cells):
         for k in range(PAIRS):
             here = cell_plane(all_ref, own_y, cell, k)
@@ -602,7 +612,7 @@
 def near_half_kernel(all_ref, next_ref, codes_ref, *refs):
     *results, middle_ref, round_ref, third_ref, line_ref = refs
     own_y = lax.axis_index("inst") >> 1
-    cells = 2 * all_ref.shape[1]
+    cells = 2 * (all_ref.shape[0] // 2)
     for cell in range(cells - MIDDLE_CELLS, cells):
         for k in range(PAIRS):
             row = (cell - (cells - MIDDLE_CELLS)) * CELL_ROWS + k * ROWS
@@ -615,7 +625,7 @@
         third = cell_plane(all_ref, own_y, cells - MIDDLE_CELLS - 1, k)
         third_ref[pl.ds(k * ROWS, ROWS), :] = third
 
-    @pl.when(lax.axis_index("cell") < all_ref.shape[1])
+    @pl.when(lax.axis_index("cell") < (all_ref.shape[0] // 2))
     def _():
         half_kernel(all_ref, next_ref, codes_ref, *results, line_ref)
 
@@ -623,7 +633,7 @@
 def far_half_kernel(all_ref, next_ref, codes_ref, *refs):
     *refs, line_ref = refs
     given, results = refs[: len(refs) // 2], refs[len(refs) // 2 :]
-    far = lax.axis_index("cell") >= all_ref.shape[1]
+    far = lax.axis_index("cell") >= (all_ref.shape[0] // 2)
 
     @pl.when(far)
     def _():
@@ -640,7 +650,7 @@
     line_ref,
 ):
     own_y = lax.axis_index("inst") >> 1
-    blocks = all_ref.shape[1]
+    blocks = (all_ref.shape[0] // 2)
     cells = 2 * blocks
     mirrored = lax.axis_index("cell") // blocks
     sign = (1 - 2 * mirrored).astype(jnp.float32)
@@ -820,7 +830,7 @@
 
 def spread_kernel(all_ref, blocks_ref, sides_ref, known_ref, spread_ref, table_ref):
     own_y = lax.axis_index("inst") >> 1
-    blocks = all_ref.shape[1]
+    blocks = (all_ref.shape[0] // 2)
     own_cell = lax.axis_index("cell")
     own_block = jnp.where(own_cell < blocks, own_cell, 2 * blocks - 1 - own_cell)
     zero = jnp.zeros((ROWS, LANES), jnp.float32)
@@ -931,12 +941,11 @@
 
 
 def share_half(copies):
-    insts, count = lax.axis_size("inst"), lax.axis_size("cell")
-    halves = [range(count // 2 - 1, -1, -1), range(count - 1, count // 2 - 1, -1)]
+    count = lax.axis_size("cell")
     groups = [
-        [inst * count + cell for inst in range(insts - 2 + core, -1, -2) for cell in half]
+        [(2 * y + core) * count + (count - 1 - block if far else block) for y, block in order]
         for core in range(2)
-        for half in halves
+        for far, order in enumerate((NEAR_ORDER, FAR_ORDER))
     ]
     return lax.all_to_all(
         copies, ("inst", "cell"), split_axis=0, concat_axis=0, tiled=True,
@@ -1004,7 +1013,7 @@
         ],
         compiler_params=params,
     )(*held)
-    shared = share_half(packed).reshape(places, blocks, BLOCK_ROWS, LANES)
+    shared = share_half(packed)
     for_partner = pl.pallas_call(
         partner_kernel,
         out_shape=float_shape(cells * CELL_ROWS, LANES),

time: 19.9 us -> 20.6 us (1.035)
  the two profiles are of different devices: /device:TPU:10 before, /device:TPU:8 now
where the time goes in v33:
time: 20.6 us; the launch traced here: 20.4 us
  blocking collectives  9.06 us (44%)
  waiting for transfers between devices  4.67 us (23%)
  starting transfers between devices  4.58 us (22%)
  Pallas kernels  2.04 us (10%)
    all_to_all x1, blocking collectives, share_half(): lax.all_to_all(copies, ('inst', 'cell'), split_axis=0, concat_axis=0, til...  9.06 us
    ppermute x2, waiting for transfers between devices, pass_round(): return lax.ppermute(block, ('inst', 'cell'), pairs)  4.67 us
    ppermute x2, starting transfers between devices, pass_round(): return lax.ppermute(block, ('inst', 'cell'), pairs)  2.67 us
    ppermute x1, starting transfers between devices, swap_halves(): lax.ppermute(block, 'cell', [(i, (i + count // 2) % count) for i in range...  1.85 us
    pallas_call x1, Pallas kernels, local_by_halves(): pl.pallas_call(pack_kernel, out_shape=(float_shape(places * blocks, BLOCK...  0.82 us
    pallas_call x1, Pallas kernels, local_by_halves(): pl.pallas_call(join_kernel, out_shape=float_shape(*state.shape), in_specs...  0.66 us
  transfers between devices with their start and end apart: 4, of which 1 were waited for; matrix products, arithmetic and copies ran while one was open for 0% of the time, Pallas kernels for 2%

profile of v33, /device:TPU:8, one launch (start us, length us, event | category | flops | bytes accessed | tf_op | source)
XLA Modules:
  0.0 20.4 jit_solution(12957527198199100206)
XLA Ops:
  0.0 0.8 %shard_map.46 = (f32[8,56,128]{2,1,0:T(8,128)S(1)}, s32[256]{0:T(256)S(1)}, s32[2,8]{1,0:T(2,128)S(1)}) custom-call(f32[2,6,2,256]{3,2,1,0:T(2,128)} %held_state_ref.1, f32[2,256]{1,0:T(2,128)} %held_rate_ref.1, s32[256]{0:T(256)} %held_next_ref.1, s32[2,8]{1,0:T(2,128)} %held_codes_ref.1), custom_call_target="tpu_custom_call" | custom-call | tf_op jit(solution)/shard_map/pallas_call | solution.py:1000
  0.8 9.1 %all_to_all.5.all_ref = f32[8,56,128]{2,1,0:T(8,128)S(1)} all-to-all(f32[8,56,128]{2,1,0:T(8,128)S(1)} %get-tuple-element.27), channel_id=1, replica_groups={{19,18,17,16,3,2,1,0},{20,21,23,22,5,7,6,4},{27,26,25,24,11,10,9,8},{28..., dimensions={0} | all-to-all | bytes 458752 | tf_op jit(solution)/shard_map/all_to_all | solution.py:950
  9.9 0.1 collective-permute-start.1
  10.0 0.4 %shard_map.47 = (f32[8,3,8,128]{3,2,1,0:T(8,128)S(1)}, f32[3,4,8,128]{3,2,1,0:T(8,128)S(1)}, f32[3,7,8,128]{3,2,1,0:T(8,128)S(1)}, f32[16,128]{1,0:T(8,128)S(1)}...) custom-call(f32[8,56,128]{2,1,0:T(8,128)S(1)} %all_to_all.5.all_ref, ...), custom_call_target="tpu_custom_call" | custom-call | tf_op jit(solution)/shard_map/pallas_call | solution.py:1034
  10.4 2.7 %collective-permute-start = (f32[96,128]{1,0:T(8,128)S(1)}, f32[96,128]{1,0:T(8,128)S(1)}, u32[]{:S(2)}, u32[]{:S(2)}) collective-permute-start(f32[96,128]{1,0:T(8,128)S(1)} %get-tuple-element.31), channel_id=1, source_target_pairs={{4,0},{5,1},{0,2},{1,3},{2,6},{3,7},{6,4},{7,5},{12,8},{13,9},{8,1... | collective-permute-start | bytes 147464 | tf_op jit(solution)/shard_map/ppermute | solution.py:978
  13.1 0.0 collective-permute-done.1.time_ref
  13.1 1.8 %collective-permute-start.3 = (f32[88,128]{1,0:T(8,128)S(1)}, f32[88,128]{1,0:T(8,128)S(1)}, u32[]{:S(2)}, u32[]{:S(2)}) collective-permute-start(f32[88,128]{1,0:T(8,128)S(1)} %get-tuple-element.41.here_side_ref), channel_id=1, source_target_pairs={{0,4},{1,5},{2,6},{3,7},{4,0},{5,1},{6,2},{7,3},{8,12},{9,13},{10,... | collective-permute-start | bytes 135176 | tf_op jit(solution)/shard_map/ppermute | solution.py:963
  15.0 0.0 collective-permute-start.2
  15.0 0.0 collective-permute-done.first_ref
  15.0 4.7 %collective-permute-done.2.second_ref = f32[48,128]{1,0:T(8,128)S(1)} collective-permute-done((f32[48,128]{1,0:T(8,128)S(1)}, f32[48,128]{1,0:T(8,128)S(1)}, u32[]{:S(2)}, u32[]{:S(2)}) %collective-permute-start.2) | collective-permute-done | bytes 24608 | tf_op jit(solution)/shard_map/ppermute | solution.py:978
  19.7 0.0 collective-permute-done.3.there_side_ref
  19.7 0.1 shard_map.51
  19.8 0.7 %shard_map.53 = f32[2,6,2,256]{3,2,1,0:T(2,128)} custom-call(f32[6,8,128]{2,1,0:T(8,128)S(1)} %get-tuple-element.42.side_ref, f32[6,8,128]{2,1,0:T(8,128)S(1)} %get-tuple-element.43.other_ref, f32[14,8,128]{2,1,0:T(8,128)S(1)} %get-tuple-element.44.matrix_ref, f32[88,128]{1,0:T(8,128)S(1)} %collective-permute-done.3.there_side_ref, ...), custom_call_target="tpu_custom_call" | custom-call | tf_op jit(solution)/shard_map/pallas_call | solution.py:1091
  (4 shorter events, 0.1 us)
Async XLA Ops:
  9.9 3.1 %collective-permute-start.1 = (f32[192,128]{1,0:T(8,128)S(1)}, f32[192,128]{1,0:T(8,128)S(1)}, u32[]{:S(2)}, u32[]{:S(2)}) collective-permute-start(f32[192,128]{1,0:T(8,128)S(1)} %shard_map.49), channel_id=1, source_target_pairs={{0,8},{8,0},{16,24},{24,16},{1,9},{9,1},{17,25},{25,17},{2,10},{10... | collective-permute-start | bytes 294920 | tf_op jit(solution)/shard_map/ppermute | solution.py:958
  10.4 4.6 %collective-permute-start = (f32[96,128]{1,0:T(8,128)S(1)}, f32[96,128]{1,0:T(8,128)S(1)}, u32[]{:S(2)}, u32[]{:S(2)}) collective-permute-start(f32[96,128]{1,0:T(8,128)S(1)} %get-tuple-element.31), channel_id=1, source_target_pairs={{4,0},{5,1},{0,2},{1,3},{2,6},{3,7},{6,4},{7,5},{12,8},{13,9},{8,1... | collective-permute-start | bytes 147464 | tf_op jit(solution)/shard_map/ppermute | solution.py:978
  13.1 6.6 %collective-permute-start.3 = (f32[88,128]{1,0:T(8,128)S(1)}, f32[88,128]{1,0:T(8,128)S(1)}, u32[]{:S(2)}, u32[]{:S(2)}) collective-permute-start(f32[88,128]{1,0:T(8,128)S(1)} %get-tuple-element.41.here_side_ref), channel_id=1, source_target_pairs={{0,4},{1,5},{2,6},{3,7},{4,0},{5,1},{6,2},{7,3},{8,12},{9,13},{10,... | collective-permute-start | bytes 135176 | tf_op jit(solution)/shard_map/ppermute | solution.py:963
  15.0 4.7 %collective-permute-start.2 = (f32[48,128]{1,0:T(8,128)S(1)}, f32[48,128]{1,0:T(8,128)S(1)}, u32[]{:S(2)}, u32[]{:S(2)}) collective-permute-start(f32[48,128]{1,0:T(8,128)S(1)} %get-tuple-element.40), channel_id=1, source_target_pairs={{6,2},{7,3},{2,4},{3,5},{4,6},{5,7},{0,8},{1,9},{14,10},{15,11},{1... | collective-permute-start | bytes 73736 | tf_op jit(solution)/shard_map/ppermute | solution.py:978

commit v34 on v33

--- a/solution.py
+++ b/solution.py
@@ -447,7 +447,7 @@
 
 
 NEAR_ORDER = ((1, 3), (1, 2), (1, 1), (1, 0), (0, 3), (0, 2), (0, 1), (0, 0))
-FAR_ORDER = ((1, 3), (1, 2), (1, 0), (1, 1), (0, 2), (0, 0), (0, 1), (0, 3))
+FAR_ORDER = ((1, 3), (1, 2), (1, 1), (1, 0), (0, 0), (0, 1), (0, 2), (0, 3))
 
 
 def at_block(ref, y, block):

time: 20.6 us -> 20.6 us (level)
  no operation moved by 1% of the time
where the time goes in v34:
time: 20.6 us; the launch traced here: 20.4 us
  blocking collectives  9.06 us (44%)
  waiting for transfers between devices  4.67 us (23%)
  starting transfers between devices  4.59 us (22%)
  Pallas kernels  2.04 us (10%)
    all_to_all x1, blocking collectives, share_half(): lax.all_to_all(copies, ('inst', 'cell'), split_axis=0, concat_axis=0, til...  9.06 us
    ppermute x2, waiting for transfers between devices, pass_round(): return lax.ppermute(block, ('inst', 'cell'), pairs)  4.67 us
    ppermute x2, starting transfers between devices, pass_round(): return lax.ppermute(block, ('inst', 'cell'), pairs)  2.67 us
    ppermute x1, starting transfers between devices, swap_halves(): lax.ppermute(block, 'cell', [(i, (i + count // 2) % count) for i in range...  1.85 us
    pallas_call x1, Pallas kernels, local_by_halves(): pl.pallas_call(pack_kernel, out_shape=(float_shape(places * blocks, BLOCK...  0.82 us
    pallas_call x1, Pallas kernels, local_by_halves(): pl.pallas_call(join_kernel, out_shape=float_shape(*state.shape), in_specs...  0.66 us
  transfers between devices with their start and end apart: 4, of which 1 were waited for; matrix products, arithmetic and copies ran while one was open for 0% of the time, Pallas kernels for 2%

profile of v34, /device:TPU:8, one launch (start us, length us, event | category | flops | bytes accessed | tf_op | source)
XLA Modules:
  0.0 20.4 jit_solution(5682426633361579507)
XLA Ops:
  0.0 0.8 %shard_map.46 = (f32[8,56,128]{2,1,0:T(8,128)S(1)}, s32[256]{0:T(256)S(1)}, s32[2,8]{1,0:T(2,128)S(1)}) custom-call(f32[2,6,2,256]{3,2,1,0:T(2,128)} %held_state_ref.1, f32[2,256]{1,0:T(2,128)} %held_rate_ref.1, s32[256]{0:T(256)} %held_next_ref.1, s32[2,8]{1,0:T(2,128)} %held_codes_ref.1), custom_call_target="tpu_custom_call" | custom-call | tf_op jit(solution)/shard_map/pallas_call | solution.py:1000
  0.8 9.1 %all_to_all.5.all_ref = f32[8,56,128]{2,1,0:T(8,128)S(1)} all-to-all(f32[8,56,128]{2,1,0:T(8,128)S(1)} %get-tuple-element.27), channel_id=1, replica_groups={{19,18,17,16,3,2,1,0},{20,21,22,23,7,6,5,4},{27,26,25,24,11,10,9,8},{28..., dimensions={0} | all-to-all | bytes 458752 | tf_op jit(solution)/shard_map/all_to_all | solution.py:950
  9.9 0.1 collective-permute-start.1
  10.0 0.4 %shard_map.47 = (f32[8,3,8,128]{3,2,1,0:T(8,128)S(1)}, f32[3,4,8,128]{3,2,1,0:T(8,128)S(1)}, f32[3,7,8,128]{3,2,1,0:T(8,128)S(1)}, f32[16,128]{1,0:T(8,128)S(1)}...) custom-call(f32[8,56,128]{2,1,0:T(8,128)S(1)} %all_to_all.5.all_ref, ...), custom_call_target="tpu_custom_call" | custom-call | tf_op jit(solution)/shard_map/pallas_call | solution.py:1034
  10.4 2.7 %collective-permute-start = (f32[96,128]{1,0:T(8,128)S(1)}, f32[96,128]{1,0:T(8,128)S(1)}, u32[]{:S(2)}, u32[]{:S(2)}) collective-permute-start(f32[96,128]{1,0:T(8,128)S(1)} %get-tuple-element.31), channel_id=1, source_target_pairs={{4,0},{5,1},{0,2},{1,3},{2,6},{3,7},{6,4},{7,5},{12,8},{13,9},{8,1... | collective-permute-start | bytes 147464 | tf_op jit(solution)/shard_map/ppermute | solution.py:978
  13.1 0.0 collective-permute-done.1.time_ref
  13.1 1.8 %collective-permute-start.3 = (f32[88,128]{1,0:T(8,128)S(1)}, f32[88,128]{1,0:T(8,128)S(1)}, u32[]{:S(2)}, u32[]{:S(2)}) collective-permute-start(f32[88,128]{1,0:T(8,128)S(1)} %get-tuple-element.41.here_side_ref), channel_id=1, source_target_pairs={{0,4},{1,5},{2,6},{3,7},{4,0},{5,1},{6,2},{7,3},{8,12},{9,13},{10,... | collective-permute-start | bytes 135176 | tf_op jit(solution)/shard_map/ppermute | solution.py:963
  15.0 0.0 collective-permute-start.2
  15.0 0.0 collective-permute-done.first_ref
  15.0 4.7 %collective-permute-done.2.second_ref = f32[48,128]{1,0:T(8,128)S(1)} collective-permute-done((f32[48,128]{1,0:T(8,128)S(1)}, f32[48,128]{1,0:T(8,128)S(1)}, u32[]{:S(2)}, u32[]{:S(2)}) %collective-permute-start.2) | collective-permute-done | bytes 24608 | tf_op jit(solution)/shard_map/ppermute | solution.py:978
  19.7 0.0 collective-permute-done.3.there_side_ref
  19.7 0.1 shard_map.51
  19.8 0.7 %shard_map.53 = f32[2,6,2,256]{3,2,1,0:T(2,128)} custom-call(f32[6,8,128]{2,1,0:T(8,128)S(1)} %get-tuple-element.42.side_ref, f32[6,8,128]{2,1,0:T(8,128)S(1)} %get-tuple-element.43.other_ref, f32[14,8,128]{2,1,0:T(8,128)S(1)} %get-tuple-element.44.matrix_ref, f32[88,128]{1,0:T(8,128)S(1)} %collective-permute-done.3.there_side_ref, ...), custom_call_target="tpu_custom_call" | custom-call | tf_op jit(solution)/shard_map/pallas_call | solution.py:1091
  (4 shorter events, 0.1 us)
Async XLA Ops:
  9.9 3.1 %collective-permute-start.1 = (f32[192,128]{1,0:T(8,128)S(1)}, f32[192,128]{1,0:T(8,128)S(1)}, u32[]{:S(2)}, u32[]{:S(2)}) collective-permute-start(f32[192,128]{1,0:T(8,128)S(1)} %shard_map.49), channel_id=1, source_target_pairs={{0,8},{8,0},{16,24},{24,16},{1,9},{9,1},{17,25},{25,17},{2,10},{10... | collective-permute-start | bytes 294920 | tf_op jit(solution)/shard_map/ppermute | solution.py:958
  10.4 4.6 %collective-permute-start = (f32[96,128]{1,0:T(8,128)S(1)}, f32[96,128]{1,0:T(8,128)S(1)}, u32[]{:S(2)}, u32[]{:S(2)}) collective-permute-start(f32[96,128]{1,0:T(8,128)S(1)} %get-tuple-element.31), channel_id=1, source_target_pairs={{4,0},{5,1},{0,2},{1,3},{2,6},{3,7},{6,4},{7,5},{12,8},{13,9},{8,1... | collective-permute-start | bytes 147464 | tf_op jit(solution)/shard_map/ppermute | solution.py:978
  13.1 6.6 %collective-permute-start.3 = (f32[88,128]{1,0:T(8,128)S(1)}, f32[88,128]{1,0:T(8,128)S(1)}, u32[]{:S(2)}, u32[]{:S(2)}) collective-permute-start(f32[88,128]{1,0:T(8,128)S(1)} %get-tuple-element.41.here_side_ref), channel_id=1, source_target_pairs={{0,4},{1,5},{2,6},{3,7},{4,0},{5,1},{6,2},{7,3},{8,12},{9,13},{10,... | collective-permute-start | bytes 135176 | tf_op jit(solution)/shard_map/ppermute | solution.py:963
  15.0 4.7 %collective-permute-start.2 = (f32[48,128]{1,0:T(8,128)S(1)}, f32[48,128]{1,0:T(8,128)S(1)}, u32[]{:S(2)}, u32[]{:S(2)}) collective-permute-start(f32[48,128]{1,0:T(8,128)S(1)} %get-tuple-element.40), channel_id=1, source_target_pairs={{6,2},{7,3},{2,4},{3,5},{4,6},{5,7},{0,8},{1,9},{14,10},{15,11},{1... | collective-permute-start | bytes 73736 | tf_op jit(solution)/shard_map/ppermute | solution.py:978

commit v35 on v30

--- a/solution.py
+++ b/solution.py
@@ -615,7 +615,7 @@
         third = cell_plane(all_ref, own_y, cells - MIDDLE_CELLS - 1, k)
         third_ref[pl.ds(k * ROWS, ROWS), :] = third
 
-    @pl.when(lax.axis_index("cell") < all_ref.shape[1])
+    @pl.when(lax.axis_index("cell") // (all_ref.shape[1] // 2) == 1)
     def _():
         half_kernel(all_ref, next_ref, codes_ref, *results, line_ref)
 
@@ -623,7 +623,7 @@
 def far_half_kernel(all_ref, next_ref, codes_ref, *refs):
     *refs, line_ref = refs
     given, results = refs[: len(refs) // 2], refs[len(refs) // 2 :]
-    far = lax.axis_index("cell") >= all_ref.shape[1]
+    far = lax.axis_index("cell") // (all_ref.shape[1] // 2) != 1
 
     @pl.when(far)
     def _():

time: 19.9 us -> 19.9 us (level)
  the two profiles are of different devices: /device:TPU:10 before, /device:TPU:0 now
where the time goes in v35:
time: 19.9 us; the launch traced here: 19.6 us
  blocking collectives  10.9 us (55%)
  starting transfers between devices  3.61 us (18%)
  waiting for transfers between devices  2.97 us (15%)
  Pallas kernels  2.02 us (10%)
    all_to_all x1, blocking collectives, share_half(): lax.all_to_all(copies, ('inst', 'cell'), split_axis=0, concat_axis=0, til...  10.9 us
    ppermute x1, starting transfers between devices, swap_halves(): lax.ppermute(block, 'cell', [(i, (i + count // 2) % count) for i in range...  2 us
    ppermute x1, waiting for transfers between devices, swap_halves(): lax.ppermute(block, 'cell', [(i, (i + count // 2) % count) for i in range...  1.81 us
    ppermute x2, starting transfers between devices, pass_round(): return lax.ppermute(block, ('inst', 'cell'), pairs)  1.54 us
    ppermute x2, waiting for transfers between devices, pass_round(): return lax.ppermute(block, ('inst', 'cell'), pairs)  1.16 us
    pallas_call x1, Pallas kernels, local_by_halves(): pl.pallas_call(pack_kernel, out_shape=(float_shape(places * blocks, BLOCK...  0.82 us
    pallas_call x1, Pallas kernels, local_by_halves(): pl.pallas_call(join_kernel, out_shape=float_shape(*state.shape), in_specs...  0.66 us
  transfers between devices with their start and end apart: 4, of which 3 were waited for; matrix products, arithmetic and copies ran while one was open for 0% of the time, Pallas kernels for 2%

profile of v35, /device:TPU:0, one launch (start us, length us, event | category | flops | bytes accessed | tf_op | source)
XLA Modules:
  0.0 19.6 jit_solution(14178775688614210472)
XLA Ops:
  0.0 0.8 %shard_map.46 = (f32[8,56,128]{2,1,0:T(8,128)S(1)}, s32[256]{0:T(256)S(1)}, s32[2,8]{1,0:T(2,128)S(1)}) custom-call(f32[2,6,2,256]{3,2,1,0:T(2,128)} %held_state_ref.1, f32[2,256]{1,0:T(2,128)} %held_rate_ref.1, s32[256]{0:T(256)} %held_next_ref.1, s32[2,8]{1,0:T(2,128)} %held_codes_ref.1), custom_call_target="tpu_custom_call" | custom-call | tf_op jit(solution)/shard_map/pallas_call | solution.py:991
  0.8 10.9 %all_to_all.5 = f32[8,56,128]{2,1,0:T(8,128)S(1)} all-to-all(f32[8,56,128]{2,1,0:T(8,128)S(1)} %get-tuple-element.27), channel_id=1, replica_groups={{19,18,17,16,3,2,1,0},{23,22,21,20,7,6,5,4},{27,26,25,24,11,10,9,8},{31..., dimensions={0} | all-to-all | bytes 458752 | tf_op jit(solution)/shard_map/all_to_all | solution.py:941
  11.8 0.1 collective-permute-start.1
  11.9 1.5 %collective-permute-start = (f32[96,128]{1,0:T(8,128)S(1)}, f32[96,128]{1,0:T(8,128)S(1)}, u32[]{:S(2)}, u32[]{:S(2)}) collective-permute-start(f32[96,128]{1,0:T(8,128)S(1)} %get-tuple-element.31), channel_id=1, source_target_pairs={{4,0},{5,1},{0,2},{1,3},{2,6},{3,7},{6,4},{7,5},{12,8},{13,9},{8,1... | collective-permute-start | bytes 147464 | tf_op jit(solution)/shard_map/ppermute | solution.py:969
  13.5 0.3 %shard_map.48 = (f32[8,3,8,128]{3,2,1,0:T(8,128)S(1)}, f32[3,4,8,128]{3,2,1,0:T(8,128)S(1)}, f32[3,7,8,128]{3,2,1,0:T(8,128)S(1)}, f32[16,128]{1,0:T(8,128)S(1)}) custom-call(f32[2,4,56,128]{3,2,1,0:T(8,128)S(1)} %bitcast.3, s32[256]{0:T(256)S(1)} %get-tuple-element.28.next_ref, ...), custom_call_target="tpu_custom_call", output_to_operand_aliasing={{0}: (3, {}), {1}: (4, {}), {2}: (5, {}), {3}: (6, {})} | custom-call | flops 1000000 | bytes 1000000 | tf_op jit(solution)/shard_map/pallas_call | solution.py:1039
  13.8 0.0 collective-permute-done.1.time_ref
  13.9 2.0 %collective-permute-start.3 = (f32[88,128]{1,0:T(8,128)S(1)}, f32[88,128]{1,0:T(8,128)S(1)}, u32[]{:S(2)}, u32[]{:S(2)}) collective-permute-start(f32[88,128]{1,0:T(8,128)S(1)} %get-tuple-element.41.here_side_ref), channel_id=1, source_target_pairs={{0,4},{1,5},{2,6},{3,7},{4,0},{5,1},{6,2},{7,3},{8,12},{9,13},{10,... | collective-permute-start | bytes 135176 | tf_op jit(solution)/shard_map/ppermute | solution.py:954
  15.9 0.0 collective-permute-start.2
  15.9 1.1 %collective-permute-done.first_ref = f32[96,128]{1,0:T(8,128)S(1)} collective-permute-done((f32[96,128]{1,0:T(8,128)S(1)}, f32[96,128]{1,0:T(8,128)S(1)}, u32[]{:S(2)}, u32[]{:S(2)}) %collective-permute-start) | collective-permute-done | bytes 49184 | tf_op jit(solution)/shard_map/ppermute | solution.py:969
  17.0 0.1 collective-permute-done.2.second_ref
  17.1 1.8 %collective-permute-done.3.there_side_ref = f32[88,128]{1,0:T(8,128)S(1)} collective-permute-done((f32[88,128]{1,0:T(8,128)S(1)}, f32[88,128]{1,0:T(8,128)S(1)}, u32[]{:S(2)}, u32[]{:S(2)}) %collective-permute-start.3) | collective-permute-done | bytes 45088 | tf_op jit(solution)/shard_map/ppermute | solution.py:954
  18.9 0.1 shard_map.51
  18.9 0.7 %shard_map.53 = f32[2,6,2,256]{3,2,1,0:T(2,128)} custom-call(f32[6,8,128]{2,1,0:T(8,128)S(1)} %get-tuple-element.42.side_ref, f32[6,8,128]{2,1,0:T(8,128)S(1)} %get-tuple-element.43.other_ref, f32[14,8,128]{2,1,0:T(8,128)S(1)} %get-tuple-element.44.matrix_ref, f32[88,128]{1,0:T(8,128)S(1)} %collective-permute-done.3.there_side_ref, ...), custom_call_target="tpu_custom_call" | custom-call | tf_op jit(solution)/shard_map/pallas_call | solution.py:1082
  (4 shorter events, 0.1 us)
Async XLA Ops:
  11.8 2.0 %collective-permute-start.1 = (f32[192,128]{1,0:T(8,128)S(1)}, f32[192,128]{1,0:T(8,128)S(1)}, u32[]{:S(2)}, u32[]{:S(2)}) collective-permute-start(f32[192,128]{1,0:T(8,128)S(1)} %shard_map.49), channel_id=1, source_target_pairs={{0,8},{8,0},{16,24},{24,16},{1,9},{9,1},{17,25},{25,17},{2,10},{10... | collective-permute-start | bytes 294920 | tf_op jit(solution)/shard_map/ppermute | solution.py:949
  11.9 5.0 %collective-permute-start = (f32[96,128]{1,0:T(8,128)S(1)}, f32[96,128]{1,0:T(8,128)S(1)}, u32[]{:S(2)}, u32[]{:S(2)}) collective-permute-start(f32[96,128]{1,0:T(8,128)S(1)} %get-tuple-element.31), channel_id=1, source_target_pairs={{4,0},{5,1},{0,2},{1,3},{2,6},{3,7},{6,4},{7,5},{12,8},{13,9},{8,1... | collective-permute-start | bytes 147464 | tf_op jit(solution)/shard_map/ppermute | solution.py:969
  13.9 5.0 %collective-permute-start.3 = (f32[88,128]{1,0:T(8,128)S(1)}, f32[88,128]{1,0:T(8,128)S(1)}, u32[]{:S(2)}, u32[]{:S(2)}) collective-permute-start(f32[88,128]{1,0:T(8,128)S(1)} %get-tuple-element.41.here_side_ref), channel_id=1, source_target_pairs={{0,4},{1,5},{2,6},{3,7},{4,0},{5,1},{6,2},{7,3},{8,12},{9,13},{10,... | collective-permute-start | bytes 135176 | tf_op jit(solution)/shard_map/ppermute | solution.py:954
  15.9 1.2 %collective-permute-start.2 = (f32[48,128]{1,0:T(8,128)S(1)}, f32[48,128]{1,0:T(8,128)S(1)}, u32[]{:S(2)}, u32[]{:S(2)}) collective-permute-start(f32[48,128]{1,0:T(8,128)S(1)} %get-tuple-element.40), channel_id=1, source_target_pairs={{6,2},{7,3},{2,4},{3,5},{4,6},{5,7},{0,8},{1,9},{14,10},{15,11},{1... | collective-permute-start | bytes 73736 | tf_op jit(solution)/shard_map/ppermute | solution.py:969

commit v36 on v32

--- a/solution.py
+++ b/solution.py
@@ -608,7 +608,7 @@
             plane = cell_plane(all_ref, own_y, cells - 1 - back, k)
             middle_ref[pl.ds(n * CELL_ROWS + k * ROWS, ROWS), :] = plane
 
-    @pl.when(lax.axis_index("cell") < all_ref.shape[1])
+    @pl.when(lax.axis_index("cell") // (all_ref.shape[1] // 2) == 1)
     def _():
         half_kernel(all_ref, next_ref, codes_ref, *results, line_ref)
 
@@ -616,7 +616,7 @@
 def far_half_kernel(all_ref, next_ref, codes_ref, *refs):
     *refs, line_ref = refs
     given, results = refs[: len(refs) // 2], refs[len(refs) // 2 :]
-    far = lax.axis_index("cell") >= all_ref.shape[1]
+    far = lax.axis_index("cell") // (all_ref.shape[1] // 2) != 1
 
     @pl.when(far)
     def _():

time: 20 us -> 20.1 us (level)
  the two profiles are of different devices: /device:TPU:10 before, /device:TPU:0 now
where the time goes in v36:
time: 20.1 us; the launch traced here: 19.9 us
  blocking collectives  10.9 us (54%)
  starting transfers between devices  3.61 us (18%)
  waiting for transfers between devices  3.24 us (16%)
  Pallas kernels  2.02 us (10%)
    all_to_all x1, blocking collectives, share_half(): lax.all_to_all(copies, ('inst', 'cell'), split_axis=0, concat_axis=0, til...  10.9 us
    ppermute x1, waiting for transfers between devices, swap_halves(): lax.ppermute(block, 'cell', [(i, (i + count // 2) % count) for i in range...  2.07 us
    ppermute x1, starting transfers between devices, swap_halves(): lax.ppermute(block, 'cell', [(i, (i + count // 2) % count) for i in range...  2.01 us
    ppermute x2, starting transfers between devices, pass_round(): return lax.ppermute(block, ('inst', 'cell'), pairs)  1.54 us
    ppermute x2, waiting for transfers between devices, pass_round(): return lax.ppermute(block, ('inst', 'cell'), pairs)  1.17 us
    pallas_call x1, Pallas kernels, local_by_halves(): pl.pallas_call(pack_kernel, out_shape=(float_shape(places * blocks, BLOCK...  0.82 us
    pallas_call x1, Pallas kernels, local_by_halves(): pl.pallas_call(join_kernel, out_shape=float_shape(*state.shape), in_specs...  0.66 us
  transfers between devices with their start and end apart: 4, of which 3 were waited for; matrix products, arithmetic and copies ran while one was open for 0% of the time, Pallas kernels for 2%

profile of v36, /device:TPU:0, one launch (start us, length us, event | category | flops | bytes accessed | tf_op | source)
XLA Modules:
  0.0 19.9 jit_solution(9652983662203395940)
XLA Ops:
  0.0 0.8 %shard_map.46 = (f32[8,56,128]{2,1,0:T(8,128)S(1)}, s32[256]{0:T(256)S(1)}, s32[2,8]{1,0:T(2,128)S(1)}) custom-call(f32[2,6,2,256]{3,2,1,0:T(2,128)} %held_state_ref.1, f32[2,256]{1,0:T(2,128)} %held_rate_ref.1, s32[256]{0:T(256)} %held_next_ref.1, s32[2,8]{1,0:T(2,128)} %held_codes_ref.1), custom_call_target="tpu_custom_call" | custom-call | tf_op jit(solution)/shard_map/pallas_call | solution.py:978
  0.8 10.9 %all_to_all.5 = f32[8,56,128]{2,1,0:T(8,128)S(1)} all-to-all(f32[8,56,128]{2,1,0:T(8,128)S(1)} %get-tuple-element.25), channel_id=1, replica_groups={{19,18,17,16,3,2,1,0},{23,22,21,20,7,6,5,4},{27,26,25,24,11,10,9,8},{31..., dimensions={0} | all-to-all | bytes 458752 | tf_op jit(solution)/shard_map/all_to_all | solution.py:928
  11.8 0.1 collective-permute-start.1
  11.9 1.5 %collective-permute-start = (f32[72,128]{1,0:T(8,128)S(1)}, f32[72,128]{1,0:T(8,128)S(1)}, u32[]{:S(2)}, u32[]{:S(2)}) collective-permute-start(f32[72,128]{1,0:T(8,128)S(1)} %get-tuple-element.28.here_ref), channel_id=1, source_target_pairs={{4,0},{5,1},{0,2},{1,3},{2,4},{3,5},{6,14},{7,15},{12,8},{13,9},{8... | collective-permute-start | bytes 110600 | tf_op jit(solution)/shard_map/ppermute | solution.py:956
  13.5 0.3 %shard_map.48 = (f32[8,3,8,128]{3,2,1,0:T(8,128)S(1)}, f32[3,4,8,128]{3,2,1,0:T(8,128)S(1)}, f32[3,7,8,128]{3,2,1,0:T(8,128)S(1)}, f32[16,128]{1,0:T(8,128)S(1)}) custom-call(f32[2,4,56,128]{3,2,1,0:T(8,128)S(1)} %bitcast.3, s32[256]{0:T(256)S(1)} %get-tuple-element.26.next_ref, ...), custom_call_target="tpu_custom_call", output_to_operand_aliasing={{0}: (3, {}), {1}: (4, {}), {2}: (5, {}), {3}: (6, {})} | custom-call | flops 1000000 | bytes 1000000 | tf_op jit(solution)/shard_map/pallas_call | solution.py:1022
  13.8 0.0 collective-permute-done.1.time_ref
  13.8 2.0 %collective-permute-start.3 = (f32[72,128]{1,0:T(8,128)S(1)}, f32[72,128]{1,0:T(8,128)S(1)}, u32[]{:S(2)}, u32[]{:S(2)}) collective-permute-start(f32[72,128]{1,0:T(8,128)S(1)} %get-tuple-element.37.here_side_ref), channel_id=1, source_target_pairs={{0,4},{1,5},{2,6},{3,7},{4,0},{5,1},{6,2},{7,3},{8,12},{9,13},{10,... | collective-permute-start | bytes 110600 | tf_op jit(solution)/shard_map/ppermute | solution.py:941
  15.9 0.0 collective-permute-start.2
  15.9 0.9 %collective-permute-done.first_ref = f32[72,128]{1,0:T(8,128)S(1)} collective-permute-done((f32[72,128]{1,0:T(8,128)S(1)}, f32[72,128]{1,0:T(8,128)S(1)}, u32[]{:S(2)}, u32[]{:S(2)}) %collective-permute-start) | collective-permute-done | bytes 36896 | tf_op jit(solution)/shard_map/ppermute | solution.py:956
  16.8 0.2 %collective-permute-done.2.second_ref = f32[64,128]{1,0:T(8,128)S(1)} collective-permute-done((f32[64,128]{1,0:T(8,128)S(1)}, f32[64,128]{1,0:T(8,128)S(1)}, u32[]{:S(2)}, u32[]{:S(2)}) %collective-permute-start.2) | collective-permute-done | bytes 32800 | tf_op jit(solution)/shard_map/ppermute | solution.py:956
  17.1 2.1 %collective-permute-done.3.there_side_ref = f32[72,128]{1,0:T(8,128)S(1)} collective-permute-done((f32[72,128]{1,0:T(8,128)S(1)}, f32[72,128]{1,0:T(8,128)S(1)}, u32[]{:S(2)}, u32[]{:S(2)}) %collective-permute-start.3) | collective-permute-done | bytes 36896 | tf_op jit(solution)/shard_map/ppermute | solution.py:941
  19.1 0.1 shard_map.51
  19.2 0.7 %shard_map.53 = f32[2,6,2,256]{3,2,1,0:T(2,128)} custom-call(f32[6,8,128]{2,1,0:T(8,128)S(1)} %get-tuple-element.38.side_ref, f32[6,8,128]{2,1,0:T(8,128)S(1)} %get-tuple-element.39.other_ref, f32[14,8,128]{2,1,0:T(8,128)S(1)} %get-tuple-element.40.matrix_ref, f32[72,128]{1,0:T(8,128)S(1)} %collective-permute-done.3.there_side_ref, ...), custom_call_target="tpu_custom_call" | custom-call | tf_op jit(solution)/shard_map/pallas_call | solution.py:1065
  (4 shorter events, 0.1 us)
Async XLA Ops:
  11.8 2.0 %collective-permute-start.1 = (f32[192,128]{1,0:T(8,128)S(1)}, f32[192,128]{1,0:T(8,128)S(1)}, u32[]{:S(2)}, u32[]{:S(2)}) collective-permute-start(f32[192,128]{1,0:T(8,128)S(1)} %shard_map.49), channel_id=1, source_target_pairs={{0,8},{8,0},{16,24},{24,16},{1,9},{9,1},{17,25},{25,17},{2,10},{10... | collective-permute-start | bytes 294920 | tf_op jit(solution)/shard_map/ppermute | solution.py:936
  11.9 4.9 %collective-permute-start = (f32[72,128]{1,0:T(8,128)S(1)}, f32[72,128]{1,0:T(8,128)S(1)}, u32[]{:S(2)}, u32[]{:S(2)}) collective-permute-start(f32[72,128]{1,0:T(8,128)S(1)} %get-tuple-element.28.here_ref), channel_id=1, source_target_pairs={{4,0},{5,1},{0,2},{1,3},{2,4},{3,5},{6,14},{7,15},{12,8},{13,9},{8... | collective-permute-start | bytes 110600 | tf_op jit(solution)/shard_map/ppermute | solution.py:956
  13.8 5.3 %collective-permute-start.3 = (f32[72,128]{1,0:T(8,128)S(1)}, f32[72,128]{1,0:T(8,128)S(1)}, u32[]{:S(2)}, u32[]{:S(2)}) collective-permute-start(f32[72,128]{1,0:T(8,128)S(1)} %get-tuple-element.37.here_side_ref), channel_id=1, source_target_pairs={{0,4},{1,5},{2,6},{3,7},{4,0},{5,1},{6,2},{7,3},{8,12},{9,13},{10,... | collective-permute-start | bytes 110600 | tf_op jit(solution)/shard_map/ppermute | solution.py:941
  15.9 1.2 %collective-permute-start.2 = (f32[64,128]{1,0:T(8,128)S(1)}, f32[64,128]{1,0:T(8,128)S(1)}, u32[]{:S(2)}, u32[]{:S(2)}) collective-permute-start(f32[64,128]{1,0:T(8,128)S(1)} %get-tuple-element.36), channel_id=1, source_target_pairs={{6,2},{7,3},{2,6},{3,7},{0,8},{1,9},{4,12},{5,13},{14,10},{15,11},... | collective-permute-start | bytes 98312 | tf_op jit(solution)/shard_map/ppermute | solution.py:956
